TPU v7x, 512 devices: a whole 4x4x16 slice. The times are simulated.
512 devices in a mesh: prow: 32 (over x, y, core), hrow: 16 (over z).
Axes of the slice: x: 4, y: 4, z: 16, core: 2. Of those that a mesh axis runs over, the one named last changes fastest.
Arguments:
- packet: float32 [20480, 512], P(('prow', 'hrow')), may hold values from -20 to 20
- header: float32 [20480, 512], P(('hrow', 'prow')), may hold values from -20 to 20
- partner: int32 [20480], replicated, may hold values from 0 to 20479, as said below
Outputs:
- loss: float32 [], replicated
- packet_grad: float32 [20480, 512], P(('prow', 'hrow'))
- header_grad: float32 [20480, 512], P(('hrow', 'prow'))
Inputs may be any that keep to these rules, and one draw needn't show every extreme that they name: `partner`: each header row is matched by exactly one packet row.
All inputs are finite; a program needn't handle non-finite values.
Results may differ from a plain program's by a relative error of at most 0.0003.
Values sent between devices are 32-bit elements; how exact they have to be, the bound alone decides.
No kernel may reach another device: no remote copies, remote signals or barrier semaphores. Data moves between devices by JAX's collectives and lax.ppermute only.
A program may use at most 64 MiB of HBM per device.

v0:
```python
import jax
import jax.numpy as jnp
from jax import lax
from jax.sharding import PartitionSpec as P

inv_temp = 1.0 / 0.07
eps_norm = 1e-06


def unit_rows(values):
    norms = jnp.sqrt(jnp.sum(values * values, axis=1, keepdims=True) + eps_norm)
    return (values / norms, norms)


def unit_back(grads, units, norms):
    return (grads - units * jnp.sum(units * grads, axis=1, keepdims=True)) / norms


def per_device(packet, header, partner):
    punit, pnorm = unit_rows(packet)
    hunit, hnorm = unit_rows(header)
    own_rows = packet.shape[0]
    ptile = lax.all_gather(punit, "hrow", axis=0, tiled=True)
    htile = lax.all_gather(hunit, "prow", axis=0, tiled=True)
    tile_rows = ptile.shape[0]
    tile_cols = htile.shape[0]
    batch = tile_rows * lax.axis_size("prow")
    row_start = lax.axis_index("prow") * tile_rows
    col_start = lax.axis_index("hrow") * tile_cols
    scores = (
        lax.dot_general(
            ptile,
            htile,
            (((1,), (1,)), ((), ())),
            precision=lax.Precision.HIGHEST,
            preferred_element_type=jnp.float32,
        )
        * inv_temp
    )
    expo = jnp.exp(scores - inv_temp)
    rows = lax.psum(jnp.sum(expo, axis=1), "hrow")
    cols = lax.psum(jnp.sum(expo, axis=0), "prow")
    wanted = lax.dynamic_slice_in_dim(partner, row_start, tile_rows)
    places = col_start + jnp.arange(tile_cols, dtype=jnp.int32)
    match = (wanted[:, None] == places[None, :]).astype(jnp.float32)
    positive = jnp.sum(match * scores)
    own_row_sums = lax.dynamic_slice_in_dim(rows, lax.axis_index("hrow") * own_rows, own_rows)
    own_col_sums = lax.dynamic_slice_in_dim(cols, lax.axis_index("prow") * own_rows, own_rows)
    local_term = jnp.sum(jnp.log(own_row_sums)) + jnp.sum(jnp.log(own_col_sums)) - 2.0 * positive
    total = lax.psum(local_term, ("prow", "hrow"))
    loss = inv_temp + total / (2.0 * batch)
    coeff = 1.0 / (2.0 * batch)
    dscores = coeff * (expo / rows[:, None] + expo / cols[None, :] - 2.0 * match)
    gp_tile = (
        jnp.dot(dscores, htile, precision=lax.Precision.HIGHEST, preferred_element_type=jnp.float32)
        * inv_temp
    )
    gpunit = lax.psum_scatter(gp_tile, "hrow", scatter_dimension=0, tiled=True)
    gh_tile = (
        lax.dot_general(
            dscores,
            ptile,
            (((0,), (0,)), ((), ())),
            precision=lax.Precision.HIGHEST,
            preferred_element_type=jnp.float32,
        )
        * inv_temp
    )
    ghunit = lax.psum_scatter(gh_tile, "prow", scatter_dimension=0, tiled=True)
    packet_grad = unit_back(gpunit, punit, pnorm)
    header_grad = unit_back(ghunit, hunit, hnorm)
    return (loss, packet_grad, header_grad)


def solution(mesh):
    placed = (P(("prow", "hrow"), None), P(("hrow", "prow"), None), P())
    return jax.shard_map(
        per_device,
        mesh=mesh,
        in_specs=placed,
        out_specs=(P(), P(("prow", "hrow"), None), P(("hrow", "prow"), None)),
        check_vma=False,
    )
```

profile of v0, /device:TPU:1, one launch (start us, length us, event | category | flops | bytes accessed | tf_op | source)
XLA Modules:
  0.0 443.3 jit_solution(7538632332686008224)
XLA Ops:
  7.2 0.0 all-gather.3.cloned.1.call-start
  7.2 1.0 multiply_reduce_fusion.3
  8.2 1.6 broadcast_divide_fusion.1
  9.8 0.0 all-gather.3.cloned.1.call-update
  9.9 0.0 all-gather.5.cloned.1.call-start
  9.9 1.0 multiply_reduce_fusion.2
  10.9 1.6 broadcast_divide_fusion
  12.5 0.0 all-gather.5.cloned.1.call-update
  12.6 0.0 reduce-scatter.3.cloned.1.call-start
  12.6 0.8 dynamic_slice.11
  13.4 64.6 %all-gather.3.cloned.1.call-done = f32[640,512]{1,0:T(8,128)} async-done(((f32[40,512]{1,0:T(8,128)}), f32[640,512]{1,0:T(8,128)}) %all-gather.3.cloned.1.call-update) | async-done | bytes 1310736 | tf_op jit(solution)/shard_map/all_gather | solution.py:23
  78.0 70.6 %all-gather.5.cloned.1.call-done = f32[1280,512]{1,0:T(8,128)} async-done(((f32[40,512]{1,0:T(8,128)}), f32[1280,512]{1,0:T(8,128)}) %all-gather.5.cloned.1.call-update) | async-done | bytes 2621456 | tf_op jit(solution)/shard_map/all_gather | solution.py:24
  148.6 10.5 %fusion = (f32[]{:T(128)}, f32[1280]{0:T(1024)S(1)}, f32[640]{0:T(1024)S(1)}, f32[640,1280]{1,0:T(8,128)}) fusion(s32[1280]{0:T(1024)S(1)} %iota_add_fusion, s32[640]{0:T(1024)S(1)} %dynamic_slice.11, f32[640,512]{1,0:T(8,128)} %all-gather.3.cloned.1.call-done, f32[1280,512]{1,0:T(8,128)} %all-gather.5.cloned.1.call-done), kind=kOutput, calls=%fused_computation.4 | convolution fusion | flops 5038897152 | bytes 7224324 | tf_op jit(solution)/shard_map/dot_general | solution.py:31
  159.1 63.2 %psum.22 = f32[1280]{0:T(1024)S(1)} all-reduce(f32[1280]{0:T(1024)S(1)} %get-tuple-element.4), channel_id=1, replica_groups=mesh['prow'=32,'hrow'=16] {'prow'}, use_global_device_ids=true, to_apply=%region_6.0 | all-reduce | flops 1280 | bytes 10240 | tf_op jit(solution)/shard_map/psum | solution.py:42
  222.3 24.5 %psum.21 = f32[640]{0:T(1024)S(1)} all-reduce(f32[640]{0:T(1024)S(1)} %get-tuple-element.5), channel_id=1, replica_groups=mesh['prow'=32,'hrow'=16] {'hrow'}, use_global_device_ids=true, to_apply=%region_3.0 | all-reduce | flops 640 | bytes 5120 | tf_op jit(solution)/shard_map/psum | solution.py:41
  246.8 0.0 copy-done.2
  246.8 9.4 %convolution_multiply_fusion.2 = f32[640,512]{1,0:T(8,128)} fusion(f32[1280,512]{1,0:T(8,128)S(1)} %copy-done.2, f32[640,1280]{1,0:T(8,128)} %get-tuple-element.6, f32[1280]{0:T(1024)S(1)} %psum.22, f32[640]{0:T(1024)S(1)} %psum.21, s32[1280]{0:T(1024)S(1)} %iota_add_fusion, s32[640]{0:T(1024)S(1)} %dynamic_slice.11), kind=kOutput, calls=%fused_computation.10 | convolution fusion | flops 5040046080 | bytes 7224320 | tf_op jit(solution)/shard_map/dot_general | solution.py:55
  256.2 0.0 reduce-scatter.3.cloned.1.call-update
  256.2 0.0 copy-start
  256.2 0.0 copy-start.1
  256.3 0.2 reduce-scatter.5.cloned.1.call-start
  256.5 10.6 %convolution_multiply_fusion.1 = f32[1280,512]{1,0:T(8,128)} fusion(f32[640,512]{1,0:T(8,128)} %all-gather.3.cloned.1.call-done, f32[640,1280]{1,0:T(8,128)} %get-tuple-element.6, f32[1280]{0:T(1024)S(1)} %psum.22, f32[640]{0:T(1024)S(1)} %psum.21, s32[1280]{0:T(1024)S(1)} %iota_add_fusion, s32[640]{0:T(1024)S(1)} %dynamic_slice.11), kind=kOutput, calls=%fused_computation.3 | convolution fusion | flops 5040373760 | bytes 7224320 | tf_op jit(solution)/shard_map/dot_general | solution.py:60
  267.1 0.0 reduce-scatter.5.cloned.1.call-update
  267.7 0.7 log_reduce_fusion
  268.4 0.7 log_reduce_fusion.1
  270.4 108.2 %psum.23 = f32[]{:T(128)} all-reduce(f32[]{:T(128)S(6)} %sub.16), channel_id=1, replica_groups=mesh['prow'=32,'hrow'=16] {'prow','hrow'}, use_global_device_ids=true, to_apply=%region_9.0 | all-reduce | flops 1 | bytes 8 | tf_op jit(solution)/shard_map/psum | solution.py:50
  379.3 0.0 reduce-scatter.3.cloned.1.call-done
  379.3 1.1 multiply_reduce_fusion.1
  380.4 1.6 subtract_divide_fusion.1
  382.0 51.0 %reduce-scatter.5.cloned.1.call-done = f32[40,512]{1,0:T(8,128)} async-done(((f32[1280,512]{1,0:T(8,128)}), f32[40,512]{1,0:T(8,128)}) %reduce-scatter.5.cloned.1.call-update) | async-done | bytes 81936 | tf_op jit(solution)/shard_map/reduce_scatter | solution.py:69
  433.0 1.1 multiply_reduce_fusion
  434.0 1.6 subtract_divide_fusion
  (6 shorter events, 0.0 us)
Async XLA Ops:
  7.2 70.9 %all-gather.3.cloned.1.call-start = ((), (), s32[]{:S(2)}) async-start(), calls=%async_computation.2 | async-start | bytes 1392640 | tf_op jit(solution)/shard_map/all_gather | solution.py:23
  9.9 138.7 %all-gather.5.cloned.1.call-start = ((), (), s32[]{:S(2)}) async-start(), calls=%async_computation.3 | async-start | bytes 2703360 | tf_op jit(solution)/shard_map/all_gather | solution.py:24
  12.6 366.7 %reduce-scatter.3.cloned.1.call-start = ((), (), s32[]{:S(2)}) async-start(), calls=%async_computation.4 | async-start | bytes 1392640 | tf_op jit(solution)/shard_map/reduce_scatter | solution.py:58
  148.6 98.3 %copy-start.2 = (f32[1280,512]{1,0:T(8,128)S(1)}, f32[1280,512]{1,0:T(8,128)}, u32[]{:S(2)}) copy-start(f32[1280,512]{1,0:T(8,128)} %all-gather.5.cloned.1.call-done) | copy-start | bytes 7864324
  256.2 123.1 %copy-start = (f32[40,512]{1,0:T(8,128)S(1)}, f32[40,512]{1,0:T(8,128)}, u32[]{:S(2)}) copy-start(f32[40,512]{1,0:T(8,128)} %param.3) | copy-start | bytes 245764
  256.2 176.7 %copy-start.1 = (f32[40,512]{1,0:T(8,128)S(1)}, f32[40,512]{1,0:T(8,128)}, u32[]{:S(2)}) copy-start(f32[40,512]{1,0:T(8,128)} %param.4) | copy-start | bytes 245764
  256.3 176.7 %reduce-scatter.5.cloned.1.call-start = ((), (), s32[]{:S(2)}) async-start(), calls=%async_computation.5 | async-start | bytes 2703360 | tf_op jit(solution)/shard_map/reduce_scatter | solution.py:69
Sparse Core Ops, SparseCore 0:
  10.7 67.3 all-gather.2
  81.7 66.8 all-gather.4
  256.3 63.3 reduce-scatter.2
  324.1 108.8 reduce-scatter.4
where the time goes:
time: 444 us; the launch traced here: 443 us
  blocking collectives  196 us (44%)
  waiting for transfers between devices  186 us (42%)
  matrix products  30.4 us (7%)
  between operations  17.6 us (4%)
  other arithmetic  12 us (3%)
    psum x1, blocking collectives, per_device(): total = lax.psum(local_term, ('prow', 'hrow'))  108 us
    all_gather x1, waiting for transfers between devices, per_device(): htile = lax.all_gather(hunit, 'prow', axis=0, tiled=True)  70.6 us
    all_gather x1, waiting for transfers between devices, per_device(): ptile = lax.all_gather(punit, 'hrow', axis=0, tiled=True)  64.6 us
    psum x1, blocking collectives, per_device(): cols = lax.psum(jnp.sum(expo, axis=0), 'prow')  63.2 us
    reduce_scatter x1, waiting for transfers between devices, per_device(): ghunit = lax.psum_scatter(gh_tile, 'prow', scatter_dimension=0, tiled=True)  51 us
    psum x1, blocking collectives, per_device(): rows = lax.psum(jnp.sum(expo, axis=1), 'hrow')  24.5 us
    dot_general x1, matrix products, per_device(): lax.dot_general(dscores, ptile, (((0,), (0,)), ((), ())), precision=lax.P...  10.6 us
    dot_general x1, matrix products, per_device(): lax.dot_general(ptile, htile, (((1,), (1,)), ((), ())), precision=lax.Pre...  10.5 us
  transfers between devices with their start and end apart: 4, of which 3 were waited for; matrix products, arithmetic and copies ran while one was open for 4% of the time, Pallas kernels for 0%

commit v1 on v0

v1 whole, which is shorter than its diff:
```python
import functools

import jax
import jax.numpy as jnp
import numpy as np
from jax import lax
from jax.experimental import pallas as pl
from jax.experimental.pallas import tpu as pltpu
from jax.sharding import Mesh, PartitionSpec as P

inv_temp = 1.0 / 0.07
eps_norm = 1e-06
NX, NY, NC, NZ = 4, 4, 2, 16
ALL = ("x", "y", "core", "z")
B = 40
D = 512
ROWS = NC * NZ * B
COLS = NX * NY * B
BATCH = NX * NY * ROWS
PLACES = (0, 1, -1, 2)
VMEM_LIMIT = 48 * 2**20


def take_from(value, dx=0, dy=0, dz=0, dc=0):
    pairs = []
    for x in range(NX):
        for y in range(NY):
            for c in range(NC):
                s = 1 - 2 * c
                for z in range(NZ):
                    sx, sy, sz = (x + s * dx) % NX, (y + s * dy) % NY, (z + s * dz) % NZ
                    src = ((sx * NY + sy) * NC + (c ^ dc)) * NZ + sz
                    pairs.append((src, ((x * NY + y) * NC + c) * NZ + z))
    return lax.ppermute(value, ALL, pairs)


def row_blocks(c, z):
    s = 1 - 2 * c
    o = 1 - c

    def at(core, k):
        return core * NZ + lax.rem(z + s * k + 2 * NZ, NZ)

    found = [("own", None, at(c, 0)), ("oth", None, at(o, 0))]
    for k in range(1, 8):
        found.append((f"n{k}", 0, at(c, -k)))
        found.append((f"n{k}", 1, at(o, -k)))
    found.append(("n8", None, at(c, -8)))
    for k in range(1, 5):
        found.append(("ma", 2 * (k - 1), at(o, k)))
        found.append(("ma", 2 * (k - 1) + 1, at(c, k)))
    for k in range(5, 8):
        found.append(("mb", 2 * (k - 5), at(o, k)))
        found.append(("mb", 2 * (k - 5) + 1, at(c, k)))
    found.append(("mb", 6, at(o, 8)))
    return found


ROW_NAMES = ("own", "oth", "n1", "n2", "n3", "n4", "n5", "n6", "n7", "n8", "ma", "mb")
ROW_SHAPES = ((B, D),) * 2 + ((2, B, D),) * 7 + ((B, D), (8, B, D), (7, B, D))


def col_blocks(x, y, c):
    s = 1 - 2 * c
    found = []
    for i, dy in enumerate(PLACES):
        for j, dx in enumerate(PLACES):
            bx = lax.rem(x + s * dx + NX, NX)
            by = lax.rem(y + s * dy + NY, NY)
            found.append((i, j, bx * NY + by))
    return found


def block_at(ref, block):
    return ref.at[pl.ds(pl.multiple_of(block * B, 8), B), :]


def split(value):
    high = value.astype(jnp.bfloat16)
    return high, (value - high.astype(jnp.float32)).astype(jnp.bfloat16)


def product(a_high, a_low, b_high, b_low, dims):
    dot = functools.partial(
        lax.dot_general, dimension_numbers=(dims, ((), ())), preferred_element_type=jnp.float32
    )
    return dot(a_high, b_high) + (dot(a_high, b_low) + dot(a_low, b_high))


def eye():
    return lax.broadcasted_iota(jnp.int32, (128, 128), 0) == lax.broadcasted_iota(
        jnp.int32, (128, 128), 1
    )


def to_lanes(column):
    return jnp.sum(jnp.where(eye(), column, 0.0), axis=0, keepdims=True)


def to_rows(lanes):
    return jnp.sum(jnp.where(eye(), lanes, 0.0), axis=1, keepdims=True)


STEP = 256


def scores_kernel(place, ids, wanted, *refs):
    rows_in = dict(zip(ROW_NAMES, refs[:12]))
    cols_in = refs[12:16]
    expo, ph, plow, hh, hlow, row_sums, col_sums, punit, hunit = refs[16:]
    x, y, c, z = place[0], place[1], place[2], place[3]

    def unit(v):
        return v * (1.0 / jnp.sqrt(jnp.sum(v * v, axis=1, keepdims=True) + eps_norm))

    for i, j, block in col_blocks(x, y, c):
        block_at(hunit, block)[...] = unit(cols_in[i][j])
    for name, index, block in row_blocks(c, z):
        v = rows_in[name][...] if index is None else rows_in[name][index]
        block_at(punit, block)[...] = unit(v)
    hh[...], hlow[...] = split(hunit[...])
    places = ids[...]

    def step(i, carry):
        total, positive = carry
        here = pl.ds(pl.multiple_of(i * STEP, STEP), STEP)
        high, low = split(punit[here, :])
        ph[here, :] = high
        plow[here, :] = low
        scores = product(high, low, hh[...], hlow[...], ((1,), (1,))) * inv_temp
        e = jnp.exp(scores - inv_temp)
        expo[here, :] = e
        sums = jnp.sum(e, axis=1, keepdims=True)
        for k in range(STEP // 128):
            row_sums[pl.ds(i * (STEP // 128) + k, 1), :] = to_lanes(sums[k * 128 : (k + 1) * 128])
        match = wanted[here, :] == places
        total = total + jnp.sum(e.reshape(STEP // 8, 8, COLS), axis=0)
        positive = positive + jnp.sum(
            jnp.where(match, scores, 0.0).reshape(STEP // 8, 8, COLS), axis=0
        )
        return total, positive

    zero = jnp.zeros((8, COLS), jnp.float32)
    row_sums[...] = jnp.zeros_like(row_sums)
    total, positive = lax.fori_loop(0, ROWS // STEP, step, (zero, zero))
    total = jnp.sum(total, axis=0, keepdims=True)
    positive = jnp.sum(positive, axis=0, keepdims=True)
    col_sums[...] = jnp.zeros_like(col_sums)
    for k in range(COLS // 128):
        col_sums[pl.ds(k, 1), :] = total[:, k * 128 : (k + 1) * 128]
    row_sums[pl.ds(10, 1), :] = sum(positive[:, k * 128 : (k + 1) * 128] for k in range(COLS // 128))


def packet_kernel(place, ids, wanted, rows_all, cols_all, expo, hh, hlow, *refs):
    rows_out = dict(zip(ROW_NAMES, refs[:12]))
    dh, dlow, grads = refs[12:]
    c, z = place[2], place[3]
    scale = inv_temp / (2.0 * BATCH)
    rows = jnp.sum(rows_all[...], axis=0)
    cols = jnp.sum(cols_all[...], axis=0)
    row_inv = scale / rows[:10]
    col_inv = jnp.concatenate([scale / cols[k : k + 1] for k in range(COLS // 128)], axis=1)
    places = ids[...]
    for i in range(ROWS // STEP):
        here = pl.ds(i * STEP, STEP)
        per_row = jnp.concatenate(
            [to_rows(row_inv[i * 2 + k : i * 2 + k + 1]) for k in range(STEP // 128)], axis=0
        )
        match = wanted[here, :] == places
        d = expo[here, :] * (per_row + col_inv) - jnp.where(match, 2.0 * scale, 0.0)
        high, low = split(d)
        dh[here, :] = high
        dlow[here, :] = low
        grads[here, :] = product(high, low, hh[...], hlow[...], ((1,), (0,)))
    for name, index, block in row_blocks(c, z):
        v = block_at(grads, block)[...]
        if index is None:
            rows_out[name][...] = v
        else:
            rows_out[name][index] = v


def header_kernel(place, dh, dlow, ph, plow, *refs):
    cols_out = refs[:4]
    grads = refs[4]
    x, y, c = place[0], place[1], place[2]
    for k in range(COLS // 128):
        here = pl.ds(k * 128, 128)
        grads[here, :] = product(dh[:, here], dlow[:, here], ph[...], plow[...], ((0,), (0,)))
    for i, j, block in col_blocks(x, y, c):
        cols_out[i][j] = block_at(grads, block)[...]


def in_vmem(count):
    return [pl.BlockSpec(memory_space=pltpu.VMEM)] * count


def call(kernel, operands, outs, scratch, flops):
    return pl.pallas_call(
        kernel,
        in_specs=[pl.BlockSpec(memory_space=pltpu.SMEM)] + in_vmem(len(operands) - 1),
        out_specs=in_vmem(len(outs)),
        out_shape=outs,
        scratch_shapes=scratch,
        compiler_params=pltpu.CompilerParams(vmem_limit_bytes=VMEM_LIMIT),
        cost_estimate=pl.CostEstimate(flops=flops, bytes_accessed=8 * 2**20, transcendentals=0),
    )(*operands)


def f32(*shape):
    return jax.ShapeDtypeStruct(shape, jnp.float32)


def b16(*shape):
    return jax.ShapeDtypeStruct(shape, jnp.bfloat16)


def unit_rows(values):
    norms = jnp.sqrt(jnp.sum(values * values, axis=1, keepdims=True) + eps_norm)
    return (values / norms, norms)


def unit_back(grads, units, norms):
    return (grads - units * jnp.sum(units * grads, axis=1, keepdims=True)) / norms


def gather_packet(packet):
    oth = take_from(packet, dc=1)
    pair = jnp.stack([packet, oth])
    near = []
    for _ in range(7):
        pair = take_from(pair, dz=-1)
        near.append(pair)
    n8 = take_from(pair[0], dz=-1)
    ma = take_from(jnp.concatenate(near[:4]), dc=1)
    mb = take_from(jnp.concatenate(near[4:] + [n8[None]]), dc=1)
    return [packet, oth] + near + [n8, ma, mb]


def gather_header(header):
    xa = take_from(header, dx=1)
    xb = take_from(header, dx=-1)
    xc = take_from(xa, dx=1)
    line = jnp.stack([header, xa, xb, xc])
    ya = take_from(line, dy=1)
    yb = take_from(line, dy=-1)
    yc = take_from(ya, dy=1)
    return [line, ya, yb, yc]


def scatter_packet(parts):
    own, oth, near, n8, ma, mb = parts[0], parts[1], parts[2:9], parts[9], parts[10], parts[11]
    far = take_from(mb, dc=1)
    close = take_from(ma, dc=1)
    got = take_from(n8 + far[6], dz=1)
    acc = near[6] + far[4:6] + jnp.stack([got, jnp.zeros_like(got)])
    for k in range(6, 0, -1):
        also = far[2 * (k - 5) : 2 * (k - 4)] if k >= 5 else close[2 * (k - 1) : 2 * k]
        acc = near[k - 1] + also + take_from(acc, dz=1)
    got = take_from(acc, dz=1)
    return own + got[0] + take_from(oth + got[1], dc=1)


def scatter_header(parts):
    line, ya, yb, yc = parts
    line = line + take_from(ya + take_from(yc, dy=-1), dy=-1) + take_from(yb, dy=1)
    return line[0] + take_from(line[1] + take_from(line[3], dx=-1), dx=-1) + take_from(line[2], dx=1)


def per_device(packet, header, partner):
    x, y, c, z = (lax.axis_index(name) for name in ALL)
    place = jnp.stack([x, y, c, z]).astype(jnp.int32)
    lane = np.arange(COLS)
    ids = jnp.asarray((lane // B) * (NC * B) + lane % B, jnp.int32)[None, :]
    ids = ids + (z * (NX * NY * NC * B) + c * B).astype(jnp.int32)
    wanted = lax.dynamic_slice_in_dim(partner, (x * NY + y) * ROWS, ROWS)[:, None]

    rows_in = gather_packet(packet)
    cols_in = gather_header(header)
    flops = 2 * 3 * ROWS * COLS * D
    expo, ph, plow, hh, hlow, row_part, col_part = call(
        scores_kernel,
        [place, ids, wanted] + rows_in + cols_in,
        [f32(ROWS, COLS), b16(ROWS, D), b16(ROWS, D), b16(COLS, D), b16(COLS, D), f32(16, 128), f32(8, 128)],
        [pltpu.VMEM((ROWS, D), jnp.float32), pltpu.VMEM((COLS, D), jnp.float32)],
        flops,
    )
    rows_all = lax.all_to_all(jnp.broadcast_to(row_part, (NC * NZ, 16, 128)), ("core", "z"), 0, 0)
    rows = jnp.sum(rows_all, axis=0)
    row_term = jnp.sum(jnp.log(rows[:10])) - 2.0 * jnp.sum(rows[10])
    last = lax.broadcasted_iota(jnp.int32, (8, 128), 0) == 7
    col_part = jnp.where(last, row_term, col_part)
    cols_all = lax.all_to_all(jnp.broadcast_to(col_part, (NX * NY, 8, 128)), ("x", "y"), 0, 0)
    cols = jnp.sum(cols_all, axis=0)
    col_term = jnp.sum(jnp.log(cols[: COLS // 128]))
    col_terms = lax.all_to_all(
        jnp.broadcast_to(col_term, (NC * NZ, 8, 128)), ("core", "z"), 0, 0
    )
    loss = inv_temp + (cols[7, 0] + jnp.sum(col_terms[:, 0, 0])) / (2.0 * BATCH)

    outs = call(
        packet_kernel,
        [place, ids, wanted, rows_all, cols_all, expo, hh, hlow],
        [f32(*shape) for shape in ROW_SHAPES] + [b16(ROWS, COLS), b16(ROWS, COLS)],
        [pltpu.VMEM((ROWS, D), jnp.float32)],
        flops,
    )
    dh, dlow = outs[12:]
    gh_parts = call(
        header_kernel,
        [place, dh, dlow, ph, plow],
        [f32(4, B, D)] * 4,
        [pltpu.VMEM((COLS, D), jnp.float32)],
        flops,
    )
    gpunit = scatter_packet(outs[:12])
    ghunit = scatter_header(gh_parts)
    punit, pnorm = unit_rows(packet)
    hunit, hnorm = unit_rows(header)
    packet_grad = unit_back(gpunit, punit, pnorm)
    header_grad = unit_back(ghunit, hunit, hnorm)
    return (loss, packet_grad, header_grad)


def solution(mesh):
    mesh = Mesh(mesh.devices.reshape(NX, NY, NC, NZ), ALL)
    by_packet, by_header = P(ALL, None), P(("z", "x", "y", "core"), None)
    return jax.shard_map(
        per_device,
        mesh=mesh,
        in_specs=(by_packet, by_header, P()),
        out_specs=(P(), by_packet, by_header),
        check_vma=False,
    )
```

time: 444 us -> 268 us (0.60)
  blocking collectives: 196 us -> 11.5 us
  starting transfers between devices: 0.34 us -> 147 us
  waiting for transfers between devices: 186 us -> 59.6 us
  matrix products: 30.4 us -> 0 us
  Pallas kernels: 0 us -> 20.8 us
  between operations: 17.6 us -> 4.98 us
  local copies, waits for them, and re-layouts: 0.79 us -> 7.51 us
    psum x3 -> x0, blocking collectives: 196 us -> none  [the longest x1 108 us: per_device(): total = lax.psum(local_term, ('prow', 'hrow'))]
    all_gather x2 -> x0, waiting for transfers between devices: 135 us -> none  [the longest x1 70.6 us: per_device(): htile = lax.all_gather(hunit, 'prow', axis=0, tiled=True)]
    ppermute x0 -> x34, starting transfers between devices: none -> 125 us  [take_from(): return lax.ppermute(value, ALL, pairs)]
    reduce_scatter x2 -> x0, waiting for transfers between devices: 51 us -> none  [the longest x1 51 us: per_device(): ghunit = lax.psum_scatter(gh_tile, 'prow', scatter_dimension=0, tiled=True)]
    ppermute x0 -> x34, waiting for transfers between devices: none -> 38 us  [take_from(): return lax.ppermute(value, ALL, pairs)]
    dot_general x3 -> x0, matrix products: 30.4 us -> none  [the longest x1 10.6 us: per_device(): lax.dot_general(dscores, ptile, (((0,), (0,)), ((), ())), precision=lax.P...]
    all_to_all x0 -> x2, starting transfers between devices: none -> 21.7 us  [the longest x1 12.6 us: per_device(): lax.all_to_all(jnp.broadcast_to(col_term, (NC * NZ, 8, 128)), ('core', 'z...]
    all_to_all x0 -> x2, waiting for transfers between devices: none -> 21.7 us  [the longest x1 21.7 us: per_device(): lax.all_to_all(jnp.broadcast_to(row_part, (NC * NZ, 16, 128)), ('core', '...]
  transfers between devices with their start and end apart: 4 -> 36, of which waited for: 3 -> 18; matrix products, arithmetic and copies ran while one was open for 4% -> 6% of each run, Pallas kernels for 0% -> 2%
where the time goes in v1:
time: 268 us; the launch traced here: 266 us
  starting transfers between devices  147 us (55%)
  waiting for transfers between devices  59.6 us (22%)
  Pallas kernels  20.8 us (8%)
  other arithmetic  15.1 us (6%)
  blocking collectives  11.5 us (4%)
  local copies, waits for them, and re-layouts  7.51 us (3%)
  between operations  4.98 us (2%)
    ppermute x34, starting transfers between devices, take_from(): return lax.ppermute(value, ALL, pairs)  125 us
    ppermute x34, waiting for transfers between devices, take_from(): return lax.ppermute(value, ALL, pairs)  38 us
    all_to_all x1, waiting for transfers between devices, per_device(): lax.all_to_all(jnp.broadcast_to(row_part, (NC * NZ, 16, 128)), ('core', '...  21.7 us
    pallas_call x3, Pallas kernels, call(): pl.pallas_call(kernel, in_specs=[pl.BlockSpec(memory_space=pltpu.SMEM)] +...  20.8 us
    all_to_all x1, starting transfers between devices, per_device(): lax.all_to_all(jnp.broadcast_to(col_term, (NC * NZ, 8, 128)), ('core', 'z...  12.6 us
    all_to_all x1, blocking collectives, per_device(): lax.all_to_all(jnp.broadcast_to(col_part, (NX * NY, 8, 128)), ('x', 'y'),...  11.5 us
    all_to_all x1, starting transfers between devices, per_device(): lax.all_to_all(jnp.broadcast_to(row_part, (NC * NZ, 16, 128)), ('core', '...  9.1 us
  transfers between devices with their start and end apart: 36, of which 18 were waited for; matrix products, arithmetic and copies ran while one was open for 6% of the time, Pallas kernels for 2%

profile of v1, /device:TPU:1, one launch (start us, length us, event | category | flops | bytes accessed | tf_op | source)
XLA Modules:
  0.0 266.4 jit_solution(8906447753209000601)
XLA Ops:
  0.6 8.8 %collective-permute-start = (f32[40,512]{1,0:T(8,128)}, f32[40,512]{1,0:T(8,128)S(1)}, u32[]{:S(2)}, u32[]{:S(2)}) collective-permute-start(f32[40,512]{1,0:T(8,128)} %refs_0_.1), channel_id=1, source_target_pairs={{16,0},{17,1},{18,2},{19,3},{20,4},{21,5},{22,6},{23,7},{24,8},{25... | collective-permute-start | bytes 245768 | tf_op jit(solution)/shard_map/ppermute | solution.py:34
  11.4 5.7 %collective-permute-start.1 = (f32[2,40,512]{2,1,0:T(8,128)S(1)}, f32[2,40,512]{2,1,0:T(8,128)S(1)}, u32[]{:S(2)}, u32[]{:S(2)}) collective-permute-start(f32[2,40,512]{2,1,0:T(8,128)S(1)} %pad_maximum_fusion.3), channel_id=1, source_target_pairs={{15,0},{0,1},{1,2},{2,3},{3,4},{4,5},{5,6},{6,7},{7,8},{8,9},{9,10... | collective-permute-start | bytes 491528 | tf_op jit(solution)/shard_map/ppermute | solution.py:34
  19.4 5.0 %collective-permute-start.2 = (f32[2,40,512]{2,1,0:T(8,128)S(1)}, f32[2,40,512]{2,1,0:T(8,128)S(1)}, u32[]{:S(2)}, u32[]{:S(2)}) collective-permute-start(f32[2,40,512]{2,1,0:T(8,128)S(1)} %collective-permute-done.1.refs_2_), channel_id=1, source_target_pairs={{15,0},{0,1},{1,2},{2,3},{3,4},{4,5},{5,6},{6,7},{7,8},{8,9},{9,10... | collective-permute-start | bytes 491528 | tf_op jit(solution)/shard_map/ppermute | solution.py:34
  26.7 5.0 %collective-permute-start.3 = (f32[2,40,512]{2,1,0:T(8,128)S(1)}, f32[2,40,512]{2,1,0:T(8,128)S(1)}, u32[]{:S(2)}, u32[]{:S(2)}) collective-permute-start(f32[2,40,512]{2,1,0:T(8,128)S(1)} %collective-permute-done.2.refs_3_), channel_id=1, source_target_pairs={{15,0},{0,1},{1,2},{2,3},{3,4},{4,5},{5,6},{6,7},{7,8},{8,9},{9,10... | collective-permute-start | bytes 491528 | tf_op jit(solution)/shard_map/ppermute | solution.py:34
  34.0 5.0 %collective-permute-start.4 = (f32[2,40,512]{2,1,0:T(8,128)S(1)}, f32[2,40,512]{2,1,0:T(8,128)S(1)}, u32[]{:S(2)}, u32[]{:S(2)}) collective-permute-start(f32[2,40,512]{2,1,0:T(8,128)S(1)} %collective-permute-done.3.refs_4_), channel_id=1, source_target_pairs={{15,0},{0,1},{1,2},{2,3},{3,4},{4,5},{5,6},{6,7},{7,8},{8,9},{9,10... | collective-permute-start | bytes 491528 | tf_op jit(solution)/shard_map/ppermute | solution.py:34
  41.2 5.0 %collective-permute-start.5 = (f32[2,40,512]{2,1,0:T(8,128)S(1)}, f32[2,40,512]{2,1,0:T(8,128)S(1)}, u32[]{:S(2)}, u32[]{:S(2)}) collective-permute-start(f32[2,40,512]{2,1,0:T(8,128)S(1)} %collective-permute-done.4.refs_5_), channel_id=1, source_target_pairs={{15,0},{0,1},{1,2},{2,3},{3,4},{4,5},{5,6},{6,7},{7,8},{8,9},{9,10... | collective-permute-start | bytes 491528 | tf_op jit(solution)/shard_map/ppermute | solution.py:34
  48.5 5.0 %collective-permute-start.6 = (f32[2,40,512]{2,1,0:T(8,128)S(1)}, f32[2,40,512]{2,1,0:T(8,128)S(1)}, u32[]{:S(2)}, u32[]{:S(2)}) collective-permute-start(f32[2,40,512]{2,1,0:T(8,128)S(1)} %collective-permute-done.5.refs_6_), channel_id=1, source_target_pairs={{15,0},{0,1},{1,2},{2,3},{3,4},{4,5},{5,6},{6,7},{7,8},{8,9},{9,10... | collective-permute-start | bytes 491528 | tf_op jit(solution)/shard_map/ppermute | solution.py:34
  53.5 3.1 %collective-permute-start.11 = (f32[40,512]{1,0:T(8,128)}, f32[40,512]{1,0:T(8,128)S(1)}, u32[]{:S(2)}, u32[]{:S(2)}) collective-permute-start(f32[40,512]{1,0:T(8,128)} %param.5), channel_id=1, source_target_pairs={{128,0},{129,1},{130,2},{131,3},{132,4},{133,5},{134,6},{135,7},{1... | collective-permute-start | bytes 245768 | tf_op jit(solution)/shard_map/ppermute | solution.py:34
  56.6 3.4 %collective-permute-start.12 = (f32[40,512]{1,0:T(8,128)}, f32[40,512]{1,0:T(8,128)S(1)}, u32[]{:S(2)}, u32[]{:S(2)}) collective-permute-start(f32[40,512]{1,0:T(8,128)} %param.5), channel_id=1, source_target_pairs={{384,0},{385,1},{386,2},{387,3},{388,4},{389,5},{390,6},{391,7},{3... | collective-permute-start | bytes 245768 | tf_op jit(solution)/shard_map/ppermute | solution.py:34
  67.4 3.2 %collective-permute-start.14 = (f32[4,40,512]{2,1,0:T(8,128)S(1)}, f32[4,40,512]{2,1,0:T(8,128)S(1)}, u32[]{:S(2)}, u32[]{:S(2)}) collective-permute-start(f32[4,40,512]{2,1,0:T(8,128)S(1)} %pad_maximum_fusion.2.refs_12_), channel_id=1, source_target_pairs={{32,0},{33,1},{34,2},{35,3},{36,4},{37,5},{38,6},{39,7},{40,8},{41... | collective-permute-start | bytes 983048 | tf_op jit(solution)/shard_map/ppermute | solution.py:34
  73.7 8.8 %collective-permute-start.9 = (f32[8,40,512]{2,1,0:T(8,128)}, f32[8,40,512]{2,1,0:T(8,128)S(1)}, u32[]{:S(2)}, u32[]{:S(2)}) collective-permute-start(f32[8,40,512]{2,1,0:T(8,128)} %pad_maximum_fusion), channel_id=1, source_target_pairs={{16,0},{17,1},{18,2},{19,3},{20,4},{21,5},{22,6},{23,7},{24,8},{25... | collective-permute-start | bytes 1966088 | tf_op jit(solution)/shard_map/ppermute | solution.py:34
  83.3 4.7 %collective-permute-start.10 = (f32[7,40,512]{2,1,0:T(8,128)}, f32[7,40,512]{2,1,0:T(8,128)}, u32[]{:S(2)}, u32[]{:S(2)}) collective-permute-start(f32[7,40,512]{2,1,0:T(8,128)} %pad_maximum_fusion.1), channel_id=1, source_target_pairs={{16,0},{17,1},{18,2},{19,3},{20,4},{21,5},{22,6},{23,7},{24,8},{25... | collective-permute-start | bytes 1720328 | tf_op jit(solution)/shard_map/ppermute | solution.py:34
  89.0 4.6 %collective-permute-start.15 = (f32[4,40,512]{2,1,0:T(8,128)S(1)}, f32[4,40,512]{2,1,0:T(8,128)S(1)}, u32[]{:S(2)}, u32[]{:S(2)}) collective-permute-start(f32[4,40,512]{2,1,0:T(8,128)S(1)} %pad_maximum_fusion.2.refs_12_), channel_id=1, source_target_pairs={{96,0},{97,1},{98,2},{99,3},{100,4},{101,5},{102,6},{103,7},{104,8... | collective-permute-start | bytes 983048 | tf_op jit(solution)/shard_map/ppermute | solution.py:34
  95.7 2.8 %collective-permute-done.15.refs_14_ = f32[4,40,512]{2,1,0:T(8,128)S(1)} collective-permute-done((f32[4,40,512]{2,1,0:T(8,128)S(1)}, f32[4,40,512]{2,1,0:T(8,128)S(1)}, u32[]{:S(2)}, u32[]{:S(2)}) %collective-permute-start.15) | collective-permute-done | bytes 327712 | tf_op jit(solution)/shard_map/ppermute | solution.py:34
  98.5 4.2 %collective-permute-done.16.refs_15_ = f32[4,40,512]{2,1,0:T(8,128)S(1)} collective-permute-done((f32[4,40,512]{2,1,0:T(8,128)S(1)}, f32[4,40,512]{2,1,0:T(8,128)S(1)}, u32[]{:S(2)}, u32[]{:S(2)}) %collective-permute-start.16) | collective-permute-done | bytes 327712 | tf_op jit(solution)/shard_map/ppermute | solution.py:34
  102.7 8.9 %shard_map.67 = (f32[1280,640]{1,0:T(8,128)}, bf16[1280,512]{1,0:T(8,128)(2,1)}, bf16[1280,512]{1,0:T(8,128)(2,1)}, bf16[640,512]{1,0:T(8,128)(2,1)S(1)}, bf16[6...) custom-call(s32[4]{0:T(128)S(1)} %pad_add_fusion.place, s32[1,640]{1,0:T(1,128)S(1)} %add.113.ids, ...), custom_call_target="tpu_custom_call" | custom-call | flops 2516582400 | bytes 8388608 | tf_op jit(solution)/shard_map/pallas_call | solution.py:199
  114.1 9.1 %all-to-all-start = ((f32[32,16,128]{2,1,0:T(8,128)}), f32[32,16,128]{2,1,0:T(8,128)S(1)}, u32[]{:S(2)}, u32[]{:S(2)}) async-start(f32[32,16,128]{2,1,0:T(8,128)} %broadcast_in_dim.26), calls=%async_computation | async-start | bytes 524288 | tf_op jit(solution)/shard_map/all_to_all | solution.py:288
  123.2 21.7 %all-to-all-done.rows_all = f32[32,16,128]{2,1,0:T(8,128)S(1)} async-done(((f32[32,16,128]{2,1,0:T(8,128)}), f32[32,16,128]{2,1,0:T(8,128)S(1)}, u32[]{:S(2)}, u32[]{:S(2)}) %all-to-all-start) | async-done | bytes 262176 | tf_op jit(solution)/shard_map/all_to_all | solution.py:288
  147.5 11.5 %all_to_all.15.cols_all = f32[16,8,128]{2,1,0:T(8,128)S(1)} all-to-all(f32[16,8,128]{2,1,0:T(8,128)S(1)} %broadcast_in_dim.28), channel_id=1, replica_groups=mesh['x'=4,'y'=4,'core'=2,'z'=16] {'x','y'}, dimensions={0} | all-to-all | bytes 131072 | tf_op jit(solution)/shard_map/all_to_all | solution.py:293
  161.2 7.6 %shard_map.68 = (f32[40,512]{1,0:T(8,128)S(1)}, f32[40,512]{1,0:T(8,128)S(1)}, f32[2,40,512]{2,1,0:T(8,128)S(1)}, f32[2,40,512]{2,1,0:T(8,128)S(1)}, f32[2,40,51...) custom-call(s32[4]{0:T(128)S(1)} %pad_add_fusion.place, ...), custom_call_target="tpu_custom_call" | custom-call | flops 2516582400 | bytes 8388608 | tf_op jit(solution)/shard_map/pallas_call | solution.py:199
  172.8 3.0 %collective-permute-start.19 = (f32[40,512]{1,0:T(8,128)S(1)}, f32[40,512]{1,0:T(8,128)S(1)}, u32[]{:S(2)}, u32[]{:S(2)}) collective-permute-start(f32[40,512]{1,0:T(8,128)S(1)} %fusion.13), channel_id=1, source_target_pairs={{1,0},{2,1},{3,2},{4,3},{5,4},{6,5},{7,6},{8,7},{9,8},{10,9},{11,1... | collective-permute-start | bytes 245768 | tf_op jit(solution)/shard_map/ppermute | solution.py:34
  175.9 3.3 %collective-permute-done.19 = f32[40,512]{1,0:T(8,128)S(1)} collective-permute-done((f32[40,512]{1,0:T(8,128)S(1)}, f32[40,512]{1,0:T(8,128)S(1)}, u32[]{:S(2)}, u32[]{:S(2)}) %collective-permute-start.19) | collective-permute-done | bytes 81952 | tf_op jit(solution)/shard_map/ppermute | solution.py:34
  181.4 3.3 %collective-permute-start.17 = (f32[8,40,512]{2,1,0:T(8,128)S(1)}, f32[8,40,512]{2,1,0:T(8,128)}, u32[]{:S(2)}, u32[]{:S(2)}) collective-permute-start(f32[8,40,512]{2,1,0:T(8,128)S(1)} %get-tuple-element.35), channel_id=1, source_target_pairs={{16,0},{17,1},{18,2},{19,3},{20,4},{21,5},{22,6},{23,7},{24,8},{25... | collective-permute-start | bytes 1966088 | tf_op jit(solution)/shard_map/ppermute | solution.py:34
  188.5 4.3 %shard_map.69 = (f32[4,40,512]{2,1,0:T(8,128)S(1)}, f32[4,40,512]{2,1,0:T(8,128)S(1)}, f32[4,40,512]{2,1,0:T(8,128)S(1)}, f32[4,40,512]{2,1,0:T(8,128)S(1)}) custom-call(s32[4]{0:T(128)S(1)} %pad_add_fusion.place, bf16[1280,640]{1,0:T(8,128)(2,1)S(1)} %copy-done.1, bf16[1280,640]{1,0:T(8,128)(2,1)} %get-tuple-element.46.dlow, ...), custom_call_target="tpu_custom_call" | custom-call | flops 2516582400 | bytes 8388608 | tf_op jit(solution)/shard_map/pallas_call | solution.py:199
  192.9 2.9 %collective-permute-start.28 = (f32[4,40,512]{2,1,0:T(8,128)S(1)}, f32[4,40,512]{2,1,0:T(8,128)}, u32[]{:S(2)}, u32[]{:S(2)}) collective-permute-start(f32[4,40,512]{2,1,0:T(8,128)S(1)} %get-tuple-element.51), channel_id=1, source_target_pairs={{96,0},{97,1},{98,2},{99,3},{100,4},{101,5},{102,6},{103,7},{104,8... | collective-permute-start | bytes 983048 | tf_op jit(solution)/shard_map/ppermute | solution.py:34
  203.2 4.1 %collective-permute-start.29 = (f32[4,40,512]{2,1,0:T(8,128)}, f32[4,40,512]{2,1,0:T(8,128)S(1)}, u32[]{:S(2)}, u32[]{:S(2)}) collective-permute-start(f32[4,40,512]{2,1,0:T(8,128)} %add.136), channel_id=1, source_target_pairs={{96,0},{97,1},{98,2},{99,3},{100,4},{101,5},{102,6},{103,7},{104,8... | collective-permute-start | bytes 983048 | tf_op jit(solution)/shard_map/ppermute | solution.py:34
  209.2 12.6 %all-to-all-start.2 = ((f32[32,8,128]{2,1,0:T(8,128)}), f32[32,8,128]{2,1,0:T(8,128)S(1)}, u32[]{:S(2)}, u32[]{:S(2)}) async-start(f32[32,8,128]{2,1,0:T(8,128)} %broadcast_in_dim.29), calls=%async_computation.2 | async-start | bytes 262144 | tf_op jit(solution)/shard_map/all_to_all | solution.py:296
  222.8 3.3 %collective-permute-start.23 = (f32[2,40,512]{2,1,0:T(8,128)S(1)}, f32[2,40,512]{2,1,0:T(8,128)S(1)}, u32[]{:S(2)}, u32[]{:S(2)}) collective-permute-start(f32[2,40,512]{2,1,0:T(8,128)S(1)} %fusion.3), channel_id=1, source_target_pairs={{1,0},{2,1},{3,2},{4,3},{5,4},{6,5},{7,6},{8,7},{9,8},{10,9},{11,1... | collective-permute-start | bytes 491528 | tf_op jit(solution)/shard_map/ppermute | solution.py:34
  227.2 5.4 %collective-permute-done.23 = f32[2,40,512]{2,1,0:T(8,128)S(1)} collective-permute-done((f32[2,40,512]{2,1,0:T(8,128)S(1)}, f32[2,40,512]{2,1,0:T(8,128)S(1)}, u32[]{:S(2)}, u32[]{:S(2)}) %collective-permute-start.23) | collective-permute-done | bytes 163872 | tf_op jit(solution)/shard_map/ppermute | solution.py:34
  244.3 3.9 %collective-permute-start.32 = (f32[40,512]{1,0:T(8,128)S(1)}, f32[40,512]{1,0:T(8,128)S(1)}, u32[]{:S(2)}, u32[]{:S(2)}) collective-permute-start(f32[40,512]{1,0:T(8,128)S(1)} %fusion.7), channel_id=1, source_target_pairs={{384,0},{385,1},{386,2},{387,3},{388,4},{389,5},{390,6},{391,7},{3... | collective-permute-start | bytes 245768 | tf_op jit(solution)/shard_map/ppermute | solution.py:34
  254.4 3.1 %collective-permute-done.26 = f32[2,40,512]{2,1,0:T(8,128)S(1)} collective-permute-done((f32[2,40,512]{2,1,0:T(8,128)S(1)}, f32[2,40,512]{2,1,0:T(8,128)S(1)}, u32[]{:S(2)}, u32[]{:S(2)}) %collective-permute-start.26) | collective-permute-done | bytes 163872 | tf_op jit(solution)/shard_map/ppermute | solution.py:34
  257.5 5.9 %collective-permute-start.27 = (f32[40,512]{1,0:T(8,128)S(1)}, f32[40,512]{1,0:T(8,128)S(1)}, u32[]{:S(2)}, u32[]{:S(2)}) collective-permute-start(f32[40,512]{1,0:T(8,128)S(1)} %fusion.10), channel_id=1, source_target_pairs={{16,0},{17,1},{18,2},{19,3},{20,4},{21,5},{22,6},{23,7},{24,8},{25... | collective-permute-start | bytes 245768 | tf_op jit(solution)/shard_map/ppermute | solution.py:34
  (107 shorter events, 73.3 us)
Async XLA Ops:
  0.6 9.9 %collective-permute-start = (f32[40,512]{1,0:T(8,128)}, f32[40,512]{1,0:T(8,128)S(1)}, u32[]{:S(2)}, u32[]{:S(2)}) collective-permute-start(f32[40,512]{1,0:T(8,128)} %refs_0_.1), channel_id=1, source_target_pairs={{16,0},{17,1},{18,2},{19,3},{20,4},{21,5},{22,6},{23,7},{24,8},{25... | collective-permute-start | bytes 245768 | tf_op jit(solution)/shard_map/ppermute | solution.py:34
  11.4 8.0 %collective-permute-start.1 = (f32[2,40,512]{2,1,0:T(8,128)S(1)}, f32[2,40,512]{2,1,0:T(8,128)S(1)}, u32[]{:S(2)}, u32[]{:S(2)}) collective-permute-start(f32[2,40,512]{2,1,0:T(8,128)S(1)} %pad_maximum_fusion.3), channel_id=1, source_target_pairs={{15,0},{0,1},{1,2},{2,3},{3,4},{4,5},{5,6},{6,7},{7,8},{8,9},{9,10... | collective-permute-start | bytes 491528 | tf_op jit(solution)/shard_map/ppermute | solution.py:34
  19.4 7.3 %collective-permute-start.2 = (f32[2,40,512]{2,1,0:T(8,128)S(1)}, f32[2,40,512]{2,1,0:T(8,128)S(1)}, u32[]{:S(2)}, u32[]{:S(2)}) collective-permute-start(f32[2,40,512]{2,1,0:T(8,128)S(1)} %collective-permute-done.1.refs_2_), channel_id=1, source_target_pairs={{15,0},{0,1},{1,2},{2,3},{3,4},{4,5},{5,6},{6,7},{7,8},{8,9},{9,10... | collective-permute-start | bytes 491528 | tf_op jit(solution)/shard_map/ppermute | solution.py:34
  26.7 7.3 %collective-permute-start.3 = (f32[2,40,512]{2,1,0:T(8,128)S(1)}, f32[2,40,512]{2,1,0:T(8,128)S(1)}, u32[]{:S(2)}, u32[]{:S(2)}) collective-permute-start(f32[2,40,512]{2,1,0:T(8,128)S(1)} %collective-permute-done.2.refs_3_), channel_id=1, source_target_pairs={{15,0},{0,1},{1,2},{2,3},{3,4},{4,5},{5,6},{6,7},{7,8},{8,9},{9,10... | collective-permute-start | bytes 491528 | tf_op jit(solution)/shard_map/ppermute | solution.py:34
  34.0 7.3 %collective-permute-start.4 = (f32[2,40,512]{2,1,0:T(8,128)S(1)}, f32[2,40,512]{2,1,0:T(8,128)S(1)}, u32[]{:S(2)}, u32[]{:S(2)}) collective-permute-start(f32[2,40,512]{2,1,0:T(8,128)S(1)} %collective-permute-done.3.refs_4_), channel_id=1, source_target_pairs={{15,0},{0,1},{1,2},{2,3},{3,4},{4,5},{5,6},{6,7},{7,8},{8,9},{9,10... | collective-permute-start | bytes 491528 | tf_op jit(solution)/shard_map/ppermute | solution.py:34
  41.2 7.3 %collective-permute-start.5 = (f32[2,40,512]{2,1,0:T(8,128)S(1)}, f32[2,40,512]{2,1,0:T(8,128)S(1)}, u32[]{:S(2)}, u32[]{:S(2)}) collective-permute-start(f32[2,40,512]{2,1,0:T(8,128)S(1)} %collective-permute-done.4.refs_5_), channel_id=1, source_target_pairs={{15,0},{0,1},{1,2},{2,3},{3,4},{4,5},{5,6},{6,7},{7,8},{8,9},{9,10... | collective-permute-start | bytes 491528 | tf_op jit(solution)/shard_map/ppermute | solution.py:34
  48.5 13.5 %collective-permute-start.6 = (f32[2,40,512]{2,1,0:T(8,128)S(1)}, f32[2,40,512]{2,1,0:T(8,128)S(1)}, u32[]{:S(2)}, u32[]{:S(2)}) collective-permute-start(f32[2,40,512]{2,1,0:T(8,128)S(1)} %collective-permute-done.5.refs_6_), channel_id=1, source_target_pairs={{15,0},{0,1},{1,2},{2,3},{3,4},{4,5},{5,6},{6,7},{7,8},{8,9},{9,10... | collective-permute-start | bytes 491528 | tf_op jit(solution)/shard_map/ppermute | solution.py:34
  56.6 7.6 %collective-permute-start.12 = (f32[40,512]{1,0:T(8,128)}, f32[40,512]{1,0:T(8,128)S(1)}, u32[]{:S(2)}, u32[]{:S(2)}) collective-permute-start(f32[40,512]{1,0:T(8,128)} %param.5), channel_id=1, source_target_pairs={{384,0},{385,1},{386,2},{387,3},{388,4},{389,5},{390,6},{391,7},{3... | collective-permute-start | bytes 245768 | tf_op jit(solution)/shard_map/ppermute | solution.py:34
  62.0 8.6 %collective-permute-start.7 = (f32[2,40,512]{2,1,0:T(8,128)S(1)}, f32[2,40,512]{2,1,0:T(8,128)S(1)}, u32[]{:S(2)}, u32[]{:S(2)}) collective-permute-start(f32[2,40,512]{2,1,0:T(8,128)S(1)} %collective-permute-done.6.refs_7_), channel_id=1, source_target_pairs={{15,0},{0,1},{1,2},{2,3},{3,4},{4,5},{5,6},{6,7},{7,8},{8,9},{9,10... | collective-permute-start | bytes 491528 | tf_op jit(solution)/shard_map/ppermute | solution.py:34
  67.4 26.3 %collective-permute-start.14 = (f32[4,40,512]{2,1,0:T(8,128)S(1)}, f32[4,40,512]{2,1,0:T(8,128)S(1)}, u32[]{:S(2)}, u32[]{:S(2)}) collective-permute-start(f32[4,40,512]{2,1,0:T(8,128)S(1)} %pad_maximum_fusion.2.refs_12_), channel_id=1, source_target_pairs={{32,0},{33,1},{34,2},{35,3},{36,4},{37,5},{38,6},{39,7},{40,8},{41... | collective-permute-start | bytes 983048 | tf_op jit(solution)/shard_map/ppermute | solution.py:34
  70.7 11.8 %collective-permute-start.8 = (f32[40,512]{1,0:T(8,128)S(1)}, f32[40,512]{1,0:T(8,128)S(1)}, u32[]{:S(2)}, u32[]{:S(2)}) collective-permute-start(f32[40,512]{1,0:T(8,128)S(1)} %slice_bitcast_fusion.7), channel_id=1, source_target_pairs={{15,0},{0,1},{1,2},{2,3},{3,4},{4,5},{5,6},{6,7},{7,8},{8,9},{9,10... | collective-permute-start | bytes 245768 | tf_op jit(solution)/shard_map/ppermute | solution.py:34
  73.7 29.1 %collective-permute-start.9 = (f32[8,40,512]{2,1,0:T(8,128)}, f32[8,40,512]{2,1,0:T(8,128)S(1)}, u32[]{:S(2)}, u32[]{:S(2)}) collective-permute-start(f32[8,40,512]{2,1,0:T(8,128)} %pad_maximum_fusion), channel_id=1, source_target_pairs={{16,0},{17,1},{18,2},{19,3},{20,4},{21,5},{22,6},{23,7},{24,8},{25... | collective-permute-start | bytes 1966088 | tf_op jit(solution)/shard_map/ppermute | solution.py:34
  83.3 19.4 %collective-permute-start.10 = (f32[7,40,512]{2,1,0:T(8,128)}, f32[7,40,512]{2,1,0:T(8,128)}, u32[]{:S(2)}, u32[]{:S(2)}) collective-permute-start(f32[7,40,512]{2,1,0:T(8,128)} %pad_maximum_fusion.1), channel_id=1, source_target_pairs={{16,0},{17,1},{18,2},{19,3},{20,4},{21,5},{22,6},{23,7},{24,8},{25... | collective-permute-start | bytes 1720328 | tf_op jit(solution)/shard_map/ppermute | solution.py:34
  89.0 9.5 %collective-permute-start.15 = (f32[4,40,512]{2,1,0:T(8,128)S(1)}, f32[4,40,512]{2,1,0:T(8,128)S(1)}, u32[]{:S(2)}, u32[]{:S(2)}) collective-permute-start(f32[4,40,512]{2,1,0:T(8,128)S(1)} %pad_maximum_fusion.2.refs_12_), channel_id=1, source_target_pairs={{96,0},{97,1},{98,2},{99,3},{100,4},{101,5},{102,6},{103,7},{104,8... | collective-permute-start | bytes 983048 | tf_op jit(solution)/shard_map/ppermute | solution.py:34
  93.7 9.0 %collective-permute-start.16 = (f32[4,40,512]{2,1,0:T(8,128)S(1)}, f32[4,40,512]{2,1,0:T(8,128)S(1)}, u32[]{:S(2)}, u32[]{:S(2)}) collective-permute-start(f32[4,40,512]{2,1,0:T(8,128)S(1)} %collective-permute-done.14.refs_13_), channel_id=1, source_target_pairs={{32,0},{33,1},{34,2},{35,3},{36,4},{37,5},{38,6},{39,7},{40,8},{41... | collective-permute-start | bytes 983048 | tf_op jit(solution)/shard_map/ppermute | solution.py:34
  114.1 30.8 %all-to-all-start = ((f32[32,16,128]{2,1,0:T(8,128)}), f32[32,16,128]{2,1,0:T(8,128)S(1)}, u32[]{:S(2)}, u32[]{:S(2)}) async-start(f32[32,16,128]{2,1,0:T(8,128)} %broadcast_in_dim.26), calls=%async_computation | async-start | bytes 524288 | tf_op jit(solution)/shard_map/all_to_all | solution.py:288
  179.3 7.3 %collective-permute-start.20 = (f32[2,40,512]{2,1,0:T(8,128)S(1)}, f32[2,40,512]{2,1,0:T(8,128)S(1)}, u32[]{:S(2)}, u32[]{:S(2)}) collective-permute-start(f32[2,40,512]{2,1,0:T(8,128)S(1)} %fusion), channel_id=1, source_target_pairs={{1,0},{2,1},{3,2},{4,3},{5,4},{6,5},{7,6},{8,7},{9,8},{10,9},{11,1... | collective-permute-start | bytes 491528 | tf_op jit(solution)/shard_map/ppermute | solution.py:34
  181.4 40.3 %collective-permute-start.17 = (f32[8,40,512]{2,1,0:T(8,128)S(1)}, f32[8,40,512]{2,1,0:T(8,128)}, u32[]{:S(2)}, u32[]{:S(2)}) collective-permute-start(f32[8,40,512]{2,1,0:T(8,128)S(1)} %get-tuple-element.35), channel_id=1, source_target_pairs={{16,0},{17,1},{18,2},{19,3},{20,4},{21,5},{22,6},{23,7},{24,8},{25... | collective-permute-start | bytes 1966088 | tf_op jit(solution)/shard_map/ppermute | solution.py:34
  186.6 9.2 %collective-permute-start.21 = (f32[2,40,512]{2,1,0:T(8,128)S(1)}, f32[2,40,512]{2,1,0:T(8,128)S(1)}, u32[]{:S(2)}, u32[]{:S(2)}) collective-permute-start(f32[2,40,512]{2,1,0:T(8,128)S(1)} %fusion.1), channel_id=1, source_target_pairs={{1,0},{2,1},{3,2},{4,3},{5,4},{6,5},{7,6},{8,7},{9,8},{10,9},{11,1... | collective-permute-start | bytes 491528 | tf_op jit(solution)/shard_map/ppermute | solution.py:34
  192.9 8.6 %collective-permute-start.28 = (f32[4,40,512]{2,1,0:T(8,128)S(1)}, f32[4,40,512]{2,1,0:T(8,128)}, u32[]{:S(2)}, u32[]{:S(2)}) collective-permute-start(f32[4,40,512]{2,1,0:T(8,128)S(1)} %get-tuple-element.51), channel_id=1, source_target_pairs={{96,0},{97,1},{98,2},{99,3},{100,4},{101,5},{102,6},{103,7},{104,8... | collective-permute-start | bytes 983048 | tf_op jit(solution)/shard_map/ppermute | solution.py:34
  195.8 26.0 %collective-permute-start.22 = (f32[2,40,512]{2,1,0:T(8,128)S(1)}, f32[2,40,512]{2,1,0:T(8,128)}, u32[]{:S(2)}, u32[]{:S(2)}) collective-permute-start(f32[2,40,512]{2,1,0:T(8,128)S(1)} %fusion.2), channel_id=1, source_target_pairs={{1,0},{2,1},{3,2},{4,3},{5,4},{6,5},{7,6},{8,7},{9,8},{10,9},{11,1... | collective-permute-start | bytes 491528 | tf_op jit(solution)/shard_map/ppermute | solution.py:34
  198.5 27.6 %collective-permute-start.30 = (f32[4,40,512]{2,1,0:T(8,128)S(1)}, f32[4,40,512]{2,1,0:T(8,128)}, u32[]{:S(2)}, u32[]{:S(2)}) collective-permute-start(f32[4,40,512]{2,1,0:T(8,128)S(1)} %get-tuple-element.52), channel_id=1, source_target_pairs={{32,0},{33,1},{34,2},{35,3},{36,4},{37,5},{38,6},{39,7},{40,8},{41... | collective-permute-start | bytes 983048 | tf_op jit(solution)/shard_map/ppermute | solution.py:34
  203.2 23.0 %collective-permute-start.29 = (f32[4,40,512]{2,1,0:T(8,128)}, f32[4,40,512]{2,1,0:T(8,128)S(1)}, u32[]{:S(2)}, u32[]{:S(2)}) collective-permute-start(f32[4,40,512]{2,1,0:T(8,128)} %add.136), channel_id=1, source_target_pairs={{96,0},{97,1},{98,2},{99,3},{100,4},{101,5},{102,6},{103,7},{104,8... | collective-permute-start | bytes 983048 | tf_op jit(solution)/shard_map/ppermute | solution.py:34
  209.2 43.1 %all-to-all-start.2 = ((f32[32,8,128]{2,1,0:T(8,128)}), f32[32,8,128]{2,1,0:T(8,128)S(1)}, u32[]{:S(2)}, u32[]{:S(2)}) async-start(f32[32,8,128]{2,1,0:T(8,128)} %broadcast_in_dim.29), calls=%async_computation.2 | async-start | bytes 262144 | tf_op jit(solution)/shard_map/all_to_all | solution.py:296
  222.8 9.7 %collective-permute-start.23 = (f32[2,40,512]{2,1,0:T(8,128)S(1)}, f32[2,40,512]{2,1,0:T(8,128)S(1)}, u32[]{:S(2)}, u32[]{:S(2)}) collective-permute-start(f32[2,40,512]{2,1,0:T(8,128)S(1)} %fusion.3), channel_id=1, source_target_pairs={{1,0},{2,1},{3,2},{4,3},{5,4},{6,5},{7,6},{8,7},{9,8},{10,9},{11,1... | collective-permute-start | bytes 491528 | tf_op jit(solution)/shard_map/ppermute | solution.py:34
  233.5 7.5 %collective-permute-start.24 = (f32[2,40,512]{2,1,0:T(8,128)S(1)}, f32[2,40,512]{2,1,0:T(8,128)S(1)}, u32[]{:S(2)}, u32[]{:S(2)}) collective-permute-start(f32[2,40,512]{2,1,0:T(8,128)S(1)} %fusion.4), channel_id=1, source_target_pairs={{1,0},{2,1},{3,2},{4,3},{5,4},{6,5},{7,6},{8,7},{9,8},{10,9},{11,1... | collective-permute-start | bytes 491528 | tf_op jit(solution)/shard_map/ppermute | solution.py:34
  235.7 8.6 %collective-permute-start.31 = (f32[40,512]{1,0:T(8,128)S(1)}, f32[40,512]{1,0:T(8,128)S(1)}, u32[]{:S(2)}, u32[]{:S(2)}) collective-permute-start(f32[40,512]{1,0:T(8,128)S(1)} %get-tuple-element.53), channel_id=1, source_target_pairs={{384,0},{385,1},{386,2},{387,3},{388,4},{389,5},{390,6},{391,7},{3... | collective-permute-start | bytes 245768 | tf_op jit(solution)/shard_map/ppermute | solution.py:34
  238.4 15.8 %collective-permute-start.33 = (f32[40,512]{1,0:T(8,128)S(1)}, f32[40,512]{1,0:T(8,128)S(1)}, u32[]{:S(2)}, u32[]{:S(2)}) collective-permute-start(f32[40,512]{1,0:T(8,128)S(1)} %get-tuple-element.54), channel_id=1, source_target_pairs={{128,0},{129,1},{130,2},{131,3},{132,4},{133,5},{134,6},{135,7},{1... | collective-permute-start | bytes 245768 | tf_op jit(solution)/shard_map/ppermute | solution.py:34
  242.0 7.3 %collective-permute-start.25 = (f32[2,40,512]{2,1,0:T(8,128)S(1)}, f32[2,40,512]{2,1,0:T(8,128)S(1)}, u32[]{:S(2)}, u32[]{:S(2)}) collective-permute-start(f32[2,40,512]{2,1,0:T(8,128)S(1)} %fusion.5), channel_id=1, source_target_pairs={{1,0},{2,1},{3,2},{4,3},{5,4},{6,5},{7,6},{8,7},{9,8},{10,9},{11,1... | collective-permute-start | bytes 491528 | tf_op jit(solution)/shard_map/ppermute | solution.py:34
  244.3 9.9 %collective-permute-start.32 = (f32[40,512]{1,0:T(8,128)S(1)}, f32[40,512]{1,0:T(8,128)S(1)}, u32[]{:S(2)}, u32[]{:S(2)}) collective-permute-start(f32[40,512]{1,0:T(8,128)S(1)} %fusion.7), channel_id=1, source_target_pairs={{384,0},{385,1},{386,2},{387,3},{388,4},{389,5},{390,6},{391,7},{3... | collective-permute-start | bytes 245768 | tf_op jit(solution)/shard_map/ppermute | solution.py:34
  250.2 7.3 %collective-permute-start.26 = (f32[2,40,512]{2,1,0:T(8,128)S(1)}, f32[2,40,512]{2,1,0:T(8,128)S(1)}, u32[]{:S(2)}, u32[]{:S(2)}) collective-permute-start(f32[2,40,512]{2,1,0:T(8,128)S(1)} %fusion.6), channel_id=1, source_target_pairs={{1,0},{2,1},{3,2},{4,3},{5,4},{6,5},{7,6},{8,7},{9,8},{10,9},{11,1... | collective-permute-start | bytes 491528 | tf_op jit(solution)/shard_map/ppermute | solution.py:34
  257.5 6.8 %collective-permute-start.27 = (f32[40,512]{1,0:T(8,128)S(1)}, f32[40,512]{1,0:T(8,128)S(1)}, u32[]{:S(2)}, u32[]{:S(2)}) collective-permute-start(f32[40,512]{1,0:T(8,128)S(1)} %fusion.10), channel_id=1, source_target_pairs={{16,0},{17,1},{18,2},{19,3},{20,4},{21,5},{22,6},{23,7},{24,8},{25... | collective-permute-start | bytes 245768 | tf_op jit(solution)/shard_map/ppermute | solution.py:34
  (14 other events, 176.6 us)

commit v2 on v1

v2 whole, which is shorter than its diff:
```python
import functools

import jax
import jax.numpy as jnp
import numpy as np
from jax import lax
from jax.experimental import pallas as pl
from jax.experimental.pallas import tpu as pltpu
from jax.sharding import Mesh, PartitionSpec as P

inv_temp = 1.0 / 0.07
eps_norm = 1e-06
NX, NY, NC, NZ = 4, 4, 2, 16
NH, NL = 4, 4
ALL = ("x", "y", "core", "zh", "zl")
B = 40
D = 512
ROWS = NX * NC * NL * B
COLS = NY * NH * B
BATCH = NX * NY * NC * NZ * B
E = B + 8
GROUP = 4 * B + 8
PLACES = (0, 1, -1, 2)
VMEM_LIMIT = 48 * 2**20


def permute(value, source):
    pairs = []
    for x in range(NX):
        for y in range(NY):
            for c in range(NC):
                for z in range(NZ):
                    sx, sy, sc, sz = source(x, y, c, z)
                    src = (((sx % NX) * NY + sy % NY) * NC + sc) * NZ + sz
                    pairs.append((src, ((x * NY + y) * NC + c) * NZ + z))
    return lax.ppermute(value, ALL, pairs)


def along_x(value, step):
    return permute(value, lambda x, y, c, z: (x + (1 - 2 * c) * step, y, c, z))


def along_y(value, step):
    return permute(value, lambda x, y, c, z: (x, y + (1 - 2 * c) * step, c, z))


def along_zh(value, step):
    return permute(value, lambda x, y, c, z: (x, y, c, (z + (1 - 2 * c) * NL * step) % NZ))


def swap_zl(value, bit):
    return permute(value, lambda x, y, c, z: (x, y, c, z ^ bit))


def swap_core(value):
    return permute(value, lambda x, y, c, z: (x, y, c ^ 1, z))


def row_blocks(x, c, zl):
    found = []
    for other in range(2):
        core = c if other == 0 else 1 - c
        sign = 1 - 2 * core
        for j, dx in enumerate(PLACES):
            bx = lax.rem(x + sign * dx + NX, NX)
            for k, flip in enumerate((0, 2, 1, 3)):
                found.append((other, j, k, (bx * NC + core) * NL + (zl ^ flip)))
    return found


def col_blocks(y, c, zh):
    s = 1 - 2 * c
    found = []
    for j, dy in enumerate(PLACES):
        by = lax.rem(y + s * dy + NY, NY)
        for k, dz in enumerate(PLACES):
            found.append((j, k, lax.rem(zh + s * dz + NH, NH) * NY + by))
    return found


def block_at(ref, block):
    return ref.at[pl.ds(pl.multiple_of(block * B, 8), B), :]


def split(value):
    high = value.astype(jnp.bfloat16)
    return high, (value - high.astype(jnp.float32)).astype(jnp.bfloat16)


def product(a_high, a_low, b_high, b_low, dims):
    dot = functools.partial(
        lax.dot_general, dimension_numbers=(dims, ((), ())), preferred_element_type=jnp.float32
    )
    return dot(a_high, b_high) + (dot(a_high, b_low) + dot(a_low, b_high))


def eye():
    return lax.broadcasted_iota(jnp.int32, (128, 128), 0) == lax.broadcasted_iota(
        jnp.int32, (128, 128), 1
    )


def to_lanes(column):
    return jnp.sum(jnp.where(eye(), column, 0.0), axis=0, keepdims=True)


def to_rows(lanes):
    return jnp.sum(jnp.where(eye(), lanes, 0.0), axis=1, keepdims=True)


STEP = 256


def scores_kernel(place, ids, wanted, *refs):
    rows_in, others_in, cols_in = refs[:4], refs[4], refs[5:9]
    expo, ph, plow, hh, hlow, row_sums, col_sums, punit, hunit = refs[9:]
    x, y, c, zh, zl = (place[k] for k in range(5))

    def unit(v):
        return v * (1.0 / jnp.sqrt(jnp.sum(v * v, axis=1, keepdims=True) + eps_norm))

    for j, k, block in col_blocks(y, c, zh):
        block_at(hunit, block)[...] = unit(cols_in[j][k])
    for other, j, k, block in row_blocks(x, c, zl):
        block_at(punit, block)[...] = unit(others_in[j, k] if other else rows_in[j][k])
    hh[...], hlow[...] = split(hunit[...])
    places = ids[...]

    def step(i, carry):
        total, positive = carry
        here = pl.ds(pl.multiple_of(i * STEP, STEP), STEP)
        high, low = split(punit[here, :])
        ph[here, :] = high
        plow[here, :] = low
        scores = product(high, low, hh[...], hlow[...], ((1,), (1,))) * inv_temp
        e = jnp.exp(scores - inv_temp)
        expo[here, :] = e
        sums = jnp.sum(e, axis=1, keepdims=True)
        for k in range(STEP // 128):
            lanes = pl.ds(pl.multiple_of(i * STEP + k * 128, 128), 128)
            row_sums[:, lanes] = to_lanes(sums[k * 128 : (k + 1) * 128])
        match = wanted[here, :] == places
        total = total + jnp.sum(e.reshape(STEP // 8, 8, COLS), axis=0)
        positive = positive + jnp.sum(
            jnp.where(match, scores, 0.0).reshape(STEP // 8, 8, COLS), axis=0
        )
        return total, positive

    zero = jnp.zeros((8, COLS), jnp.float32)
    total, positive = lax.fori_loop(0, ROWS // STEP, step, (zero, zero))
    col_sums[...] = jnp.sum(total, axis=0, keepdims=True)
    positive = jnp.sum(positive, axis=0, keepdims=True)
    row_sums[:, ROWS:] = sum(positive[:, k * 128 : (k + 1) * 128] for k in range(COLS // 128))


def packet_kernel(place, ids, wanted, rows, cols, expo, hh, hlow, mine, others, row_term, dh, dlow, grads):
    x, y, c, zh, zl = (place[k] for k in range(5))
    scale = inv_temp / (2.0 * BATCH)
    rows = jnp.sum(rows[...], axis=0, keepdims=True)
    cols = jnp.sum(cols[...], axis=0, keepdims=True)
    row_term[...] = jnp.zeros_like(row_term) + (
        jnp.sum(jnp.log(rows[:, :ROWS])) - 2.0 * jnp.sum(rows[:, ROWS:])
    )
    col_term = jnp.sum(jnp.log(cols))
    row_inv = scale / rows[:, :ROWS]
    col_inv = scale / cols
    places = ids[...]
    for i in range(ROWS // STEP):
        here = pl.ds(i * STEP, STEP)
        per_row = jnp.concatenate(
            [to_rows(row_inv[:, k : k + 128]) for k in range(i * STEP, (i + 1) * STEP, 128)], axis=0
        )
        match = wanted[here, :] == places
        d = expo[here, :] * (per_row + col_inv) - jnp.where(match, 2.0 * scale, 0.0)
        high, low = split(d)
        dh[here, :] = high
        dlow[here, :] = low
        grads[here, :] = product(high, low, hh[...], hlow[...], ((1,), (0,)))
    for other, j, k, block in row_blocks(x, c, zl):
        out = others if other else mine
        out[j, k * B : (k + 1) * B, :] = block_at(grads, block)[...]
    for out in (mine, others):
        out[:, 4 * B :, :] = jnp.zeros((4, 8, D), jnp.float32) + col_term


def header_kernel(place, dh, dlow, ph, plow, row_term, out, grads):
    x, y, c, zh, zl = (place[k] for k in range(5))
    for k in range(COLS // 128):
        here = pl.ds(k * 128, 128)
        grads[here, :] = product(dh[:, here], dlow[:, here], ph[...], plow[...], ((0,), (0,)))
    for j, k, block in col_blocks(y, c, zh):
        out[j, k * E : k * E + B, :] = block_at(grads, block)[...]
        out[j, k * E + B : (k + 1) * E, :] = row_term[...]


def in_vmem(count):
    return [pl.BlockSpec(memory_space=pltpu.VMEM)] * count


def call(kernel, operands, outs, scratch, flops):
    return pl.pallas_call(
        kernel,
        in_specs=[pl.BlockSpec(memory_space=pltpu.SMEM)] + in_vmem(len(operands) - 1),
        out_specs=in_vmem(len(outs)),
        out_shape=outs,
        scratch_shapes=scratch,
        compiler_params=pltpu.CompilerParams(vmem_limit_bytes=VMEM_LIMIT),
        cost_estimate=pl.CostEstimate(flops=flops, bytes_accessed=8 * 2**20, transcendentals=0),
    )(*operands)


def f32(*shape):
    return jax.ShapeDtypeStruct(shape, jnp.float32)


def b16(*shape):
    return jax.ShapeDtypeStruct(shape, jnp.bfloat16)


def unit_rows(values):
    norms = jnp.sqrt(jnp.sum(values * values, axis=1, keepdims=True) + eps_norm)
    return (values / norms, norms)


def unit_back(grads, units, norms):
    return (grads - units * jnp.sum(units * grads, axis=1, keepdims=True)) / norms


def together(*values):
    return lax.optimization_barrier(values)


def gather(packet, header):
    za = along_zh(header, 1)
    zb = along_zh(header, -1)
    two = jnp.stack([packet, swap_zl(packet, 2)])
    za, two = together(za, two)
    zc = along_zh(za, 1)
    prow = jnp.concatenate([two, swap_zl(two, 1)])
    hrow = jnp.stack([header, za, zb, zc])
    hrow, prow = together(hrow, prow)
    ya, yb = along_y(hrow, 1), along_y(hrow, -1)
    xa, xb = along_x(prow, 1), along_x(prow, -1)
    ya, yb, xa = together(ya, yb, xa)
    yc, xc = together(along_y(ya, 1), along_x(xa, 1))
    rows_in = [prow, xa, xb, xc]
    return rows_in, swap_core(jnp.stack(rows_in)), [hrow, ya, yb, yc]


def scatter(mine, others, hpart):
    mine = mine + swap_core(others)
    ya = hpart[1] + along_y(hpart[3], -1)
    ya, mine = together(ya, mine)
    xa = mine[1] + along_x(mine[3], -1)
    hrow = hpart[0] + along_y(ya, -1) + along_y(hpart[2], 1)
    xa, hrow = together(xa, hrow)
    za = hrow[E : 2 * E] + along_zh(hrow[3 * E :], -1)
    prow = mine[0] + along_x(xa, -1) + along_x(mine[2], 1)
    za, prow = together(za, prow)
    two = jnp.concatenate([prow[: 2 * B], prow[4 * B :]]) + swap_zl(prow[2 * B :], 1)
    hown = hrow[:E] + along_zh(za, -1) + along_zh(hrow[2 * E : 3 * E], 1)
    got = swap_zl(two[B:], 2)
    return two[:B] + got[:B], two[2 * B, 0] + got[B, 0], hown[:B], hown[B, 0]


def per_device(packet, header, partner):
    x, y, c, zh, zl = (lax.axis_index(name) for name in ALL)
    place = jnp.stack([x, y, c, zh, zl]).astype(jnp.int32)
    lane = np.arange(COLS)
    ids = lane // (NY * B) * (NL * NX * NY * NC * B) + lane // B % NY * (NC * B) + lane % B
    ids = jnp.asarray(ids, jnp.int32)[None, :]
    ids = ids + ((zl * NX + x) * (NY * NC * B) + c * B).astype(jnp.int32)
    wanted = lax.dynamic_slice(
        partner.reshape(NX, NY, NC, NH, NL, B), [0, y, 0, zh, 0, 0], (NX, 1, NC, 1, NL, B)
    ).reshape(ROWS, 1)

    rows_in, others_in, cols_in = gather(packet, header)
    flops = 2 * 3 * ROWS * COLS * D
    expo, ph, plow, hh, hlow, rows, cols = call(
        scores_kernel,
        [place, ids, wanted] + rows_in + [others_in] + cols_in,
        [f32(ROWS, COLS), b16(ROWS, D), b16(ROWS, D), b16(COLS, D), b16(COLS, D), f32(1, ROWS + 128), f32(1, COLS)],
        [pltpu.VMEM((ROWS, D), jnp.float32), pltpu.VMEM((COLS, D), jnp.float32)],
        flops,
    )
    rows = lax.all_to_all(
        jnp.broadcast_to(rows[None], (NX * NC * NL, 1, ROWS + 128)), ("x", "core", "zl"), 0, 0
    )
    cols = lax.all_to_all(jnp.broadcast_to(cols[None], (NY * NH, 1, COLS)), ("y", "zh"), 0, 0)
    rows, cols = rows[:, 0], cols[:, 0]

    mine, others, row_term, dh, dlow = call(
        packet_kernel,
        [place, ids, wanted, rows, cols, expo, hh, hlow],
        [f32(4, GROUP, D), f32(4, GROUP, D), f32(8, D), b16(ROWS, COLS), b16(ROWS, COLS)],
        [pltpu.VMEM((ROWS, D), jnp.float32)],
        flops,
    )
    (gh_parts,) = call(
        header_kernel,
        [place, dh, dlow, ph, plow, row_term],
        [f32(4, 4 * E, D)],
        [pltpu.VMEM((COLS, D), jnp.float32)],
        flops,
    )
    gpunit, col_terms, ghunit, row_terms = scatter(mine, others, gh_parts)
    loss = inv_temp + (row_terms + col_terms) / (2.0 * BATCH)
    punit, pnorm = unit_rows(packet)
    hunit, hnorm = unit_rows(header)
    packet_grad = unit_back(gpunit, punit, pnorm)
    header_grad = unit_back(ghunit, hunit, hnorm)
    return (loss, packet_grad, header_grad)


def solution(mesh):
    mesh = Mesh(mesh.devices.reshape(NX, NY, NC, NH, NL), ALL)
    by_packet, by_header = P(ALL, None), P(("zh", "zl", "x", "y", "core"), None)
    return jax.shard_map(
        per_device,
        mesh=mesh,
        in_specs=(by_packet, by_header, P()),
        out_specs=(P(), by_packet, by_header),
        check_vma=False,
    )
```

time: 268 us -> 224 us (0.84)
  starting transfers between devices: 147 us -> 112 us
  blocking collectives: 11.5 us -> 0 us
  other arithmetic: 15.1 us -> 5.81 us
  waiting for transfers between devices: 59.6 us -> 66.5 us
  local copies, waits for them, and re-layouts: 7.51 us -> 10.4 us
    ppermute x34 -> x24, starting transfers between devices: 125 us -> 100 us  [permute(): return lax.ppermute(value, ALL, pairs)]
    all_to_all x1 -> x0, blocking collectives: 11.5 us -> none  [per_device(): lax.all_to_all(jnp.broadcast_to(col_part, (NX * NY, 8, 128)), ('x', 'y'),...]
    all_to_all x2, starting transfers between devices: 21.7 us -> 12.2 us  [the longest x1 6.7 us: per_device(): lax.all_to_all(jnp.broadcast_to(cols[None], (NY * NH, 1, COLS)), ('y', 'z...]
    add x13 -> x9, other arithmetic: 6.83 us -> 0.68 us  [the longest x1 0.29 us: scatter(): mine = mine + swap_core(others)]
    ppermute x34 -> x24, waiting for transfers between devices: 38 us -> 43.5 us  [permute(): return lax.ppermute(value, ALL, pairs)]
    unnamed x20 -> x26, local copies, waits for them, and re-layouts: 3.89 us -> 6.48 us
  transfers between devices with their start and end apart: 36 -> 26, of which waited for: 18 -> 14; matrix products, arithmetic and copies ran while one was open for 6% -> 2% of each run, Pallas kernels for 2% -> 2%
where the time goes in v2:
time: 224 us; the launch traced here: 220 us
  starting transfers between devices  112 us (50%)
  waiting for transfers between devices  66.5 us (30%)
  Pallas kernels  20.5 us (9%)
  local copies, waits for them, and re-layouts  10.4 us (5%)
  other arithmetic  5.81 us (3%)
  between operations  4.32 us (2%)
    ppermute x24, starting transfers between devices, permute(): return lax.ppermute(value, ALL, pairs)  100 us
    ppermute x24, waiting for transfers between devices, permute(): return lax.ppermute(value, ALL, pairs)  43.5 us
    pallas_call x3, Pallas kernels, call(): pl.pallas_call(kernel, in_specs=[pl.BlockSpec(memory_space=pltpu.SMEM)] +...  20.5 us
    all_to_all x1, waiting for transfers between devices, per_device(): lax.all_to_all(jnp.broadcast_to(cols[None], (NY * NH, 1, COLS)), ('y', 'z...  13.7 us
    all_to_all x1, waiting for transfers between devices, per_device(): lax.all_to_all(jnp.broadcast_to(rows[None], (NX * NC * NL, 1, ROWS + 128)...  9.4 us
    all_to_all x1, starting transfers between devices, per_device(): lax.all_to_all(jnp.broadcast_to(cols[None], (NY * NH, 1, COLS)), ('y', 'z...  6.7 us
    unnamed x26, local copies, waits for them, and re-layouts  6.48 us
    all_to_all x1, starting transfers between devices, per_device(): lax.all_to_all(jnp.broadcast_to(rows[None], (NX * NC * NL, 1, ROWS + 128)...  5.53 us
  transfers between devices with their start and end apart: 26, of which 14 were waited for; matrix products, arithmetic and copies ran while one was open for 2% of the time, Pallas kernels for 2%

profile of v2, /device:TPU:1, one launch (start us, length us, event | category | flops | bytes accessed | tf_op | source)
XLA Modules:
  0.0 220.0 jit_solution(4202599573970907797)
XLA Ops:
  0.6 5.7 %collective-permute-start.1 = (f32[40,512]{1,0:T(8,128)}, f32[40,512]{1,0:T(8,128)S(1)}, u32[]{:S(2)}, u32[]{:S(2)}) collective-permute-start(f32[40,512]{1,0:T(8,128)} %param.4), channel_id=1, source_target_pairs={{2,0},{3,1},{0,2},{1,3},{6,4},{7,5},{4,6},{5,7},{10,8},{11,9},{8,1... | collective-permute-start | bytes 245768 | tf_op jit(solution)/shard_map/ppermute | solution.py:36
  6.4 8.8 %collective-permute-start = (f32[40,512]{1,0:T(8,128)}, f32[40,512]{1,0:T(8,128)S(1)}, u32[]{:S(2)}, u32[]{:S(2)}) collective-permute-start(f32[40,512]{1,0:T(8,128)} %param.5), channel_id=1, source_target_pairs={{4,0},{5,1},{6,2},{7,3},{8,4},{9,5},{10,6},{11,7},{12,8},{13,9},{1... | collective-permute-start | bytes 245768 | tf_op jit(solution)/shard_map/ppermute | solution.py:36
  15.2 3.8 %collective-permute-start.2 = (f32[40,512]{1,0:T(8,128)}, f32[40,512]{1,0:T(8,128)S(1)}, u32[]{:S(2)}, u32[]{:S(2)}) collective-permute-start(f32[40,512]{1,0:T(8,128)} %param.5), channel_id=1, source_target_pairs={{12,0},{13,1},{14,2},{15,3},{0,4},{1,5},{2,6},{3,7},{4,8},{5,9},{6... | collective-permute-start | bytes 245768 | tf_op jit(solution)/shard_map/ppermute | solution.py:36
  19.9 6.3 %collective-permute-start.3 = (f32[40,512]{1,0:T(8,128)S(1)}, f32[40,512]{1,0:T(8,128)S(1)}, u32[]{:S(2)}, u32[]{:S(2)}) collective-permute-start(f32[40,512]{1,0:T(8,128)S(1)} %collective-permute-done), channel_id=1, source_target_pairs={{4,0},{5,1},{6,2},{7,3},{8,4},{9,5},{10,6},{11,7},{12,8},{13,9},{1... | collective-permute-start | bytes 245768 | tf_op jit(solution)/shard_map/ppermute | solution.py:36
  26.2 4.3 %collective-permute-start.4 = (f32[2,40,512]{2,1,0:T(8,128)S(1)}, f32[2,40,512]{2,1,0:T(8,128)S(1)}, u32[]{:S(2)}, u32[]{:S(2)}) collective-permute-start(f32[2,40,512]{2,1,0:T(8,128)S(1)} %pad_maximum_fusion.3), channel_id=1, source_target_pairs={{1,0},{0,1},{3,2},{2,3},{5,4},{4,5},{7,6},{6,7},{9,8},{8,9},{11,10... | collective-permute-start | bytes 491528 | tf_op jit(solution)/shard_map/ppermute | solution.py:36
  31.5 2.8 %collective-permute-done.4 = f32[2,40,512]{2,1,0:T(8,128)S(1)} collective-permute-done((f32[2,40,512]{2,1,0:T(8,128)S(1)}, f32[2,40,512]{2,1,0:T(8,128)S(1)}, u32[]{:S(2)}, u32[]{:S(2)}) %collective-permute-start.4) | collective-permute-done | bytes 163872 | tf_op jit(solution)/shard_map/ppermute | solution.py:36
  34.3 3.1 %collective-permute-start.7 = (f32[4,40,512]{2,1,0:T(8,128)S(1)}, f32[4,40,512]{2,1,0:T(8,128)S(1)}, u32[]{:S(2)}, u32[]{:S(2)}) collective-permute-start(f32[4,40,512]{2,1,0:T(8,128)S(1)} %pad_maximum_fusion.2.refs_0_), channel_id=1, source_target_pairs={{128,0},{129,1},{130,2},{131,3},{132,4},{133,5},{134,6},{135,7},{1... | collective-permute-start | bytes 983048 | tf_op jit(solution)/shard_map/ppermute | solution.py:36
  37.4 3.2 %collective-permute-start.5 = (f32[4,40,512]{2,1,0:T(8,128)S(1)}, f32[4,40,512]{2,1,0:T(8,128)S(1)}, u32[]{:S(2)}, u32[]{:S(2)}) collective-permute-start(f32[4,40,512]{2,1,0:T(8,128)S(1)} %pad_maximum_fusion.1.refs_5_), channel_id=1, source_target_pairs={{32,0},{33,1},{34,2},{35,3},{36,4},{37,5},{38,6},{39,7},{40,8},{41... | collective-permute-start | bytes 983048 | tf_op jit(solution)/shard_map/ppermute | solution.py:36
  40.6 3.4 %collective-permute-start.6 = (f32[4,40,512]{2,1,0:T(8,128)S(1)}, f32[4,40,512]{2,1,0:T(8,128)S(1)}, u32[]{:S(2)}, u32[]{:S(2)}) collective-permute-start(f32[4,40,512]{2,1,0:T(8,128)S(1)} %pad_maximum_fusion.1.refs_5_), channel_id=1, source_target_pairs={{96,0},{97,1},{98,2},{99,3},{100,4},{101,5},{102,6},{103,7},{104,8... | collective-permute-start | bytes 983048 | tf_op jit(solution)/shard_map/ppermute | solution.py:36
  48.7 3.3 %collective-permute-start.10 = (f32[4,40,512]{2,1,0:T(8,128)S(1)}, f32[4,40,512]{2,1,0:T(8,128)S(1)}, u32[]{:S(2)}, u32[]{:S(2)}) collective-permute-start(f32[4,40,512]{2,1,0:T(8,128)S(1)} %collective-permute-done.7.refs_1_), channel_id=1, source_target_pairs={{128,0},{129,1},{130,2},{131,3},{132,4},{133,5},{134,6},{135,7},{1... | collective-permute-start | bytes 983048 | tf_op jit(solution)/shard_map/ppermute | solution.py:36
  52.0 3.3 %collective-permute-start.9 = (f32[4,40,512]{2,1,0:T(8,128)S(1)}, f32[4,40,512]{2,1,0:T(8,128)S(1)}, u32[]{:S(2)}, u32[]{:S(2)}) collective-permute-start(f32[4,40,512]{2,1,0:T(8,128)S(1)} %collective-permute-done.5.refs_6_), channel_id=1, source_target_pairs={{32,0},{33,1},{34,2},{35,3},{36,4},{37,5},{38,6},{39,7},{40,8},{41... | collective-permute-start | bytes 983048 | tf_op jit(solution)/shard_map/ppermute | solution.py:36
  55.3 3.1 %collective-permute-start.8 = (f32[4,40,512]{2,1,0:T(8,128)S(1)}, f32[4,40,512]{2,1,0:T(8,128)S(1)}, u32[]{:S(2)}, u32[]{:S(2)}) collective-permute-start(f32[4,40,512]{2,1,0:T(8,128)S(1)} %pad_maximum_fusion.2.refs_0_), channel_id=1, source_target_pairs={{384,0},{385,1},{386,2},{387,3},{388,4},{389,5},{390,6},{391,7},{3... | collective-permute-start | bytes 983048 | tf_op jit(solution)/shard_map/ppermute | solution.py:36
  58.4 5.0 %collective-permute-done.9.refs_8_ = f32[4,40,512]{2,1,0:T(8,128)S(1)} collective-permute-done((f32[4,40,512]{2,1,0:T(8,128)S(1)}, f32[4,40,512]{2,1,0:T(8,128)S(1)}, u32[]{:S(2)}, u32[]{:S(2)}) %collective-permute-start.9) | collective-permute-done | bytes 327712 | tf_op jit(solution)/shard_map/ppermute | solution.py:36
  64.6 15.5 %collective-permute-start.11 = (f32[4,4,40,512]{3,2,1,0:T(8,128)}, f32[4,4,40,512]{3,2,1,0:T(8,128)}, u32[]{:S(2)}, u32[]{:S(2)}) collective-permute-start(f32[4,4,40,512]{3,2,1,0:T(8,128)} %pad_maximum_fusion), channel_id=1, source_target_pairs={{16,0},{17,1},{18,2},{19,3},{20,4},{21,5},{22,6},{23,7},{24,8},{25... | collective-permute-start | bytes 3932168 | tf_op jit(solution)/shard_map/ppermute | solution.py:36
  83.1 8.6 %shard_map.67 = (f32[1280,640]{1,0:T(8,128)}, bf16[1280,512]{1,0:T(8,128)(2,1)S(1)}, bf16[1280,512]{1,0:T(8,128)(2,1)}, bf16[640,512]{1,0:T(8,128)(2,1)S(1)}, bf...) custom-call(s32[5]{0:T(128)S(1)} %stack.62.place, s32[1,640]{1,0:T(1,128)S(1)} %add.84.ids, ...), custom_call_target="tpu_custom_call" | custom-call | flops 2516582400 | bytes 8388608 | tf_op jit(solution)/shard_map/pallas_call | solution.py:201
  95.2 6.7 %all-to-all-start.1 = ((f32[16,1,640]{2,1,0:T(1,128)}), f32[16,1,640]{2,1,0:T(1,128)S(1)}, u32[]{:S(2)}, u32[]{:S(2)}) async-start(f32[16,1,640]{2,1,0:T(1,128)} %broadcast_in_dim.11), calls=%async_computation.1 | async-start | bytes 81920 | tf_op jit(solution)/shard_map/all_to_all | solution.py:289
  101.9 13.7 %all-to-all-done.1 = f32[16,1,640]{2,1,0:T(1,128)S(1)} async-done(((f32[16,1,640]{2,1,0:T(1,128)}), f32[16,1,640]{2,1,0:T(1,128)S(1)}, u32[]{:S(2)}, u32[]{:S(2)}) %all-to-all-start.1) | async-done | bytes 40992 | tf_op jit(solution)/shard_map/all_to_all | solution.py:289
  116.3 5.5 %all-to-all-start = ((f32[32,1,1408]{2,1,0:T(1,128)}), f32[32,1,1408]{2,1,0:T(1,128)S(1)}, u32[]{:S(2)}, u32[]{:S(2)}) async-start(f32[32,1,1408]{2,1,0:T(1,128)} %broadcast_in_dim.9), calls=%async_computation | async-start | bytes 360448 | tf_op jit(solution)/shard_map/all_to_all | solution.py:286
  121.9 9.4 %all-to-all-done = f32[32,1,1408]{2,1,0:T(1,128)S(1)} async-done(((f32[32,1,1408]{2,1,0:T(1,128)}), f32[32,1,1408]{2,1,0:T(1,128)S(1)}, u32[]{:S(2)}, u32[]{:S(2)}) %all-to-all-start) | async-done | bytes 180256 | tf_op jit(solution)/shard_map/all_to_all | solution.py:286
  133.5 7.6 %shard_map.68 = (f32[4,168,512]{2,1,0:T(8,128)S(1)}, f32[4,168,512]{2,1,0:T(8,128)S(1)}, f32[8,512]{1,0:T(8,128)S(1)}, bf16[1280,640]{1,0:T(8,128)(2,1)}, bf16[1280,640]{1,0:T(8,128)(2,1)}) custom-call(s32[5]{0:T(128)S(1)} %stack.62.place, s32[1,640]{1,0:T(1,128)S(1)} %add.84.ids, s32[1280,1]{1,0:T(8,128)S(1)} %reshape.41.wanted, f32[32,1408]{1,0:T(8,128)S(1)} %bitcast.50, ...), custom_call_target="tpu_custom_call" | custom-call | flops 2516582400 | bytes 8388608 | tf_op jit(solution)/shard_map/pallas_call | solution.py:201
  141.1 2.5 %collective-permute-start.13 = (f32[4,168,512]{2,1,0:T(8,128)S(1)}, f32[4,168,512]{2,1,0:T(8,128)S(1)}, u32[]{:S(2)}, u32[]{:S(2)}) collective-permute-start(f32[4,168,512]{2,1,0:T(8,128)S(1)} %get-tuple-element.50), channel_id=1, source_target_pairs={{16,0},{17,1},{18,2},{19,3},{20,4},{21,5},{22,6},{23,7},{24,8},{25... | collective-permute-start | bytes 4128776 | tf_op jit(solution)/shard_map/ppermute | solution.py:36
  145.1 4.3 %shard_map.69 = f32[4,192,512]{2,1,0:T(8,128)S(1)} custom-call(s32[5]{0:T(128)S(1)} %stack.62.place, bf16[1280,640]{1,0:T(8,128)(2,1)S(1)} %copy-done, bf16[1280,640]{1,0:T(8,128)(2,1)} %get-tuple-element.45.dlow, bf16[1280,512]{1,0:T(8,128)(2,1)S(1)} %copy-done.2, bf16[1280,512]{1,0:T(8,128)(2,1)S(1)} %copy-done.3, f32[8,512]{1,0:T(8,128)S(1)} %get-tuple-element.48.row_term), custom_call_target="tpu_custom_call" | custom-call | flops 2516582400 | bytes 8388608 | tf_op jit(solution)/shard_map/pallas_call | solution.py:201
  149.5 2.8 %collective-permute-start.12 = (f32[192,512]{1,0:T(8,128)S(1)}, f32[192,512]{1,0:T(8,128)S(1)}, u32[]{:S(2)}, u32[]{:S(2)}) collective-permute-start(f32[192,512]{1,0:T(8,128)S(1)} %get-tuple-element.58), channel_id=1, source_target_pairs={{96,0},{97,1},{98,2},{99,3},{100,4},{101,5},{102,6},{103,7},{104,8... | collective-permute-start | bytes 1179656 | tf_op jit(solution)/shard_map/ppermute | solution.py:36
  152.3 6.0 %collective-permute-done.12 = f32[192,512]{1,0:T(8,128)S(1)} collective-permute-done((f32[192,512]{1,0:T(8,128)S(1)}, f32[192,512]{1,0:T(8,128)S(1)}, u32[]{:S(2)}, u32[]{:S(2)}) %collective-permute-start.12) | collective-permute-done | bytes 393248 | tf_op jit(solution)/shard_map/ppermute | solution.py:36
  158.7 2.8 %collective-permute-start.14 = (f32[168,512]{1,0:T(8,128)S(1)}, f32[168,512]{1,0:T(8,128)S(1)}, u32[]{:S(2)}, u32[]{:S(2)}) collective-permute-start(f32[168,512]{1,0:T(8,128)S(1)} %get-tuple-element.60), channel_id=1, source_target_pairs={{384,0},{385,1},{386,2},{387,3},{388,4},{389,5},{390,6},{391,7},{3... | collective-permute-start | bytes 1032200 | tf_op jit(solution)/shard_map/ppermute | solution.py:36
  163.8 4.3 %collective-permute-start.15 = (f32[192,512]{1,0:T(8,128)S(1)}, f32[192,512]{1,0:T(8,128)S(1)}, u32[]{:S(2)}, u32[]{:S(2)}) collective-permute-start(f32[192,512]{1,0:T(8,128)S(1)} %fusion.2), channel_id=1, source_target_pairs={{96,0},{97,1},{98,2},{99,3},{100,4},{101,5},{102,6},{103,7},{104,8... | collective-permute-start | bytes 1179656 | tf_op jit(solution)/shard_map/ppermute | solution.py:36
  168.2 2.6 %collective-permute-start.19 = (f32[168,512]{1,0:T(8,128)S(1)}, f32[168,512]{1,0:T(8,128)S(1)}, u32[]{:S(2)}, u32[]{:S(2)}) collective-permute-start(f32[168,512]{1,0:T(8,128)S(1)} %get-tuple-element.59), channel_id=1, source_target_pairs={{128,0},{129,1},{130,2},{131,3},{132,4},{133,5},{134,6},{135,7},{1... | collective-permute-start | bytes 1032200 | tf_op jit(solution)/shard_map/ppermute | solution.py:36
  171.4 5.4 %collective-permute-done.15 = f32[192,512]{1,0:T(8,128)S(1)} collective-permute-done((f32[192,512]{1,0:T(8,128)S(1)}, f32[192,512]{1,0:T(8,128)S(1)}, u32[]{:S(2)}, u32[]{:S(2)}) %collective-permute-start.15) | collective-permute-done | bytes 393248 | tf_op jit(solution)/shard_map/ppermute | solution.py:36
  181.3 9.7 %collective-permute-done.17 = f32[48,512]{1,0:T(8,128)S(1)} collective-permute-done((f32[48,512]{1,0:T(8,128)S(1)}, f32[48,512]{1,0:T(8,128)S(1)}, u32[]{:S(2)}, u32[]{:S(2)}) %collective-permute-start.17) | collective-permute-done | bytes 98336 | tf_op jit(solution)/shard_map/ppermute | solution.py:36
  193.5 6.8 %collective-permute-start.20 = (f32[48,512]{1,0:T(8,128)S(1)}, f32[48,512]{1,0:T(8,128)S(1)}, u32[]{:S(2)}, u32[]{:S(2)}) collective-permute-start(f32[48,512]{1,0:T(8,128)S(1)} %get-tuple-element.55), channel_id=1, source_target_pairs={{12,0},{13,1},{14,2},{15,3},{0,4},{1,5},{2,6},{3,7},{4,8},{5,9},{6... | collective-permute-start | bytes 294920 | tf_op jit(solution)/shard_map/ppermute | solution.py:36
  202.3 4.8 %collective-permute-done.20 = f32[48,512]{1,0:T(8,128)S(1)} collective-permute-done((f32[48,512]{1,0:T(8,128)S(1)}, f32[48,512]{1,0:T(8,128)S(1)}, u32[]{:S(2)}, u32[]{:S(2)}) %collective-permute-start.20) | collective-permute-done | bytes 98336 | tf_op jit(solution)/shard_map/ppermute | solution.py:36
  209.1 3.9 %collective-permute-start.23 = (f32[48,512]{1,0:T(8,128)S(1)}, f32[48,512]{1,0:T(8,128)S(1)}, u32[]{:S(2)}, u32[]{:S(2)}) collective-permute-start(f32[48,512]{1,0:T(8,128)S(1)} %slice.94), channel_id=1, source_target_pairs={{2,0},{3,1},{0,2},{1,3},{6,4},{7,5},{4,6},{5,7},{10,8},{11,9},{8,1... | collective-permute-start | bytes 294920 | tf_op jit(solution)/shard_map/ppermute | solution.py:36
  (89 shorter events, 36.7 us)
Async XLA Ops:
  0.6 18.3 %collective-permute-start.1 = (f32[40,512]{1,0:T(8,128)}, f32[40,512]{1,0:T(8,128)S(1)}, u32[]{:S(2)}, u32[]{:S(2)}) collective-permute-start(f32[40,512]{1,0:T(8,128)} %param.4), channel_id=1, source_target_pairs={{2,0},{3,1},{0,2},{1,3},{6,4},{7,5},{4,6},{5,7},{10,8},{11,9},{8,1... | collective-permute-start | bytes 245768 | tf_op jit(solution)/shard_map/ppermute | solution.py:36
  6.4 13.5 %collective-permute-start = (f32[40,512]{1,0:T(8,128)}, f32[40,512]{1,0:T(8,128)S(1)}, u32[]{:S(2)}, u32[]{:S(2)}) collective-permute-start(f32[40,512]{1,0:T(8,128)} %param.5), channel_id=1, source_target_pairs={{4,0},{5,1},{6,2},{7,3},{8,4},{9,5},{10,6},{11,7},{12,8},{13,9},{1... | collective-permute-start | bytes 245768 | tf_op jit(solution)/shard_map/ppermute | solution.py:36
  15.2 15.3 %collective-permute-start.2 = (f32[40,512]{1,0:T(8,128)}, f32[40,512]{1,0:T(8,128)S(1)}, u32[]{:S(2)}, u32[]{:S(2)}) collective-permute-start(f32[40,512]{1,0:T(8,128)} %param.5), channel_id=1, source_target_pairs={{12,0},{13,1},{14,2},{15,3},{0,4},{1,5},{2,6},{3,7},{4,8},{5,9},{6... | collective-permute-start | bytes 245768 | tf_op jit(solution)/shard_map/ppermute | solution.py:36
  19.9 10.6 %collective-permute-start.3 = (f32[40,512]{1,0:T(8,128)S(1)}, f32[40,512]{1,0:T(8,128)S(1)}, u32[]{:S(2)}, u32[]{:S(2)}) collective-permute-start(f32[40,512]{1,0:T(8,128)S(1)} %collective-permute-done), channel_id=1, source_target_pairs={{4,0},{5,1},{6,2},{7,3},{8,4},{9,5},{10,6},{11,7},{12,8},{13,9},{1... | collective-permute-start | bytes 245768 | tf_op jit(solution)/shard_map/ppermute | solution.py:36
  26.2 8.1 %collective-permute-start.4 = (f32[2,40,512]{2,1,0:T(8,128)S(1)}, f32[2,40,512]{2,1,0:T(8,128)S(1)}, u32[]{:S(2)}, u32[]{:S(2)}) collective-permute-start(f32[2,40,512]{2,1,0:T(8,128)S(1)} %pad_maximum_fusion.3), channel_id=1, source_target_pairs={{1,0},{0,1},{3,2},{2,3},{5,4},{4,5},{7,6},{6,7},{9,8},{8,9},{11,10... | collective-permute-start | bytes 491528 | tf_op jit(solution)/shard_map/ppermute | solution.py:36
  34.3 45.8 %copy-start.10 = (s32[20480]{0:T(1024)S(1)}, s32[20480]{0:T(1024)}, u32[]{:S(2)}) copy-start(s32[20480]{0:T(1024)} %param.6) | copy-start | bytes 245764
  34.3 9.6 %collective-permute-start.7 = (f32[4,40,512]{2,1,0:T(8,128)S(1)}, f32[4,40,512]{2,1,0:T(8,128)S(1)}, u32[]{:S(2)}, u32[]{:S(2)}) collective-permute-start(f32[4,40,512]{2,1,0:T(8,128)S(1)} %pad_maximum_fusion.2.refs_0_), channel_id=1, source_target_pairs={{128,0},{129,1},{130,2},{131,3},{132,4},{133,5},{134,6},{135,7},{1... | collective-permute-start | bytes 983048 | tf_op jit(solution)/shard_map/ppermute | solution.py:36
  37.4 9.1 %collective-permute-start.5 = (f32[4,40,512]{2,1,0:T(8,128)S(1)}, f32[4,40,512]{2,1,0:T(8,128)S(1)}, u32[]{:S(2)}, u32[]{:S(2)}) collective-permute-start(f32[4,40,512]{2,1,0:T(8,128)S(1)} %pad_maximum_fusion.1.refs_5_), channel_id=1, source_target_pairs={{32,0},{33,1},{34,2},{35,3},{36,4},{37,5},{38,6},{39,7},{40,8},{41... | collective-permute-start | bytes 983048 | tf_op jit(solution)/shard_map/ppermute | solution.py:36
  40.6 8.1 %collective-permute-start.6 = (f32[4,40,512]{2,1,0:T(8,128)S(1)}, f32[4,40,512]{2,1,0:T(8,128)S(1)}, u32[]{:S(2)}, u32[]{:S(2)}) collective-permute-start(f32[4,40,512]{2,1,0:T(8,128)S(1)} %pad_maximum_fusion.1.refs_5_), channel_id=1, source_target_pairs={{96,0},{97,1},{98,2},{99,3},{100,4},{101,5},{102,6},{103,7},{104,8... | collective-permute-start | bytes 983048 | tf_op jit(solution)/shard_map/ppermute | solution.py:36
  48.7 9.7 %collective-permute-start.10 = (f32[4,40,512]{2,1,0:T(8,128)S(1)}, f32[4,40,512]{2,1,0:T(8,128)S(1)}, u32[]{:S(2)}, u32[]{:S(2)}) collective-permute-start(f32[4,40,512]{2,1,0:T(8,128)S(1)} %collective-permute-done.7.refs_1_), channel_id=1, source_target_pairs={{128,0},{129,1},{130,2},{131,3},{132,4},{133,5},{134,6},{135,7},{1... | collective-permute-start | bytes 983048 | tf_op jit(solution)/shard_map/ppermute | solution.py:36
  52.0 11.4 %collective-permute-start.9 = (f32[4,40,512]{2,1,0:T(8,128)S(1)}, f32[4,40,512]{2,1,0:T(8,128)S(1)}, u32[]{:S(2)}, u32[]{:S(2)}) collective-permute-start(f32[4,40,512]{2,1,0:T(8,128)S(1)} %collective-permute-done.5.refs_6_), channel_id=1, source_target_pairs={{32,0},{33,1},{34,2},{35,3},{36,4},{37,5},{38,6},{39,7},{40,8},{41... | collective-permute-start | bytes 983048 | tf_op jit(solution)/shard_map/ppermute | solution.py:36
  55.3 8.1 %collective-permute-start.8 = (f32[4,40,512]{2,1,0:T(8,128)S(1)}, f32[4,40,512]{2,1,0:T(8,128)S(1)}, u32[]{:S(2)}, u32[]{:S(2)}) collective-permute-start(f32[4,40,512]{2,1,0:T(8,128)S(1)} %pad_maximum_fusion.2.refs_0_), channel_id=1, source_target_pairs={{384,0},{385,1},{386,2},{387,3},{388,4},{389,5},{390,6},{391,7},{3... | collective-permute-start | bytes 983048 | tf_op jit(solution)/shard_map/ppermute | solution.py:36
  63.4 17.4 %copy-start.11 = (s32[640]{0:T(1024)S(1)}, s32[640]{0:T(1024)}, u32[]{:S(2)}) copy-start(s32[640]{0:T(1024)} %constant.42.clone) | copy-start | bytes 7684
  64.6 18.5 %collective-permute-start.11 = (f32[4,4,40,512]{3,2,1,0:T(8,128)}, f32[4,4,40,512]{3,2,1,0:T(8,128)}, u32[]{:S(2)}, u32[]{:S(2)}) collective-permute-start(f32[4,4,40,512]{3,2,1,0:T(8,128)} %pad_maximum_fusion), channel_id=1, source_target_pairs={{16,0},{17,1},{18,2},{19,3},{20,4},{21,5},{22,6},{23,7},{24,8},{25... | collective-permute-start | bytes 3932168 | tf_op jit(solution)/shard_map/ppermute | solution.py:36
  95.2 20.4 %all-to-all-start.1 = ((f32[16,1,640]{2,1,0:T(1,128)}), f32[16,1,640]{2,1,0:T(1,128)S(1)}, u32[]{:S(2)}, u32[]{:S(2)}) async-start(f32[16,1,640]{2,1,0:T(1,128)} %broadcast_in_dim.11), calls=%async_computation.1 | async-start | bytes 81920 | tf_op jit(solution)/shard_map/all_to_all | solution.py:289
  116.3 15.0 %all-to-all-start = ((f32[32,1,1408]{2,1,0:T(1,128)}), f32[32,1,1408]{2,1,0:T(1,128)S(1)}, u32[]{:S(2)}, u32[]{:S(2)}) async-start(f32[32,1,1408]{2,1,0:T(1,128)} %broadcast_in_dim.9), calls=%async_computation | async-start | bytes 360448 | tf_op jit(solution)/shard_map/all_to_all | solution.py:286
  133.5 10.2 %copy-start.2 = (bf16[1280,512]{1,0:T(8,128)(2,1)S(1)}, bf16[1280,512]{1,0:T(8,128)(2,1)}, u32[]{:S(2)}) copy-start(bf16[1280,512]{1,0:T(8,128)(2,1)} %copy-done.1) | copy-start | bytes 3932164
  133.5 10.2 %copy-start.3 = (bf16[1280,512]{1,0:T(8,128)(2,1)S(1)}, bf16[1280,512]{1,0:T(8,128)(2,1)}, u32[]{:S(2)}) copy-start(bf16[1280,512]{1,0:T(8,128)(2,1)} %get-tuple-element.47.plow) | copy-start | bytes 3932164
  141.1 17.2 %collective-permute-start.13 = (f32[4,168,512]{2,1,0:T(8,128)S(1)}, f32[4,168,512]{2,1,0:T(8,128)S(1)}, u32[]{:S(2)}, u32[]{:S(2)}) collective-permute-start(f32[4,168,512]{2,1,0:T(8,128)S(1)} %get-tuple-element.50), channel_id=1, source_target_pairs={{16,0},{17,1},{18,2},{19,3},{20,4},{21,5},{22,6},{23,7},{24,8},{25... | collective-permute-start | bytes 4128776 | tf_op jit(solution)/shard_map/ppermute | solution.py:36
  149.5 8.8 %collective-permute-start.12 = (f32[192,512]{1,0:T(8,128)S(1)}, f32[192,512]{1,0:T(8,128)S(1)}, u32[]{:S(2)}, u32[]{:S(2)}) collective-permute-start(f32[192,512]{1,0:T(8,128)S(1)} %get-tuple-element.58), channel_id=1, source_target_pairs={{96,0},{97,1},{98,2},{99,3},{100,4},{101,5},{102,6},{103,7},{104,8... | collective-permute-start | bytes 1179656 | tf_op jit(solution)/shard_map/ppermute | solution.py:36
  158.6 2.9 %copy-start.8 = (f32[40,512]{1,0:T(8,128)S(1)}, f32[40,512]{1,0:T(8,128)}, u32[]{:S(2)}) copy-start(f32[40,512]{1,0:T(8,128)} %param.5) | copy-start | bytes 245764
  158.7 12.1 %collective-permute-start.14 = (f32[168,512]{1,0:T(8,128)S(1)}, f32[168,512]{1,0:T(8,128)S(1)}, u32[]{:S(2)}, u32[]{:S(2)}) collective-permute-start(f32[168,512]{1,0:T(8,128)S(1)} %get-tuple-element.60), channel_id=1, source_target_pairs={{384,0},{385,1},{386,2},{387,3},{388,4},{389,5},{390,6},{391,7},{3... | collective-permute-start | bytes 1032200 | tf_op jit(solution)/shard_map/ppermute | solution.py:36
  161.6 9.7 %collective-permute-start.16 = (f32[192,512]{1,0:T(8,128)S(1)}, f32[192,512]{1,0:T(8,128)S(1)}, u32[]{:S(2)}, u32[]{:S(2)}) collective-permute-start(f32[192,512]{1,0:T(8,128)S(1)} %get-tuple-element.57), channel_id=1, source_target_pairs={{32,0},{33,1},{34,2},{35,3},{36,4},{37,5},{38,6},{39,7},{40,8},{41... | collective-permute-start | bytes 1179656 | tf_op jit(solution)/shard_map/ppermute | solution.py:36
  163.8 12.9 %collective-permute-start.15 = (f32[192,512]{1,0:T(8,128)S(1)}, f32[192,512]{1,0:T(8,128)S(1)}, u32[]{:S(2)}, u32[]{:S(2)}) collective-permute-start(f32[192,512]{1,0:T(8,128)S(1)} %fusion.2), channel_id=1, source_target_pairs={{96,0},{97,1},{98,2},{99,3},{100,4},{101,5},{102,6},{103,7},{104,8... | collective-permute-start | bytes 1179656 | tf_op jit(solution)/shard_map/ppermute | solution.py:36
  168.1 13.0 %copy-start.9 = (f32[40,512]{1,0:T(8,128)S(1)}, f32[40,512]{1,0:T(8,128)}, u32[]{:S(2)}) copy-start(f32[40,512]{1,0:T(8,128)} %param.4) | copy-start | bytes 245764
  168.2 25.2 %collective-permute-start.19 = (f32[168,512]{1,0:T(8,128)S(1)}, f32[168,512]{1,0:T(8,128)S(1)}, u32[]{:S(2)}, u32[]{:S(2)}) collective-permute-start(f32[168,512]{1,0:T(8,128)S(1)} %get-tuple-element.59), channel_id=1, source_target_pairs={{128,0},{129,1},{130,2},{131,3},{132,4},{133,5},{134,6},{135,7},{1... | collective-permute-start | bytes 1032200 | tf_op jit(solution)/shard_map/ppermute | solution.py:36
  176.9 16.5 %collective-permute-start.18 = (f32[168,512]{1,0:T(8,128)S(1)}, f32[168,512]{1,0:T(8,128)S(1)}, u32[]{:S(2)}, u32[]{:S(2)}) collective-permute-start(f32[168,512]{1,0:T(8,128)S(1)} %bitcast_add_fusion.1), channel_id=1, source_target_pairs={{384,0},{385,1},{386,2},{387,3},{388,4},{389,5},{390,6},{391,7},{3... | collective-permute-start | bytes 1032200 | tf_op jit(solution)/shard_map/ppermute | solution.py:36
  178.9 12.1 %collective-permute-start.17 = (f32[48,512]{1,0:T(8,128)S(1)}, f32[48,512]{1,0:T(8,128)S(1)}, u32[]{:S(2)}, u32[]{:S(2)}) collective-permute-start(f32[48,512]{1,0:T(8,128)S(1)} %slice.74), channel_id=1, source_target_pairs={{12,0},{13,1},{14,2},{15,3},{0,4},{1,5},{2,6},{3,7},{4,8},{5,9},{6... | collective-permute-start | bytes 294920 | tf_op jit(solution)/shard_map/ppermute | solution.py:36
  191.0 11.3 %collective-permute-start.21 = (f32[48,512]{1,0:T(8,128)S(1)}, f32[48,512]{1,0:T(8,128)S(1)}, u32[]{:S(2)}, u32[]{:S(2)}) collective-permute-start(f32[48,512]{1,0:T(8,128)S(1)} %get-tuple-element.62), channel_id=1, source_target_pairs={{4,0},{5,1},{6,2},{7,3},{8,4},{9,5},{10,6},{11,7},{12,8},{13,9},{1... | collective-permute-start | bytes 294920 | tf_op jit(solution)/shard_map/ppermute | solution.py:36
  193.5 13.6 %collective-permute-start.20 = (f32[48,512]{1,0:T(8,128)S(1)}, f32[48,512]{1,0:T(8,128)S(1)}, u32[]{:S(2)}, u32[]{:S(2)}) collective-permute-start(f32[48,512]{1,0:T(8,128)S(1)} %get-tuple-element.55), channel_id=1, source_target_pairs={{12,0},{13,1},{14,2},{15,3},{0,4},{1,5},{2,6},{3,7},{4,8},{5,9},{6... | collective-permute-start | bytes 294920 | tf_op jit(solution)/shard_map/ppermute | solution.py:36
  200.4 8.7 %collective-permute-start.22 = (f32[88,512]{1,0:T(8,128)S(1)}, f32[88,512]{1,0:T(8,128)S(1)}, u32[]{:S(2)}, u32[]{:S(2)}) collective-permute-start(f32[88,512]{1,0:T(8,128)S(1)} %slice.81), channel_id=1, source_target_pairs={{1,0},{0,1},{3,2},{2,3},{5,4},{4,5},{7,6},{6,7},{9,8},{8,9},{11,10... | collective-permute-start | bytes 540680 | tf_op jit(solution)/shard_map/ppermute | solution.py:36
  209.1 6.3 %collective-permute-start.23 = (f32[48,512]{1,0:T(8,128)S(1)}, f32[48,512]{1,0:T(8,128)S(1)}, u32[]{:S(2)}, u32[]{:S(2)}) collective-permute-start(f32[48,512]{1,0:T(8,128)S(1)} %slice.94), channel_id=1, source_target_pairs={{2,0},{3,1},{0,2},{1,3},{6,4},{7,5},{4,6},{5,7},{10,8},{11,9},{8,1... | collective-permute-start | bytes 294920 | tf_op jit(solution)/shard_map/ppermute | solution.py:36
  (6 other events, 6.5 us)

commit v3 on v2

v3 whole, which is shorter than its diff:
```python
import functools

import jax
import jax.numpy as jnp
import numpy as np
from jax import lax
from jax.experimental import pallas as pl
from jax.experimental.pallas import tpu as pltpu
from jax.sharding import Mesh, PartitionSpec as P

inv_temp = 1.0 / 0.07
eps_norm = 1e-06
NX, NY, NC, NZ = 4, 4, 2, 16
NH, NL = 4, 4
ALL = ("x", "y", "core", "zh", "zl")
B = 40
D = 512
ROWS = NX * NC * NL * B
COLS = NY * NH * B
BATCH = NX * NY * NC * NZ * B
PAIR = 2 * B + 8
PLACES = (0, 1, -1, 2)
FLIPS = (0, 2, 1, 3)
VMEM_LIMIT = 48 * 2**20


def permute(value, source):
    pairs = []
    for x in range(NX):
        for y in range(NY):
            for c in range(NC):
                for z in range(NZ):
                    sx, sy, sc, sz = source(x, y, c, z)
                    src = (((sx % NX) * NY + sy % NY) * NC + sc) * NZ + sz
                    pairs.append((src, ((x * NY + y) * NC + c) * NZ + z))
    return lax.ppermute(value, ALL, pairs)


def along_xy(value, step):
    return permute(value, lambda x, y, c, z: (x + (1 - c) * step, y + c * step, c, z))


def along_z(value, flip, step):
    return permute(
        value, lambda x, y, c, z: (x, y, c, (z + NL * step) % NZ if c else z ^ flip)
    )


def swap_core(value):
    return permute(value, lambda x, y, c, z: (x, y, c ^ 1, z))


def groups():
    index = np.arange(NX * NY * NC * NZ).reshape(NX, NY, NC, NH, NL)
    found = []
    for i in range(4):
        for j in range(4):
            found.append(index[:, i, 0, j, :].reshape(-1).tolist())
            found.append(index[i, :, 1, :, j].reshape(-1).tolist())
    return found


def row_blocks(x, zl):
    found = []
    for j, dx in enumerate(PLACES):
        bx = lax.rem(x + dx + NX, NX)
        for k, flip in enumerate(FLIPS):
            for core in range(NC):
                found.append((j, k, core, (bx * NC + core) * NL + (zl ^ flip)))
    return found


def col_blocks(y, zh):
    found = []
    for j, dy in enumerate(PLACES):
        by = lax.rem(y + dy + NY, NY)
        for k, dz in enumerate(PLACES):
            found.append((j, k, lax.rem(zh + dz + NH, NH) * NY + by))
    return found


def block_at(ref, block):
    return ref.at[pl.ds(pl.multiple_of(block * B, 8), B), :]


def split(value):
    high = value.astype(jnp.bfloat16)
    return high, (value - high.astype(jnp.float32)).astype(jnp.bfloat16)


def product(a_high, a_low, b_high, b_low, dims):
    dot = functools.partial(
        lax.dot_general, dimension_numbers=(dims, ((), ())), preferred_element_type=jnp.float32
    )
    return dot(a_high, b_high) + (dot(a_high, b_low) + dot(a_low, b_high))


def eye():
    return lax.broadcasted_iota(jnp.int32, (128, 128), 0) == lax.broadcasted_iota(
        jnp.int32, (128, 128), 1
    )


def to_lanes(column):
    return jnp.sum(jnp.where(eye(), column, 0.0), axis=0, keepdims=True)


def to_rows(lanes):
    return jnp.sum(jnp.where(eye(), lanes, 0.0), axis=1, keepdims=True)


STEP = 256
SUMS = ROWS + 128


def scores_kernel(place, ids, wanted, *refs):
    mine, others = refs[:4], refs[4:8]
    expo, ph, plow, hh, hlow, keep, send, punit, hunit, row_sums = refs[8:]
    x, y, c, zh, zl = (place[k] for k in range(5))

    def unit(v):
        return v * (1.0 / jnp.sqrt(jnp.sum(v * v, axis=1, keepdims=True) + eps_norm))

    def fill(rows_in, cols_in, other):
        for j, k, block in col_blocks(y, zh):
            block_at(hunit, block)[...] = unit(cols_in[j][k, other * B : (other + 1) * B, :])
        for j, k, core, block in row_blocks(x, zl):
            block_at(punit, block)[...] = unit(rows_in[j][k, core * B : (core + 1) * B, :])

    @pl.when(c == 0)
    def _():
        fill(mine, others, 1)

    @pl.when(c == 1)
    def _():
        fill(others, mine, 0)

    hh[...], hlow[...] = split(hunit[...])
    places = ids[...]

    def step(i, carry):
        total, positive = carry
        here = pl.ds(pl.multiple_of(i * STEP, STEP), STEP)
        high, low = split(punit[here, :])
        ph[here, :] = high
        plow[here, :] = low
        scores = product(high, low, hh[...], hlow[...], ((1,), (1,))) * inv_temp
        e = jnp.exp(scores - inv_temp)
        expo[here, :] = e
        sums = jnp.sum(e, axis=1, keepdims=True)
        for k in range(STEP // 128):
            lanes = pl.ds(pl.multiple_of(i * STEP + k * 128, 128), 128)
            row_sums[:, lanes] = to_lanes(sums[k * 128 : (k + 1) * 128])
        match = wanted[here, :] == places
        total = total + jnp.sum(e.reshape(STEP // 8, 8, COLS), axis=0)
        positive = positive + jnp.sum(
            jnp.where(match, scores, 0.0).reshape(STEP // 8, 8, COLS), axis=0
        )
        return total, positive

    zero = jnp.zeros((8, COLS), jnp.float32)
    total, positive = lax.fori_loop(0, ROWS // STEP, step, (zero, zero))
    positive = jnp.sum(positive, axis=0, keepdims=True)
    row_sums[:, ROWS:] = sum(positive[:, k * 128 : (k + 1) * 128] for k in range(COLS // 128))
    total = jnp.sum(total, axis=0, keepdims=True)
    none, rest = jnp.zeros_like(total), jnp.zeros((1, SUMS - ROWS), jnp.float32)

    @pl.when(c == 0)
    def _():
        keep[...] = row_sums[...]
        send[...] = jnp.concatenate([total, none, rest], axis=1)

    @pl.when(c == 1)
    def _():
        keep[...] = jnp.concatenate([none, total, rest], axis=1)
        send[...] = row_sums[...]


def grads_kernel(place, ids, wanted, sums, other_sums, expo, ph, plow, hh, hlow, *refs):
    keeps, sends = refs[:2], refs[2:4]
    dh, dlow, pgrads, hgrads = refs[4:]
    x, y, c, zh, zl = (place[k] for k in range(5))
    first = c == 0
    scale = inv_temp / (2.0 * BATCH)
    rows = jnp.where(first, sums[...], other_sums[...])
    cols = jnp.where(first, other_sums[...], sums[...])
    row_term = jnp.sum(jnp.log(rows[:, :ROWS])) - 2.0 * jnp.sum(rows[:, ROWS:])
    col_term = jnp.sum(jnp.log(cols[:, : 2 * COLS]))
    row_inv = scale / rows[:, :ROWS]
    col_inv = scale / jnp.where(first, cols[:, :COLS], cols[:, COLS : 2 * COLS])
    places = ids[...]
    for i in range(ROWS // STEP):
        here = pl.ds(i * STEP, STEP)
        per_row = jnp.concatenate(
            [to_rows(row_inv[:, k : k + 128]) for k in range(i * STEP, (i + 1) * STEP, 128)], axis=0
        )
        match = wanted[here, :] == places
        d = expo[here, :] * (per_row + col_inv) - jnp.where(match, 2.0 * scale, 0.0)
        high, low = split(d)
        dh[here, :] = high
        dlow[here, :] = low
        pgrads[here, :] = product(high, low, hh[...], hlow[...], ((1,), (0,)))
    for k in range(COLS // 128):
        here = pl.ds(k * 128, 128)
        hgrads[here, :] = product(dh[:, here], dlow[:, here], ph[...], plow[...], ((0,), (0,)))

    def at(outs, j):
        line = (3, 1, 2, 0)[j]
        return outs[line // 2].at[line % 2]

    def packets(outs, term):
        for j, k, core, block in row_blocks(x, zl):
            at(outs, j)[k, core * B : (core + 1) * B, :] = block_at(pgrads, block)[...]
        for j in range(4):
            at(outs, j)[:, 2 * B :, :] = jnp.zeros((4, 8, D), jnp.float32) + term

    def headers(outs, term, other):
        for j, k, block in col_blocks(y, zh):
            at(outs, j)[k, other * B : (other + 1) * B, :] = block_at(hgrads, block)[...]
            at(outs, j)[k, (1 - other) * B : (2 - other) * B, :] = jnp.zeros((B, D), jnp.float32)
        for j in range(4):
            at(outs, j)[:, 2 * B :, :] = jnp.zeros((4, 8, D), jnp.float32) + term

    @pl.when(first)
    def _():
        packets(keeps, col_term)
        headers(sends, 0.0, 1)

    @pl.when(c == 1)
    def _():
        headers(keeps, row_term, 0)
        packets(sends, 0.0)


def in_vmem(count):
    return [pl.BlockSpec(memory_space=pltpu.VMEM)] * count


def call(kernel, operands, outs, scratch, flops):
    return pl.pallas_call(
        kernel,
        in_specs=[pl.BlockSpec(memory_space=pltpu.SMEM)] + in_vmem(len(operands) - 1),
        out_specs=in_vmem(len(outs)),
        out_shape=outs,
        scratch_shapes=scratch,
        compiler_params=pltpu.CompilerParams(vmem_limit_bytes=VMEM_LIMIT),
        cost_estimate=pl.CostEstimate(flops=flops, bytes_accessed=8 * 2**20, transcendentals=0),
    )(*operands)


def f32(*shape):
    return jax.ShapeDtypeStruct(shape, jnp.float32)


def b16(*shape):
    return jax.ShapeDtypeStruct(shape, jnp.bfloat16)


def unit_rows(values):
    norms = jnp.sqrt(jnp.sum(values * values, axis=1, keepdims=True) + eps_norm)
    return (values / norms, norms)


def unit_back(grads, units, norms):
    return (grads - units * jnp.sum(units * grads, axis=1, keepdims=True)) / norms


def together(*values):
    return lax.optimization_barrier(values)


def gather(first, packet, header):
    pair = jnp.concatenate(
        [
            jnp.where(first, packet, header),
            swap_core(jnp.where(first, header, packet)),
        ]
    )
    za = along_z(pair, 2, 1)
    zb = along_z(pair, 1, -1)
    line = jnp.stack([pair, za, zb, along_z(za, 1, 1)])
    ahead, behind = along_xy(line, 1), along_xy(line, -1)
    ahead, behind, line_again = together(ahead, behind, line)
    lines = [line, ahead, behind, along_xy(ahead, 1)]
    return lines, [swap_core(line) for line in lines]


def scatter(keeps, sends):
    far, ahead = (keeps[0] + swap_core(sends[0]))[:]
    behind, line = (keeps[1] + swap_core(sends[1]))[:]
    line = line + along_xy(ahead + along_xy(far, -1), -1) + along_xy(behind, 1)
    za = line[1] + along_z(line[3], 1, -1)
    return line[0] + along_z(za, 2, -1) + along_z(line[2], 1, 1)


def per_device(packet, header, partner):
    x, y, c, zh, zl = (lax.axis_index(name) for name in ALL)
    place = jnp.stack([x, y, c, zh, zl]).astype(jnp.int32)
    lane = np.arange(COLS)
    ids = lane // (NY * B) * (NL * NX * NY * NC * B) + lane // B % NY * (NC * B) + lane % B
    ids = jnp.asarray(ids, jnp.int32)[None, :]
    ids = ids + ((zl * NX + x) * (NY * NC * B) + c * B).astype(jnp.int32)
    wanted = lax.dynamic_slice(
        partner.reshape(NX, NY, NC, NH, NL, B), [0, y, 0, zh, 0, 0], (NX, 1, NC, 1, NL, B)
    ).reshape(ROWS, 1)

    first = c == 0
    lines, other_lines = gather(first, packet, header)
    flops = 2 * 3 * ROWS * COLS * D
    expo, ph, plow, hh, hlow, keep, send = call(
        scores_kernel,
        [place, ids, wanted] + lines + other_lines,
        [f32(ROWS, COLS), b16(ROWS, D), b16(ROWS, D), b16(COLS, D), b16(COLS, D)] + [f32(1, SUMS)] * 2,
        [pltpu.VMEM((ROWS, D), jnp.float32), pltpu.VMEM((COLS, D), jnp.float32), pltpu.VMEM((1, SUMS), jnp.float32)],
        flops,
    )
    sums = lax.all_to_all(
        jnp.broadcast_to((keep + swap_core(send))[None], (16, 1, SUMS)),
        ALL, 0, 0, axis_index_groups=groups(),
    )
    sums = jnp.sum(sums, axis=0)
    parts = call(
        grads_kernel,
        [place, ids, wanted, sums, swap_core(sums), expo, ph, plow, hh, hlow],
        [f32(2, 4, PAIR, D)] * 4,
        [
            pltpu.VMEM((ROWS, COLS), jnp.bfloat16),
            pltpu.VMEM((ROWS, COLS), jnp.bfloat16),
            pltpu.VMEM((ROWS, D), jnp.float32),
            pltpu.VMEM((COLS, D), jnp.float32),
        ],
        2 * flops,
    )
    pair = scatter(parts[:2], parts[2:])
    got = swap_core(pair[B:])
    own, other = pair[:B], got[:B]
    gpunit, ghunit = jnp.where(first, own, other), jnp.where(first, other, own)
    loss = inv_temp + (pair[2 * B, 0] + got[B, 0]) / (2.0 * BATCH)
    punit, pnorm = unit_rows(packet)
    hunit, hnorm = unit_rows(header)
    packet_grad = unit_back(gpunit, punit, pnorm)
    header_grad = unit_back(ghunit, hunit, hnorm)
    return (loss, packet_grad, header_grad)


def solution(mesh):
    mesh = Mesh(mesh.devices.reshape(NX, NY, NC, NH, NL), ALL)
    by_packet, by_header = P(ALL, None), P(("zh", "zl", "x", "y", "core"), None)
    return jax.shard_map(
        per_device,
        mesh=mesh,
        in_specs=(by_packet, by_header, P()),
        out_specs=(P(), by_packet, by_header),
        check_vma=False,
    )
```

time: 224 us -> 202 us (0.902)
  starting transfers between devices: 112 us -> 79.2 us
  blocking collectives: 0 us -> 25.7 us
  waiting for transfers between devices: 66.5 us -> 58.1 us
  other arithmetic: 5.81 us -> 3.25 us
    all_to_all x0 -> x1, blocking collectives: none -> 25.7 us  [per_device(): lax.all_to_all(jnp.broadcast_to((keep + swap_core(send))[None], (16, 1, S...]
    all_to_all x2 -> x0, waiting for transfers between devices: 23.1 us -> none  [the longest x1 13.7 us: per_device(): lax.all_to_all(jnp.broadcast_to(cols[None], (NY * NH, 1, COLS)), ('y', 'z...]
    ppermute x24 -> x22, starting transfers between devices: 100 us -> 79.2 us  [permute(): return lax.ppermute(value, ALL, pairs)]
    ppermute x24 -> x22, waiting for transfers between devices: 43.5 us -> 58.1 us  [permute(): return lax.ppermute(value, ALL, pairs)]
    all_to_all x2 -> x0, starting transfers between devices: 12.2 us -> none  [the longest x1 6.7 us: per_device(): lax.all_to_all(jnp.broadcast_to(cols[None], (NY * NH, 1, COLS)), ('y', 'z...]
    another operation x3 -> x2, other arithmetic: 3 us -> 0.07 us  [gather(): line = jnp.stack([pair, za, zb, along_z(za, 1, 1)])]
    unnamed x26 -> x22, local copies, waits for them, and re-layouts: 6.48 us -> 6.54 us
    pallas_call x3 -> x2, Pallas kernels: 20.5 us -> 20.5 us  [call(): pl.pallas_call(kernel, in_specs=[pl.BlockSpec(memory_space=pltpu.SMEM)] +...]
  transfers between devices with their start and end apart: 26 -> 22, of which waited for: 14 -> 16; matrix products, arithmetic and copies ran while one was open for 2% -> 1% of each run, Pallas kernels for 2% -> 0%
where the time goes in v3:
time: 202 us; the launch traced here: 199 us
  starting transfers between devices  79.2 us (39%)
  waiting for transfers between devices  58.1 us (29%)
  blocking collectives  25.7 us (13%)
  Pallas kernels  20.5 us (10%)
  local copies, waits for them, and re-layouts  8.47 us (4%)
  between operations  3.52 us (2%)
  other arithmetic  3.25 us (2%)
    ppermute x22, starting transfers between devices, permute(): return lax.ppermute(value, ALL, pairs)  79.2 us
    ppermute x22, waiting for transfers between devices, permute(): return lax.ppermute(value, ALL, pairs)  58.1 us
    all_to_all x1, blocking collectives, per_device(): lax.all_to_all(jnp.broadcast_to((keep + swap_core(send))[None], (16, 1, S...  25.7 us
    pallas_call x2, Pallas kernels, call(): pl.pallas_call(kernel, in_specs=[pl.BlockSpec(memory_space=pltpu.SMEM)] +...  20.5 us
    unnamed x22, local copies, waits for them, and re-layouts  6.54 us
  transfers between devices with their start and end apart: 22, of which 16 were waited for; matrix products, arithmetic and copies ran while one was open for 1% of the time, Pallas kernels for 0%

profile of v3, /device:TPU:1, one launch (start us, length us, event | category | flops | bytes accessed | tf_op | source)
XLA Modules:
  0.0 198.8 jit_solution(12012880845696629022)
XLA Ops:
  1.7 8.8 %collective-permute-start = (f32[40,512]{1,0:T(8,128)S(1)}, f32[40,512]{1,0:T(8,128)S(1)}, u32[]{:S(2)}, u32[]{:S(2)}) collective-permute-start(f32[40,512]{1,0:T(8,128)S(1)} %get-tuple-element.38), channel_id=1, source_target_pairs={{16,0},{17,1},{18,2},{19,3},{20,4},{21,5},{22,6},{23,7},{24,8},{25... | collective-permute-start | bytes 245768 | tf_op jit(solution)/shard_map/ppermute | solution.py:36
  11.5 7.1 %collective-permute-start.1 = (f32[80,512]{1,0:T(8,128)S(1)}, f32[80,512]{1,0:T(8,128)S(1)}, u32[]{:S(2)}, u32[]{:S(2)}) collective-permute-start(f32[80,512]{1,0:T(8,128)S(1)} %get-tuple-element.36), channel_id=1, source_target_pairs={{2,0},{3,1},{0,2},{1,3},{6,4},{7,5},{4,6},{5,7},{10,8},{11,9},{8,1... | collective-permute-start | bytes 491528 | tf_op jit(solution)/shard_map/ppermute | solution.py:36
  18.6 2.1 %collective-permute-start.2 = (f32[80,512]{1,0:T(8,128)S(1)}, f32[80,512]{1,0:T(8,128)S(1)}, u32[]{:S(2)}, u32[]{:S(2)}) collective-permute-start(f32[80,512]{1,0:T(8,128)S(1)} %get-tuple-element.36), channel_id=1, source_target_pairs={{1,0},{0,1},{3,2},{2,3},{5,4},{4,5},{7,6},{6,7},{9,8},{8,9},{11,10... | collective-permute-start | bytes 491528 | tf_op jit(solution)/shard_map/ppermute | solution.py:36
  20.7 2.9 %collective-permute-done.1 = f32[80,512]{1,0:T(8,128)S(1)} collective-permute-done((f32[80,512]{1,0:T(8,128)S(1)}, f32[80,512]{1,0:T(8,128)S(1)}, u32[]{:S(2)}, u32[]{:S(2)}) %collective-permute-start.1) | collective-permute-done | bytes 163872 | tf_op jit(solution)/shard_map/ppermute | solution.py:36
  23.5 6.0 %collective-permute-start.3 = (f32[80,512]{1,0:T(8,128)S(1)}, f32[80,512]{1,0:T(8,128)S(1)}, u32[]{:S(2)}, u32[]{:S(2)}) collective-permute-start(f32[80,512]{1,0:T(8,128)S(1)} %collective-permute-done.1), channel_id=1, source_target_pairs={{1,0},{0,1},{3,2},{2,3},{5,4},{4,5},{7,6},{6,7},{9,8},{8,9},{11,10... | collective-permute-start | bytes 491528 | tf_op jit(solution)/shard_map/ppermute | solution.py:36
  29.6 2.6 %collective-permute-done.2 = f32[80,512]{1,0:T(8,128)S(1)} collective-permute-done((f32[80,512]{1,0:T(8,128)S(1)}, f32[80,512]{1,0:T(8,128)S(1)}, u32[]{:S(2)}, u32[]{:S(2)}) %collective-permute-start.2) | collective-permute-done | bytes 163872 | tf_op jit(solution)/shard_map/ppermute | solution.py:36
  34.1 9.5 %collective-permute-start.5 = (f32[4,80,512]{2,1,0:T(8,128)S(1)}, f32[4,80,512]{2,1,0:T(8,128)S(1)}, u32[]{:S(2)}, u32[]{:S(2)}) collective-permute-start(f32[4,80,512]{2,1,0:T(8,128)S(1)} %pad_maximum_fusion.refs_0_), channel_id=1, source_target_pairs={{384,0},{385,1},{386,2},{387,3},{388,4},{389,5},{390,6},{391,7},{3... | collective-permute-start | bytes 1966088 | tf_op jit(solution)/shard_map/ppermute | solution.py:36
  43.6 3.4 %collective-permute-start.4 = (f32[4,80,512]{2,1,0:T(8,128)S(1)}, f32[4,80,512]{2,1,0:T(8,128)S(1)}, u32[]{:S(2)}, u32[]{:S(2)}) collective-permute-start(f32[4,80,512]{2,1,0:T(8,128)S(1)} %pad_maximum_fusion.refs_0_), channel_id=1, source_target_pairs={{128,0},{129,1},{130,2},{131,3},{132,4},{133,5},{134,6},{135,7},{1... | collective-permute-start | bytes 1966088 | tf_op jit(solution)/shard_map/ppermute | solution.py:36
  47.0 6.0 %collective-permute-done.5.refs_2_ = f32[4,80,512]{2,1,0:T(8,128)S(1)} collective-permute-done((f32[4,80,512]{2,1,0:T(8,128)S(1)}, f32[4,80,512]{2,1,0:T(8,128)S(1)}, u32[]{:S(2)}, u32[]{:S(2)}) %collective-permute-start.5) | collective-permute-done | bytes 655392 | tf_op jit(solution)/shard_map/ppermute | solution.py:36
  53.0 2.2 %collective-permute-done.4.refs_1_ = f32[4,80,512]{2,1,0:T(8,128)S(1)} collective-permute-done((f32[4,80,512]{2,1,0:T(8,128)S(1)}, f32[4,80,512]{2,1,0:T(8,128)S(1)}, u32[]{:S(2)}, u32[]{:S(2)}) %collective-permute-start.4) | collective-permute-done | bytes 655392 | tf_op jit(solution)/shard_map/ppermute | solution.py:36
  55.2 4.3 %collective-permute-start.6 = (f32[4,80,512]{2,1,0:T(8,128)S(1)}, f32[4,80,512]{2,1,0:T(8,128)S(1)}, u32[]{:S(2)}, u32[]{:S(2)}) collective-permute-start(f32[4,80,512]{2,1,0:T(8,128)S(1)} %collective-permute-done.4.refs_1_), channel_id=1, source_target_pairs={{128,0},{129,1},{130,2},{131,3},{132,4},{133,5},{134,6},{135,7},{1... | collective-permute-start | bytes 1966088 | tf_op jit(solution)/shard_map/ppermute | solution.py:36
  59.5 1.9 collective-permute-start.7
  61.4 2.4 %collective-permute-start.8 = (f32[4,80,512]{2,1,0:T(8,128)S(1)}, f32[4,80,512]{2,1,0:T(8,128)}, u32[]{:S(2)}, u32[]{:S(2)}) collective-permute-start(f32[4,80,512]{2,1,0:T(8,128)S(1)} %collective-permute-done.4.refs_1_), channel_id=1, source_target_pairs={{16,0},{17,1},{18,2},{19,3},{20,4},{21,5},{22,6},{23,7},{24,8},{25... | collective-permute-start | bytes 1966088 | tf_op jit(solution)/shard_map/ppermute | solution.py:36
  63.8 1.9 collective-permute-start.9
  71.1 9.8 %shard_map.67 = (f32[1280,640]{1,0:T(8,128)}, bf16[1280,512]{1,0:T(8,128)(2,1)}, bf16[1280,512]{1,0:T(8,128)(2,1)}, bf16[640,512]{1,0:T(8,128)(2,1)S(1)}, bf16[6...) custom-call(s32[5]{0:T(128)S(1)} %stack.38.place, s32[1,640]{1,0:T(1,128)S(1)} %add.71.ids, ...), custom_call_target="tpu_custom_call" | custom-call | flops 2516582400 | bytes 8388608 | tf_op jit(solution)/shard_map/pallas_call | solution.py:240
  82.6 2.0 %collective-permute-start.11 = (f32[1,1408]{1,0:T(1,128)S(1)}, f32[1,1408]{1,0:T(1,128)S(1)}, u32[]{:S(2)}, u32[]{:S(2)}) collective-permute-start(f32[1,1408]{1,0:T(1,128)S(1)} %get-tuple-element.19), channel_id=1, source_target_pairs={{16,0},{17,1},{18,2},{19,3},{20,4},{21,5},{22,6},{23,7},{24,8},{25... | collective-permute-start | bytes 16904 | tf_op jit(solution)/shard_map/ppermute | solution.py:36
  85.8 25.7 %all_to_all.5 = f32[16,1,1408]{2,1,0:T(1,128)S(1)} all-to-all(f32[16,1,1408]{2,1,0:T(1,128)S(1)} %broadcast_in_dim.5), channel_id=1, replica_groups={{0,1,2,3,128,129,130,131,256,257,258,259,384,385,386,387},{16,20,24,28,..., dimensions={0} | all-to-all | bytes 180224 | tf_op jit(solution)/shard_map/all_to_all | solution.py:317
  111.6 1.9 collective-permute-start.12
  119.4 10.7 %shard_map.68 = (f32[2,4,88,512]{3,2,1,0:T(8,128)S(1)}, f32[2,4,88,512]{3,2,1,0:T(8,128)}, f32[2,4,88,512]{3,2,1,0:T(8,128)}, f32[2,4,88,512]{3,2,1,0:T(8,128)}) custom-call(s32[5]{0:T(128)S(1)} %stack.38.place, s32[1,640]{1,0:T(1,128)S(1)} %add.71.ids, s32[1280,1]{1,0:T(8,128)S(1)} %reshape.38.wanted, f32[1,1408]{1,0:T(1,128)S(1)} %reduce_sum.48.sums, ...), custom_call_target="tpu_custom_call" | custom-call | flops 5033164800 | bytes 8388608 | tf_op jit(solution)/shard_map/pallas_call | solution.py:240
  130.1 2.1 %collective-permute-start.14 = (f32[2,4,88,512]{3,2,1,0:T(8,128)}, f32[2,4,88,512]{3,2,1,0:T(8,128)S(1)}, u32[]{:S(2)}, u32[]{:S(2)}) collective-permute-start(f32[2,4,88,512]{3,2,1,0:T(8,128)} %get-tuple-element.28), channel_id=1, source_target_pairs={{16,0},{17,1},{18,2},{19,3},{20,4},{21,5},{22,6},{23,7},{24,8},{25... | collective-permute-start | bytes 4325384 | tf_op jit(solution)/shard_map/ppermute | solution.py:36
  132.2 2.2 %collective-permute-start.13 = (f32[2,4,88,512]{3,2,1,0:T(8,128)}, f32[2,4,88,512]{3,2,1,0:T(8,128)S(1)}, u32[]{:S(2)}, u32[]{:S(2)}) collective-permute-start(f32[2,4,88,512]{3,2,1,0:T(8,128)} %get-tuple-element.26), channel_id=1, source_target_pairs={{16,0},{17,1},{18,2},{19,3},{20,4},{21,5},{22,6},{23,7},{24,8},{25... | collective-permute-start | bytes 4325384 | tf_op jit(solution)/shard_map/ppermute | solution.py:36
  135.8 2.1 %collective-permute-start.15 = (f32[4,88,512]{2,1,0:T(8,128)S(1)}, f32[4,88,512]{2,1,0:T(8,128)S(1)}, u32[]{:S(2)}, u32[]{:S(2)}) collective-permute-start(f32[4,88,512]{2,1,0:T(8,128)S(1)} %slice_bitcast_fusion.1), channel_id=1, source_target_pairs={{384,0},{385,1},{386,2},{387,3},{388,4},{389,5},{390,6},{391,7},{3... | collective-permute-start | bytes 2162696 | tf_op jit(solution)/shard_map/ppermute | solution.py:36
  138.3 4.6 %collective-permute-start.17 = (f32[4,88,512]{2,1,0:T(8,128)S(1)}, f32[4,88,512]{2,1,0:T(8,128)S(1)}, u32[]{:S(2)}, u32[]{:S(2)}) collective-permute-start(f32[4,88,512]{2,1,0:T(8,128)S(1)} %slice_bitcast_fusion), channel_id=1, source_target_pairs={{128,0},{129,1},{130,2},{131,3},{132,4},{133,5},{134,6},{135,7},{1... | collective-permute-start | bytes 2162696 | tf_op jit(solution)/shard_map/ppermute | solution.py:36
  142.8 6.6 %collective-permute-done.15 = f32[4,88,512]{2,1,0:T(8,128)S(1)} collective-permute-done((f32[4,88,512]{2,1,0:T(8,128)S(1)}, f32[4,88,512]{2,1,0:T(8,128)S(1)}, u32[]{:S(2)}, u32[]{:S(2)}) %collective-permute-start.15) | collective-permute-done | bytes 720928 | tf_op jit(solution)/shard_map/ppermute | solution.py:36
  149.6 1.9 collective-permute-start.16
  151.5 11.6 %collective-permute-done.16 = f32[4,88,512]{2,1,0:T(8,128)S(1)} collective-permute-done((f32[4,88,512]{2,1,0:T(8,128)S(1)}, f32[4,88,512]{2,1,0:T(8,128)S(1)}, u32[]{:S(2)}, u32[]{:S(2)}) %collective-permute-start.16) | collective-permute-done | bytes 720928 | tf_op jit(solution)/shard_map/ppermute | solution.py:36
  163.4 2.2 %collective-permute-start.18 = (f32[88,512]{1,0:T(8,128)S(1)}, f32[88,512]{1,0:T(8,128)S(1)}, u32[]{:S(2)}, u32[]{:S(2)}) collective-permute-start(f32[88,512]{1,0:T(8,128)S(1)} %get-tuple-element.31), channel_id=1, source_target_pairs={{1,0},{0,1},{3,2},{2,3},{5,4},{4,5},{7,6},{6,7},{9,8},{8,9},{11,10... | collective-permute-start | bytes 540680 | tf_op jit(solution)/shard_map/ppermute | solution.py:36
  165.6 7.1 %collective-permute-start.20 = (f32[88,512]{1,0:T(8,128)S(1)}, f32[88,512]{1,0:T(8,128)S(1)}, u32[]{:S(2)}, u32[]{:S(2)}) collective-permute-start(f32[88,512]{1,0:T(8,128)S(1)} %get-tuple-element.32), channel_id=1, source_target_pairs={{1,0},{0,1},{3,2},{2,3},{5,4},{4,5},{7,6},{6,7},{9,8},{8,9},{11,10... | collective-permute-start | bytes 540680 | tf_op jit(solution)/shard_map/ppermute | solution.py:36
  172.8 8.2 %collective-permute-done.18 = f32[88,512]{1,0:T(8,128)S(1)} collective-permute-done((f32[88,512]{1,0:T(8,128)S(1)}, f32[88,512]{1,0:T(8,128)S(1)}, u32[]{:S(2)}, u32[]{:S(2)}) %collective-permute-start.18) | collective-permute-done | bytes 180256 | tf_op jit(solution)/shard_map/ppermute | solution.py:36
  181.0 1.9 collective-permute-start.19
  183.0 8.6 %collective-permute-done.19 = f32[88,512]{1,0:T(8,128)S(1)} collective-permute-done((f32[88,512]{1,0:T(8,128)S(1)}, f32[88,512]{1,0:T(8,128)S(1)}, u32[]{:S(2)}, u32[]{:S(2)}) %collective-permute-start.19) | collective-permute-done | bytes 180256 | tf_op jit(solution)/shard_map/ppermute | solution.py:36
  191.7 1.9 collective-permute-start.21
  (65 shorter events, 22.9 us)
Async XLA Ops:
  0.6 68.3 %copy-start.10 = (s32[640]{0:T(1024)S(1)}, s32[640]{0:T(1024)}, u32[]{:S(2)}) copy-start(s32[640]{0:T(1024)} %constant.42.clone) | copy-start | bytes 7684
  0.6 68.3 %copy-start.9 = (s32[20480]{0:T(1024)S(1)}, s32[20480]{0:T(1024)}, u32[]{:S(2)}) copy-start(s32[20480]{0:T(1024)} %param.6) | copy-start | bytes 245764
  1.7 9.7 %collective-permute-start = (f32[40,512]{1,0:T(8,128)S(1)}, f32[40,512]{1,0:T(8,128)S(1)}, u32[]{:S(2)}, u32[]{:S(2)}) collective-permute-start(f32[40,512]{1,0:T(8,128)S(1)} %get-tuple-element.38), channel_id=1, source_target_pairs={{16,0},{17,1},{18,2},{19,3},{20,4},{21,5},{22,6},{23,7},{24,8},{25... | collective-permute-start | bytes 245768 | tf_op jit(solution)/shard_map/ppermute | solution.py:36
  11.5 12.1 %collective-permute-start.1 = (f32[80,512]{1,0:T(8,128)S(1)}, f32[80,512]{1,0:T(8,128)S(1)}, u32[]{:S(2)}, u32[]{:S(2)}) collective-permute-start(f32[80,512]{1,0:T(8,128)S(1)} %get-tuple-element.36), channel_id=1, source_target_pairs={{2,0},{3,1},{0,2},{1,3},{6,4},{7,5},{4,6},{5,7},{10,8},{11,9},{8,1... | collective-permute-start | bytes 491528 | tf_op jit(solution)/shard_map/ppermute | solution.py:36
  18.6 13.6 %collective-permute-start.2 = (f32[80,512]{1,0:T(8,128)S(1)}, f32[80,512]{1,0:T(8,128)S(1)}, u32[]{:S(2)}, u32[]{:S(2)}) collective-permute-start(f32[80,512]{1,0:T(8,128)S(1)} %get-tuple-element.36), channel_id=1, source_target_pairs={{1,0},{0,1},{3,2},{2,3},{5,4},{4,5},{7,6},{6,7},{9,8},{8,9},{11,10... | collective-permute-start | bytes 491528 | tf_op jit(solution)/shard_map/ppermute | solution.py:36
  23.5 10.5 %collective-permute-start.3 = (f32[80,512]{1,0:T(8,128)S(1)}, f32[80,512]{1,0:T(8,128)S(1)}, u32[]{:S(2)}, u32[]{:S(2)}) collective-permute-start(f32[80,512]{1,0:T(8,128)S(1)} %collective-permute-done.1), channel_id=1, source_target_pairs={{1,0},{0,1},{3,2},{2,3},{5,4},{4,5},{7,6},{6,7},{9,8},{8,9},{11,10... | collective-permute-start | bytes 491528 | tf_op jit(solution)/shard_map/ppermute | solution.py:36
  34.1 18.9 %collective-permute-start.5 = (f32[4,80,512]{2,1,0:T(8,128)S(1)}, f32[4,80,512]{2,1,0:T(8,128)S(1)}, u32[]{:S(2)}, u32[]{:S(2)}) collective-permute-start(f32[4,80,512]{2,1,0:T(8,128)S(1)} %pad_maximum_fusion.refs_0_), channel_id=1, source_target_pairs={{384,0},{385,1},{386,2},{387,3},{388,4},{389,5},{390,6},{391,7},{3... | collective-permute-start | bytes 1966088 | tf_op jit(solution)/shard_map/ppermute | solution.py:36
  43.6 11.6 %collective-permute-start.4 = (f32[4,80,512]{2,1,0:T(8,128)S(1)}, f32[4,80,512]{2,1,0:T(8,128)S(1)}, u32[]{:S(2)}, u32[]{:S(2)}) collective-permute-start(f32[4,80,512]{2,1,0:T(8,128)S(1)} %pad_maximum_fusion.refs_0_), channel_id=1, source_target_pairs={{128,0},{129,1},{130,2},{131,3},{132,4},{133,5},{134,6},{135,7},{1... | collective-permute-start | bytes 1966088 | tf_op jit(solution)/shard_map/ppermute | solution.py:36
  55.2 11.8 %collective-permute-start.6 = (f32[4,80,512]{2,1,0:T(8,128)S(1)}, f32[4,80,512]{2,1,0:T(8,128)S(1)}, u32[]{:S(2)}, u32[]{:S(2)}) collective-permute-start(f32[4,80,512]{2,1,0:T(8,128)S(1)} %collective-permute-done.4.refs_1_), channel_id=1, source_target_pairs={{128,0},{129,1},{130,2},{131,3},{132,4},{133,5},{134,6},{135,7},{1... | collective-permute-start | bytes 1966088 | tf_op jit(solution)/shard_map/ppermute | solution.py:36
  59.5 10.2 %collective-permute-start.7 = (f32[4,80,512]{2,1,0:T(8,128)S(1)}, f32[4,80,512]{2,1,0:T(8,128)}, u32[]{:S(2)}, u32[]{:S(2)}) collective-permute-start(f32[4,80,512]{2,1,0:T(8,128)S(1)} %pad_maximum_fusion.refs_0_), channel_id=1, source_target_pairs={{16,0},{17,1},{18,2},{19,3},{20,4},{21,5},{22,6},{23,7},{24,8},{25... | collective-permute-start | bytes 1966088 | tf_op jit(solution)/shard_map/ppermute | solution.py:36
  61.4 8.3 %collective-permute-start.8 = (f32[4,80,512]{2,1,0:T(8,128)S(1)}, f32[4,80,512]{2,1,0:T(8,128)}, u32[]{:S(2)}, u32[]{:S(2)}) collective-permute-start(f32[4,80,512]{2,1,0:T(8,128)S(1)} %collective-permute-done.4.refs_1_), channel_id=1, source_target_pairs={{16,0},{17,1},{18,2},{19,3},{20,4},{21,5},{22,6},{23,7},{24,8},{25... | collective-permute-start | bytes 1966088 | tf_op jit(solution)/shard_map/ppermute | solution.py:36
  63.8 5.9 %collective-permute-start.9 = (f32[4,80,512]{2,1,0:T(8,128)S(1)}, f32[4,80,512]{2,1,0:T(8,128)}, u32[]{:S(2)}, u32[]{:S(2)}) collective-permute-start(f32[4,80,512]{2,1,0:T(8,128)S(1)} %collective-permute-done.5.refs_2_), channel_id=1, source_target_pairs={{16,0},{17,1},{18,2},{19,3},{20,4},{21,5},{22,6},{23,7},{24,8},{25... | collective-permute-start | bytes 1966088 | tf_op jit(solution)/shard_map/ppermute | solution.py:36
  67.0 4.1 %collective-permute-start.10 = (f32[4,80,512]{2,1,0:T(8,128)S(1)}, f32[4,80,512]{2,1,0:T(8,128)}, u32[]{:S(2)}, u32[]{:S(2)}) collective-permute-start(f32[4,80,512]{2,1,0:T(8,128)S(1)} %collective-permute-done.6.refs_3_), channel_id=1, source_target_pairs={{16,0},{17,1},{18,2},{19,3},{20,4},{21,5},{22,6},{23,7},{24,8},{25... | collective-permute-start | bytes 1966088 | tf_op jit(solution)/shard_map/ppermute | solution.py:36
  80.9 0.9 copy-start.2
  82.6 3.1 %collective-permute-start.11 = (f32[1,1408]{1,0:T(1,128)S(1)}, f32[1,1408]{1,0:T(1,128)S(1)}, u32[]{:S(2)}, u32[]{:S(2)}) collective-permute-start(f32[1,1408]{1,0:T(1,128)S(1)} %get-tuple-element.19), channel_id=1, source_target_pairs={{16,0},{17,1},{18,2},{19,3},{20,4},{21,5},{22,6},{23,7},{24,8},{25... | collective-permute-start | bytes 16904 | tf_op jit(solution)/shard_map/ppermute | solution.py:36
  111.6 3.1 %collective-permute-start.12 = (f32[1,1408]{1,0:T(1,128)S(1)}, f32[1,1408]{1,0:T(1,128)S(1)}, u32[]{:S(2)}, u32[]{:S(2)}) collective-permute-start(f32[1,1408]{1,0:T(1,128)S(1)} %reduce_sum.48.sums), channel_id=1, source_target_pairs={{16,0},{17,1},{18,2},{19,3},{20,4},{21,5},{22,6},{23,7},{24,8},{25... | collective-permute-start | bytes 16904 | tf_op jit(solution)/shard_map/ppermute | solution.py:36
  114.6 1.3 copy-start
  116.0 1.3 copy-start.1
  117.3 1.1 copy-start.3
  118.4 1.1 copy-start.5
  130.1 5.3 %collective-permute-start.14 = (f32[2,4,88,512]{3,2,1,0:T(8,128)}, f32[2,4,88,512]{3,2,1,0:T(8,128)S(1)}, u32[]{:S(2)}, u32[]{:S(2)}) collective-permute-start(f32[2,4,88,512]{3,2,1,0:T(8,128)} %get-tuple-element.28), channel_id=1, source_target_pairs={{16,0},{17,1},{18,2},{19,3},{20,4},{21,5},{22,6},{23,7},{24,8},{25... | collective-permute-start | bytes 4325384 | tf_op jit(solution)/shard_map/ppermute | solution.py:36
  132.2 5.7 %collective-permute-start.13 = (f32[2,4,88,512]{3,2,1,0:T(8,128)}, f32[2,4,88,512]{3,2,1,0:T(8,128)S(1)}, u32[]{:S(2)}, u32[]{:S(2)}) collective-permute-start(f32[2,4,88,512]{3,2,1,0:T(8,128)} %get-tuple-element.26), channel_id=1, source_target_pairs={{16,0},{17,1},{18,2},{19,3},{20,4},{21,5},{22,6},{23,7},{24,8},{25... | collective-permute-start | bytes 4325384 | tf_op jit(solution)/shard_map/ppermute | solution.py:36
  135.7 2.1 %copy-start.6 = (f32[2,4,88,512]{3,2,1,0:T(8,128)S(1)}, f32[2,4,88,512]{3,2,1,0:T(8,128)}, u32[]{:S(2)}) copy-start(f32[2,4,88,512]{3,2,1,0:T(8,128)} %get-tuple-element.25) | copy-start | bytes 4325380
  135.8 13.7 %collective-permute-start.15 = (f32[4,88,512]{2,1,0:T(8,128)S(1)}, f32[4,88,512]{2,1,0:T(8,128)S(1)}, u32[]{:S(2)}, u32[]{:S(2)}) collective-permute-start(f32[4,88,512]{2,1,0:T(8,128)S(1)} %slice_bitcast_fusion.1), channel_id=1, source_target_pairs={{384,0},{385,1},{386,2},{387,3},{388,4},{389,5},{390,6},{391,7},{3... | collective-permute-start | bytes 2162696 | tf_op jit(solution)/shard_map/ppermute | solution.py:36
  138.3 13.3 %collective-permute-start.17 = (f32[4,88,512]{2,1,0:T(8,128)S(1)}, f32[4,88,512]{2,1,0:T(8,128)S(1)}, u32[]{:S(2)}, u32[]{:S(2)}) collective-permute-start(f32[4,88,512]{2,1,0:T(8,128)S(1)} %slice_bitcast_fusion), channel_id=1, source_target_pairs={{128,0},{129,1},{130,2},{131,3},{132,4},{133,5},{134,6},{135,7},{1... | collective-permute-start | bytes 2162696 | tf_op jit(solution)/shard_map/ppermute | solution.py:36
  149.6 13.5 %collective-permute-start.16 = (f32[4,88,512]{2,1,0:T(8,128)S(1)}, f32[4,88,512]{2,1,0:T(8,128)S(1)}, u32[]{:S(2)}, u32[]{:S(2)}) collective-permute-start(f32[4,88,512]{2,1,0:T(8,128)S(1)} %fusion), channel_id=1, source_target_pairs={{384,0},{385,1},{386,2},{387,3},{388,4},{389,5},{390,6},{391,7},{3... | collective-permute-start | bytes 2162696 | tf_op jit(solution)/shard_map/ppermute | solution.py:36
  163.4 33.3 %copy-start.7 = (f32[40,512]{1,0:T(8,128)S(1)}, f32[40,512]{1,0:T(8,128)}, u32[]{:S(2)}) copy-start(f32[40,512]{1,0:T(8,128)} %param.4) | copy-start | bytes 245764
  163.4 33.3 %copy-start.8 = (f32[40,512]{1,0:T(8,128)S(1)}, f32[40,512]{1,0:T(8,128)}, u32[]{:S(2)}) copy-start(f32[40,512]{1,0:T(8,128)} %param.5) | copy-start | bytes 245764
  163.4 17.6 %collective-permute-start.18 = (f32[88,512]{1,0:T(8,128)S(1)}, f32[88,512]{1,0:T(8,128)S(1)}, u32[]{:S(2)}, u32[]{:S(2)}) collective-permute-start(f32[88,512]{1,0:T(8,128)S(1)} %get-tuple-element.31), channel_id=1, source_target_pairs={{1,0},{0,1},{3,2},{2,3},{5,4},{4,5},{7,6},{6,7},{9,8},{8,9},{11,10... | collective-permute-start | bytes 540680 | tf_op jit(solution)/shard_map/ppermute | solution.py:36
  165.6 17.3 %collective-permute-start.20 = (f32[88,512]{1,0:T(8,128)S(1)}, f32[88,512]{1,0:T(8,128)S(1)}, u32[]{:S(2)}, u32[]{:S(2)}) collective-permute-start(f32[88,512]{1,0:T(8,128)S(1)} %get-tuple-element.32), channel_id=1, source_target_pairs={{1,0},{0,1},{3,2},{2,3},{5,4},{4,5},{7,6},{6,7},{9,8},{8,9},{11,10... | collective-permute-start | bytes 540680 | tf_op jit(solution)/shard_map/ppermute | solution.py:36
  181.0 10.6 %collective-permute-start.19 = (f32[88,512]{1,0:T(8,128)S(1)}, f32[88,512]{1,0:T(8,128)S(1)}, u32[]{:S(2)}, u32[]{:S(2)}) collective-permute-start(f32[88,512]{1,0:T(8,128)S(1)} %fusion.3), channel_id=1, source_target_pairs={{2,0},{3,1},{0,2},{1,3},{6,4},{7,5},{4,6},{5,7},{10,8},{11,9},{8,1... | collective-permute-start | bytes 540680 | tf_op jit(solution)/shard_map/ppermute | solution.py:36
  191.7 3.2 %collective-permute-start.21 = (f32[48,512]{1,0:T(8,128)S(1)}, f32[48,512]{1,0:T(8,128)S(1)}, u32[]{:S(2)}, u32[]{:S(2)}) collective-permute-start(f32[48,512]{1,0:T(8,128)S(1)} %slice.41), channel_id=1, source_target_pairs={{16,0},{17,1},{18,2},{19,3},{20,4},{21,5},{22,6},{23,7},{24,8},{25... | collective-permute-start | bytes 294920 | tf_op jit(solution)/shard_map/ppermute | solution.py:36
  (1 other events, 0.9 us)

commit v4 on v3

--- a/solution.py
+++ b/solution.py
@@ -111,11 +111,20 @@
 
 STEP = 256
 SUMS = ROWS + 128
+KEPT_F32 = 6 * ROWS
+KEPT_B16 = 16 * ROWS
+
+
+def kept(whole):
+    starts = (0, ROWS, 2 * ROWS, 2 * ROWS + COLS)
+    return [whole.at[pl.ds(start, n), :] for start, n in zip(starts, (ROWS, ROWS, COLS, COLS))]
 
 
 def scores_kernel(place, ids, wanted, *refs):
     mine, others = refs[:4], refs[4:8]
-    expo, ph, plow, hh, hlow, keep, send, punit, hunit, row_sums = refs[8:]
+    expo_out, halves_out, keep, send = refs[8:12]
+    punit, hunit, row_sums, expo, ph, plow, hh, hlow, sems = refs[12:]
+    ph_out, plow_out, hh_out, hlow_out = kept(halves_out)
     x, y, c, zh, zl = (place[k] for k in range(5))
 
     def unit(v):
@@ -136,30 +145,46 @@
         fill(others, mine, 0)
 
     hh[...], hlow[...] = split(hunit[...])
+    whole = [
+        pltpu.make_async_copy(hh, hh_out, sems.at[3]),
+        pltpu.make_async_copy(hlow, hlow_out, sems.at[4]),
+    ]
+    for copy in whole:
+        copy.start()
     places = ids[...]
 
-    def step(i, carry):
-        total, positive = carry
-        here = pl.ds(pl.multiple_of(i * STEP, STEP), STEP)
+    def copies(here):
+        pairs = ((expo, expo_out), (ph, ph_out), (plow, plow_out))
+        return [
+            pltpu.make_async_copy(a.at[here, :], b.at[here, :], sems.at[k])
+            for k, (a, b) in enumerate(pairs)
+        ]
+
+    total = positive = jnp.zeros((8, COLS), jnp.float32)
+    for i in range(ROWS // STEP):
+        here = pl.ds(i * STEP, STEP)
         high, low = split(punit[here, :])
         ph[here, :] = high
         plow[here, :] = low
         scores = product(high, low, hh[...], hlow[...], ((1,), (1,))) * inv_temp
         e = jnp.exp(scores - inv_temp)
         expo[here, :] = e
+        if i:
+            for copy in copies(pl.ds((i - 1) * STEP, STEP)):
+                copy.wait()
+        for copy in copies(here):
+            copy.start()
         sums = jnp.sum(e, axis=1, keepdims=True)
-        for k in range(STEP // 128):
-            lanes = pl.ds(pl.multiple_of(i * STEP + k * 128, 128), 128)
-            row_sums[:, lanes] = to_lanes(sums[k * 128 : (k + 1) * 128])
+        for k in range(0, STEP, 128):
+            row_sums[:, pl.ds(i * STEP + k, 128)] = to_lanes(sums[k : k + 128])
+        total = total + jnp.sum(e.reshape(STEP // 8, 8, COLS), axis=0)
         match = wanted[here, :] == places
-        total = total + jnp.sum(e.reshape(STEP // 8, 8, COLS), axis=0)
         positive = positive + jnp.sum(
             jnp.where(match, scores, 0.0).reshape(STEP // 8, 8, COLS), axis=0
         )
-        return total, positive
-
-    zero = jnp.zeros((8, COLS), jnp.float32)
-    total, positive = lax.fori_loop(0, ROWS // STEP, step, (zero, zero))
+
+    for copy in copies(pl.ds(ROWS - STEP, STEP)) + whole:
+        copy.wait()
     positive = jnp.sum(positive, axis=0, keepdims=True)
     row_sums[:, ROWS:] = sum(positive[:, k * 128 : (k + 1) * 128] for k in range(COLS // 128))
     total = jnp.sum(total, axis=0, keepdims=True)
@@ -176,9 +201,21 @@
         send[...] = row_sums[...]
 
 
-def grads_kernel(place, ids, wanted, sums, other_sums, expo, ph, plow, hh, hlow, *refs):
+def grads_kernel(place, ids, wanted, sums, other_sums, expo_in, halves_in, *refs):
     keeps, sends = refs[:2], refs[2:4]
-    dh, dlow, pgrads, hgrads = refs[4:]
+    dh, dlow, pgrads, hgrads, expo, ph, plow, hh, hlow, sems = refs[4:]
+    ph_in, plow_in, hh_in, hlow_in = kept(halves_in)
+    steps = [pl.ds(i * STEP, STEP) for i in range(ROWS // STEP)]
+    whole = [
+        pltpu.make_async_copy(a, b, sems.at[k])
+        for k, (a, b) in enumerate(((hh_in, hh), (hlow_in, hlow), (ph_in, ph), (plow_in, plow)))
+    ]
+    chunks = [
+        pltpu.make_async_copy(expo_in.at[here, :], expo.at[here, :], sems.at[4 + i])
+        for i, here in enumerate(steps)
+    ]
+    for copy in whole[:2] + chunks + whole[2:]:
+        copy.start()
     x, y, c, zh, zl = (place[k] for k in range(5))
     first = c == 0
     scale = inv_temp / (2.0 * BATCH)
@@ -189,8 +226,10 @@
     row_inv = scale / rows[:, :ROWS]
     col_inv = scale / jnp.where(first, cols[:, :COLS], cols[:, COLS : 2 * COLS])
     places = ids[...]
-    for i in range(ROWS // STEP):
-        here = pl.ds(i * STEP, STEP)
+    for copy in whole[:2]:
+        copy.wait()
+    for i, here in enumerate(steps):
+        chunks[i].wait()
         per_row = jnp.concatenate(
             [to_rows(row_inv[:, k : k + 128]) for k in range(i * STEP, (i + 1) * STEP, 128)], axis=0
         )
@@ -200,6 +239,8 @@
         dh[here, :] = high
         dlow[here, :] = low
         pgrads[here, :] = product(high, low, hh[...], hlow[...], ((1,), (0,)))
+    for copy in whole[2:]:
+        copy.wait()
     for k in range(COLS // 128):
         here = pl.ds(k * 128, 128)
         hgrads[here, :] = product(dh[:, here], dlow[:, here], ph[...], plow[...], ((0,), (0,)))
@@ -232,15 +273,32 @@
         packets(sends, 0.0)
 
 
-def in_vmem(count):
-    return [pl.BlockSpec(memory_space=pltpu.VMEM)] * count
-
-
-def call(kernel, operands, outs, scratch, flops):
+def last_kernel(place, packet, header, pair, got, packet_grad, header_grad, loss):
+    first = place[2] == 0
+    own, other = pair[:B, :], got[:B, :]
+
+    def back(values, grads):
+        norms = jnp.sqrt(jnp.sum(values * values, axis=1, keepdims=True) + eps_norm)
+        inverse = 1.0 / norms
+        units = values * inverse
+        return (grads - units * jnp.sum(units * grads, axis=1, keepdims=True)) * inverse
+
+    packet_grad[...] = back(packet[...], jnp.where(first, own, other))
+    header_grad[...] = back(header[...], jnp.where(first, other, own))
+    term = jnp.max(pair[2 * B :, :128] + got[B:, :128])
+    loss[0, 0] = inv_temp + term / (2.0 * BATCH)
+
+
+IN_VMEM = pl.BlockSpec(memory_space=pltpu.VMEM)
+IN_SMEM = pl.BlockSpec(memory_space=pltpu.SMEM)
+IN_PLACE = pl.BlockSpec(memory_space=pl.ANY)
+
+
+def call(kernel, operands, in_specs, outs, out_specs, scratch, flops):
     return pl.pallas_call(
         kernel,
-        in_specs=[pl.BlockSpec(memory_space=pltpu.SMEM)] + in_vmem(len(operands) - 1),
-        out_specs=in_vmem(len(outs)),
+        in_specs=[IN_SMEM] + in_specs,
+        out_specs=out_specs,
         out_shape=outs,
         scratch_shapes=scratch,
         compiler_params=pltpu.CompilerParams(vmem_limit_bytes=VMEM_LIMIT),
@@ -254,15 +312,6 @@
 
 def b16(*shape):
     return jax.ShapeDtypeStruct(shape, jnp.bfloat16)
-
-
-def unit_rows(values):
-    norms = jnp.sqrt(jnp.sum(values * values, axis=1, keepdims=True) + eps_norm)
-    return (values / norms, norms)
-
-
-def unit_back(grads, units, norms):
-    return (grads - units * jnp.sum(units * grads, axis=1, keepdims=True)) / norms
 
 
 def together(*values):
@@ -280,7 +329,6 @@
     zb = along_z(pair, 1, -1)
     line = jnp.stack([pair, za, zb, along_z(za, 1, 1)])
     ahead, behind = along_xy(line, 1), along_xy(line, -1)
-    ahead, behind, line_again = together(ahead, behind, line)
     lines = [line, ahead, behind, along_xy(ahead, 1)]
     return lines, [swap_core(line) for line in lines]
 
@@ -288,9 +336,9 @@
 def scatter(keeps, sends):
     far, ahead = (keeps[0] + swap_core(sends[0]))[:]
     behind, line = (keeps[1] + swap_core(sends[1]))[:]
-    line = line + along_xy(ahead + along_xy(far, -1), -1) + along_xy(behind, 1)
-    za = line[1] + along_z(line[3], 1, -1)
-    return line[0] + along_z(za, 2, -1) + along_z(line[2], 1, 1)
+    line = line + along_xy(ahead, -1) + along_xy(behind + along_xy(far, 1), 1)
+    zb = line[2] + along_z(line[3], 2, 1)
+    return line[0] + along_z(line[1], 2, -1) + along_z(zb, 1, 1)
 
 
 def per_device(packet, header, partner):
@@ -307,11 +355,18 @@
     first = c == 0
     lines, other_lines = gather(first, packet, header)
     flops = 2 * 3 * ROWS * COLS * D
-    expo, ph, plow, hh, hlow, keep, send = call(
+    tiles = [((ROWS, COLS), jnp.float32)] + [((ROWS, D), jnp.bfloat16)] * 2
+    tiles += [((COLS, D), jnp.bfloat16)] * 2
+    held = [pltpu.VMEM(*tile) for tile in tiles]
+    expo, halves, keep, send = call(
         scores_kernel,
         [place, ids, wanted] + lines + other_lines,
-        [f32(ROWS, COLS), b16(ROWS, D), b16(ROWS, D), b16(COLS, D), b16(COLS, D)] + [f32(1, SUMS)] * 2,
-        [pltpu.VMEM((ROWS, D), jnp.float32), pltpu.VMEM((COLS, D), jnp.float32), pltpu.VMEM((1, SUMS), jnp.float32)],
+        [IN_VMEM] * 10,
+        [f32(KEPT_F32, COLS), b16(KEPT_B16, D), f32(1, SUMS), f32(1, SUMS)],
+        [IN_PLACE] * 2 + [IN_VMEM] * 2,
+        [pltpu.VMEM((ROWS, D), jnp.float32), pltpu.VMEM((COLS, D), jnp.float32), pltpu.VMEM((1, SUMS), jnp.float32)]
+        + held
+        + [pltpu.SemaphoreType.DMA((5,))],
         flops,
     )
     sums = lax.all_to_all(
@@ -321,26 +376,31 @@
     sums = jnp.sum(sums, axis=0)
     parts = call(
         grads_kernel,
-        [place, ids, wanted, sums, swap_core(sums), expo, ph, plow, hh, hlow],
+        [place, ids, wanted, sums, swap_core(sums), expo, halves],
+        [IN_VMEM] * 4 + [IN_PLACE] * 2,
         [f32(2, 4, PAIR, D)] * 4,
+        [IN_VMEM] * 4,
         [
             pltpu.VMEM((ROWS, COLS), jnp.bfloat16),
             pltpu.VMEM((ROWS, COLS), jnp.bfloat16),
             pltpu.VMEM((ROWS, D), jnp.float32),
             pltpu.VMEM((COLS, D), jnp.float32),
-        ],
+        ]
+        + held
+        + [pltpu.SemaphoreType.DMA((4 + ROWS // STEP,))],
         2 * flops,
     )
     pair = scatter(parts[:2], parts[2:])
-    got = swap_core(pair[B:])
-    own, other = pair[:B], got[:B]
-    gpunit, ghunit = jnp.where(first, own, other), jnp.where(first, other, own)
-    loss = inv_temp + (pair[2 * B, 0] + got[B, 0]) / (2.0 * BATCH)
-    punit, pnorm = unit_rows(packet)
-    hunit, hnorm = unit_rows(header)
-    packet_grad = unit_back(gpunit, punit, pnorm)
-    header_grad = unit_back(ghunit, hunit, hnorm)
-    return (loss, packet_grad, header_grad)
+    packet_grad, header_grad, loss = call(
+        last_kernel,
+        [place, packet, header, pair, swap_core(pair[B:])],
+        [IN_VMEM] * 4,
+        [f32(B, D), f32(B, D), f32(1, 1)],
+        [IN_VMEM, IN_VMEM, IN_SMEM],
+        [],
+        10 * B * D,
+    )
+    return (loss[0, 0], packet_grad, header_grad)
 
 
 def solution(mesh):

time: 202 us -> 194 us (0.960)
  starting transfers between devices: 79.2 us -> 92.4 us
  waiting for transfers between devices: 58.1 us -> 48 us
  local copies, waits for them, and re-layouts: 8.47 us -> 0.94 us
  between operations: 3.52 us -> 1.21 us
  Pallas kernels: 20.5 us -> 22.8 us
    ppermute x22, starting transfers between devices: 79.2 us -> 92.4 us  [permute(): return lax.ppermute(value, ALL, pairs)]
    ppermute x22, waiting for transfers between devices: 58.1 us -> 48 us  [permute(): return lax.ppermute(value, ALL, pairs)]
    unnamed x22 -> x8, local copies, waits for them, and re-layouts: 6.54 us -> 0.02 us
    pallas_call x2 -> x3, Pallas kernels: 20.5 us -> 22.8 us  [call(): pl.pallas_call(kernel, in_specs=[IN_SMEM] + in_specs, out_specs=out_specs...]
where the time goes in v4:
time: 194 us; the launch traced here: 193 us
  starting transfers between devices  92.4 us (48%)
  waiting for transfers between devices  48 us (25%)
  blocking collectives  25.2 us (13%)
  Pallas kernels  22.8 us (12%)
  other arithmetic  2.16 us (1%)
    ppermute x22, starting transfers between devices, permute(): return lax.ppermute(value, ALL, pairs)  92.4 us
    ppermute x22, waiting for transfers between devices, permute(): return lax.ppermute(value, ALL, pairs)  48 us
    all_to_all x1, blocking collectives, per_device(): lax.all_to_all(jnp.broadcast_to((keep + swap_core(send))[None], (16, 1, S...  25.2 us
    pallas_call x3, Pallas kernels, call(): pl.pallas_call(kernel, in_specs=[IN_SMEM] + in_specs, out_specs=out_specs...  22.8 us
  transfers between devices with their start and end apart: 22, of which 16 were waited for; matrix products, arithmetic and copies ran while one was open for 1% of the time, Pallas kernels for 0%

profile of v4, /device:TPU:1, one launch (start us, length us, event | category | flops | bytes accessed | tf_op | source)
XLA Modules:
  0.0 192.7 jit_solution(6818645378067268011)
XLA Ops:
  1.6 8.8 %collective-permute-start = (f32[40,512]{1,0:T(8,128)S(1)}, f32[40,512]{1,0:T(8,128)S(1)}, u32[]{:S(2)}, u32[]{:S(2)}) collective-permute-start(f32[40,512]{1,0:T(8,128)S(1)} %get-tuple-element.32), channel_id=1, source_target_pairs={{16,0},{17,1},{18,2},{19,3},{20,4},{21,5},{22,6},{23,7},{24,8},{25... | collective-permute-start | bytes 245768 | tf_op jit(solution)/shard_map/ppermute | solution.py:36
  11.4 7.1 %collective-permute-start.1 = (f32[80,512]{1,0:T(8,128)S(1)}, f32[80,512]{1,0:T(8,128)S(1)}, u32[]{:S(2)}, u32[]{:S(2)}) collective-permute-start(f32[80,512]{1,0:T(8,128)S(1)} %get-tuple-element.30), channel_id=1, source_target_pairs={{2,0},{3,1},{0,2},{1,3},{6,4},{7,5},{4,6},{5,7},{10,8},{11,9},{8,1... | collective-permute-start | bytes 491528 | tf_op jit(solution)/shard_map/ppermute | solution.py:36
  18.5 2.1 %collective-permute-start.2 = (f32[80,512]{1,0:T(8,128)S(1)}, f32[80,512]{1,0:T(8,128)S(1)}, u32[]{:S(2)}, u32[]{:S(2)}) collective-permute-start(f32[80,512]{1,0:T(8,128)S(1)} %get-tuple-element.30), channel_id=1, source_target_pairs={{1,0},{0,1},{3,2},{2,3},{5,4},{4,5},{7,6},{6,7},{9,8},{8,9},{11,10... | collective-permute-start | bytes 491528 | tf_op jit(solution)/shard_map/ppermute | solution.py:36
  20.6 2.9 %collective-permute-done.1 = f32[80,512]{1,0:T(8,128)S(1)} collective-permute-done((f32[80,512]{1,0:T(8,128)S(1)}, f32[80,512]{1,0:T(8,128)S(1)}, u32[]{:S(2)}, u32[]{:S(2)}) %collective-permute-start.1) | collective-permute-done | bytes 163872 | tf_op jit(solution)/shard_map/ppermute | solution.py:36
  23.4 6.0 %collective-permute-start.3 = (f32[80,512]{1,0:T(8,128)S(1)}, f32[80,512]{1,0:T(8,128)S(1)}, u32[]{:S(2)}, u32[]{:S(2)}) collective-permute-start(f32[80,512]{1,0:T(8,128)S(1)} %collective-permute-done.1), channel_id=1, source_target_pairs={{1,0},{0,1},{3,2},{2,3},{5,4},{4,5},{7,6},{6,7},{9,8},{8,9},{11,10... | collective-permute-start | bytes 491528 | tf_op jit(solution)/shard_map/ppermute | solution.py:36
  29.5 2.6 %collective-permute-done.2 = f32[80,512]{1,0:T(8,128)S(1)} collective-permute-done((f32[80,512]{1,0:T(8,128)S(1)}, f32[80,512]{1,0:T(8,128)S(1)}, u32[]{:S(2)}, u32[]{:S(2)}) %collective-permute-start.2) | collective-permute-done | bytes 163872 | tf_op jit(solution)/shard_map/ppermute | solution.py:36
  34.0 10.9 %collective-permute-start.4 = (f32[4,80,512]{2,1,0:T(8,128)S(1)}, f32[4,80,512]{2,1,0:T(8,128)S(1)}, u32[]{:S(2)}, u32[]{:S(2)}) collective-permute-start(f32[4,80,512]{2,1,0:T(8,128)S(1)} %pad_maximum_fusion.refs_0_), channel_id=1, source_target_pairs={{128,0},{129,1},{130,2},{131,3},{132,4},{133,5},{134,6},{135,7},{1... | collective-permute-start | bytes 1966088 | tf_op jit(solution)/shard_map/ppermute | solution.py:36
  44.9 1.9 collective-permute-start.5
  46.8 5.6 %collective-permute-done.4.refs_1_ = f32[4,80,512]{2,1,0:T(8,128)S(1)} collective-permute-done((f32[4,80,512]{2,1,0:T(8,128)S(1)}, f32[4,80,512]{2,1,0:T(8,128)S(1)}, u32[]{:S(2)}, u32[]{:S(2)}) %collective-permute-start.4) | collective-permute-done | bytes 655392 | tf_op jit(solution)/shard_map/ppermute | solution.py:36
  52.4 5.0 %collective-permute-start.6 = (f32[4,80,512]{2,1,0:T(8,128)S(1)}, f32[4,80,512]{2,1,0:T(8,128)S(1)}, u32[]{:S(2)}, u32[]{:S(2)}) collective-permute-start(f32[4,80,512]{2,1,0:T(8,128)S(1)} %collective-permute-done.4.refs_1_), channel_id=1, source_target_pairs={{128,0},{129,1},{130,2},{131,3},{132,4},{133,5},{134,6},{135,7},{1... | collective-permute-start | bytes 1966088 | tf_op jit(solution)/shard_map/ppermute | solution.py:36
  57.4 1.9 collective-permute-start.7
  59.4 2.4 %collective-permute-start.8 = (f32[4,80,512]{2,1,0:T(8,128)S(1)}, f32[4,80,512]{2,1,0:T(8,128)}, u32[]{:S(2)}, u32[]{:S(2)}) collective-permute-start(f32[4,80,512]{2,1,0:T(8,128)S(1)} %collective-permute-done.4.refs_1_), channel_id=1, source_target_pairs={{16,0},{17,1},{18,2},{19,3},{20,4},{21,5},{22,6},{23,7},{24,8},{25... | collective-permute-start | bytes 1966088 | tf_op jit(solution)/shard_map/ppermute | solution.py:36
  61.8 1.9 collective-permute-start.9
  69.1 10.0 %shard_map.67 = (f32[7680,640]{1,0:T(8,128)}, bf16[20480,512]{1,0:T(8,128)(2,1)}, f32[1,1408]{1,0:T(1,128)S(1)}, f32[1,1408]{1,0:T(1,128)S(1)}) custom-call(s32[5]{0:T(128)S(1)} %stack.38.place, s32[1,640]{1,0:T(1,128)S(1)} %add.51.ids, s32[1280,1]{1,0:T(8,128)S(1)} %reshape.19.wanted, f32[4,80,512]{2,1,0:T(8,128)S(1)} %pad_maximum_fusion.refs_0_, ...), custom_call_target="tpu_custom_call" | custom-call | flops 2516582400 | bytes 8388608 | tf_op jit(solution)/shard_map/pallas_call | solution.py:298
  79.0 2.0 %collective-permute-start.11 = (f32[1,1408]{1,0:T(1,128)S(1)}, f32[1,1408]{1,0:T(1,128)S(1)}, u32[]{:S(2)}, u32[]{:S(2)}) collective-permute-start(f32[1,1408]{1,0:T(1,128)S(1)} %get-tuple-element.15), channel_id=1, source_target_pairs={{16,0},{17,1},{18,2},{19,3},{20,4},{21,5},{22,6},{23,7},{24,8},{25... | collective-permute-start | bytes 16904 | tf_op jit(solution)/shard_map/ppermute | solution.py:36
  82.2 25.2 %all_to_all.5 = f32[16,1,1408]{2,1,0:T(1,128)S(1)} all-to-all(f32[16,1,1408]{2,1,0:T(1,128)S(1)} %broadcast_in_dim.10), channel_id=1, replica_groups={{0,1,2,3,128,129,130,131,256,257,258,259,384,385,386,387},{16,20,24,28,..., dimensions={0} | all-to-all | bytes 180224 | tf_op jit(solution)/shard_map/all_to_all | solution.py:372
  107.5 2.1 %collective-permute-start.12 = (f32[1,1408]{1,0:T(1,128)S(1)}, f32[1,1408]{1,0:T(1,128)S(1)}, u32[]{:S(2)}, u32[]{:S(2)}) collective-permute-start(f32[1,1408]{1,0:T(1,128)S(1)} %reduce_sum.12.sums), channel_id=1, source_target_pairs={{16,0},{17,1},{18,2},{19,3},{20,4},{21,5},{22,6},{23,7},{24,8},{25... | collective-permute-start | bytes 16904 | tf_op jit(solution)/shard_map/ppermute | solution.py:36
  110.6 11.4 %shard_map.68 = (f32[2,4,88,512]{3,2,1,0:T(8,128)S(1)}, f32[2,4,88,512]{3,2,1,0:T(8,128)S(1)}, f32[2,4,88,512]{3,2,1,0:T(8,128)S(1)}, f32[2,4,88,512]{3,2,1,0:T(8,128)}) custom-call(s32[5]{0:T(128)S(1)} %stack.38.place, s32[1,640]{1,0:T(1,128)S(1)} %add.51.ids, s32[1280,1]{1,0:T(8,128)S(1)} %reshape.19.wanted, f32[1,1408]{1,0:T(1,128)S(1)} %reduce_sum.12.sums, ...), custom_call_target="tpu_custom_call" | custom-call | flops 5033164800 | bytes 8388608 | tf_op jit(solution)/shard_map/pallas_call | solution.py:298
  122.0 2.1 %collective-permute-start.14 = (f32[2,4,88,512]{3,2,1,0:T(8,128)S(1)}, f32[2,4,88,512]{3,2,1,0:T(8,128)S(1)}, u32[]{:S(2)}, u32[]{:S(2)}) collective-permute-start(f32[2,4,88,512]{3,2,1,0:T(8,128)S(1)} %get-tuple-element.21), channel_id=1, source_target_pairs={{16,0},{17,1},{18,2},{19,3},{20,4},{21,5},{22,6},{23,7},{24,8},{25... | collective-permute-start | bytes 4325384 | tf_op jit(solution)/shard_map/ppermute | solution.py:36
  124.1 2.2 %collective-permute-start.13 = (f32[2,4,88,512]{3,2,1,0:T(8,128)}, f32[2,4,88,512]{3,2,1,0:T(8,128)S(1)}, u32[]{:S(2)}, u32[]{:S(2)}) collective-permute-start(f32[2,4,88,512]{3,2,1,0:T(8,128)} %get-tuple-element.19), channel_id=1, source_target_pairs={{16,0},{17,1},{18,2},{19,3},{20,4},{21,5},{22,6},{23,7},{24,8},{25... | collective-permute-start | bytes 4325384 | tf_op jit(solution)/shard_map/ppermute | solution.py:36
  127.5 2.5 %collective-permute-start.16 = (f32[4,88,512]{2,1,0:T(8,128)S(1)}, f32[4,88,512]{2,1,0:T(8,128)S(1)}, u32[]{:S(2)}, u32[]{:S(2)}) collective-permute-start(f32[4,88,512]{2,1,0:T(8,128)S(1)} %get-tuple-element.26), channel_id=1, source_target_pairs={{128,0},{129,1},{130,2},{131,3},{132,4},{133,5},{134,6},{135,7},{1... | collective-permute-start | bytes 2162696 | tf_op jit(solution)/shard_map/ppermute | solution.py:36
  130.0 2.8 %collective-permute-start.15 = (f32[4,88,512]{2,1,0:T(8,128)S(1)}, f32[4,88,512]{2,1,0:T(8,128)S(1)}, u32[]{:S(2)}, u32[]{:S(2)}) collective-permute-start(f32[4,88,512]{2,1,0:T(8,128)S(1)} %get-tuple-element.25), channel_id=1, source_target_pairs={{384,0},{385,1},{386,2},{387,3},{388,4},{389,5},{390,6},{391,7},{3... | collective-permute-start | bytes 2162696 | tf_op jit(solution)/shard_map/ppermute | solution.py:36
  133.1 6.7 %collective-permute-done.16 = f32[4,88,512]{2,1,0:T(8,128)S(1)} collective-permute-done((f32[4,88,512]{2,1,0:T(8,128)S(1)}, f32[4,88,512]{2,1,0:T(8,128)S(1)}, u32[]{:S(2)}, u32[]{:S(2)}) %collective-permute-start.16) | collective-permute-done | bytes 720928 | tf_op jit(solution)/shard_map/ppermute | solution.py:36
  140.0 3.7 %collective-permute-start.17 = (f32[4,88,512]{2,1,0:T(8,128)S(1)}, f32[4,88,512]{2,1,0:T(8,128)S(1)}, u32[]{:S(2)}, u32[]{:S(2)}) collective-permute-start(f32[4,88,512]{2,1,0:T(8,128)S(1)} %fusion), channel_id=1, source_target_pairs={{128,0},{129,1},{130,2},{131,3},{132,4},{133,5},{134,6},{135,7},{1... | collective-permute-start | bytes 2162696 | tf_op jit(solution)/shard_map/ppermute | solution.py:36
  143.7 8.6 %collective-permute-done.17 = f32[4,88,512]{2,1,0:T(8,128)S(1)} collective-permute-done((f32[4,88,512]{2,1,0:T(8,128)S(1)}, f32[4,88,512]{2,1,0:T(8,128)S(1)}, u32[]{:S(2)}, u32[]{:S(2)}) %collective-permute-start.17) | collective-permute-done | bytes 720928 | tf_op jit(solution)/shard_map/ppermute | solution.py:36
  152.6 2.5 %collective-permute-start.19 = (f32[88,512]{1,0:T(8,128)S(1)}, f32[88,512]{1,0:T(8,128)S(1)}, u32[]{:S(2)}, u32[]{:S(2)}) collective-permute-start(f32[88,512]{1,0:T(8,128)S(1)} %get-tuple-element.28), channel_id=1, source_target_pairs={{2,0},{3,1},{0,2},{1,3},{6,4},{7,5},{4,6},{5,7},{10,8},{11,9},{8,1... | collective-permute-start | bytes 540680 | tf_op jit(solution)/shard_map/ppermute | solution.py:36
  155.1 6.8 %collective-permute-start.18 = (f32[88,512]{1,0:T(8,128)S(1)}, f32[88,512]{1,0:T(8,128)S(1)}, u32[]{:S(2)}, u32[]{:S(2)}) collective-permute-start(f32[88,512]{1,0:T(8,128)S(1)} %get-tuple-element.27), channel_id=1, source_target_pairs={{2,0},{3,1},{0,2},{1,3},{6,4},{7,5},{4,6},{5,7},{10,8},{11,9},{8,1... | collective-permute-start | bytes 540680 | tf_op jit(solution)/shard_map/ppermute | solution.py:36
  161.9 3.1 %collective-permute-done.19 = f32[88,512]{1,0:T(8,128)S(1)} collective-permute-done((f32[88,512]{1,0:T(8,128)S(1)}, f32[88,512]{1,0:T(8,128)S(1)}, u32[]{:S(2)}, u32[]{:S(2)}) %collective-permute-start.19) | collective-permute-done | bytes 180256 | tf_op jit(solution)/shard_map/ppermute | solution.py:36
  165.0 2.3 %collective-permute-start.20 = (f32[88,512]{1,0:T(8,128)S(1)}, f32[88,512]{1,0:T(8,128)S(1)}, u32[]{:S(2)}, u32[]{:S(2)}) collective-permute-start(f32[88,512]{1,0:T(8,128)S(1)} %fusion.3), channel_id=1, source_target_pairs={{1,0},{0,1},{3,2},{2,3},{5,4},{4,5},{7,6},{6,7},{9,8},{8,9},{11,10... | collective-permute-start | bytes 540680 | tf_op jit(solution)/shard_map/ppermute | solution.py:36
  167.3 4.8 %collective-permute-done.18 = f32[88,512]{1,0:T(8,128)S(1)} collective-permute-done((f32[88,512]{1,0:T(8,128)S(1)}, f32[88,512]{1,0:T(8,128)S(1)}, u32[]{:S(2)}, u32[]{:S(2)}) %collective-permute-start.18) | collective-permute-done | bytes 180256 | tf_op jit(solution)/shard_map/ppermute | solution.py:36
  172.2 4.7 %collective-permute-done.20 = f32[88,512]{1,0:T(8,128)S(1)} collective-permute-done((f32[88,512]{1,0:T(8,128)S(1)}, f32[88,512]{1,0:T(8,128)S(1)}, u32[]{:S(2)}, u32[]{:S(2)}) %collective-permute-start.20) | collective-permute-done | bytes 180256 | tf_op jit(solution)/shard_map/ppermute | solution.py:36
  176.9 13.3 %collective-permute-start.21 = (f32[48,512]{1,0:T(8,128)S(1)}, f32[48,512]{1,0:T(8,128)S(1)}, u32[]{:S(2)}, u32[]{:S(2)}) collective-permute-start(f32[48,512]{1,0:T(8,128)S(1)} %slice.24), channel_id=1, source_target_pairs={{16,0},{17,1},{18,2},{19,3},{20,4},{21,5},{22,6},{23,7},{24,8},{25... | collective-permute-start | bytes 294920 | tf_op jit(solution)/shard_map/ppermute | solution.py:36
  (46 shorter events, 15.5 us)
Async XLA Ops:
  0.6 66.3 %copy-start.3 = (s32[640]{0:T(1024)S(1)}, s32[640]{0:T(1024)}, u32[]{:S(2)}) copy-start(s32[640]{0:T(1024)} %constant.33.clone) | copy-start | bytes 7684
  0.6 66.3 %copy-start.2 = (s32[20480]{0:T(1024)S(1)}, s32[20480]{0:T(1024)}, u32[]{:S(2)}) copy-start(s32[20480]{0:T(1024)} %param.6) | copy-start | bytes 245764
  1.6 9.7 %collective-permute-start = (f32[40,512]{1,0:T(8,128)S(1)}, f32[40,512]{1,0:T(8,128)S(1)}, u32[]{:S(2)}, u32[]{:S(2)}) collective-permute-start(f32[40,512]{1,0:T(8,128)S(1)} %get-tuple-element.32), channel_id=1, source_target_pairs={{16,0},{17,1},{18,2},{19,3},{20,4},{21,5},{22,6},{23,7},{24,8},{25... | collective-permute-start | bytes 245768 | tf_op jit(solution)/shard_map/ppermute | solution.py:36
  11.4 12.1 %collective-permute-start.1 = (f32[80,512]{1,0:T(8,128)S(1)}, f32[80,512]{1,0:T(8,128)S(1)}, u32[]{:S(2)}, u32[]{:S(2)}) collective-permute-start(f32[80,512]{1,0:T(8,128)S(1)} %get-tuple-element.30), channel_id=1, source_target_pairs={{2,0},{3,1},{0,2},{1,3},{6,4},{7,5},{4,6},{5,7},{10,8},{11,9},{8,1... | collective-permute-start | bytes 491528 | tf_op jit(solution)/shard_map/ppermute | solution.py:36
  18.5 13.6 %collective-permute-start.2 = (f32[80,512]{1,0:T(8,128)S(1)}, f32[80,512]{1,0:T(8,128)S(1)}, u32[]{:S(2)}, u32[]{:S(2)}) collective-permute-start(f32[80,512]{1,0:T(8,128)S(1)} %get-tuple-element.30), channel_id=1, source_target_pairs={{1,0},{0,1},{3,2},{2,3},{5,4},{4,5},{7,6},{6,7},{9,8},{8,9},{11,10... | collective-permute-start | bytes 491528 | tf_op jit(solution)/shard_map/ppermute | solution.py:36
  23.4 10.5 %collective-permute-start.3 = (f32[80,512]{1,0:T(8,128)S(1)}, f32[80,512]{1,0:T(8,128)S(1)}, u32[]{:S(2)}, u32[]{:S(2)}) collective-permute-start(f32[80,512]{1,0:T(8,128)S(1)} %collective-permute-done.1), channel_id=1, source_target_pairs={{1,0},{0,1},{3,2},{2,3},{5,4},{4,5},{7,6},{6,7},{9,8},{8,9},{11,10... | collective-permute-start | bytes 491528 | tf_op jit(solution)/shard_map/ppermute | solution.py:36
  34.0 18.4 %collective-permute-start.4 = (f32[4,80,512]{2,1,0:T(8,128)S(1)}, f32[4,80,512]{2,1,0:T(8,128)S(1)}, u32[]{:S(2)}, u32[]{:S(2)}) collective-permute-start(f32[4,80,512]{2,1,0:T(8,128)S(1)} %pad_maximum_fusion.refs_0_), channel_id=1, source_target_pairs={{128,0},{129,1},{130,2},{131,3},{132,4},{133,5},{134,6},{135,7},{1... | collective-permute-start | bytes 1966088 | tf_op jit(solution)/shard_map/ppermute | solution.py:36
  44.9 16.9 %collective-permute-start.5 = (f32[4,80,512]{2,1,0:T(8,128)S(1)}, f32[4,80,512]{2,1,0:T(8,128)S(1)}, u32[]{:S(2)}, u32[]{:S(2)}) collective-permute-start(f32[4,80,512]{2,1,0:T(8,128)S(1)} %pad_maximum_fusion.refs_0_), channel_id=1, source_target_pairs={{384,0},{385,1},{386,2},{387,3},{388,4},{389,5},{390,6},{391,7},{3... | collective-permute-start | bytes 1966088 | tf_op jit(solution)/shard_map/ppermute | solution.py:36
  52.4 12.5 %collective-permute-start.6 = (f32[4,80,512]{2,1,0:T(8,128)S(1)}, f32[4,80,512]{2,1,0:T(8,128)S(1)}, u32[]{:S(2)}, u32[]{:S(2)}) collective-permute-start(f32[4,80,512]{2,1,0:T(8,128)S(1)} %collective-permute-done.4.refs_1_), channel_id=1, source_target_pairs={{128,0},{129,1},{130,2},{131,3},{132,4},{133,5},{134,6},{135,7},{1... | collective-permute-start | bytes 1966088 | tf_op jit(solution)/shard_map/ppermute | solution.py:36
  57.4 10.2 %collective-permute-start.7 = (f32[4,80,512]{2,1,0:T(8,128)S(1)}, f32[4,80,512]{2,1,0:T(8,128)}, u32[]{:S(2)}, u32[]{:S(2)}) collective-permute-start(f32[4,80,512]{2,1,0:T(8,128)S(1)} %pad_maximum_fusion.refs_0_), channel_id=1, source_target_pairs={{16,0},{17,1},{18,2},{19,3},{20,4},{21,5},{22,6},{23,7},{24,8},{25... | collective-permute-start | bytes 1966088 | tf_op jit(solution)/shard_map/ppermute | solution.py:36
  59.4 8.3 %collective-permute-start.8 = (f32[4,80,512]{2,1,0:T(8,128)S(1)}, f32[4,80,512]{2,1,0:T(8,128)}, u32[]{:S(2)}, u32[]{:S(2)}) collective-permute-start(f32[4,80,512]{2,1,0:T(8,128)S(1)} %collective-permute-done.4.refs_1_), channel_id=1, source_target_pairs={{16,0},{17,1},{18,2},{19,3},{20,4},{21,5},{22,6},{23,7},{24,8},{25... | collective-permute-start | bytes 1966088 | tf_op jit(solution)/shard_map/ppermute | solution.py:36
  61.8 5.9 %collective-permute-start.9 = (f32[4,80,512]{2,1,0:T(8,128)S(1)}, f32[4,80,512]{2,1,0:T(8,128)}, u32[]{:S(2)}, u32[]{:S(2)}) collective-permute-start(f32[4,80,512]{2,1,0:T(8,128)S(1)} %collective-permute-done.5.refs_2_), channel_id=1, source_target_pairs={{16,0},{17,1},{18,2},{19,3},{20,4},{21,5},{22,6},{23,7},{24,8},{25... | collective-permute-start | bytes 1966088 | tf_op jit(solution)/shard_map/ppermute | solution.py:36
  65.0 4.1 %collective-permute-start.10 = (f32[4,80,512]{2,1,0:T(8,128)S(1)}, f32[4,80,512]{2,1,0:T(8,128)}, u32[]{:S(2)}, u32[]{:S(2)}) collective-permute-start(f32[4,80,512]{2,1,0:T(8,128)S(1)} %collective-permute-done.6.refs_3_), channel_id=1, source_target_pairs={{16,0},{17,1},{18,2},{19,3},{20,4},{21,5},{22,6},{23,7},{24,8},{25... | collective-permute-start | bytes 1966088 | tf_op jit(solution)/shard_map/ppermute | solution.py:36
  79.0 3.1 %collective-permute-start.11 = (f32[1,1408]{1,0:T(1,128)S(1)}, f32[1,1408]{1,0:T(1,128)S(1)}, u32[]{:S(2)}, u32[]{:S(2)}) collective-permute-start(f32[1,1408]{1,0:T(1,128)S(1)} %get-tuple-element.15), channel_id=1, source_target_pairs={{16,0},{17,1},{18,2},{19,3},{20,4},{21,5},{22,6},{23,7},{24,8},{25... | collective-permute-start | bytes 16904 | tf_op jit(solution)/shard_map/ppermute | solution.py:36
  107.5 3.1 %collective-permute-start.12 = (f32[1,1408]{1,0:T(1,128)S(1)}, f32[1,1408]{1,0:T(1,128)S(1)}, u32[]{:S(2)}, u32[]{:S(2)}) collective-permute-start(f32[1,1408]{1,0:T(1,128)S(1)} %reduce_sum.12.sums), channel_id=1, source_target_pairs={{16,0},{17,1},{18,2},{19,3},{20,4},{21,5},{22,6},{23,7},{24,8},{25... | collective-permute-start | bytes 16904 | tf_op jit(solution)/shard_map/ppermute | solution.py:36
  122.0 5.1 %collective-permute-start.14 = (f32[2,4,88,512]{3,2,1,0:T(8,128)S(1)}, f32[2,4,88,512]{3,2,1,0:T(8,128)S(1)}, u32[]{:S(2)}, u32[]{:S(2)}) collective-permute-start(f32[2,4,88,512]{3,2,1,0:T(8,128)S(1)} %get-tuple-element.21), channel_id=1, source_target_pairs={{16,0},{17,1},{18,2},{19,3},{20,4},{21,5},{22,6},{23,7},{24,8},{25... | collective-permute-start | bytes 4325384 | tf_op jit(solution)/shard_map/ppermute | solution.py:36
  124.1 8.8 %collective-permute-start.13 = (f32[2,4,88,512]{3,2,1,0:T(8,128)}, f32[2,4,88,512]{3,2,1,0:T(8,128)S(1)}, u32[]{:S(2)}, u32[]{:S(2)}) collective-permute-start(f32[2,4,88,512]{3,2,1,0:T(8,128)} %get-tuple-element.19), channel_id=1, source_target_pairs={{16,0},{17,1},{18,2},{19,3},{20,4},{21,5},{22,6},{23,7},{24,8},{25... | collective-permute-start | bytes 4325384 | tf_op jit(solution)/shard_map/ppermute | solution.py:36
  127.5 12.3 %collective-permute-start.16 = (f32[4,88,512]{2,1,0:T(8,128)S(1)}, f32[4,88,512]{2,1,0:T(8,128)S(1)}, u32[]{:S(2)}, u32[]{:S(2)}) collective-permute-start(f32[4,88,512]{2,1,0:T(8,128)S(1)} %get-tuple-element.26), channel_id=1, source_target_pairs={{128,0},{129,1},{130,2},{131,3},{132,4},{133,5},{134,6},{135,7},{1... | collective-permute-start | bytes 2162696 | tf_op jit(solution)/shard_map/ppermute | solution.py:36
  130.0 13.7 %collective-permute-start.15 = (f32[4,88,512]{2,1,0:T(8,128)S(1)}, f32[4,88,512]{2,1,0:T(8,128)S(1)}, u32[]{:S(2)}, u32[]{:S(2)}) collective-permute-start(f32[4,88,512]{2,1,0:T(8,128)S(1)} %get-tuple-element.25), channel_id=1, source_target_pairs={{384,0},{385,1},{386,2},{387,3},{388,4},{389,5},{390,6},{391,7},{3... | collective-permute-start | bytes 2162696 | tf_op jit(solution)/shard_map/ppermute | solution.py:36
  140.0 12.3 %collective-permute-start.17 = (f32[4,88,512]{2,1,0:T(8,128)S(1)}, f32[4,88,512]{2,1,0:T(8,128)S(1)}, u32[]{:S(2)}, u32[]{:S(2)}) collective-permute-start(f32[4,88,512]{2,1,0:T(8,128)S(1)} %fusion), channel_id=1, source_target_pairs={{128,0},{129,1},{130,2},{131,3},{132,4},{133,5},{134,6},{135,7},{1... | collective-permute-start | bytes 2162696 | tf_op jit(solution)/shard_map/ppermute | solution.py:36
  152.5 38.7 %copy-start = (f32[40,512]{1,0:T(8,128)S(1)}, f32[40,512]{1,0:T(8,128)}, u32[]{:S(2)}) copy-start(f32[40,512]{1,0:T(8,128)} %packet.1) | copy-start | bytes 245764
  152.5 38.7 %copy-start.1 = (f32[40,512]{1,0:T(8,128)S(1)}, f32[40,512]{1,0:T(8,128)}, u32[]{:S(2)}) copy-start(f32[40,512]{1,0:T(8,128)} %header.1) | copy-start | bytes 245764
  152.6 12.4 %collective-permute-start.19 = (f32[88,512]{1,0:T(8,128)S(1)}, f32[88,512]{1,0:T(8,128)S(1)}, u32[]{:S(2)}, u32[]{:S(2)}) collective-permute-start(f32[88,512]{1,0:T(8,128)S(1)} %get-tuple-element.28), channel_id=1, source_target_pairs={{2,0},{3,1},{0,2},{1,3},{6,4},{7,5},{4,6},{5,7},{10,8},{11,9},{8,1... | collective-permute-start | bytes 540680 | tf_op jit(solution)/shard_map/ppermute | solution.py:36
  155.1 17.1 %collective-permute-start.18 = (f32[88,512]{1,0:T(8,128)S(1)}, f32[88,512]{1,0:T(8,128)S(1)}, u32[]{:S(2)}, u32[]{:S(2)}) collective-permute-start(f32[88,512]{1,0:T(8,128)S(1)} %get-tuple-element.27), channel_id=1, source_target_pairs={{2,0},{3,1},{0,2},{1,3},{6,4},{7,5},{4,6},{5,7},{10,8},{11,9},{8,1... | collective-permute-start | bytes 540680 | tf_op jit(solution)/shard_map/ppermute | solution.py:36
  165.0 11.9 %collective-permute-start.20 = (f32[88,512]{1,0:T(8,128)S(1)}, f32[88,512]{1,0:T(8,128)S(1)}, u32[]{:S(2)}, u32[]{:S(2)}) collective-permute-start(f32[88,512]{1,0:T(8,128)S(1)} %fusion.3), channel_id=1, source_target_pairs={{1,0},{0,1},{3,2},{2,3},{5,4},{4,5},{7,6},{6,7},{9,8},{8,9},{11,10... | collective-permute-start | bytes 540680 | tf_op jit(solution)/shard_map/ppermute | solution.py:36
  176.9 14.2 %collective-permute-start.21 = (f32[48,512]{1,0:T(8,128)S(1)}, f32[48,512]{1,0:T(8,128)S(1)}, u32[]{:S(2)}, u32[]{:S(2)}) collective-permute-start(f32[48,512]{1,0:T(8,128)S(1)} %slice.24), channel_id=1, source_target_pairs={{16,0},{17,1},{18,2},{19,3},{20,4},{21,5},{22,6},{23,7},{24,8},{25... | collective-permute-start | bytes 294920 | tf_op jit(solution)/shard_map/ppermute | solution.py:36

commit v5 on v4

--- a/solution.py
+++ b/solution.py
@@ -42,7 +42,8 @@
 
 def along_z(value, flip, step):
     return permute(
-        value, lambda x, y, c, z: (x, y, c, (z + NL * step) % NZ if c else z ^ flip)
+        value,
+        lambda x, y, c, z: (x, y, c, (z + NL * step * (1 - 2 * (z % 2))) % NZ if c else z ^ flip),
     )
 
 
@@ -70,12 +71,13 @@
     return found
 
 
-def col_blocks(y, zh):
+def col_blocks(y, zh, zl):
     found = []
+    s = 1 - 2 * lax.rem(zl, 2)
     for j, dy in enumerate(PLACES):
         by = lax.rem(y + dy + NY, NY)
         for k, dz in enumerate(PLACES):
-            found.append((j, k, lax.rem(zh + dz + NH, NH) * NY + by))
+            found.append((j, k, lax.rem(zh + s * dz + NH, NH) * NY + by))
     return found
 
 
@@ -93,6 +95,16 @@
         lax.dot_general, dimension_numbers=(dims, ((), ())), preferred_element_type=jnp.float32
     )
     return dot(a_high, b_high) + (dot(a_high, b_low) + dot(a_low, b_high))
+
+
+def wide_product(high, low, both, axis):
+    dot = functools.partial(
+        lax.dot_general,
+        dimension_numbers=(((axis,), (0,)), ((), ())),
+        preferred_element_type=jnp.float32,
+    )
+    wide = dot(high, both[...])
+    return wide[:, :D] + (wide[:, D:] + dot(low, both[:, :D]))
 
 
 def eye():
@@ -131,7 +143,7 @@
         return v * (1.0 / jnp.sqrt(jnp.sum(v * v, axis=1, keepdims=True) + eps_norm))
 
     def fill(rows_in, cols_in, other):
-        for j, k, block in col_blocks(y, zh):
+        for j, k, block in col_blocks(y, zh, zl):
             block_at(hunit, block)[...] = unit(cols_in[j][k, other * B : (other + 1) * B, :])
         for j, k, core, block in row_blocks(x, zl):
             block_at(punit, block)[...] = unit(rows_in[j][k, core * B : (core + 1) * B, :])
@@ -203,7 +215,10 @@
 
 def grads_kernel(place, ids, wanted, sums, other_sums, expo_in, halves_in, *refs):
     keeps, sends = refs[:2], refs[2:4]
-    dh, dlow, pgrads, hgrads, expo, ph, plow, hh, hlow, sems = refs[4:]
+    dh, dlow, pgrads, hgrads, expo, pboth, hboth, sems = refs[4:]
+    high_half, low_half = pl.ds(0, D), pl.ds(D, D)
+    hh, hlow = hboth.at[:, high_half], hboth.at[:, low_half]
+    ph, plow = pboth.at[:, high_half], pboth.at[:, low_half]
     ph_in, plow_in, hh_in, hlow_in = kept(halves_in)
     steps = [pl.ds(i * STEP, STEP) for i in range(ROWS // STEP)]
     whole = [
@@ -238,12 +253,12 @@
         high, low = split(d)
         dh[here, :] = high
         dlow[here, :] = low
-        pgrads[here, :] = product(high, low, hh[...], hlow[...], ((1,), (0,)))
+        pgrads[here, :] = wide_product(high, low, hboth, 1)
     for copy in whole[2:]:
         copy.wait()
     for k in range(COLS // 128):
         here = pl.ds(k * 128, 128)
-        hgrads[here, :] = product(dh[:, here], dlow[:, here], ph[...], plow[...], ((0,), (0,)))
+        hgrads[here, :] = wide_product(dh[:, here], dlow[:, here], pboth, 0)
 
     def at(outs, j):
         line = (3, 1, 2, 0)[j]
@@ -256,7 +271,7 @@
             at(outs, j)[:, 2 * B :, :] = jnp.zeros((4, 8, D), jnp.float32) + term
 
     def headers(outs, term, other):
-        for j, k, block in col_blocks(y, zh):
+        for j, k, block in col_blocks(y, zh, zl):
             at(outs, j)[k, other * B : (other + 1) * B, :] = block_at(hgrads, block)[...]
             at(outs, j)[k, (1 - other) * B : (2 - other) * B, :] = jnp.zeros((B, D), jnp.float32)
         for j in range(4):
@@ -337,8 +352,8 @@
     far, ahead = (keeps[0] + swap_core(sends[0]))[:]
     behind, line = (keeps[1] + swap_core(sends[1]))[:]
     line = line + along_xy(ahead, -1) + along_xy(behind + along_xy(far, 1), 1)
-    zb = line[2] + along_z(line[3], 2, 1)
-    return line[0] + along_z(line[1], 2, -1) + along_z(zb, 1, 1)
+    za = line[1] + along_z(line[3], 1, -1)
+    return line[0] + along_z(za, 2, -1) + along_z(line[2], 1, 1)
 
 
 def per_device(packet, header, partner):
@@ -385,9 +400,11 @@
             pltpu.VMEM((ROWS, COLS), jnp.bfloat16),
             pltpu.VMEM((ROWS, D), jnp.float32),
             pltpu.VMEM((COLS, D), jnp.float32),
-        ]
-        + held
-        + [pltpu.SemaphoreType.DMA((4 + ROWS // STEP,))],
+            pltpu.VMEM((ROWS, COLS), jnp.float32),
+            pltpu.VMEM((ROWS, 2 * D), jnp.bfloat16),
+            pltpu.VMEM((COLS, 2 * D), jnp.bfloat16),
+            pltpu.SemaphoreType.DMA((4 + ROWS // STEP,)),
+        ],
         2 * flops,
     )
     pair = scatter(parts[:2], parts[2:])

time: 194 us -> 183 us (0.943)
  starting transfers between devices: 92.4 us -> 85.6 us
  waiting for transfers between devices: 48 us -> 44.2 us
    ppermute x22, starting transfers between devices: 92.4 us -> 85.6 us  [permute(): return lax.ppermute(value, ALL, pairs)]
    ppermute x22, waiting for transfers between devices: 48 us -> 44.2 us  [permute(): return lax.ppermute(value, ALL, pairs)]
where the time goes in v5:
time: 183 us; the launch traced here: 180 us
  starting transfers between devices  85.6 us (47%)
  waiting for transfers between devices  44.2 us (24%)
  blocking collectives  23.5 us (13%)
  Pallas kernels  22.7 us (12%)
  other arithmetic  2.16 us (1%)
    ppermute x22, starting transfers between devices, permute(): return lax.ppermute(value, ALL, pairs)  85.6 us
    ppermute x22, waiting for transfers between devices, permute(): return lax.ppermute(value, ALL, pairs)  44.2 us
    all_to_all x1, blocking collectives, per_device(): lax.all_to_all(jnp.broadcast_to((keep + swap_core(send))[None], (16, 1, S...  23.5 us
    pallas_call x3, Pallas kernels, call(): pl.pallas_call(kernel, in_specs=[IN_SMEM] + in_specs, out_specs=out_specs...  22.7 us
  transfers between devices with their start and end apart: 22, of which 16 were waited for; matrix products, arithmetic and copies ran while one was open for 1% of the time, Pallas kernels for 0%

profile of v5, /device:TPU:1, one launch (start us, length us, event | category | flops | bytes accessed | tf_op | source)
XLA Modules:
  0.0 180.3 jit_solution(15940420452806825459)
XLA Ops:
  1.6 8.8 %collective-permute-start = (f32[40,512]{1,0:T(8,128)S(1)}, f32[40,512]{1,0:T(8,128)S(1)}, u32[]{:S(2)}, u32[]{:S(2)}) collective-permute-start(f32[40,512]{1,0:T(8,128)S(1)} %get-tuple-element.32), channel_id=1, source_target_pairs={{16,0},{17,1},{18,2},{19,3},{20,4},{21,5},{22,6},{23,7},{24,8},{25... | collective-permute-start | bytes 245768 | tf_op jit(solution)/shard_map/ppermute | solution.py:36
  11.4 7.1 %collective-permute-start.1 = (f32[80,512]{1,0:T(8,128)S(1)}, f32[80,512]{1,0:T(8,128)S(1)}, u32[]{:S(2)}, u32[]{:S(2)}) collective-permute-start(f32[80,512]{1,0:T(8,128)S(1)} %get-tuple-element.30), channel_id=1, source_target_pairs={{2,0},{3,1},{0,2},{1,3},{6,4},{7,5},{4,6},{5,7},{10,8},{11,9},{8,1... | collective-permute-start | bytes 491528 | tf_op jit(solution)/shard_map/ppermute | solution.py:36
  18.5 2.1 %collective-permute-start.2 = (f32[80,512]{1,0:T(8,128)S(1)}, f32[80,512]{1,0:T(8,128)S(1)}, u32[]{:S(2)}, u32[]{:S(2)}) collective-permute-start(f32[80,512]{1,0:T(8,128)S(1)} %get-tuple-element.30), channel_id=1, source_target_pairs={{1,0},{0,1},{3,2},{2,3},{5,4},{4,5},{7,6},{6,7},{9,8},{8,9},{11,10... | collective-permute-start | bytes 491528 | tf_op jit(solution)/shard_map/ppermute | solution.py:36
  21.9 6.8 %collective-permute-start.3 = (f32[80,512]{1,0:T(8,128)S(1)}, f32[80,512]{1,0:T(8,128)S(1)}, u32[]{:S(2)}, u32[]{:S(2)}) collective-permute-start(f32[80,512]{1,0:T(8,128)S(1)} %collective-permute-done.1), channel_id=1, source_target_pairs={{1,0},{0,1},{3,2},{2,3},{5,4},{4,5},{7,6},{6,7},{9,8},{8,9},{11,10... | collective-permute-start | bytes 491528 | tf_op jit(solution)/shard_map/ppermute | solution.py:36
  29.3 3.0 %collective-permute-done.3 = f32[80,512]{1,0:T(8,128)S(1)} collective-permute-done((f32[80,512]{1,0:T(8,128)S(1)}, f32[80,512]{1,0:T(8,128)S(1)}, u32[]{:S(2)}, u32[]{:S(2)}) %collective-permute-start.3) | collective-permute-done | bytes 163872 | tf_op jit(solution)/shard_map/ppermute | solution.py:36
  32.3 8.5 %collective-permute-start.4 = (f32[4,80,512]{2,1,0:T(8,128)S(1)}, f32[4,80,512]{2,1,0:T(8,128)S(1)}, u32[]{:S(2)}, u32[]{:S(2)}) collective-permute-start(f32[4,80,512]{2,1,0:T(8,128)S(1)} %pad_maximum_fusion.refs_0_), channel_id=1, source_target_pairs={{128,0},{129,1},{130,2},{131,3},{132,4},{133,5},{134,6},{135,7},{1... | collective-permute-start | bytes 1966088 | tf_op jit(solution)/shard_map/ppermute | solution.py:36
  40.8 1.9 %collective-permute-start.5 = (f32[4,80,512]{2,1,0:T(8,128)S(1)}, f32[4,80,512]{2,1,0:T(8,128)S(1)}, u32[]{:S(2)}, u32[]{:S(2)}) collective-permute-start(f32[4,80,512]{2,1,0:T(8,128)S(1)} %pad_maximum_fusion.refs_0_), channel_id=1, source_target_pairs={{384,0},{385,1},{386,2},{387,3},{388,4},{389,5},{390,6},{391,7},{3... | collective-permute-start | bytes 1966088 | tf_op jit(solution)/shard_map/ppermute | solution.py:36
  42.8 5.6 %collective-permute-done.4.refs_1_ = f32[4,80,512]{2,1,0:T(8,128)S(1)} collective-permute-done((f32[4,80,512]{2,1,0:T(8,128)S(1)}, f32[4,80,512]{2,1,0:T(8,128)S(1)}, u32[]{:S(2)}, u32[]{:S(2)}) %collective-permute-start.4) | collective-permute-done | bytes 655392 | tf_op jit(solution)/shard_map/ppermute | solution.py:36
  48.3 5.0 %collective-permute-start.6 = (f32[4,80,512]{2,1,0:T(8,128)S(1)}, f32[4,80,512]{2,1,0:T(8,128)S(1)}, u32[]{:S(2)}, u32[]{:S(2)}) collective-permute-start(f32[4,80,512]{2,1,0:T(8,128)S(1)} %collective-permute-done.4.refs_1_), channel_id=1, source_target_pairs={{128,0},{129,1},{130,2},{131,3},{132,4},{133,5},{134,6},{135,7},{1... | collective-permute-start | bytes 1966088 | tf_op jit(solution)/shard_map/ppermute | solution.py:36
  53.4 1.9 %collective-permute-start.7 = (f32[4,80,512]{2,1,0:T(8,128)S(1)}, f32[4,80,512]{2,1,0:T(8,128)}, u32[]{:S(2)}, u32[]{:S(2)}) collective-permute-start(f32[4,80,512]{2,1,0:T(8,128)S(1)} %pad_maximum_fusion.refs_0_), channel_id=1, source_target_pairs={{16,0},{17,1},{18,2},{19,3},{20,4},{21,5},{22,6},{23,7},{24,8},{25... | collective-permute-start | bytes 1966088 | tf_op jit(solution)/shard_map/ppermute | solution.py:36
  55.3 2.4 %collective-permute-start.8 = (f32[4,80,512]{2,1,0:T(8,128)S(1)}, f32[4,80,512]{2,1,0:T(8,128)}, u32[]{:S(2)}, u32[]{:S(2)}) collective-permute-start(f32[4,80,512]{2,1,0:T(8,128)S(1)} %collective-permute-done.4.refs_1_), channel_id=1, source_target_pairs={{16,0},{17,1},{18,2},{19,3},{20,4},{21,5},{22,6},{23,7},{24,8},{25... | collective-permute-start | bytes 1966088 | tf_op jit(solution)/shard_map/ppermute | solution.py:36
  57.7 1.9 %collective-permute-start.9 = (f32[4,80,512]{2,1,0:T(8,128)S(1)}, f32[4,80,512]{2,1,0:T(8,128)}, u32[]{:S(2)}, u32[]{:S(2)}) collective-permute-start(f32[4,80,512]{2,1,0:T(8,128)S(1)} %collective-permute-done.5.refs_2_), channel_id=1, source_target_pairs={{16,0},{17,1},{18,2},{19,3},{20,4},{21,5},{22,6},{23,7},{24,8},{25... | collective-permute-start | bytes 1966088 | tf_op jit(solution)/shard_map/ppermute | solution.py:36
  60.9 1.9 %collective-permute-start.10 = (f32[4,80,512]{2,1,0:T(8,128)S(1)}, f32[4,80,512]{2,1,0:T(8,128)}, u32[]{:S(2)}, u32[]{:S(2)}) collective-permute-start(f32[4,80,512]{2,1,0:T(8,128)S(1)} %collective-permute-done.6.refs_3_), channel_id=1, source_target_pairs={{16,0},{17,1},{18,2},{19,3},{20,4},{21,5},{22,6},{23,7},{24,8},{25... | collective-permute-start | bytes 1966088 | tf_op jit(solution)/shard_map/ppermute | solution.py:36
  63.6 1.4 collective-permute-done.10.refs_7_
  65.0 10.0 %shard_map.67 = (f32[7680,640]{1,0:T(8,128)}, bf16[20480,512]{1,0:T(8,128)(2,1)}, f32[1,1408]{1,0:T(1,128)S(1)}, f32[1,1408]{1,0:T(1,128)S(1)}) custom-call(s32[5]{0:T(128)S(1)} %stack.38.place, s32[1,640]{1,0:T(1,128)S(1)} %add.51.ids, s32[1280,1]{1,0:T(8,128)S(1)} %reshape.19.wanted, f32[4,80,512]{2,1,0:T(8,128)S(1)} %pad_maximum_fusion.refs_0_, ...), custom_call_target="tpu_custom_call" | custom-call | flops 2516582400 | bytes 8388608 | tf_op jit(solution)/shard_map/pallas_call | solution.py:313
  75.0 2.0 %collective-permute-start.11 = (f32[1,1408]{1,0:T(1,128)S(1)}, f32[1,1408]{1,0:T(1,128)S(1)}, u32[]{:S(2)}, u32[]{:S(2)}) collective-permute-start(f32[1,1408]{1,0:T(1,128)S(1)} %get-tuple-element.15), channel_id=1, source_target_pairs={{16,0},{17,1},{18,2},{19,3},{20,4},{21,5},{22,6},{23,7},{24,8},{25... | collective-permute-start | bytes 16904 | tf_op jit(solution)/shard_map/ppermute | solution.py:36
  78.1 23.5 %all_to_all.5 = f32[16,1,1408]{2,1,0:T(1,128)S(1)} all-to-all(f32[16,1,1408]{2,1,0:T(1,128)S(1)} %broadcast_in_dim.10), channel_id=1, replica_groups={{0,1,2,3,128,129,130,131,256,257,258,259,384,385,386,387},{16,20,24,28,..., dimensions={0} | all-to-all | bytes 180224 | tf_op jit(solution)/shard_map/all_to_all | solution.py:387
  101.7 2.1 %collective-permute-start.12 = (f32[1,1408]{1,0:T(1,128)S(1)}, f32[1,1408]{1,0:T(1,128)S(1)}, u32[]{:S(2)}, u32[]{:S(2)}) collective-permute-start(f32[1,1408]{1,0:T(1,128)S(1)} %reduce_sum.12.sums), channel_id=1, source_target_pairs={{16,0},{17,1},{18,2},{19,3},{20,4},{21,5},{22,6},{23,7},{24,8},{25... | collective-permute-start | bytes 16904 | tf_op jit(solution)/shard_map/ppermute | solution.py:36
  104.7 11.3 %shard_map.68 = (f32[2,4,88,512]{3,2,1,0:T(8,128)S(1)}, f32[2,4,88,512]{3,2,1,0:T(8,128)S(1)}, f32[2,4,88,512]{3,2,1,0:T(8,128)S(1)}, f32[2,4,88,512]{3,2,1,0:T(8,128)}) custom-call(s32[5]{0:T(128)S(1)} %stack.38.place, s32[1,640]{1,0:T(1,128)S(1)} %add.51.ids, s32[1280,1]{1,0:T(8,128)S(1)} %reshape.19.wanted, f32[1,1408]{1,0:T(1,128)S(1)} %reduce_sum.12.sums, ...), custom_call_target="tpu_custom_call" | custom-call | flops 5033164800 | bytes 8388608 | tf_op jit(solution)/shard_map/pallas_call | solution.py:313
  116.0 2.1 %collective-permute-start.14 = (f32[2,4,88,512]{3,2,1,0:T(8,128)S(1)}, f32[2,4,88,512]{3,2,1,0:T(8,128)S(1)}, u32[]{:S(2)}, u32[]{:S(2)}) collective-permute-start(f32[2,4,88,512]{3,2,1,0:T(8,128)S(1)} %get-tuple-element.21), channel_id=1, source_target_pairs={{16,0},{17,1},{18,2},{19,3},{20,4},{21,5},{22,6},{23,7},{24,8},{25... | collective-permute-start | bytes 4325384 | tf_op jit(solution)/shard_map/ppermute | solution.py:36
  118.1 2.2 %collective-permute-start.13 = (f32[2,4,88,512]{3,2,1,0:T(8,128)}, f32[2,4,88,512]{3,2,1,0:T(8,128)S(1)}, u32[]{:S(2)}, u32[]{:S(2)}) collective-permute-start(f32[2,4,88,512]{3,2,1,0:T(8,128)} %get-tuple-element.19), channel_id=1, source_target_pairs={{16,0},{17,1},{18,2},{19,3},{20,4},{21,5},{22,6},{23,7},{24,8},{25... | collective-permute-start | bytes 4325384 | tf_op jit(solution)/shard_map/ppermute | solution.py:36
  121.6 2.6 %collective-permute-start.16 = (f32[4,88,512]{2,1,0:T(8,128)S(1)}, f32[4,88,512]{2,1,0:T(8,128)S(1)}, u32[]{:S(2)}, u32[]{:S(2)}) collective-permute-start(f32[4,88,512]{2,1,0:T(8,128)S(1)} %get-tuple-element.26), channel_id=1, source_target_pairs={{128,0},{129,1},{130,2},{131,3},{132,4},{133,5},{134,6},{135,7},{1... | collective-permute-start | bytes 2162696 | tf_op jit(solution)/shard_map/ppermute | solution.py:36
  124.2 2.7 %collective-permute-start.15 = (f32[4,88,512]{2,1,0:T(8,128)S(1)}, f32[4,88,512]{2,1,0:T(8,128)S(1)}, u32[]{:S(2)}, u32[]{:S(2)}) collective-permute-start(f32[4,88,512]{2,1,0:T(8,128)S(1)} %get-tuple-element.25), channel_id=1, source_target_pairs={{384,0},{385,1},{386,2},{387,3},{388,4},{389,5},{390,6},{391,7},{3... | collective-permute-start | bytes 2162696 | tf_op jit(solution)/shard_map/ppermute | solution.py:36
  127.2 6.7 %collective-permute-done.16 = f32[4,88,512]{2,1,0:T(8,128)S(1)} collective-permute-done((f32[4,88,512]{2,1,0:T(8,128)S(1)}, f32[4,88,512]{2,1,0:T(8,128)S(1)}, u32[]{:S(2)}, u32[]{:S(2)}) %collective-permute-start.16) | collective-permute-done | bytes 720928 | tf_op jit(solution)/shard_map/ppermute | solution.py:36
  134.0 3.8 %collective-permute-start.17 = (f32[4,88,512]{2,1,0:T(8,128)S(1)}, f32[4,88,512]{2,1,0:T(8,128)S(1)}, u32[]{:S(2)}, u32[]{:S(2)}) collective-permute-start(f32[4,88,512]{2,1,0:T(8,128)S(1)} %fusion), channel_id=1, source_target_pairs={{128,0},{129,1},{130,2},{131,3},{132,4},{133,5},{134,6},{135,7},{1... | collective-permute-start | bytes 2162696 | tf_op jit(solution)/shard_map/ppermute | solution.py:36
  137.9 8.5 %collective-permute-done.17 = f32[4,88,512]{2,1,0:T(8,128)S(1)} collective-permute-done((f32[4,88,512]{2,1,0:T(8,128)S(1)}, f32[4,88,512]{2,1,0:T(8,128)S(1)}, u32[]{:S(2)}, u32[]{:S(2)}) %collective-permute-start.17) | collective-permute-done | bytes 720928 | tf_op jit(solution)/shard_map/ppermute | solution.py:36
  146.7 2.2 %collective-permute-start.18 = (f32[88,512]{1,0:T(8,128)S(1)}, f32[88,512]{1,0:T(8,128)S(1)}, u32[]{:S(2)}, u32[]{:S(2)}) collective-permute-start(f32[88,512]{1,0:T(8,128)S(1)} %get-tuple-element.27), channel_id=1, source_target_pairs={{1,0},{0,1},{3,2},{2,3},{5,4},{4,5},{7,6},{6,7},{9,8},{8,9},{11,10... | collective-permute-start | bytes 540680 | tf_op jit(solution)/shard_map/ppermute | solution.py:36
  148.9 7.1 %collective-permute-start.20 = (f32[88,512]{1,0:T(8,128)S(1)}, f32[88,512]{1,0:T(8,128)S(1)}, u32[]{:S(2)}, u32[]{:S(2)}) collective-permute-start(f32[88,512]{1,0:T(8,128)S(1)} %get-tuple-element.28), channel_id=1, source_target_pairs={{1,0},{0,1},{3,2},{2,3},{5,4},{4,5},{7,6},{6,7},{9,8},{8,9},{11,10... | collective-permute-start | bytes 540680 | tf_op jit(solution)/shard_map/ppermute | solution.py:36
  157.0 2.1 %collective-permute-start.19 = (f32[88,512]{1,0:T(8,128)S(1)}, f32[88,512]{1,0:T(8,128)S(1)}, u32[]{:S(2)}, u32[]{:S(2)}) collective-permute-start(f32[88,512]{1,0:T(8,128)S(1)} %fusion.3), channel_id=1, source_target_pairs={{2,0},{3,1},{0,2},{1,3},{6,4},{7,5},{4,6},{5,7},{10,8},{11,9},{8,1... | collective-permute-start | bytes 540680 | tf_op jit(solution)/shard_map/ppermute | solution.py:36
  159.1 10.3 %collective-permute-done.19 = f32[88,512]{1,0:T(8,128)S(1)} collective-permute-done((f32[88,512]{1,0:T(8,128)S(1)}, f32[88,512]{1,0:T(8,128)S(1)}, u32[]{:S(2)}, u32[]{:S(2)}) %collective-permute-start.19) | collective-permute-done | bytes 180256 | tf_op jit(solution)/shard_map/ppermute | solution.py:36
  169.4 8.3 %collective-permute-start.21 = (f32[48,512]{1,0:T(8,128)S(1)}, f32[48,512]{1,0:T(8,128)S(1)}, u32[]{:S(2)}, u32[]{:S(2)}) collective-permute-start(f32[48,512]{1,0:T(8,128)S(1)} %slice.24), channel_id=1, source_target_pairs={{16,0},{17,1},{18,2},{19,3},{20,4},{21,5},{22,6},{23,7},{24,8},{25... | collective-permute-start | bytes 294920 | tf_op jit(solution)/shard_map/ppermute | solution.py:36
  178.7 1.4 shard_map.69
  (46 shorter events, 11.9 us)
Async XLA Ops:
  0.6 62.2 %copy-start.3 = (s32[640]{0:T(1024)S(1)}, s32[640]{0:T(1024)}, u32[]{:S(2)}) copy-start(s32[640]{0:T(1024)} %constant.33.clone) | copy-start | bytes 7684
  0.6 62.2 %copy-start.2 = (s32[20480]{0:T(1024)S(1)}, s32[20480]{0:T(1024)}, u32[]{:S(2)}) copy-start(s32[20480]{0:T(1024)} %param.6) | copy-start | bytes 245764
  1.6 9.7 %collective-permute-start = (f32[40,512]{1,0:T(8,128)S(1)}, f32[40,512]{1,0:T(8,128)S(1)}, u32[]{:S(2)}, u32[]{:S(2)}) collective-permute-start(f32[40,512]{1,0:T(8,128)S(1)} %get-tuple-element.32), channel_id=1, source_target_pairs={{16,0},{17,1},{18,2},{19,3},{20,4},{21,5},{22,6},{23,7},{24,8},{25... | collective-permute-start | bytes 245768 | tf_op jit(solution)/shard_map/ppermute | solution.py:36
  11.4 10.6 %collective-permute-start.1 = (f32[80,512]{1,0:T(8,128)S(1)}, f32[80,512]{1,0:T(8,128)S(1)}, u32[]{:S(2)}, u32[]{:S(2)}) collective-permute-start(f32[80,512]{1,0:T(8,128)S(1)} %get-tuple-element.30), channel_id=1, source_target_pairs={{2,0},{3,1},{0,2},{1,3},{6,4},{7,5},{4,6},{5,7},{10,8},{11,9},{8,1... | collective-permute-start | bytes 491528 | tf_op jit(solution)/shard_map/ppermute | solution.py:36
  18.5 10.8 %collective-permute-start.2 = (f32[80,512]{1,0:T(8,128)S(1)}, f32[80,512]{1,0:T(8,128)S(1)}, u32[]{:S(2)}, u32[]{:S(2)}) collective-permute-start(f32[80,512]{1,0:T(8,128)S(1)} %get-tuple-element.30), channel_id=1, source_target_pairs={{1,0},{0,1},{3,2},{2,3},{5,4},{4,5},{7,6},{6,7},{9,8},{8,9},{11,10... | collective-permute-start | bytes 491528 | tf_op jit(solution)/shard_map/ppermute | solution.py:36
  21.9 10.3 %collective-permute-start.3 = (f32[80,512]{1,0:T(8,128)S(1)}, f32[80,512]{1,0:T(8,128)S(1)}, u32[]{:S(2)}, u32[]{:S(2)}) collective-permute-start(f32[80,512]{1,0:T(8,128)S(1)} %collective-permute-done.1), channel_id=1, source_target_pairs={{1,0},{0,1},{3,2},{2,3},{5,4},{4,5},{7,6},{6,7},{9,8},{8,9},{11,10... | collective-permute-start | bytes 491528 | tf_op jit(solution)/shard_map/ppermute | solution.py:36
  32.3 16.0 %collective-permute-start.4 = (f32[4,80,512]{2,1,0:T(8,128)S(1)}, f32[4,80,512]{2,1,0:T(8,128)S(1)}, u32[]{:S(2)}, u32[]{:S(2)}) collective-permute-start(f32[4,80,512]{2,1,0:T(8,128)S(1)} %pad_maximum_fusion.refs_0_), channel_id=1, source_target_pairs={{128,0},{129,1},{130,2},{131,3},{132,4},{133,5},{134,6},{135,7},{1... | collective-permute-start | bytes 1966088 | tf_op jit(solution)/shard_map/ppermute | solution.py:36
  40.8 16.9 %collective-permute-start.5 = (f32[4,80,512]{2,1,0:T(8,128)S(1)}, f32[4,80,512]{2,1,0:T(8,128)S(1)}, u32[]{:S(2)}, u32[]{:S(2)}) collective-permute-start(f32[4,80,512]{2,1,0:T(8,128)S(1)} %pad_maximum_fusion.refs_0_), channel_id=1, source_target_pairs={{384,0},{385,1},{386,2},{387,3},{388,4},{389,5},{390,6},{391,7},{3... | collective-permute-start | bytes 1966088 | tf_op jit(solution)/shard_map/ppermute | solution.py:36
  48.3 12.5 %collective-permute-start.6 = (f32[4,80,512]{2,1,0:T(8,128)S(1)}, f32[4,80,512]{2,1,0:T(8,128)S(1)}, u32[]{:S(2)}, u32[]{:S(2)}) collective-permute-start(f32[4,80,512]{2,1,0:T(8,128)S(1)} %collective-permute-done.4.refs_1_), channel_id=1, source_target_pairs={{128,0},{129,1},{130,2},{131,3},{132,4},{133,5},{134,6},{135,7},{1... | collective-permute-start | bytes 1966088 | tf_op jit(solution)/shard_map/ppermute | solution.py:36
  53.4 10.2 %collective-permute-start.7 = (f32[4,80,512]{2,1,0:T(8,128)S(1)}, f32[4,80,512]{2,1,0:T(8,128)}, u32[]{:S(2)}, u32[]{:S(2)}) collective-permute-start(f32[4,80,512]{2,1,0:T(8,128)S(1)} %pad_maximum_fusion.refs_0_), channel_id=1, source_target_pairs={{16,0},{17,1},{18,2},{19,3},{20,4},{21,5},{22,6},{23,7},{24,8},{25... | collective-permute-start | bytes 1966088 | tf_op jit(solution)/shard_map/ppermute | solution.py:36
  55.3 8.3 %collective-permute-start.8 = (f32[4,80,512]{2,1,0:T(8,128)S(1)}, f32[4,80,512]{2,1,0:T(8,128)}, u32[]{:S(2)}, u32[]{:S(2)}) collective-permute-start(f32[4,80,512]{2,1,0:T(8,128)S(1)} %collective-permute-done.4.refs_1_), channel_id=1, source_target_pairs={{16,0},{17,1},{18,2},{19,3},{20,4},{21,5},{22,6},{23,7},{24,8},{25... | collective-permute-start | bytes 1966088 | tf_op jit(solution)/shard_map/ppermute | solution.py:36
  57.7 5.9 %collective-permute-start.9 = (f32[4,80,512]{2,1,0:T(8,128)S(1)}, f32[4,80,512]{2,1,0:T(8,128)}, u32[]{:S(2)}, u32[]{:S(2)}) collective-permute-start(f32[4,80,512]{2,1,0:T(8,128)S(1)} %collective-permute-done.5.refs_2_), channel_id=1, source_target_pairs={{16,0},{17,1},{18,2},{19,3},{20,4},{21,5},{22,6},{23,7},{24,8},{25... | collective-permute-start | bytes 1966088 | tf_op jit(solution)/shard_map/ppermute | solution.py:36
  60.9 4.1 %collective-permute-start.10 = (f32[4,80,512]{2,1,0:T(8,128)S(1)}, f32[4,80,512]{2,1,0:T(8,128)}, u32[]{:S(2)}, u32[]{:S(2)}) collective-permute-start(f32[4,80,512]{2,1,0:T(8,128)S(1)} %collective-permute-done.6.refs_3_), channel_id=1, source_target_pairs={{16,0},{17,1},{18,2},{19,3},{20,4},{21,5},{22,6},{23,7},{24,8},{25... | collective-permute-start | bytes 1966088 | tf_op jit(solution)/shard_map/ppermute | solution.py:36
  75.0 3.1 %collective-permute-start.11 = (f32[1,1408]{1,0:T(1,128)S(1)}, f32[1,1408]{1,0:T(1,128)S(1)}, u32[]{:S(2)}, u32[]{:S(2)}) collective-permute-start(f32[1,1408]{1,0:T(1,128)S(1)} %get-tuple-element.15), channel_id=1, source_target_pairs={{16,0},{17,1},{18,2},{19,3},{20,4},{21,5},{22,6},{23,7},{24,8},{25... | collective-permute-start | bytes 16904 | tf_op jit(solution)/shard_map/ppermute | solution.py:36
  101.7 3.1 %collective-permute-start.12 = (f32[1,1408]{1,0:T(1,128)S(1)}, f32[1,1408]{1,0:T(1,128)S(1)}, u32[]{:S(2)}, u32[]{:S(2)}) collective-permute-start(f32[1,1408]{1,0:T(1,128)S(1)} %reduce_sum.12.sums), channel_id=1, source_target_pairs={{16,0},{17,1},{18,2},{19,3},{20,4},{21,5},{22,6},{23,7},{24,8},{25... | collective-permute-start | bytes 16904 | tf_op jit(solution)/shard_map/ppermute | solution.py:36
  116.0 5.1 %collective-permute-start.14 = (f32[2,4,88,512]{3,2,1,0:T(8,128)S(1)}, f32[2,4,88,512]{3,2,1,0:T(8,128)S(1)}, u32[]{:S(2)}, u32[]{:S(2)}) collective-permute-start(f32[2,4,88,512]{3,2,1,0:T(8,128)S(1)} %get-tuple-element.21), channel_id=1, source_target_pairs={{16,0},{17,1},{18,2},{19,3},{20,4},{21,5},{22,6},{23,7},{24,8},{25... | collective-permute-start | bytes 4325384 | tf_op jit(solution)/shard_map/ppermute | solution.py:36
  118.1 8.8 %collective-permute-start.13 = (f32[2,4,88,512]{3,2,1,0:T(8,128)}, f32[2,4,88,512]{3,2,1,0:T(8,128)S(1)}, u32[]{:S(2)}, u32[]{:S(2)}) collective-permute-start(f32[2,4,88,512]{3,2,1,0:T(8,128)} %get-tuple-element.19), channel_id=1, source_target_pairs={{16,0},{17,1},{18,2},{19,3},{20,4},{21,5},{22,6},{23,7},{24,8},{25... | collective-permute-start | bytes 4325384 | tf_op jit(solution)/shard_map/ppermute | solution.py:36
  121.6 12.3 %collective-permute-start.16 = (f32[4,88,512]{2,1,0:T(8,128)S(1)}, f32[4,88,512]{2,1,0:T(8,128)S(1)}, u32[]{:S(2)}, u32[]{:S(2)}) collective-permute-start(f32[4,88,512]{2,1,0:T(8,128)S(1)} %get-tuple-element.26), channel_id=1, source_target_pairs={{128,0},{129,1},{130,2},{131,3},{132,4},{133,5},{134,6},{135,7},{1... | collective-permute-start | bytes 2162696 | tf_op jit(solution)/shard_map/ppermute | solution.py:36
  124.2 13.7 %collective-permute-start.15 = (f32[4,88,512]{2,1,0:T(8,128)S(1)}, f32[4,88,512]{2,1,0:T(8,128)S(1)}, u32[]{:S(2)}, u32[]{:S(2)}) collective-permute-start(f32[4,88,512]{2,1,0:T(8,128)S(1)} %get-tuple-element.25), channel_id=1, source_target_pairs={{384,0},{385,1},{386,2},{387,3},{388,4},{389,5},{390,6},{391,7},{3... | collective-permute-start | bytes 2162696 | tf_op jit(solution)/shard_map/ppermute | solution.py:36
  134.0 12.3 %collective-permute-start.17 = (f32[4,88,512]{2,1,0:T(8,128)S(1)}, f32[4,88,512]{2,1,0:T(8,128)S(1)}, u32[]{:S(2)}, u32[]{:S(2)}) collective-permute-start(f32[4,88,512]{2,1,0:T(8,128)S(1)} %fusion), channel_id=1, source_target_pairs={{128,0},{129,1},{130,2},{131,3},{132,4},{133,5},{134,6},{135,7},{1... | collective-permute-start | bytes 2162696 | tf_op jit(solution)/shard_map/ppermute | solution.py:36
  146.6 32.1 %copy-start = (f32[40,512]{1,0:T(8,128)S(1)}, f32[40,512]{1,0:T(8,128)}, u32[]{:S(2)}) copy-start(f32[40,512]{1,0:T(8,128)} %packet.1) | copy-start | bytes 245764
  146.6 32.1 %copy-start.1 = (f32[40,512]{1,0:T(8,128)S(1)}, f32[40,512]{1,0:T(8,128)}, u32[]{:S(2)}) copy-start(f32[40,512]{1,0:T(8,128)} %header.1) | copy-start | bytes 245764
  146.7 10.3 %collective-permute-start.18 = (f32[88,512]{1,0:T(8,128)S(1)}, f32[88,512]{1,0:T(8,128)S(1)}, u32[]{:S(2)}, u32[]{:S(2)}) collective-permute-start(f32[88,512]{1,0:T(8,128)S(1)} %get-tuple-element.27), channel_id=1, source_target_pairs={{1,0},{0,1},{3,2},{2,3},{5,4},{4,5},{7,6},{6,7},{9,8},{8,9},{11,10... | collective-permute-start | bytes 540680 | tf_op jit(solution)/shard_map/ppermute | solution.py:36
  148.9 10.2 %collective-permute-start.20 = (f32[88,512]{1,0:T(8,128)S(1)}, f32[88,512]{1,0:T(8,128)S(1)}, u32[]{:S(2)}, u32[]{:S(2)}) collective-permute-start(f32[88,512]{1,0:T(8,128)S(1)} %get-tuple-element.28), channel_id=1, source_target_pairs={{1,0},{0,1},{3,2},{2,3},{5,4},{4,5},{7,6},{6,7},{9,8},{8,9},{11,10... | collective-permute-start | bytes 540680 | tf_op jit(solution)/shard_map/ppermute | solution.py:36
  157.0 12.4 %collective-permute-start.19 = (f32[88,512]{1,0:T(8,128)S(1)}, f32[88,512]{1,0:T(8,128)S(1)}, u32[]{:S(2)}, u32[]{:S(2)}) collective-permute-start(f32[88,512]{1,0:T(8,128)S(1)} %fusion.3), channel_id=1, source_target_pairs={{2,0},{3,1},{0,2},{1,3},{6,4},{7,5},{4,6},{5,7},{10,8},{11,9},{8,1... | collective-permute-start | bytes 540680 | tf_op jit(solution)/shard_map/ppermute | solution.py:36
  169.4 9.3 %collective-permute-start.21 = (f32[48,512]{1,0:T(8,128)S(1)}, f32[48,512]{1,0:T(8,128)S(1)}, u32[]{:S(2)}, u32[]{:S(2)}) collective-permute-start(f32[48,512]{1,0:T(8,128)S(1)} %slice.24), channel_id=1, source_target_pairs={{16,0},{17,1},{18,2},{19,3},{20,4},{21,5},{22,6},{23,7},{24,8},{25... | collective-permute-start | bytes 294920 | tf_op jit(solution)/shard_map/ppermute | solution.py:36

commit v6 on v5

--- a/solution.py
+++ b/solution.py
@@ -1,4 +1,5 @@
 import functools
+import math
 
 import jax
 import jax.numpy as jnp
@@ -10,6 +11,7 @@
 
 inv_temp = 1.0 / 0.07
 eps_norm = 1e-06
+LOG2_SCALE = inv_temp * math.log2(math.e)
 NX, NY, NC, NZ = 4, 4, 2, 16
 NH, NL = 4, 4
 ALL = ("x", "y", "core", "zh", "zl")
@@ -157,6 +159,7 @@
         fill(others, mine, 0)
 
     hh[...], hlow[...] = split(hunit[...])
+    turned_high, turned_low = split(hunit[...].T)
     whole = [
         pltpu.make_async_copy(hh, hh_out, sems.at[3]),
         pltpu.make_async_copy(hlow, hlow_out, sems.at[4]),
@@ -178,8 +181,8 @@
         high, low = split(punit[here, :])
         ph[here, :] = high
         plow[here, :] = low
-        scores = product(high, low, hh[...], hlow[...], ((1,), (1,))) * inv_temp
-        e = jnp.exp(scores - inv_temp)
+        cosines = product(high, low, turned_high, turned_low, ((1,), (0,)))
+        e = jnp.exp2(cosines * LOG2_SCALE - LOG2_SCALE)
         expo[here, :] = e
         if i:
             for copy in copies(pl.ds((i - 1) * STEP, STEP)):
@@ -192,13 +195,15 @@
         total = total + jnp.sum(e.reshape(STEP // 8, 8, COLS), axis=0)
         match = wanted[here, :] == places
         positive = positive + jnp.sum(
-            jnp.where(match, scores, 0.0).reshape(STEP // 8, 8, COLS), axis=0
+            jnp.where(match, cosines, 0.0).reshape(STEP // 8, 8, COLS), axis=0
         )
 
     for copy in copies(pl.ds(ROWS - STEP, STEP)) + whole:
         copy.wait()
     positive = jnp.sum(positive, axis=0, keepdims=True)
-    row_sums[:, ROWS:] = sum(positive[:, k * 128 : (k + 1) * 128] for k in range(COLS // 128))
+    row_sums[:, ROWS:] = inv_temp * sum(
+        positive[:, k * 128 : (k + 1) * 128] for k in range(COLS // 128)
+    )
     total = jnp.sum(total, axis=0, keepdims=True)
     none, rest = jnp.zeros_like(total), jnp.zeros((1, SUMS - ROWS), jnp.float32)
 
@@ -351,7 +356,9 @@
 def scatter(keeps, sends):
     far, ahead = (keeps[0] + swap_core(sends[0]))[:]
     behind, line = (keeps[1] + swap_core(sends[1]))[:]
-    line = line + along_xy(ahead, -1) + along_xy(behind + along_xy(far, 1), 1)
+    behind = jnp.concatenate([behind[:2] + along_xy(far[:2], 1), behind[2:]])
+    ahead = jnp.concatenate([ahead[:2], ahead[2:] + along_xy(far[2:], -1)])
+    line = line + along_xy(ahead, -1) + along_xy(behind, 1)
     za = line[1] + along_z(line[3], 1, -1)
     return line[0] + along_z(za, 2, -1) + along_z(line[2], 1, 1)
 

time: 183 us -> 182 us (level)
  the two profiles are of different devices: /device:TPU:1 before, /device:TPU:39 now
where the time goes in v6:
time: 182 us; the launch traced here: 181 us
  starting transfers between devices  80.3 us (44%)
  waiting for transfers between devices  49.6 us (27%)
  blocking collectives  24.4 us (13%)
  Pallas kernels  22.5 us (12%)
  other arithmetic  2.23 us (1%)
    ppermute x23, starting transfers between devices, permute(): return lax.ppermute(value, ALL, pairs)  80.3 us
    ppermute x23, waiting for transfers between devices, permute(): return lax.ppermute(value, ALL, pairs)  49.6 us
    all_to_all x1, blocking collectives, per_device(): lax.all_to_all(jnp.broadcast_to((keep + swap_core(send))[None], (16, 1, S...  24.4 us
    pallas_call x3, Pallas kernels, call(): pl.pallas_call(kernel, in_specs=[IN_SMEM] + in_specs, out_specs=out_specs...  22.5 us
  transfers between devices with their start and end apart: 23, of which 15 were waited for; matrix products, arithmetic and copies ran while one was open for 1% of the time, Pallas kernels for 0%

profile of v6, /device:TPU:39, one launch (start us, length us, event | category | flops | bytes accessed | tf_op | source)
XLA Modules:
  0.0 181.3 jit_solution(6154170863765663614)
XLA Ops:
  1.6 2.6 %collective-permute-start = (f32[40,512]{1,0:T(8,128)S(1)}, f32[40,512]{1,0:T(8,128)S(1)}, u32[]{:S(2)}, u32[]{:S(2)}) collective-permute-start(f32[40,512]{1,0:T(8,128)S(1)} %get-tuple-element.33), channel_id=1, source_target_pairs={{16,0},{17,1},{18,2},{19,3},{20,4},{21,5},{22,6},{23,7},{24,8},{25... | collective-permute-start | bytes 245768 | tf_op jit(solution)/shard_map/ppermute | solution.py:38
  5.2 8.8 %collective-permute-start.1 = (f32[80,512]{1,0:T(8,128)S(1)}, f32[80,512]{1,0:T(8,128)S(1)}, u32[]{:S(2)}, u32[]{:S(2)}) collective-permute-start(f32[80,512]{1,0:T(8,128)S(1)} %get-tuple-element.31), channel_id=1, source_target_pairs={{2,0},{3,1},{0,2},{1,3},{6,4},{7,5},{4,6},{5,7},{10,8},{11,9},{8,1... | collective-permute-start | bytes 491528 | tf_op jit(solution)/shard_map/ppermute | solution.py:38
  14.0 4.7 %collective-permute-start.2 = (f32[80,512]{1,0:T(8,128)S(1)}, f32[80,512]{1,0:T(8,128)S(1)}, u32[]{:S(2)}, u32[]{:S(2)}) collective-permute-start(f32[80,512]{1,0:T(8,128)S(1)} %get-tuple-element.31), channel_id=1, source_target_pairs={{1,0},{0,1},{3,2},{2,3},{5,4},{4,5},{7,6},{6,7},{9,8},{8,9},{11,10... | collective-permute-start | bytes 491528 | tf_op jit(solution)/shard_map/ppermute | solution.py:38
  19.6 9.6 %collective-permute-start.3 = (f32[80,512]{1,0:T(8,128)S(1)}, f32[80,512]{1,0:T(8,128)S(1)}, u32[]{:S(2)}, u32[]{:S(2)}) collective-permute-start(f32[80,512]{1,0:T(8,128)S(1)} %collective-permute-done.1), channel_id=1, source_target_pairs={{1,0},{0,1},{3,2},{2,3},{5,4},{4,5},{7,6},{6,7},{9,8},{8,9},{11,10... | collective-permute-start | bytes 491528 | tf_op jit(solution)/shard_map/ppermute | solution.py:38
  29.2 8.0 %collective-permute-done.3 = f32[80,512]{1,0:T(8,128)S(1)} collective-permute-done((f32[80,512]{1,0:T(8,128)S(1)}, f32[80,512]{1,0:T(8,128)S(1)}, u32[]{:S(2)}, u32[]{:S(2)}) %collective-permute-start.3) | collective-permute-done | bytes 163872 | tf_op jit(solution)/shard_map/ppermute | solution.py:38
  37.3 4.6 %collective-permute-start.4 = (f32[4,80,512]{2,1,0:T(8,128)S(1)}, f32[4,80,512]{2,1,0:T(8,128)S(1)}, u32[]{:S(2)}, u32[]{:S(2)}) collective-permute-start(f32[4,80,512]{2,1,0:T(8,128)S(1)} %pad_maximum_fusion.2.refs_0_), channel_id=1, source_target_pairs={{128,0},{129,1},{130,2},{131,3},{132,4},{133,5},{134,6},{135,7},{1... | collective-permute-start | bytes 1966088 | tf_op jit(solution)/shard_map/ppermute | solution.py:38
  41.9 1.9 %collective-permute-start.5 = (f32[4,80,512]{2,1,0:T(8,128)S(1)}, f32[4,80,512]{2,1,0:T(8,128)S(1)}, u32[]{:S(2)}, u32[]{:S(2)}) collective-permute-start(f32[4,80,512]{2,1,0:T(8,128)S(1)} %pad_maximum_fusion.2.refs_0_), channel_id=1, source_target_pairs={{384,0},{385,1},{386,2},{387,3},{388,4},{389,5},{390,6},{391,7},{3... | collective-permute-start | bytes 1966088 | tf_op jit(solution)/shard_map/ppermute | solution.py:38
  43.9 5.6 %collective-permute-done.4.refs_1_ = f32[4,80,512]{2,1,0:T(8,128)S(1)} collective-permute-done((f32[4,80,512]{2,1,0:T(8,128)S(1)}, f32[4,80,512]{2,1,0:T(8,128)S(1)}, u32[]{:S(2)}, u32[]{:S(2)}) %collective-permute-start.4) | collective-permute-done | bytes 655392 | tf_op jit(solution)/shard_map/ppermute | solution.py:38
  49.5 5.3 %collective-permute-start.6 = (f32[4,80,512]{2,1,0:T(8,128)S(1)}, f32[4,80,512]{2,1,0:T(8,128)S(1)}, u32[]{:S(2)}, u32[]{:S(2)}) collective-permute-start(f32[4,80,512]{2,1,0:T(8,128)S(1)} %collective-permute-done.4.refs_1_), channel_id=1, source_target_pairs={{128,0},{129,1},{130,2},{131,3},{132,4},{133,5},{134,6},{135,7},{1... | collective-permute-start | bytes 1966088 | tf_op jit(solution)/shard_map/ppermute | solution.py:38
  54.8 1.9 %collective-permute-start.7 = (f32[4,80,512]{2,1,0:T(8,128)S(1)}, f32[4,80,512]{2,1,0:T(8,128)}, u32[]{:S(2)}, u32[]{:S(2)}) collective-permute-start(f32[4,80,512]{2,1,0:T(8,128)S(1)} %pad_maximum_fusion.2.refs_0_), channel_id=1, source_target_pairs={{16,0},{17,1},{18,2},{19,3},{20,4},{21,5},{22,6},{23,7},{24,8},{25... | collective-permute-start | bytes 1966088 | tf_op jit(solution)/shard_map/ppermute | solution.py:38
  56.7 2.4 %collective-permute-start.8 = (f32[4,80,512]{2,1,0:T(8,128)S(1)}, f32[4,80,512]{2,1,0:T(8,128)}, u32[]{:S(2)}, u32[]{:S(2)}) collective-permute-start(f32[4,80,512]{2,1,0:T(8,128)S(1)} %collective-permute-done.4.refs_1_), channel_id=1, source_target_pairs={{16,0},{17,1},{18,2},{19,3},{20,4},{21,5},{22,6},{23,7},{24,8},{25... | collective-permute-start | bytes 1966088 | tf_op jit(solution)/shard_map/ppermute | solution.py:38
  59.1 1.9 %collective-permute-start.9 = (f32[4,80,512]{2,1,0:T(8,128)S(1)}, f32[4,80,512]{2,1,0:T(8,128)}, u32[]{:S(2)}, u32[]{:S(2)}) collective-permute-start(f32[4,80,512]{2,1,0:T(8,128)S(1)} %collective-permute-done.5.refs_2_), channel_id=1, source_target_pairs={{16,0},{17,1},{18,2},{19,3},{20,4},{21,5},{22,6},{23,7},{24,8},{25... | collective-permute-start | bytes 1966088 | tf_op jit(solution)/shard_map/ppermute | solution.py:38
  62.3 1.9 %collective-permute-start.10 = (f32[4,80,512]{2,1,0:T(8,128)S(1)}, f32[4,80,512]{2,1,0:T(8,128)}, u32[]{:S(2)}, u32[]{:S(2)}) collective-permute-start(f32[4,80,512]{2,1,0:T(8,128)S(1)} %collective-permute-done.6.refs_3_), channel_id=1, source_target_pairs={{16,0},{17,1},{18,2},{19,3},{20,4},{21,5},{22,6},{23,7},{24,8},{25... | collective-permute-start | bytes 1966088 | tf_op jit(solution)/shard_map/ppermute | solution.py:38
  66.4 9.8 %shard_map.67 = (f32[7680,640]{1,0:T(8,128)}, bf16[20480,512]{1,0:T(8,128)(2,1)}, f32[1,1408]{1,0:T(1,128)S(1)}, f32[1,1408]{1,0:T(1,128)S(1)}) custom-call(s32[5]{0:T(128)S(1)} %stack.38.place, s32[1,640]{1,0:T(1,128)S(1)} %add.54.ids, s32[1280,1]{1,0:T(8,128)S(1)} %reshape.25.wanted, f32[4,80,512]{2,1,0:T(8,128)S(1)} %pad_maximum_fusion.2.refs_0_, ...), custom_call_target="tpu_custom_call" | custom-call | flops 2516582400 | bytes 8388608 | tf_op jit(solution)/shard_map/pallas_call | solution.py:318
  76.2 2.0 %collective-permute-start.11 = (f32[1,1408]{1,0:T(1,128)S(1)}, f32[1,1408]{1,0:T(1,128)S(1)}, u32[]{:S(2)}, u32[]{:S(2)}) collective-permute-start(f32[1,1408]{1,0:T(1,128)S(1)} %get-tuple-element.15), channel_id=1, source_target_pairs={{16,0},{17,1},{18,2},{19,3},{20,4},{21,5},{22,6},{23,7},{24,8},{25... | collective-permute-start | bytes 16904 | tf_op jit(solution)/shard_map/ppermute | solution.py:38
  79.4 24.4 %all_to_all.5 = f32[16,1,1408]{2,1,0:T(1,128)S(1)} all-to-all(f32[16,1,1408]{2,1,0:T(1,128)S(1)} %broadcast_in_dim.10), channel_id=1, replica_groups={{0,1,2,3,128,129,130,131,256,257,258,259,384,385,386,387},{16,20,24,28,..., dimensions={0} | all-to-all | bytes 180224 | tf_op jit(solution)/shard_map/all_to_all | solution.py:394
  103.8 2.1 %collective-permute-start.12 = (f32[1,1408]{1,0:T(1,128)S(1)}, f32[1,1408]{1,0:T(1,128)S(1)}, u32[]{:S(2)}, u32[]{:S(2)}) collective-permute-start(f32[1,1408]{1,0:T(1,128)S(1)} %reduce_sum.12.sums), channel_id=1, source_target_pairs={{16,0},{17,1},{18,2},{19,3},{20,4},{21,5},{22,6},{23,7},{24,8},{25... | collective-permute-start | bytes 16904 | tf_op jit(solution)/shard_map/ppermute | solution.py:38
  106.9 11.3 %shard_map.68 = (f32[2,4,88,512]{3,2,1,0:T(8,128)S(1)}, f32[2,4,88,512]{3,2,1,0:T(8,128)S(1)}, f32[2,4,88,512]{3,2,1,0:T(8,128)S(1)}, f32[2,4,88,512]{3,2,1,0:T(8,128)}) custom-call(s32[5]{0:T(128)S(1)} %stack.38.place, s32[1,640]{1,0:T(1,128)S(1)} %add.54.ids, s32[1280,1]{1,0:T(8,128)S(1)} %reshape.25.wanted, f32[1,1408]{1,0:T(1,128)S(1)} %reduce_sum.12.sums, ...), custom_call_target="tpu_custom_call" | custom-call | flops 5033164800 | bytes 8388608 | tf_op jit(solution)/shard_map/pallas_call | solution.py:318
  118.2 2.1 %collective-permute-start.14 = (f32[2,4,88,512]{3,2,1,0:T(8,128)S(1)}, f32[2,4,88,512]{3,2,1,0:T(8,128)S(1)}, u32[]{:S(2)}, u32[]{:S(2)}) collective-permute-start(f32[2,4,88,512]{3,2,1,0:T(8,128)S(1)} %get-tuple-element.21), channel_id=1, source_target_pairs={{16,0},{17,1},{18,2},{19,3},{20,4},{21,5},{22,6},{23,7},{24,8},{25... | collective-permute-start | bytes 4325384 | tf_op jit(solution)/shard_map/ppermute | solution.py:38
  120.3 2.2 %collective-permute-start.13 = (f32[2,4,88,512]{3,2,1,0:T(8,128)}, f32[2,4,88,512]{3,2,1,0:T(8,128)S(1)}, u32[]{:S(2)}, u32[]{:S(2)}) collective-permute-start(f32[2,4,88,512]{3,2,1,0:T(8,128)} %get-tuple-element.19), channel_id=1, source_target_pairs={{16,0},{17,1},{18,2},{19,3},{20,4},{21,5},{22,6},{23,7},{24,8},{25... | collective-permute-start | bytes 4325384 | tf_op jit(solution)/shard_map/ppermute | solution.py:38
  123.8 1.9 %collective-permute-start.15 = (f32[2,88,512]{2,1,0:T(8,128)S(1)}, f32[2,88,512]{2,1,0:T(8,128)S(1)}, u32[]{:S(2)}, u32[]{:S(2)}) collective-permute-start(f32[2,88,512]{2,1,0:T(8,128)S(1)} %get-tuple-element.27), channel_id=1, source_target_pairs={{384,0},{385,1},{386,2},{387,3},{388,4},{389,5},{390,6},{391,7},{3... | collective-permute-start | bytes 1081352 | tf_op jit(solution)/shard_map/ppermute | solution.py:38
  125.7 4.6 %collective-permute-start.17 = (f32[2,88,512]{2,1,0:T(8,128)S(1)}, f32[2,88,512]{2,1,0:T(8,128)S(1)}, u32[]{:S(2)}, u32[]{:S(2)}) collective-permute-start(f32[2,88,512]{2,1,0:T(8,128)S(1)} %get-tuple-element.26), channel_id=1, source_target_pairs={{128,0},{129,1},{130,2},{131,3},{132,4},{133,5},{134,6},{135,7},{1... | collective-permute-start | bytes 1081352 | tf_op jit(solution)/shard_map/ppermute | solution.py:38
  130.7 2.8 %collective-permute-done.15 = f32[2,88,512]{2,1,0:T(8,128)S(1)} collective-permute-done((f32[2,88,512]{2,1,0:T(8,128)S(1)}, f32[2,88,512]{2,1,0:T(8,128)S(1)}, u32[]{:S(2)}, u32[]{:S(2)}) %collective-permute-start.15) | collective-permute-done | bytes 360480 | tf_op jit(solution)/shard_map/ppermute | solution.py:38
  133.6 1.9 %collective-permute-start.16 = (f32[4,88,512]{2,1,0:T(8,128)S(1)}, f32[4,88,512]{2,1,0:T(8,128)S(1)}, u32[]{:S(2)}, u32[]{:S(2)}) collective-permute-start(f32[4,88,512]{2,1,0:T(8,128)S(1)} %pad_maximum_fusion), channel_id=1, source_target_pairs={{384,0},{385,1},{386,2},{387,3},{388,4},{389,5},{390,6},{391,7},{3... | collective-permute-start | bytes 2162696 | tf_op jit(solution)/shard_map/ppermute | solution.py:38
  135.6 4.6 %collective-permute-start.18 = (f32[4,88,512]{2,1,0:T(8,128)S(1)}, f32[4,88,512]{2,1,0:T(8,128)S(1)}, u32[]{:S(2)}, u32[]{:S(2)}) collective-permute-start(f32[4,88,512]{2,1,0:T(8,128)S(1)} %pad_maximum_fusion.1), channel_id=1, source_target_pairs={{128,0},{129,1},{130,2},{131,3},{132,4},{133,5},{134,6},{135,7},{1... | collective-permute-start | bytes 2162696 | tf_op jit(solution)/shard_map/ppermute | solution.py:38
  140.2 6.9 %collective-permute-done.16 = f32[4,88,512]{2,1,0:T(8,128)S(1)} collective-permute-done((f32[4,88,512]{2,1,0:T(8,128)S(1)}, f32[4,88,512]{2,1,0:T(8,128)S(1)}, u32[]{:S(2)}, u32[]{:S(2)}) %collective-permute-start.16) | collective-permute-done | bytes 720928 | tf_op jit(solution)/shard_map/ppermute | solution.py:38
  148.7 2.1 %collective-permute-start.19 = (f32[88,512]{1,0:T(8,128)S(1)}, f32[88,512]{1,0:T(8,128)S(1)}, u32[]{:S(2)}, u32[]{:S(2)}) collective-permute-start(f32[88,512]{1,0:T(8,128)S(1)} %get-tuple-element.28), channel_id=1, source_target_pairs={{1,0},{0,1},{3,2},{2,3},{5,4},{4,5},{7,6},{6,7},{9,8},{8,9},{11,10... | collective-permute-start | bytes 540680 | tf_op jit(solution)/shard_map/ppermute | solution.py:38
  150.8 7.3 %collective-permute-start.21 = (f32[88,512]{1,0:T(8,128)S(1)}, f32[88,512]{1,0:T(8,128)S(1)}, u32[]{:S(2)}, u32[]{:S(2)}) collective-permute-start(f32[88,512]{1,0:T(8,128)S(1)} %get-tuple-element.29), channel_id=1, source_target_pairs={{1,0},{0,1},{3,2},{2,3},{5,4},{4,5},{7,6},{6,7},{9,8},{8,9},{11,10... | collective-permute-start | bytes 540680 | tf_op jit(solution)/shard_map/ppermute | solution.py:38
  158.0 7.1 %collective-permute-done.19 = f32[88,512]{1,0:T(8,128)S(1)} collective-permute-done((f32[88,512]{1,0:T(8,128)S(1)}, f32[88,512]{1,0:T(8,128)S(1)}, u32[]{:S(2)}, u32[]{:S(2)}) %collective-permute-start.19) | collective-permute-done | bytes 180256 | tf_op jit(solution)/shard_map/ppermute | solution.py:38
  165.2 1.9 %collective-permute-start.20 = (f32[88,512]{1,0:T(8,128)S(1)}, f32[88,512]{1,0:T(8,128)S(1)}, u32[]{:S(2)}, u32[]{:S(2)}) collective-permute-start(f32[88,512]{1,0:T(8,128)S(1)} %fusion.4), channel_id=1, source_target_pairs={{2,0},{3,1},{0,2},{1,3},{6,4},{7,5},{4,6},{5,7},{10,8},{11,9},{8,1... | collective-permute-start | bytes 540680 | tf_op jit(solution)/shard_map/ppermute | solution.py:38
  167.1 9.4 %collective-permute-done.20 = f32[88,512]{1,0:T(8,128)S(1)} collective-permute-done((f32[88,512]{1,0:T(8,128)S(1)}, f32[88,512]{1,0:T(8,128)S(1)}, u32[]{:S(2)}, u32[]{:S(2)}) %collective-permute-start.20) | collective-permute-done | bytes 180256 | tf_op jit(solution)/shard_map/ppermute | solution.py:38
  176.6 1.9 %collective-permute-start.22 = (f32[48,512]{1,0:T(8,128)S(1)}, f32[48,512]{1,0:T(8,128)S(1)}, u32[]{:S(2)}, u32[]{:S(2)}) collective-permute-start(f32[48,512]{1,0:T(8,128)S(1)} %slice.84), channel_id=1, source_target_pairs={{16,0},{17,1},{18,2},{19,3},{20,4},{21,5},{22,6},{23,7},{24,8},{25... | collective-permute-start | bytes 294920 | tf_op jit(solution)/shard_map/ppermute | solution.py:38
  (52 shorter events, 14.4 us)
Async XLA Ops:
  0.6 63.6 %copy-start.3 = (s32[640]{0:T(1024)S(1)}, s32[640]{0:T(1024)}, u32[]{:S(2)}) copy-start(s32[640]{0:T(1024)} %constant.33.clone) | copy-start | bytes 7684
  0.6 63.6 %copy-start.2 = (s32[20480]{0:T(1024)S(1)}, s32[20480]{0:T(1024)}, u32[]{:S(2)}) copy-start(s32[20480]{0:T(1024)} %param.6) | copy-start | bytes 245764
  1.6 3.5 %collective-permute-start = (f32[40,512]{1,0:T(8,128)S(1)}, f32[40,512]{1,0:T(8,128)S(1)}, u32[]{:S(2)}, u32[]{:S(2)}) collective-permute-start(f32[40,512]{1,0:T(8,128)S(1)} %get-tuple-element.33), channel_id=1, source_target_pairs={{16,0},{17,1},{18,2},{19,3},{20,4},{21,5},{22,6},{23,7},{24,8},{25... | collective-permute-start | bytes 245768 | tf_op jit(solution)/shard_map/ppermute | solution.py:38
  5.2 14.5 %collective-permute-start.1 = (f32[80,512]{1,0:T(8,128)S(1)}, f32[80,512]{1,0:T(8,128)S(1)}, u32[]{:S(2)}, u32[]{:S(2)}) collective-permute-start(f32[80,512]{1,0:T(8,128)S(1)} %get-tuple-element.31), channel_id=1, source_target_pairs={{2,0},{3,1},{0,2},{1,3},{6,4},{7,5},{4,6},{5,7},{10,8},{11,9},{8,1... | collective-permute-start | bytes 491528 | tf_op jit(solution)/shard_map/ppermute | solution.py:38
  14.0 15.3 %collective-permute-start.2 = (f32[80,512]{1,0:T(8,128)S(1)}, f32[80,512]{1,0:T(8,128)S(1)}, u32[]{:S(2)}, u32[]{:S(2)}) collective-permute-start(f32[80,512]{1,0:T(8,128)S(1)} %get-tuple-element.31), channel_id=1, source_target_pairs={{1,0},{0,1},{3,2},{2,3},{5,4},{4,5},{7,6},{6,7},{9,8},{8,9},{11,10... | collective-permute-start | bytes 491528 | tf_op jit(solution)/shard_map/ppermute | solution.py:38
  19.6 17.6 %collective-permute-start.3 = (f32[80,512]{1,0:T(8,128)S(1)}, f32[80,512]{1,0:T(8,128)S(1)}, u32[]{:S(2)}, u32[]{:S(2)}) collective-permute-start(f32[80,512]{1,0:T(8,128)S(1)} %collective-permute-done.1), channel_id=1, source_target_pairs={{1,0},{0,1},{3,2},{2,3},{5,4},{4,5},{7,6},{6,7},{9,8},{8,9},{11,10... | collective-permute-start | bytes 491528 | tf_op jit(solution)/shard_map/ppermute | solution.py:38
  37.3 12.2 %collective-permute-start.4 = (f32[4,80,512]{2,1,0:T(8,128)S(1)}, f32[4,80,512]{2,1,0:T(8,128)S(1)}, u32[]{:S(2)}, u32[]{:S(2)}) collective-permute-start(f32[4,80,512]{2,1,0:T(8,128)S(1)} %pad_maximum_fusion.2.refs_0_), channel_id=1, source_target_pairs={{128,0},{129,1},{130,2},{131,3},{132,4},{133,5},{134,6},{135,7},{1... | collective-permute-start | bytes 1966088 | tf_op jit(solution)/shard_map/ppermute | solution.py:38
  41.9 17.2 %collective-permute-start.5 = (f32[4,80,512]{2,1,0:T(8,128)S(1)}, f32[4,80,512]{2,1,0:T(8,128)S(1)}, u32[]{:S(2)}, u32[]{:S(2)}) collective-permute-start(f32[4,80,512]{2,1,0:T(8,128)S(1)} %pad_maximum_fusion.2.refs_0_), channel_id=1, source_target_pairs={{384,0},{385,1},{386,2},{387,3},{388,4},{389,5},{390,6},{391,7},{3... | collective-permute-start | bytes 1966088 | tf_op jit(solution)/shard_map/ppermute | solution.py:38
  49.5 12.8 %collective-permute-start.6 = (f32[4,80,512]{2,1,0:T(8,128)S(1)}, f32[4,80,512]{2,1,0:T(8,128)S(1)}, u32[]{:S(2)}, u32[]{:S(2)}) collective-permute-start(f32[4,80,512]{2,1,0:T(8,128)S(1)} %collective-permute-done.4.refs_1_), channel_id=1, source_target_pairs={{128,0},{129,1},{130,2},{131,3},{132,4},{133,5},{134,6},{135,7},{1... | collective-permute-start | bytes 1966088 | tf_op jit(solution)/shard_map/ppermute | solution.py:38
  54.8 10.2 %collective-permute-start.7 = (f32[4,80,512]{2,1,0:T(8,128)S(1)}, f32[4,80,512]{2,1,0:T(8,128)}, u32[]{:S(2)}, u32[]{:S(2)}) collective-permute-start(f32[4,80,512]{2,1,0:T(8,128)S(1)} %pad_maximum_fusion.2.refs_0_), channel_id=1, source_target_pairs={{16,0},{17,1},{18,2},{19,3},{20,4},{21,5},{22,6},{23,7},{24,8},{25... | collective-permute-start | bytes 1966088 | tf_op jit(solution)/shard_map/ppermute | solution.py:38
  56.7 8.3 %collective-permute-start.8 = (f32[4,80,512]{2,1,0:T(8,128)S(1)}, f32[4,80,512]{2,1,0:T(8,128)}, u32[]{:S(2)}, u32[]{:S(2)}) collective-permute-start(f32[4,80,512]{2,1,0:T(8,128)S(1)} %collective-permute-done.4.refs_1_), channel_id=1, source_target_pairs={{16,0},{17,1},{18,2},{19,3},{20,4},{21,5},{22,6},{23,7},{24,8},{25... | collective-permute-start | bytes 1966088 | tf_op jit(solution)/shard_map/ppermute | solution.py:38
  59.1 5.9 %collective-permute-start.9 = (f32[4,80,512]{2,1,0:T(8,128)S(1)}, f32[4,80,512]{2,1,0:T(8,128)}, u32[]{:S(2)}, u32[]{:S(2)}) collective-permute-start(f32[4,80,512]{2,1,0:T(8,128)S(1)} %collective-permute-done.5.refs_2_), channel_id=1, source_target_pairs={{16,0},{17,1},{18,2},{19,3},{20,4},{21,5},{22,6},{23,7},{24,8},{25... | collective-permute-start | bytes 1966088 | tf_op jit(solution)/shard_map/ppermute | solution.py:38
  62.3 4.1 %collective-permute-start.10 = (f32[4,80,512]{2,1,0:T(8,128)S(1)}, f32[4,80,512]{2,1,0:T(8,128)}, u32[]{:S(2)}, u32[]{:S(2)}) collective-permute-start(f32[4,80,512]{2,1,0:T(8,128)S(1)} %collective-permute-done.6.refs_3_), channel_id=1, source_target_pairs={{16,0},{17,1},{18,2},{19,3},{20,4},{21,5},{22,6},{23,7},{24,8},{25... | collective-permute-start | bytes 1966088 | tf_op jit(solution)/shard_map/ppermute | solution.py:38
  76.2 3.1 %collective-permute-start.11 = (f32[1,1408]{1,0:T(1,128)S(1)}, f32[1,1408]{1,0:T(1,128)S(1)}, u32[]{:S(2)}, u32[]{:S(2)}) collective-permute-start(f32[1,1408]{1,0:T(1,128)S(1)} %get-tuple-element.15), channel_id=1, source_target_pairs={{16,0},{17,1},{18,2},{19,3},{20,4},{21,5},{22,6},{23,7},{24,8},{25... | collective-permute-start | bytes 16904 | tf_op jit(solution)/shard_map/ppermute | solution.py:38
  103.8 3.1 %collective-permute-start.12 = (f32[1,1408]{1,0:T(1,128)S(1)}, f32[1,1408]{1,0:T(1,128)S(1)}, u32[]{:S(2)}, u32[]{:S(2)}) collective-permute-start(f32[1,1408]{1,0:T(1,128)S(1)} %reduce_sum.12.sums), channel_id=1, source_target_pairs={{16,0},{17,1},{18,2},{19,3},{20,4},{21,5},{22,6},{23,7},{24,8},{25... | collective-permute-start | bytes 16904 | tf_op jit(solution)/shard_map/ppermute | solution.py:38
  118.2 5.1 %collective-permute-start.14 = (f32[2,4,88,512]{3,2,1,0:T(8,128)S(1)}, f32[2,4,88,512]{3,2,1,0:T(8,128)S(1)}, u32[]{:S(2)}, u32[]{:S(2)}) collective-permute-start(f32[2,4,88,512]{3,2,1,0:T(8,128)S(1)} %get-tuple-element.21), channel_id=1, source_target_pairs={{16,0},{17,1},{18,2},{19,3},{20,4},{21,5},{22,6},{23,7},{24,8},{25... | collective-permute-start | bytes 4325384 | tf_op jit(solution)/shard_map/ppermute | solution.py:38
  120.3 10.0 %collective-permute-start.13 = (f32[2,4,88,512]{3,2,1,0:T(8,128)}, f32[2,4,88,512]{3,2,1,0:T(8,128)S(1)}, u32[]{:S(2)}, u32[]{:S(2)}) collective-permute-start(f32[2,4,88,512]{3,2,1,0:T(8,128)} %get-tuple-element.19), channel_id=1, source_target_pairs={{16,0},{17,1},{18,2},{19,3},{20,4},{21,5},{22,6},{23,7},{24,8},{25... | collective-permute-start | bytes 4325384 | tf_op jit(solution)/shard_map/ppermute | solution.py:38
  123.8 9.7 %collective-permute-start.15 = (f32[2,88,512]{2,1,0:T(8,128)S(1)}, f32[2,88,512]{2,1,0:T(8,128)S(1)}, u32[]{:S(2)}, u32[]{:S(2)}) collective-permute-start(f32[2,88,512]{2,1,0:T(8,128)S(1)} %get-tuple-element.27), channel_id=1, source_target_pairs={{384,0},{385,1},{386,2},{387,3},{388,4},{389,5},{390,6},{391,7},{3... | collective-permute-start | bytes 1081352 | tf_op jit(solution)/shard_map/ppermute | solution.py:38
  125.7 9.8 %collective-permute-start.17 = (f32[2,88,512]{2,1,0:T(8,128)S(1)}, f32[2,88,512]{2,1,0:T(8,128)S(1)}, u32[]{:S(2)}, u32[]{:S(2)}) collective-permute-start(f32[2,88,512]{2,1,0:T(8,128)S(1)} %get-tuple-element.26), channel_id=1, source_target_pairs={{128,0},{129,1},{130,2},{131,3},{132,4},{133,5},{134,6},{135,7},{1... | collective-permute-start | bytes 1081352 | tf_op jit(solution)/shard_map/ppermute | solution.py:38
  133.6 13.5 %collective-permute-start.16 = (f32[4,88,512]{2,1,0:T(8,128)S(1)}, f32[4,88,512]{2,1,0:T(8,128)S(1)}, u32[]{:S(2)}, u32[]{:S(2)}) collective-permute-start(f32[4,88,512]{2,1,0:T(8,128)S(1)} %pad_maximum_fusion), channel_id=1, source_target_pairs={{384,0},{385,1},{386,2},{387,3},{388,4},{389,5},{390,6},{391,7},{3... | collective-permute-start | bytes 2162696 | tf_op jit(solution)/shard_map/ppermute | solution.py:38
  135.6 12.8 %collective-permute-start.18 = (f32[4,88,512]{2,1,0:T(8,128)S(1)}, f32[4,88,512]{2,1,0:T(8,128)S(1)}, u32[]{:S(2)}, u32[]{:S(2)}) collective-permute-start(f32[4,88,512]{2,1,0:T(8,128)S(1)} %pad_maximum_fusion.1), channel_id=1, source_target_pairs={{128,0},{129,1},{130,2},{131,3},{132,4},{133,5},{134,6},{135,7},{1... | collective-permute-start | bytes 2162696 | tf_op jit(solution)/shard_map/ppermute | solution.py:38
  148.6 31.1 %copy-start = (f32[40,512]{1,0:T(8,128)S(1)}, f32[40,512]{1,0:T(8,128)}, u32[]{:S(2)}) copy-start(f32[40,512]{1,0:T(8,128)} %packet.1) | copy-start | bytes 245764
  148.7 31.1 %copy-start.1 = (f32[40,512]{1,0:T(8,128)S(1)}, f32[40,512]{1,0:T(8,128)}, u32[]{:S(2)}) copy-start(f32[40,512]{1,0:T(8,128)} %header.1) | copy-start | bytes 245764
  148.7 16.5 %collective-permute-start.19 = (f32[88,512]{1,0:T(8,128)S(1)}, f32[88,512]{1,0:T(8,128)S(1)}, u32[]{:S(2)}, u32[]{:S(2)}) collective-permute-start(f32[88,512]{1,0:T(8,128)S(1)} %get-tuple-element.28), channel_id=1, source_target_pairs={{1,0},{0,1},{3,2},{2,3},{5,4},{4,5},{7,6},{6,7},{9,8},{8,9},{11,10... | collective-permute-start | bytes 540680 | tf_op jit(solution)/shard_map/ppermute | solution.py:38
  150.8 16.4 %collective-permute-start.21 = (f32[88,512]{1,0:T(8,128)S(1)}, f32[88,512]{1,0:T(8,128)S(1)}, u32[]{:S(2)}, u32[]{:S(2)}) collective-permute-start(f32[88,512]{1,0:T(8,128)S(1)} %get-tuple-element.29), channel_id=1, source_target_pairs={{1,0},{0,1},{3,2},{2,3},{5,4},{4,5},{7,6},{6,7},{9,8},{8,9},{11,10... | collective-permute-start | bytes 540680 | tf_op jit(solution)/shard_map/ppermute | solution.py:38
  165.2 11.3 %collective-permute-start.20 = (f32[88,512]{1,0:T(8,128)S(1)}, f32[88,512]{1,0:T(8,128)S(1)}, u32[]{:S(2)}, u32[]{:S(2)}) collective-permute-start(f32[88,512]{1,0:T(8,128)S(1)} %fusion.4), channel_id=1, source_target_pairs={{2,0},{3,1},{0,2},{1,3},{6,4},{7,5},{4,6},{5,7},{10,8},{11,9},{8,1... | collective-permute-start | bytes 540680 | tf_op jit(solution)/shard_map/ppermute | solution.py:38
  176.6 3.2 %collective-permute-start.22 = (f32[48,512]{1,0:T(8,128)S(1)}, f32[48,512]{1,0:T(8,128)S(1)}, u32[]{:S(2)}, u32[]{:S(2)}) collective-permute-start(f32[48,512]{1,0:T(8,128)S(1)} %slice.84), channel_id=1, source_target_pairs={{16,0},{17,1},{18,2},{19,3},{20,4},{21,5},{22,6},{23,7},{24,8},{25... | collective-permute-start | bytes 294920 | tf_op jit(solution)/shard_map/ppermute | solution.py:38

commit v7 on v6

--- a/solution.py
+++ b/solution.py
@@ -135,20 +135,24 @@
 
 
 def scores_kernel(place, ids, wanted, *refs):
-    mine, others = refs[:4], refs[4:8]
-    expo_out, halves_out, keep, send = refs[8:12]
-    punit, hunit, row_sums, expo, ph, plow, hh, hlow, sems = refs[12:]
+    mine, others = refs[:5], refs[5:10]
+    expo_out, halves_out, keep, send = refs[10:14]
+    punit, hunit, row_sums, expo, ph, plow, hh, hlow, sems = refs[14:]
     ph_out, plow_out, hh_out, hlow_out = kept(halves_out)
     x, y, c, zh, zl = (place[k] for k in range(5))
 
     def unit(v):
         return v * (1.0 / jnp.sqrt(jnp.sum(v * v, axis=1, keepdims=True) + eps_norm))
 
+    def block_of(lines, j, k, half):
+        pair = lines[j].at[k] if j < 3 else lines[3 + k // 2].at[k % 2]
+        return pair[half * B : (half + 1) * B, :]
+
     def fill(rows_in, cols_in, other):
         for j, k, block in col_blocks(y, zh, zl):
-            block_at(hunit, block)[...] = unit(cols_in[j][k, other * B : (other + 1) * B, :])
+            block_at(hunit, block)[...] = unit(block_of(cols_in, j, k, other))
         for j, k, core, block in row_blocks(x, zl):
-            block_at(punit, block)[...] = unit(rows_in[j][k, core * B : (core + 1) * B, :])
+            block_at(punit, block)[...] = unit(block_of(rows_in, j, k, core))
 
     @pl.when(c == 0)
     def _():
@@ -349,7 +353,7 @@
     zb = along_z(pair, 1, -1)
     line = jnp.stack([pair, za, zb, along_z(za, 1, 1)])
     ahead, behind = along_xy(line, 1), along_xy(line, -1)
-    lines = [line, ahead, behind, along_xy(ahead, 1)]
+    lines = [line, ahead, behind, along_xy(ahead[:2], 1), along_xy(behind[2:], -1)]
     return lines, [swap_core(line) for line in lines]
 
 
@@ -383,7 +387,7 @@
     expo, halves, keep, send = call(
         scores_kernel,
         [place, ids, wanted] + lines + other_lines,
-        [IN_VMEM] * 10,
+        [IN_VMEM] * 12,
         [f32(KEPT_F32, COLS), b16(KEPT_B16, D), f32(1, SUMS), f32(1, SUMS)],
         [IN_PLACE] * 2 + [IN_VMEM] * 2,
         [pltpu.VMEM((ROWS, D), jnp.float32), pltpu.VMEM((COLS, D), jnp.float32), pltpu.VMEM((1, SUMS), jnp.float32)]

time: 182 us -> 183 us (level)
  the two profiles are of different devices: /device:TPU:39 before, /device:TPU:1 now
where the time goes in v7:
time: 183 us; the launch traced here: 182 us
  starting transfers between devices  91 us (50%)
  waiting for transfers between devices  41.3 us (23%)
  Pallas kernels  22.6 us (12%)
  blocking collectives  22.4 us (12%)
  other arithmetic  2.2 us (1%)
    ppermute x25, starting transfers between devices, permute(): return lax.ppermute(value, ALL, pairs)  91 us
    ppermute x25, waiting for transfers between devices, permute(): return lax.ppermute(value, ALL, pairs)  41.3 us
    pallas_call x3, Pallas kernels, call(): pl.pallas_call(kernel, in_specs=[IN_SMEM] + in_specs, out_specs=out_specs...  22.6 us
    all_to_all x1, blocking collectives, per_device(): lax.all_to_all(jnp.broadcast_to((keep + swap_core(send))[None], (16, 1, S...  22.4 us
  transfers between devices with their start and end apart: 25, of which 16 were waited for; matrix products, arithmetic and copies ran while one was open for 1% of the time, Pallas kernels for 0%

profile of v7, /device:TPU:1, one launch (start us, length us, event | category | flops | bytes accessed | tf_op | source)
XLA Modules:
  0.0 181.8 jit_solution(4866829801239258863)
XLA Ops:
  1.6 8.8 %collective-permute-start = (f32[40,512]{1,0:T(8,128)S(1)}, f32[40,512]{1,0:T(8,128)S(1)}, u32[]{:S(2)}, u32[]{:S(2)}) collective-permute-start(f32[40,512]{1,0:T(8,128)S(1)} %get-tuple-element.33), channel_id=1, source_target_pairs={{16,0},{17,1},{18,2},{19,3},{20,4},{21,5},{22,6},{23,7},{24,8},{25... | collective-permute-start | bytes 245768 | tf_op jit(solution)/shard_map/ppermute | solution.py:38
  11.3 7.2 %collective-permute-start.1 = (f32[80,512]{1,0:T(8,128)S(1)}, f32[80,512]{1,0:T(8,128)S(1)}, u32[]{:S(2)}, u32[]{:S(2)}) collective-permute-start(f32[80,512]{1,0:T(8,128)S(1)} %get-tuple-element.31), channel_id=1, source_target_pairs={{2,0},{3,1},{0,2},{1,3},{6,4},{7,5},{4,6},{5,7},{10,8},{11,9},{8,1... | collective-permute-start | bytes 491528 | tf_op jit(solution)/shard_map/ppermute | solution.py:38
  18.6 2.1 %collective-permute-start.2 = (f32[80,512]{1,0:T(8,128)S(1)}, f32[80,512]{1,0:T(8,128)S(1)}, u32[]{:S(2)}, u32[]{:S(2)}) collective-permute-start(f32[80,512]{1,0:T(8,128)S(1)} %get-tuple-element.31), channel_id=1, source_target_pairs={{1,0},{0,1},{3,2},{2,3},{5,4},{4,5},{7,6},{6,7},{9,8},{8,9},{11,10... | collective-permute-start | bytes 491528 | tf_op jit(solution)/shard_map/ppermute | solution.py:38
  22.0 6.8 %collective-permute-start.3 = (f32[80,512]{1,0:T(8,128)S(1)}, f32[80,512]{1,0:T(8,128)S(1)}, u32[]{:S(2)}, u32[]{:S(2)}) collective-permute-start(f32[80,512]{1,0:T(8,128)S(1)} %collective-permute-done.1), channel_id=1, source_target_pairs={{1,0},{0,1},{3,2},{2,3},{5,4},{4,5},{7,6},{6,7},{9,8},{8,9},{11,10... | collective-permute-start | bytes 491528 | tf_op jit(solution)/shard_map/ppermute | solution.py:38
  29.4 3.0 %collective-permute-done.3 = f32[80,512]{1,0:T(8,128)S(1)} collective-permute-done((f32[80,512]{1,0:T(8,128)S(1)}, f32[80,512]{1,0:T(8,128)S(1)}, u32[]{:S(2)}, u32[]{:S(2)}) %collective-permute-start.3) | collective-permute-done | bytes 163872 | tf_op jit(solution)/shard_map/ppermute | solution.py:38
  32.4 7.1 %collective-permute-start.5 = (f32[4,80,512]{2,1,0:T(8,128)S(1)}, f32[4,80,512]{2,1,0:T(8,128)S(1)}, u32[]{:S(2)}, u32[]{:S(2)}) collective-permute-start(f32[4,80,512]{2,1,0:T(8,128)S(1)} %pad_maximum_fusion.2.refs_0_), channel_id=1, source_target_pairs={{384,0},{385,1},{386,2},{387,3},{388,4},{389,5},{390,6},{391,7},{3... | collective-permute-start | bytes 1966088 | tf_op jit(solution)/shard_map/ppermute | solution.py:38
  39.5 3.4 %collective-permute-start.4 = (f32[4,80,512]{2,1,0:T(8,128)S(1)}, f32[4,80,512]{2,1,0:T(8,128)S(1)}, u32[]{:S(2)}, u32[]{:S(2)}) collective-permute-start(f32[4,80,512]{2,1,0:T(8,128)S(1)} %pad_maximum_fusion.2.refs_0_), channel_id=1, source_target_pairs={{128,0},{129,1},{130,2},{131,3},{132,4},{133,5},{134,6},{135,7},{1... | collective-permute-start | bytes 1966088 | tf_op jit(solution)/shard_map/ppermute | solution.py:38
  42.9 6.0 %collective-permute-done.5.refs_2_ = f32[4,80,512]{2,1,0:T(8,128)S(1)} collective-permute-done((f32[4,80,512]{2,1,0:T(8,128)S(1)}, f32[4,80,512]{2,1,0:T(8,128)S(1)}, u32[]{:S(2)}, u32[]{:S(2)}) %collective-permute-start.5) | collective-permute-done | bytes 655392 | tf_op jit(solution)/shard_map/ppermute | solution.py:38
  48.9 1.9 %collective-permute-start.7 = (f32[2,80,512]{2,1,0:T(8,128)S(1)}, f32[2,80,512]{2,1,0:T(8,128)}, u32[]{:S(2)}, u32[]{:S(2)}) collective-permute-start(f32[2,80,512]{2,1,0:T(8,128)S(1)} %slice.83), channel_id=1, source_target_pairs={{384,0},{385,1},{386,2},{387,3},{388,4},{389,5},{390,6},{391,7},{3... | collective-permute-start | bytes 983048 | tf_op jit(solution)/shard_map/ppermute | solution.py:38
  51.2 4.6 %collective-permute-start.6 = (f32[2,80,512]{2,1,0:T(8,128)S(1)}, f32[2,80,512]{2,1,0:T(8,128)}, u32[]{:S(2)}, u32[]{:S(2)}) collective-permute-start(f32[2,80,512]{2,1,0:T(8,128)S(1)} %slice.82), channel_id=1, source_target_pairs={{128,0},{129,1},{130,2},{131,3},{132,4},{133,5},{134,6},{135,7},{1... | collective-permute-start | bytes 983048 | tf_op jit(solution)/shard_map/ppermute | solution.py:38
  55.8 1.9 %collective-permute-start.8 = (f32[4,80,512]{2,1,0:T(8,128)S(1)}, f32[4,80,512]{2,1,0:T(8,128)S(1)}, u32[]{:S(2)}, u32[]{:S(2)}) collective-permute-start(f32[4,80,512]{2,1,0:T(8,128)S(1)} %pad_maximum_fusion.2.refs_0_), channel_id=1, source_target_pairs={{16,0},{17,1},{18,2},{19,3},{20,4},{21,5},{22,6},{23,7},{24,8},{25... | collective-permute-start | bytes 1966088 | tf_op jit(solution)/shard_map/ppermute | solution.py:38
  57.8 2.4 %collective-permute-start.10 = (f32[4,80,512]{2,1,0:T(8,128)S(1)}, f32[4,80,512]{2,1,0:T(8,128)}, u32[]{:S(2)}, u32[]{:S(2)}) collective-permute-start(f32[4,80,512]{2,1,0:T(8,128)S(1)} %collective-permute-done.5.refs_2_), channel_id=1, source_target_pairs={{16,0},{17,1},{18,2},{19,3},{20,4},{21,5},{22,6},{23,7},{24,8},{25... | collective-permute-start | bytes 1966088 | tf_op jit(solution)/shard_map/ppermute | solution.py:38
  60.2 1.9 %collective-permute-start.9 = (f32[4,80,512]{2,1,0:T(8,128)S(1)}, f32[4,80,512]{2,1,0:T(8,128)}, u32[]{:S(2)}, u32[]{:S(2)}) collective-permute-start(f32[4,80,512]{2,1,0:T(8,128)S(1)} %collective-permute-done.4.refs_1_), channel_id=1, source_target_pairs={{16,0},{17,1},{18,2},{19,3},{20,4},{21,5},{22,6},{23,7},{24,8},{25... | collective-permute-start | bytes 1966088 | tf_op jit(solution)/shard_map/ppermute | solution.py:38
  62.1 2.4 %collective-permute-start.12 = (f32[2,80,512]{2,1,0:T(8,128)}, f32[2,80,512]{2,1,0:T(8,128)}, u32[]{:S(2)}, u32[]{:S(2)}) collective-permute-start(f32[2,80,512]{2,1,0:T(8,128)} %collective-permute-done.7.refs_4_), channel_id=1, source_target_pairs={{16,0},{17,1},{18,2},{19,3},{20,4},{21,5},{22,6},{23,7},{24,8},{25... | collective-permute-start | bytes 983048 | tf_op jit(solution)/shard_map/ppermute | solution.py:38
  64.6 1.9 %collective-permute-start.11 = (f32[2,80,512]{2,1,0:T(8,128)}, f32[2,80,512]{2,1,0:T(8,128)}, u32[]{:S(2)}, u32[]{:S(2)}) collective-permute-start(f32[2,80,512]{2,1,0:T(8,128)} %collective-permute-done.6.refs_3_), channel_id=1, source_target_pairs={{16,0},{17,1},{18,2},{19,3},{20,4},{21,5},{22,6},{23,7},{24,8},{25... | collective-permute-start | bytes 983048 | tf_op jit(solution)/shard_map/ppermute | solution.py:38
  68.4 9.9 %shard_map.67 = (f32[7680,640]{1,0:T(8,128)}, bf16[20480,512]{1,0:T(8,128)(2,1)}, f32[1,1408]{1,0:T(1,128)S(1)}, f32[1,1408]{1,0:T(1,128)S(1)}) custom-call(s32[5]{0:T(128)S(1)} %stack.38.place, s32[1,640]{1,0:T(1,128)S(1)} %add.54.ids, s32[1280,1]{1,0:T(8,128)S(1)} %reshape.25.wanted, f32[4,80,512]{2,1,0:T(8,128)S(1)} %pad_maximum_fusion.2.refs_0_, ...), custom_call_target="tpu_custom_call" | custom-call | flops 2516582400 | bytes 8388608 | tf_op jit(solution)/shard_map/pallas_call | solution.py:322
  78.3 2.0 %collective-permute-start.13 = (f32[1,1408]{1,0:T(1,128)S(1)}, f32[1,1408]{1,0:T(1,128)S(1)}, u32[]{:S(2)}, u32[]{:S(2)}) collective-permute-start(f32[1,1408]{1,0:T(1,128)S(1)} %get-tuple-element.15), channel_id=1, source_target_pairs={{16,0},{17,1},{18,2},{19,3},{20,4},{21,5},{22,6},{23,7},{24,8},{25... | collective-permute-start | bytes 16904 | tf_op jit(solution)/shard_map/ppermute | solution.py:38
  81.4 22.4 %all_to_all.5 = f32[16,1,1408]{2,1,0:T(1,128)S(1)} all-to-all(f32[16,1,1408]{2,1,0:T(1,128)S(1)} %broadcast_in_dim.10), channel_id=1, replica_groups={{0,1,2,3,128,129,130,131,256,257,258,259,384,385,386,387},{16,20,24,28,..., dimensions={0} | all-to-all | bytes 180224 | tf_op jit(solution)/shard_map/all_to_all | solution.py:398
  104.0 2.1 %collective-permute-start.14 = (f32[1,1408]{1,0:T(1,128)S(1)}, f32[1,1408]{1,0:T(1,128)S(1)}, u32[]{:S(2)}, u32[]{:S(2)}) collective-permute-start(f32[1,1408]{1,0:T(1,128)S(1)} %reduce_sum.12.sums), channel_id=1, source_target_pairs={{16,0},{17,1},{18,2},{19,3},{20,4},{21,5},{22,6},{23,7},{24,8},{25... | collective-permute-start | bytes 16904 | tf_op jit(solution)/shard_map/ppermute | solution.py:38
  107.0 11.3 %shard_map.68 = (f32[2,4,88,512]{3,2,1,0:T(8,128)S(1)}, f32[2,4,88,512]{3,2,1,0:T(8,128)S(1)}, f32[2,4,88,512]{3,2,1,0:T(8,128)S(1)}, f32[2,4,88,512]{3,2,1,0:T(8,128)}) custom-call(s32[5]{0:T(128)S(1)} %stack.38.place, s32[1,640]{1,0:T(1,128)S(1)} %add.54.ids, s32[1280,1]{1,0:T(8,128)S(1)} %reshape.25.wanted, f32[1,1408]{1,0:T(1,128)S(1)} %reduce_sum.12.sums, ...), custom_call_target="tpu_custom_call" | custom-call | flops 5033164800 | bytes 8388608 | tf_op jit(solution)/shard_map/pallas_call | solution.py:322
  118.3 2.1 %collective-permute-start.16 = (f32[2,4,88,512]{3,2,1,0:T(8,128)S(1)}, f32[2,4,88,512]{3,2,1,0:T(8,128)S(1)}, u32[]{:S(2)}, u32[]{:S(2)}) collective-permute-start(f32[2,4,88,512]{3,2,1,0:T(8,128)S(1)} %get-tuple-element.21), channel_id=1, source_target_pairs={{16,0},{17,1},{18,2},{19,3},{20,4},{21,5},{22,6},{23,7},{24,8},{25... | collective-permute-start | bytes 4325384 | tf_op jit(solution)/shard_map/ppermute | solution.py:38
  120.4 2.2 %collective-permute-start.15 = (f32[2,4,88,512]{3,2,1,0:T(8,128)}, f32[2,4,88,512]{3,2,1,0:T(8,128)S(1)}, u32[]{:S(2)}, u32[]{:S(2)}) collective-permute-start(f32[2,4,88,512]{3,2,1,0:T(8,128)} %get-tuple-element.19), channel_id=1, source_target_pairs={{16,0},{17,1},{18,2},{19,3},{20,4},{21,5},{22,6},{23,7},{24,8},{25... | collective-permute-start | bytes 4325384 | tf_op jit(solution)/shard_map/ppermute | solution.py:38
  123.9 1.9 %collective-permute-start.17 = (f32[2,88,512]{2,1,0:T(8,128)S(1)}, f32[2,88,512]{2,1,0:T(8,128)S(1)}, u32[]{:S(2)}, u32[]{:S(2)}) collective-permute-start(f32[2,88,512]{2,1,0:T(8,128)S(1)} %get-tuple-element.27), channel_id=1, source_target_pairs={{384,0},{385,1},{386,2},{387,3},{388,4},{389,5},{390,6},{391,7},{3... | collective-permute-start | bytes 1081352 | tf_op jit(solution)/shard_map/ppermute | solution.py:38
  125.8 4.6 %collective-permute-start.19 = (f32[2,88,512]{2,1,0:T(8,128)S(1)}, f32[2,88,512]{2,1,0:T(8,128)S(1)}, u32[]{:S(2)}, u32[]{:S(2)}) collective-permute-start(f32[2,88,512]{2,1,0:T(8,128)S(1)} %get-tuple-element.26), channel_id=1, source_target_pairs={{128,0},{129,1},{130,2},{131,3},{132,4},{133,5},{134,6},{135,7},{1... | collective-permute-start | bytes 1081352 | tf_op jit(solution)/shard_map/ppermute | solution.py:38
  130.8 2.8 %collective-permute-done.17 = f32[2,88,512]{2,1,0:T(8,128)S(1)} collective-permute-done((f32[2,88,512]{2,1,0:T(8,128)S(1)}, f32[2,88,512]{2,1,0:T(8,128)S(1)}, u32[]{:S(2)}, u32[]{:S(2)}) %collective-permute-start.17) | collective-permute-done | bytes 360480 | tf_op jit(solution)/shard_map/ppermute | solution.py:38
  135.7 4.6 %collective-permute-start.20 = (f32[4,88,512]{2,1,0:T(8,128)S(1)}, f32[4,88,512]{2,1,0:T(8,128)S(1)}, u32[]{:S(2)}, u32[]{:S(2)}) collective-permute-start(f32[4,88,512]{2,1,0:T(8,128)S(1)} %pad_maximum_fusion.1), channel_id=1, source_target_pairs={{128,0},{129,1},{130,2},{131,3},{132,4},{133,5},{134,6},{135,7},{1... | collective-permute-start | bytes 2162696 | tf_op jit(solution)/shard_map/ppermute | solution.py:38
  140.3 6.9 %collective-permute-done.18 = f32[4,88,512]{2,1,0:T(8,128)S(1)} collective-permute-done((f32[4,88,512]{2,1,0:T(8,128)S(1)}, f32[4,88,512]{2,1,0:T(8,128)S(1)}, u32[]{:S(2)}, u32[]{:S(2)}) %collective-permute-start.18) | collective-permute-done | bytes 720928 | tf_op jit(solution)/shard_map/ppermute | solution.py:38
  148.8 2.2 %collective-permute-start.21 = (f32[88,512]{1,0:T(8,128)S(1)}, f32[88,512]{1,0:T(8,128)S(1)}, u32[]{:S(2)}, u32[]{:S(2)}) collective-permute-start(f32[88,512]{1,0:T(8,128)S(1)} %get-tuple-element.28), channel_id=1, source_target_pairs={{1,0},{0,1},{3,2},{2,3},{5,4},{4,5},{7,6},{6,7},{9,8},{8,9},{11,10... | collective-permute-start | bytes 540680 | tf_op jit(solution)/shard_map/ppermute | solution.py:38
  151.0 7.1 %collective-permute-start.23 = (f32[88,512]{1,0:T(8,128)S(1)}, f32[88,512]{1,0:T(8,128)S(1)}, u32[]{:S(2)}, u32[]{:S(2)}) collective-permute-start(f32[88,512]{1,0:T(8,128)S(1)} %get-tuple-element.29), channel_id=1, source_target_pairs={{1,0},{0,1},{3,2},{2,3},{5,4},{4,5},{7,6},{6,7},{9,8},{8,9},{11,10... | collective-permute-start | bytes 540680 | tf_op jit(solution)/shard_map/ppermute | solution.py:38
  158.1 4.9 %collective-permute-done.21 = f32[88,512]{1,0:T(8,128)S(1)} collective-permute-done((f32[88,512]{1,0:T(8,128)S(1)}, f32[88,512]{1,0:T(8,128)S(1)}, u32[]{:S(2)}, u32[]{:S(2)}) %collective-permute-start.21) | collective-permute-done | bytes 180256 | tf_op jit(solution)/shard_map/ppermute | solution.py:38
  165.0 8.3 %collective-permute-done.22 = f32[88,512]{1,0:T(8,128)S(1)} collective-permute-done((f32[88,512]{1,0:T(8,128)S(1)}, f32[88,512]{1,0:T(8,128)S(1)}, u32[]{:S(2)}, u32[]{:S(2)}) %collective-permute-start.22) | collective-permute-done | bytes 180256 | tf_op jit(solution)/shard_map/ppermute | solution.py:38
  173.4 5.9 %collective-permute-start.24 = (f32[48,512]{1,0:T(8,128)S(1)}, f32[48,512]{1,0:T(8,128)S(1)}, u32[]{:S(2)}, u32[]{:S(2)}) collective-permute-start(f32[48,512]{1,0:T(8,128)S(1)} %slice.94), channel_id=1, source_target_pairs={{16,0},{17,1},{18,2},{19,3},{20,4},{21,5},{22,6},{23,7},{24,8},{25... | collective-permute-start | bytes 294920 | tf_op jit(solution)/shard_map/ppermute | solution.py:38
  (58 shorter events, 17.8 us)
Async XLA Ops:
  1.6 9.7 %collective-permute-start = (f32[40,512]{1,0:T(8,128)S(1)}, f32[40,512]{1,0:T(8,128)S(1)}, u32[]{:S(2)}, u32[]{:S(2)}) collective-permute-start(f32[40,512]{1,0:T(8,128)S(1)} %get-tuple-element.33), channel_id=1, source_target_pairs={{16,0},{17,1},{18,2},{19,3},{20,4},{21,5},{22,6},{23,7},{24,8},{25... | collective-permute-start | bytes 245768 | tf_op jit(solution)/shard_map/ppermute | solution.py:38
  11.3 55.2 %copy-start.3 = (s32[640]{0:T(1024)S(1)}, s32[640]{0:T(1024)}, u32[]{:S(2)}) copy-start(s32[640]{0:T(1024)} %constant.33.clone) | copy-start | bytes 7684
  11.3 55.2 %copy-start.2 = (s32[20480]{0:T(1024)S(1)}, s32[20480]{0:T(1024)}, u32[]{:S(2)}) copy-start(s32[20480]{0:T(1024)} %param.6) | copy-start | bytes 245764
  11.3 10.7 %collective-permute-start.1 = (f32[80,512]{1,0:T(8,128)S(1)}, f32[80,512]{1,0:T(8,128)S(1)}, u32[]{:S(2)}, u32[]{:S(2)}) collective-permute-start(f32[80,512]{1,0:T(8,128)S(1)} %get-tuple-element.31), channel_id=1, source_target_pairs={{2,0},{3,1},{0,2},{1,3},{6,4},{7,5},{4,6},{5,7},{10,8},{11,9},{8,1... | collective-permute-start | bytes 491528 | tf_op jit(solution)/shard_map/ppermute | solution.py:38
  18.6 10.8 %collective-permute-start.2 = (f32[80,512]{1,0:T(8,128)S(1)}, f32[80,512]{1,0:T(8,128)S(1)}, u32[]{:S(2)}, u32[]{:S(2)}) collective-permute-start(f32[80,512]{1,0:T(8,128)S(1)} %get-tuple-element.31), channel_id=1, source_target_pairs={{1,0},{0,1},{3,2},{2,3},{5,4},{4,5},{7,6},{6,7},{9,8},{8,9},{11,10... | collective-permute-start | bytes 491528 | tf_op jit(solution)/shard_map/ppermute | solution.py:38
  22.0 10.3 %collective-permute-start.3 = (f32[80,512]{1,0:T(8,128)S(1)}, f32[80,512]{1,0:T(8,128)S(1)}, u32[]{:S(2)}, u32[]{:S(2)}) collective-permute-start(f32[80,512]{1,0:T(8,128)S(1)} %collective-permute-done.1), channel_id=1, source_target_pairs={{1,0},{0,1},{3,2},{2,3},{5,4},{4,5},{7,6},{6,7},{9,8},{8,9},{11,10... | collective-permute-start | bytes 491528 | tf_op jit(solution)/shard_map/ppermute | solution.py:38
  32.4 16.5 %collective-permute-start.5 = (f32[4,80,512]{2,1,0:T(8,128)S(1)}, f32[4,80,512]{2,1,0:T(8,128)S(1)}, u32[]{:S(2)}, u32[]{:S(2)}) collective-permute-start(f32[4,80,512]{2,1,0:T(8,128)S(1)} %pad_maximum_fusion.2.refs_0_), channel_id=1, source_target_pairs={{384,0},{385,1},{386,2},{387,3},{388,4},{389,5},{390,6},{391,7},{3... | collective-permute-start | bytes 1966088 | tf_op jit(solution)/shard_map/ppermute | solution.py:38
  39.5 11.7 %collective-permute-start.4 = (f32[4,80,512]{2,1,0:T(8,128)S(1)}, f32[4,80,512]{2,1,0:T(8,128)S(1)}, u32[]{:S(2)}, u32[]{:S(2)}) collective-permute-start(f32[4,80,512]{2,1,0:T(8,128)S(1)} %pad_maximum_fusion.2.refs_0_), channel_id=1, source_target_pairs={{128,0},{129,1},{130,2},{131,3},{132,4},{133,5},{134,6},{135,7},{1... | collective-permute-start | bytes 1966088 | tf_op jit(solution)/shard_map/ppermute | solution.py:38
  48.9 13.2 %collective-permute-start.7 = (f32[2,80,512]{2,1,0:T(8,128)S(1)}, f32[2,80,512]{2,1,0:T(8,128)}, u32[]{:S(2)}, u32[]{:S(2)}) collective-permute-start(f32[2,80,512]{2,1,0:T(8,128)S(1)} %slice.83), channel_id=1, source_target_pairs={{384,0},{385,1},{386,2},{387,3},{388,4},{389,5},{390,6},{391,7},{3... | collective-permute-start | bytes 983048 | tf_op jit(solution)/shard_map/ppermute | solution.py:38
  51.2 13.3 %collective-permute-start.6 = (f32[2,80,512]{2,1,0:T(8,128)S(1)}, f32[2,80,512]{2,1,0:T(8,128)}, u32[]{:S(2)}, u32[]{:S(2)}) collective-permute-start(f32[2,80,512]{2,1,0:T(8,128)S(1)} %slice.82), channel_id=1, source_target_pairs={{128,0},{129,1},{130,2},{131,3},{132,4},{133,5},{134,6},{135,7},{1... | collective-permute-start | bytes 983048 | tf_op jit(solution)/shard_map/ppermute | solution.py:38
  55.8 11.4 %collective-permute-start.8 = (f32[4,80,512]{2,1,0:T(8,128)S(1)}, f32[4,80,512]{2,1,0:T(8,128)S(1)}, u32[]{:S(2)}, u32[]{:S(2)}) collective-permute-start(f32[4,80,512]{2,1,0:T(8,128)S(1)} %pad_maximum_fusion.2.refs_0_), channel_id=1, source_target_pairs={{16,0},{17,1},{18,2},{19,3},{20,4},{21,5},{22,6},{23,7},{24,8},{25... | collective-permute-start | bytes 1966088 | tf_op jit(solution)/shard_map/ppermute | solution.py:38
  57.8 9.5 %collective-permute-start.10 = (f32[4,80,512]{2,1,0:T(8,128)S(1)}, f32[4,80,512]{2,1,0:T(8,128)}, u32[]{:S(2)}, u32[]{:S(2)}) collective-permute-start(f32[4,80,512]{2,1,0:T(8,128)S(1)} %collective-permute-done.5.refs_2_), channel_id=1, source_target_pairs={{16,0},{17,1},{18,2},{19,3},{20,4},{21,5},{22,6},{23,7},{24,8},{25... | collective-permute-start | bytes 1966088 | tf_op jit(solution)/shard_map/ppermute | solution.py:38
  60.2 8.3 %collective-permute-start.9 = (f32[4,80,512]{2,1,0:T(8,128)S(1)}, f32[4,80,512]{2,1,0:T(8,128)}, u32[]{:S(2)}, u32[]{:S(2)}) collective-permute-start(f32[4,80,512]{2,1,0:T(8,128)S(1)} %collective-permute-done.4.refs_1_), channel_id=1, source_target_pairs={{16,0},{17,1},{18,2},{19,3},{20,4},{21,5},{22,6},{23,7},{24,8},{25... | collective-permute-start | bytes 1966088 | tf_op jit(solution)/shard_map/ppermute | solution.py:38
  62.1 5.1 %collective-permute-start.12 = (f32[2,80,512]{2,1,0:T(8,128)}, f32[2,80,512]{2,1,0:T(8,128)}, u32[]{:S(2)}, u32[]{:S(2)}) collective-permute-start(f32[2,80,512]{2,1,0:T(8,128)} %collective-permute-done.7.refs_4_), channel_id=1, source_target_pairs={{16,0},{17,1},{18,2},{19,3},{20,4},{21,5},{22,6},{23,7},{24,8},{25... | collective-permute-start | bytes 983048 | tf_op jit(solution)/shard_map/ppermute | solution.py:38
  64.6 3.9 %collective-permute-start.11 = (f32[2,80,512]{2,1,0:T(8,128)}, f32[2,80,512]{2,1,0:T(8,128)}, u32[]{:S(2)}, u32[]{:S(2)}) collective-permute-start(f32[2,80,512]{2,1,0:T(8,128)} %collective-permute-done.6.refs_3_), channel_id=1, source_target_pairs={{16,0},{17,1},{18,2},{19,3},{20,4},{21,5},{22,6},{23,7},{24,8},{25... | collective-permute-start | bytes 983048 | tf_op jit(solution)/shard_map/ppermute | solution.py:38
  78.3 3.1 %collective-permute-start.13 = (f32[1,1408]{1,0:T(1,128)S(1)}, f32[1,1408]{1,0:T(1,128)S(1)}, u32[]{:S(2)}, u32[]{:S(2)}) collective-permute-start(f32[1,1408]{1,0:T(1,128)S(1)} %get-tuple-element.15), channel_id=1, source_target_pairs={{16,0},{17,1},{18,2},{19,3},{20,4},{21,5},{22,6},{23,7},{24,8},{25... | collective-permute-start | bytes 16904 | tf_op jit(solution)/shard_map/ppermute | solution.py:38
  104.0 3.1 %collective-permute-start.14 = (f32[1,1408]{1,0:T(1,128)S(1)}, f32[1,1408]{1,0:T(1,128)S(1)}, u32[]{:S(2)}, u32[]{:S(2)}) collective-permute-start(f32[1,1408]{1,0:T(1,128)S(1)} %reduce_sum.12.sums), channel_id=1, source_target_pairs={{16,0},{17,1},{18,2},{19,3},{20,4},{21,5},{22,6},{23,7},{24,8},{25... | collective-permute-start | bytes 16904 | tf_op jit(solution)/shard_map/ppermute | solution.py:38
  118.3 5.1 %collective-permute-start.16 = (f32[2,4,88,512]{3,2,1,0:T(8,128)S(1)}, f32[2,4,88,512]{3,2,1,0:T(8,128)S(1)}, u32[]{:S(2)}, u32[]{:S(2)}) collective-permute-start(f32[2,4,88,512]{3,2,1,0:T(8,128)S(1)} %get-tuple-element.21), channel_id=1, source_target_pairs={{16,0},{17,1},{18,2},{19,3},{20,4},{21,5},{22,6},{23,7},{24,8},{25... | collective-permute-start | bytes 4325384 | tf_op jit(solution)/shard_map/ppermute | solution.py:38
  120.4 10.0 %collective-permute-start.15 = (f32[2,4,88,512]{3,2,1,0:T(8,128)}, f32[2,4,88,512]{3,2,1,0:T(8,128)S(1)}, u32[]{:S(2)}, u32[]{:S(2)}) collective-permute-start(f32[2,4,88,512]{3,2,1,0:T(8,128)} %get-tuple-element.19), channel_id=1, source_target_pairs={{16,0},{17,1},{18,2},{19,3},{20,4},{21,5},{22,6},{23,7},{24,8},{25... | collective-permute-start | bytes 4325384 | tf_op jit(solution)/shard_map/ppermute | solution.py:38
  123.9 9.7 %collective-permute-start.17 = (f32[2,88,512]{2,1,0:T(8,128)S(1)}, f32[2,88,512]{2,1,0:T(8,128)S(1)}, u32[]{:S(2)}, u32[]{:S(2)}) collective-permute-start(f32[2,88,512]{2,1,0:T(8,128)S(1)} %get-tuple-element.27), channel_id=1, source_target_pairs={{384,0},{385,1},{386,2},{387,3},{388,4},{389,5},{390,6},{391,7},{3... | collective-permute-start | bytes 1081352 | tf_op jit(solution)/shard_map/ppermute | solution.py:38
  125.8 9.8 %collective-permute-start.19 = (f32[2,88,512]{2,1,0:T(8,128)S(1)}, f32[2,88,512]{2,1,0:T(8,128)S(1)}, u32[]{:S(2)}, u32[]{:S(2)}) collective-permute-start(f32[2,88,512]{2,1,0:T(8,128)S(1)} %get-tuple-element.26), channel_id=1, source_target_pairs={{128,0},{129,1},{130,2},{131,3},{132,4},{133,5},{134,6},{135,7},{1... | collective-permute-start | bytes 1081352 | tf_op jit(solution)/shard_map/ppermute | solution.py:38
  133.7 13.5 %collective-permute-start.18 = (f32[4,88,512]{2,1,0:T(8,128)S(1)}, f32[4,88,512]{2,1,0:T(8,128)S(1)}, u32[]{:S(2)}, u32[]{:S(2)}) collective-permute-start(f32[4,88,512]{2,1,0:T(8,128)S(1)} %pad_maximum_fusion), channel_id=1, source_target_pairs={{384,0},{385,1},{386,2},{387,3},{388,4},{389,5},{390,6},{391,7},{3... | collective-permute-start | bytes 2162696 | tf_op jit(solution)/shard_map/ppermute | solution.py:38
  135.7 12.8 %collective-permute-start.20 = (f32[4,88,512]{2,1,0:T(8,128)S(1)}, f32[4,88,512]{2,1,0:T(8,128)S(1)}, u32[]{:S(2)}, u32[]{:S(2)}) collective-permute-start(f32[4,88,512]{2,1,0:T(8,128)S(1)} %pad_maximum_fusion.1), channel_id=1, source_target_pairs={{128,0},{129,1},{130,2},{131,3},{132,4},{133,5},{134,6},{135,7},{1... | collective-permute-start | bytes 2162696 | tf_op jit(solution)/shard_map/ppermute | solution.py:38
  148.7 31.5 %copy-start = (f32[40,512]{1,0:T(8,128)S(1)}, f32[40,512]{1,0:T(8,128)}, u32[]{:S(2)}) copy-start(f32[40,512]{1,0:T(8,128)} %packet.1) | copy-start | bytes 245764
  148.8 31.5 %copy-start.1 = (f32[40,512]{1,0:T(8,128)S(1)}, f32[40,512]{1,0:T(8,128)}, u32[]{:S(2)}) copy-start(f32[40,512]{1,0:T(8,128)} %header.1) | copy-start | bytes 245764
  148.8 14.3 %collective-permute-start.21 = (f32[88,512]{1,0:T(8,128)S(1)}, f32[88,512]{1,0:T(8,128)S(1)}, u32[]{:S(2)}, u32[]{:S(2)}) collective-permute-start(f32[88,512]{1,0:T(8,128)S(1)} %get-tuple-element.28), channel_id=1, source_target_pairs={{1,0},{0,1},{3,2},{2,3},{5,4},{4,5},{7,6},{6,7},{9,8},{8,9},{11,10... | collective-permute-start | bytes 540680 | tf_op jit(solution)/shard_map/ppermute | solution.py:38
  151.0 14.0 %collective-permute-start.23 = (f32[88,512]{1,0:T(8,128)S(1)}, f32[88,512]{1,0:T(8,128)S(1)}, u32[]{:S(2)}, u32[]{:S(2)}) collective-permute-start(f32[88,512]{1,0:T(8,128)S(1)} %get-tuple-element.29), channel_id=1, source_target_pairs={{1,0},{0,1},{3,2},{2,3},{5,4},{4,5},{7,6},{6,7},{9,8},{8,9},{11,10... | collective-permute-start | bytes 540680 | tf_op jit(solution)/shard_map/ppermute | solution.py:38
  163.1 10.2 %collective-permute-start.22 = (f32[88,512]{1,0:T(8,128)S(1)}, f32[88,512]{1,0:T(8,128)S(1)}, u32[]{:S(2)}, u32[]{:S(2)}) collective-permute-start(f32[88,512]{1,0:T(8,128)S(1)} %fusion.4), channel_id=1, source_target_pairs={{2,0},{3,1},{0,2},{1,3},{6,4},{7,5},{4,6},{5,7},{10,8},{11,9},{8,1... | collective-permute-start | bytes 540680 | tf_op jit(solution)/shard_map/ppermute | solution.py:38
  173.4 6.8 %collective-permute-start.24 = (f32[48,512]{1,0:T(8,128)S(1)}, f32[48,512]{1,0:T(8,128)S(1)}, u32[]{:S(2)}, u32[]{:S(2)}) collective-permute-start(f32[48,512]{1,0:T(8,128)S(1)} %slice.94), channel_id=1, source_target_pairs={{16,0},{17,1},{18,2},{19,3},{20,4},{21,5},{22,6},{23,7},{24,8},{25... | collective-permute-start | bytes 294920 | tf_op jit(solution)/shard_map/ppermute | solution.py:38

commit v8 on v6

--- a/solution.py
+++ b/solution.py
@@ -123,7 +123,7 @@
     return jnp.sum(jnp.where(eye(), lanes, 0.0), axis=1, keepdims=True)
 
 
-STEP = 256
+STEP = 640
 SUMS = ROWS + 128
 KEPT_F32 = 6 * ROWS
 KEPT_B16 = 16 * ROWS
@@ -261,9 +261,7 @@
         pgrads[here, :] = wide_product(high, low, hboth, 1)
     for copy in whole[2:]:
         copy.wait()
-    for k in range(COLS // 128):
-        here = pl.ds(k * 128, 128)
-        hgrads[here, :] = wide_product(dh[:, here], dlow[:, here], pboth, 0)
+    hgrads[...] = wide_product(dh[...], dlow[...], pboth, 0)
 
     def at(outs, j):
         line = (3, 1, 2, 0)[j]

time: 182 us -> 182 us (level)
  no operation moved by 1% of the time
where the time goes in v8:
time: 182 us; the launch traced here: 181 us
  starting transfers between devices  80.3 us (44%)
  waiting for transfers between devices  49.6 us (27%)
  blocking collectives  24.4 us (13%)
  Pallas kernels  22.2 us (12%)
  other arithmetic  2.23 us (1%)
    ppermute x23, starting transfers between devices, permute(): return lax.ppermute(value, ALL, pairs)  80.3 us
    ppermute x23, waiting for transfers between devices, permute(): return lax.ppermute(value, ALL, pairs)  49.6 us
    all_to_all x1, blocking collectives, per_device(): lax.all_to_all(jnp.broadcast_to((keep + swap_core(send))[None], (16, 1, S...  24.4 us
    pallas_call x3, Pallas kernels, call(): pl.pallas_call(kernel, in_specs=[IN_SMEM] + in_specs, out_specs=out_specs...  22.2 us
  transfers between devices with their start and end apart: 23, of which 15 were waited for; matrix products, arithmetic and copies ran while one was open for 1% of the time, Pallas kernels for 0%

profile of v8, /device:TPU:39, one launch (start us, length us, event | category | flops | bytes accessed | tf_op | source)
XLA Modules:
  0.0 181.0 jit_solution(1894318454054880884)
XLA Ops:
  1.6 2.6 %collective-permute-start = (f32[40,512]{1,0:T(8,128)S(1)}, f32[40,512]{1,0:T(8,128)S(1)}, u32[]{:S(2)}, u32[]{:S(2)}) collective-permute-start(f32[40,512]{1,0:T(8,128)S(1)} %get-tuple-element.33), channel_id=1, source_target_pairs={{16,0},{17,1},{18,2},{19,3},{20,4},{21,5},{22,6},{23,7},{24,8},{25... | collective-permute-start | bytes 245768 | tf_op jit(solution)/shard_map/ppermute | solution.py:38
  5.2 8.8 %collective-permute-start.1 = (f32[80,512]{1,0:T(8,128)S(1)}, f32[80,512]{1,0:T(8,128)S(1)}, u32[]{:S(2)}, u32[]{:S(2)}) collective-permute-start(f32[80,512]{1,0:T(8,128)S(1)} %get-tuple-element.31), channel_id=1, source_target_pairs={{2,0},{3,1},{0,2},{1,3},{6,4},{7,5},{4,6},{5,7},{10,8},{11,9},{8,1... | collective-permute-start | bytes 491528 | tf_op jit(solution)/shard_map/ppermute | solution.py:38
  14.0 4.7 %collective-permute-start.2 = (f32[80,512]{1,0:T(8,128)S(1)}, f32[80,512]{1,0:T(8,128)S(1)}, u32[]{:S(2)}, u32[]{:S(2)}) collective-permute-start(f32[80,512]{1,0:T(8,128)S(1)} %get-tuple-element.31), channel_id=1, source_target_pairs={{1,0},{0,1},{3,2},{2,3},{5,4},{4,5},{7,6},{6,7},{9,8},{8,9},{11,10... | collective-permute-start | bytes 491528 | tf_op jit(solution)/shard_map/ppermute | solution.py:38
  19.6 9.6 %collective-permute-start.3 = (f32[80,512]{1,0:T(8,128)S(1)}, f32[80,512]{1,0:T(8,128)S(1)}, u32[]{:S(2)}, u32[]{:S(2)}) collective-permute-start(f32[80,512]{1,0:T(8,128)S(1)} %collective-permute-done.1), channel_id=1, source_target_pairs={{1,0},{0,1},{3,2},{2,3},{5,4},{4,5},{7,6},{6,7},{9,8},{8,9},{11,10... | collective-permute-start | bytes 491528 | tf_op jit(solution)/shard_map/ppermute | solution.py:38
  29.2 8.0 %collective-permute-done.3 = f32[80,512]{1,0:T(8,128)S(1)} collective-permute-done((f32[80,512]{1,0:T(8,128)S(1)}, f32[80,512]{1,0:T(8,128)S(1)}, u32[]{:S(2)}, u32[]{:S(2)}) %collective-permute-start.3) | collective-permute-done | bytes 163872 | tf_op jit(solution)/shard_map/ppermute | solution.py:38
  37.3 4.6 %collective-permute-start.4 = (f32[4,80,512]{2,1,0:T(8,128)S(1)}, f32[4,80,512]{2,1,0:T(8,128)S(1)}, u32[]{:S(2)}, u32[]{:S(2)}) collective-permute-start(f32[4,80,512]{2,1,0:T(8,128)S(1)} %pad_maximum_fusion.2.refs_0_), channel_id=1, source_target_pairs={{128,0},{129,1},{130,2},{131,3},{132,4},{133,5},{134,6},{135,7},{1... | collective-permute-start | bytes 1966088 | tf_op jit(solution)/shard_map/ppermute | solution.py:38
  41.9 1.9 %collective-permute-start.5 = (f32[4,80,512]{2,1,0:T(8,128)S(1)}, f32[4,80,512]{2,1,0:T(8,128)S(1)}, u32[]{:S(2)}, u32[]{:S(2)}) collective-permute-start(f32[4,80,512]{2,1,0:T(8,128)S(1)} %pad_maximum_fusion.2.refs_0_), channel_id=1, source_target_pairs={{384,0},{385,1},{386,2},{387,3},{388,4},{389,5},{390,6},{391,7},{3... | collective-permute-start | bytes 1966088 | tf_op jit(solution)/shard_map/ppermute | solution.py:38
  43.9 5.6 %collective-permute-done.4.refs_1_ = f32[4,80,512]{2,1,0:T(8,128)S(1)} collective-permute-done((f32[4,80,512]{2,1,0:T(8,128)S(1)}, f32[4,80,512]{2,1,0:T(8,128)S(1)}, u32[]{:S(2)}, u32[]{:S(2)}) %collective-permute-start.4) | collective-permute-done | bytes 655392 | tf_op jit(solution)/shard_map/ppermute | solution.py:38
  49.5 5.3 %collective-permute-start.6 = (f32[4,80,512]{2,1,0:T(8,128)S(1)}, f32[4,80,512]{2,1,0:T(8,128)S(1)}, u32[]{:S(2)}, u32[]{:S(2)}) collective-permute-start(f32[4,80,512]{2,1,0:T(8,128)S(1)} %collective-permute-done.4.refs_1_), channel_id=1, source_target_pairs={{128,0},{129,1},{130,2},{131,3},{132,4},{133,5},{134,6},{135,7},{1... | collective-permute-start | bytes 1966088 | tf_op jit(solution)/shard_map/ppermute | solution.py:38
  54.8 1.9 %collective-permute-start.7 = (f32[4,80,512]{2,1,0:T(8,128)S(1)}, f32[4,80,512]{2,1,0:T(8,128)}, u32[]{:S(2)}, u32[]{:S(2)}) collective-permute-start(f32[4,80,512]{2,1,0:T(8,128)S(1)} %pad_maximum_fusion.2.refs_0_), channel_id=1, source_target_pairs={{16,0},{17,1},{18,2},{19,3},{20,4},{21,5},{22,6},{23,7},{24,8},{25... | collective-permute-start | bytes 1966088 | tf_op jit(solution)/shard_map/ppermute | solution.py:38
  56.7 2.4 %collective-permute-start.8 = (f32[4,80,512]{2,1,0:T(8,128)S(1)}, f32[4,80,512]{2,1,0:T(8,128)}, u32[]{:S(2)}, u32[]{:S(2)}) collective-permute-start(f32[4,80,512]{2,1,0:T(8,128)S(1)} %collective-permute-done.4.refs_1_), channel_id=1, source_target_pairs={{16,0},{17,1},{18,2},{19,3},{20,4},{21,5},{22,6},{23,7},{24,8},{25... | collective-permute-start | bytes 1966088 | tf_op jit(solution)/shard_map/ppermute | solution.py:38
  59.1 1.9 %collective-permute-start.9 = (f32[4,80,512]{2,1,0:T(8,128)S(1)}, f32[4,80,512]{2,1,0:T(8,128)}, u32[]{:S(2)}, u32[]{:S(2)}) collective-permute-start(f32[4,80,512]{2,1,0:T(8,128)S(1)} %collective-permute-done.5.refs_2_), channel_id=1, source_target_pairs={{16,0},{17,1},{18,2},{19,3},{20,4},{21,5},{22,6},{23,7},{24,8},{25... | collective-permute-start | bytes 1966088 | tf_op jit(solution)/shard_map/ppermute | solution.py:38
  62.3 1.9 %collective-permute-start.10 = (f32[4,80,512]{2,1,0:T(8,128)S(1)}, f32[4,80,512]{2,1,0:T(8,128)}, u32[]{:S(2)}, u32[]{:S(2)}) collective-permute-start(f32[4,80,512]{2,1,0:T(8,128)S(1)} %collective-permute-done.6.refs_3_), channel_id=1, source_target_pairs={{16,0},{17,1},{18,2},{19,3},{20,4},{21,5},{22,6},{23,7},{24,8},{25... | collective-permute-start | bytes 1966088 | tf_op jit(solution)/shard_map/ppermute | solution.py:38
  66.4 10.0 %shard_map.67 = (f32[7680,640]{1,0:T(8,128)}, bf16[20480,512]{1,0:T(8,128)(2,1)}, f32[1,1408]{1,0:T(1,128)S(1)}, f32[1,1408]{1,0:T(1,128)S(1)}) custom-call(s32[5]{0:T(128)S(1)} %stack.38.place, s32[1,640]{1,0:T(1,128)S(1)} %add.54.ids, s32[1280,1]{1,0:T(8,128)S(1)} %reshape.25.wanted, f32[4,80,512]{2,1,0:T(8,128)S(1)} %pad_maximum_fusion.2.refs_0_, ...), custom_call_target="tpu_custom_call" | custom-call | flops 2516582400 | bytes 8388608 | tf_op jit(solution)/shard_map/pallas_call | solution.py:316
  76.4 2.0 %collective-permute-start.11 = (f32[1,1408]{1,0:T(1,128)S(1)}, f32[1,1408]{1,0:T(1,128)S(1)}, u32[]{:S(2)}, u32[]{:S(2)}) collective-permute-start(f32[1,1408]{1,0:T(1,128)S(1)} %get-tuple-element.15), channel_id=1, source_target_pairs={{16,0},{17,1},{18,2},{19,3},{20,4},{21,5},{22,6},{23,7},{24,8},{25... | collective-permute-start | bytes 16904 | tf_op jit(solution)/shard_map/ppermute | solution.py:38
  79.5 24.4 %all_to_all.5 = f32[16,1,1408]{2,1,0:T(1,128)S(1)} all-to-all(f32[16,1,1408]{2,1,0:T(1,128)S(1)} %broadcast_in_dim.10), channel_id=1, replica_groups={{0,1,2,3,128,129,130,131,256,257,258,259,384,385,386,387},{16,20,24,28,..., dimensions={0} | all-to-all | bytes 180224 | tf_op jit(solution)/shard_map/all_to_all | solution.py:392
  104.0 2.1 %collective-permute-start.12 = (f32[1,1408]{1,0:T(1,128)S(1)}, f32[1,1408]{1,0:T(1,128)S(1)}, u32[]{:S(2)}, u32[]{:S(2)}) collective-permute-start(f32[1,1408]{1,0:T(1,128)S(1)} %reduce_sum.12.sums), channel_id=1, source_target_pairs={{16,0},{17,1},{18,2},{19,3},{20,4},{21,5},{22,6},{23,7},{24,8},{25... | collective-permute-start | bytes 16904 | tf_op jit(solution)/shard_map/ppermute | solution.py:38
  107.1 10.8 %shard_map.68 = (f32[2,4,88,512]{3,2,1,0:T(8,128)S(1)}, f32[2,4,88,512]{3,2,1,0:T(8,128)S(1)}, f32[2,4,88,512]{3,2,1,0:T(8,128)S(1)}, f32[2,4,88,512]{3,2,1,0:T(8,128)}) custom-call(s32[5]{0:T(128)S(1)} %stack.38.place, s32[1,640]{1,0:T(1,128)S(1)} %add.54.ids, s32[1280,1]{1,0:T(8,128)S(1)} %reshape.25.wanted, f32[1,1408]{1,0:T(1,128)S(1)} %reduce_sum.12.sums, ...), custom_call_target="tpu_custom_call" | custom-call | flops 5033164800 | bytes 8388608 | tf_op jit(solution)/shard_map/pallas_call | solution.py:316
  117.9 2.1 %collective-permute-start.14 = (f32[2,4,88,512]{3,2,1,0:T(8,128)S(1)}, f32[2,4,88,512]{3,2,1,0:T(8,128)S(1)}, u32[]{:S(2)}, u32[]{:S(2)}) collective-permute-start(f32[2,4,88,512]{3,2,1,0:T(8,128)S(1)} %get-tuple-element.21), channel_id=1, source_target_pairs={{16,0},{17,1},{18,2},{19,3},{20,4},{21,5},{22,6},{23,7},{24,8},{25... | collective-permute-start | bytes 4325384 | tf_op jit(solution)/shard_map/ppermute | solution.py:38
  120.0 2.2 %collective-permute-start.13 = (f32[2,4,88,512]{3,2,1,0:T(8,128)}, f32[2,4,88,512]{3,2,1,0:T(8,128)S(1)}, u32[]{:S(2)}, u32[]{:S(2)}) collective-permute-start(f32[2,4,88,512]{3,2,1,0:T(8,128)} %get-tuple-element.19), channel_id=1, source_target_pairs={{16,0},{17,1},{18,2},{19,3},{20,4},{21,5},{22,6},{23,7},{24,8},{25... | collective-permute-start | bytes 4325384 | tf_op jit(solution)/shard_map/ppermute | solution.py:38
  123.4 1.9 %collective-permute-start.15 = (f32[2,88,512]{2,1,0:T(8,128)S(1)}, f32[2,88,512]{2,1,0:T(8,128)S(1)}, u32[]{:S(2)}, u32[]{:S(2)}) collective-permute-start(f32[2,88,512]{2,1,0:T(8,128)S(1)} %get-tuple-element.27), channel_id=1, source_target_pairs={{384,0},{385,1},{386,2},{387,3},{388,4},{389,5},{390,6},{391,7},{3... | collective-permute-start | bytes 1081352 | tf_op jit(solution)/shard_map/ppermute | solution.py:38
  125.4 4.6 %collective-permute-start.17 = (f32[2,88,512]{2,1,0:T(8,128)S(1)}, f32[2,88,512]{2,1,0:T(8,128)S(1)}, u32[]{:S(2)}, u32[]{:S(2)}) collective-permute-start(f32[2,88,512]{2,1,0:T(8,128)S(1)} %get-tuple-element.26), channel_id=1, source_target_pairs={{128,0},{129,1},{130,2},{131,3},{132,4},{133,5},{134,6},{135,7},{1... | collective-permute-start | bytes 1081352 | tf_op jit(solution)/shard_map/ppermute | solution.py:38
  130.3 2.8 %collective-permute-done.15 = f32[2,88,512]{2,1,0:T(8,128)S(1)} collective-permute-done((f32[2,88,512]{2,1,0:T(8,128)S(1)}, f32[2,88,512]{2,1,0:T(8,128)S(1)}, u32[]{:S(2)}, u32[]{:S(2)}) %collective-permute-start.15) | collective-permute-done | bytes 360480 | tf_op jit(solution)/shard_map/ppermute | solution.py:38
  133.2 1.9 %collective-permute-start.16 = (f32[4,88,512]{2,1,0:T(8,128)S(1)}, f32[4,88,512]{2,1,0:T(8,128)S(1)}, u32[]{:S(2)}, u32[]{:S(2)}) collective-permute-start(f32[4,88,512]{2,1,0:T(8,128)S(1)} %pad_maximum_fusion), channel_id=1, source_target_pairs={{384,0},{385,1},{386,2},{387,3},{388,4},{389,5},{390,6},{391,7},{3... | collective-permute-start | bytes 2162696 | tf_op jit(solution)/shard_map/ppermute | solution.py:38
  135.3 4.6 %collective-permute-start.18 = (f32[4,88,512]{2,1,0:T(8,128)S(1)}, f32[4,88,512]{2,1,0:T(8,128)S(1)}, u32[]{:S(2)}, u32[]{:S(2)}) collective-permute-start(f32[4,88,512]{2,1,0:T(8,128)S(1)} %pad_maximum_fusion.1), channel_id=1, source_target_pairs={{128,0},{129,1},{130,2},{131,3},{132,4},{133,5},{134,6},{135,7},{1... | collective-permute-start | bytes 2162696 | tf_op jit(solution)/shard_map/ppermute | solution.py:38
  139.8 6.9 %collective-permute-done.16 = f32[4,88,512]{2,1,0:T(8,128)S(1)} collective-permute-done((f32[4,88,512]{2,1,0:T(8,128)S(1)}, f32[4,88,512]{2,1,0:T(8,128)S(1)}, u32[]{:S(2)}, u32[]{:S(2)}) %collective-permute-start.16) | collective-permute-done | bytes 720928 | tf_op jit(solution)/shard_map/ppermute | solution.py:38
  148.3 2.1 %collective-permute-start.19 = (f32[88,512]{1,0:T(8,128)S(1)}, f32[88,512]{1,0:T(8,128)S(1)}, u32[]{:S(2)}, u32[]{:S(2)}) collective-permute-start(f32[88,512]{1,0:T(8,128)S(1)} %get-tuple-element.28), channel_id=1, source_target_pairs={{1,0},{0,1},{3,2},{2,3},{5,4},{4,5},{7,6},{6,7},{9,8},{8,9},{11,10... | collective-permute-start | bytes 540680 | tf_op jit(solution)/shard_map/ppermute | solution.py:38
  150.4 7.3 %collective-permute-start.21 = (f32[88,512]{1,0:T(8,128)S(1)}, f32[88,512]{1,0:T(8,128)S(1)}, u32[]{:S(2)}, u32[]{:S(2)}) collective-permute-start(f32[88,512]{1,0:T(8,128)S(1)} %get-tuple-element.29), channel_id=1, source_target_pairs={{1,0},{0,1},{3,2},{2,3},{5,4},{4,5},{7,6},{6,7},{9,8},{8,9},{11,10... | collective-permute-start | bytes 540680 | tf_op jit(solution)/shard_map/ppermute | solution.py:38
  157.7 7.1 %collective-permute-done.19 = f32[88,512]{1,0:T(8,128)S(1)} collective-permute-done((f32[88,512]{1,0:T(8,128)S(1)}, f32[88,512]{1,0:T(8,128)S(1)}, u32[]{:S(2)}, u32[]{:S(2)}) %collective-permute-start.19) | collective-permute-done | bytes 180256 | tf_op jit(solution)/shard_map/ppermute | solution.py:38
  164.8 1.9 %collective-permute-start.20 = (f32[88,512]{1,0:T(8,128)S(1)}, f32[88,512]{1,0:T(8,128)S(1)}, u32[]{:S(2)}, u32[]{:S(2)}) collective-permute-start(f32[88,512]{1,0:T(8,128)S(1)} %fusion.4), channel_id=1, source_target_pairs={{2,0},{3,1},{0,2},{1,3},{6,4},{7,5},{4,6},{5,7},{10,8},{11,9},{8,1... | collective-permute-start | bytes 540680 | tf_op jit(solution)/shard_map/ppermute | solution.py:38
  166.8 9.4 %collective-permute-done.20 = f32[88,512]{1,0:T(8,128)S(1)} collective-permute-done((f32[88,512]{1,0:T(8,128)S(1)}, f32[88,512]{1,0:T(8,128)S(1)}, u32[]{:S(2)}, u32[]{:S(2)}) %collective-permute-start.20) | collective-permute-done | bytes 180256 | tf_op jit(solution)/shard_map/ppermute | solution.py:38
  176.2 1.9 %collective-permute-start.22 = (f32[48,512]{1,0:T(8,128)S(1)}, f32[48,512]{1,0:T(8,128)S(1)}, u32[]{:S(2)}, u32[]{:S(2)}) collective-permute-start(f32[48,512]{1,0:T(8,128)S(1)} %slice.84), channel_id=1, source_target_pairs={{16,0},{17,1},{18,2},{19,3},{20,4},{21,5},{22,6},{23,7},{24,8},{25... | collective-permute-start | bytes 294920 | tf_op jit(solution)/shard_map/ppermute | solution.py:38
  (52 shorter events, 14.4 us)
Async XLA Ops:
  0.6 63.6 %copy-start.3 = (s32[640]{0:T(1024)S(1)}, s32[640]{0:T(1024)}, u32[]{:S(2)}) copy-start(s32[640]{0:T(1024)} %constant.33.clone) | copy-start | bytes 7684
  0.6 63.6 %copy-start.2 = (s32[20480]{0:T(1024)S(1)}, s32[20480]{0:T(1024)}, u32[]{:S(2)}) copy-start(s32[20480]{0:T(1024)} %param.6) | copy-start | bytes 245764
  1.6 3.5 %collective-permute-start = (f32[40,512]{1,0:T(8,128)S(1)}, f32[40,512]{1,0:T(8,128)S(1)}, u32[]{:S(2)}, u32[]{:S(2)}) collective-permute-start(f32[40,512]{1,0:T(8,128)S(1)} %get-tuple-element.33), channel_id=1, source_target_pairs={{16,0},{17,1},{18,2},{19,3},{20,4},{21,5},{22,6},{23,7},{24,8},{25... | collective-permute-start | bytes 245768 | tf_op jit(solution)/shard_map/ppermute | solution.py:38
  5.2 14.5 %collective-permute-start.1 = (f32[80,512]{1,0:T(8,128)S(1)}, f32[80,512]{1,0:T(8,128)S(1)}, u32[]{:S(2)}, u32[]{:S(2)}) collective-permute-start(f32[80,512]{1,0:T(8,128)S(1)} %get-tuple-element.31), channel_id=1, source_target_pairs={{2,0},{3,1},{0,2},{1,3},{6,4},{7,5},{4,6},{5,7},{10,8},{11,9},{8,1... | collective-permute-start | bytes 491528 | tf_op jit(solution)/shard_map/ppermute | solution.py:38
  14.0 15.3 %collective-permute-start.2 = (f32[80,512]{1,0:T(8,128)S(1)}, f32[80,512]{1,0:T(8,128)S(1)}, u32[]{:S(2)}, u32[]{:S(2)}) collective-permute-start(f32[80,512]{1,0:T(8,128)S(1)} %get-tuple-element.31), channel_id=1, source_target_pairs={{1,0},{0,1},{3,2},{2,3},{5,4},{4,5},{7,6},{6,7},{9,8},{8,9},{11,10... | collective-permute-start | bytes 491528 | tf_op jit(solution)/shard_map/ppermute | solution.py:38
  19.6 17.6 %collective-permute-start.3 = (f32[80,512]{1,0:T(8,128)S(1)}, f32[80,512]{1,0:T(8,128)S(1)}, u32[]{:S(2)}, u32[]{:S(2)}) collective-permute-start(f32[80,512]{1,0:T(8,128)S(1)} %collective-permute-done.1), channel_id=1, source_target_pairs={{1,0},{0,1},{3,2},{2,3},{5,4},{4,5},{7,6},{6,7},{9,8},{8,9},{11,10... | collective-permute-start | bytes 491528 | tf_op jit(solution)/shard_map/ppermute | solution.py:38
  37.3 12.2 %collective-permute-start.4 = (f32[4,80,512]{2,1,0:T(8,128)S(1)}, f32[4,80,512]{2,1,0:T(8,128)S(1)}, u32[]{:S(2)}, u32[]{:S(2)}) collective-permute-start(f32[4,80,512]{2,1,0:T(8,128)S(1)} %pad_maximum_fusion.2.refs_0_), channel_id=1, source_target_pairs={{128,0},{129,1},{130,2},{131,3},{132,4},{133,5},{134,6},{135,7},{1... | collective-permute-start | bytes 1966088 | tf_op jit(solution)/shard_map/ppermute | solution.py:38
  41.9 17.2 %collective-permute-start.5 = (f32[4,80,512]{2,1,0:T(8,128)S(1)}, f32[4,80,512]{2,1,0:T(8,128)S(1)}, u32[]{:S(2)}, u32[]{:S(2)}) collective-permute-start(f32[4,80,512]{2,1,0:T(8,128)S(1)} %pad_maximum_fusion.2.refs_0_), channel_id=1, source_target_pairs={{384,0},{385,1},{386,2},{387,3},{388,4},{389,5},{390,6},{391,7},{3... | collective-permute-start | bytes 1966088 | tf_op jit(solution)/shard_map/ppermute | solution.py:38
  49.5 12.8 %collective-permute-start.6 = (f32[4,80,512]{2,1,0:T(8,128)S(1)}, f32[4,80,512]{2,1,0:T(8,128)S(1)}, u32[]{:S(2)}, u32[]{:S(2)}) collective-permute-start(f32[4,80,512]{2,1,0:T(8,128)S(1)} %collective-permute-done.4.refs_1_), channel_id=1, source_target_pairs={{128,0},{129,1},{130,2},{131,3},{132,4},{133,5},{134,6},{135,7},{1... | collective-permute-start | bytes 1966088 | tf_op jit(solution)/shard_map/ppermute | solution.py:38
  54.8 10.2 %collective-permute-start.7 = (f32[4,80,512]{2,1,0:T(8,128)S(1)}, f32[4,80,512]{2,1,0:T(8,128)}, u32[]{:S(2)}, u32[]{:S(2)}) collective-permute-start(f32[4,80,512]{2,1,0:T(8,128)S(1)} %pad_maximum_fusion.2.refs_0_), channel_id=1, source_target_pairs={{16,0},{17,1},{18,2},{19,3},{20,4},{21,5},{22,6},{23,7},{24,8},{25... | collective-permute-start | bytes 1966088 | tf_op jit(solution)/shard_map/ppermute | solution.py:38
  56.7 8.3 %collective-permute-start.8 = (f32[4,80,512]{2,1,0:T(8,128)S(1)}, f32[4,80,512]{2,1,0:T(8,128)}, u32[]{:S(2)}, u32[]{:S(2)}) collective-permute-start(f32[4,80,512]{2,1,0:T(8,128)S(1)} %collective-permute-done.4.refs_1_), channel_id=1, source_target_pairs={{16,0},{17,1},{18,2},{19,3},{20,4},{21,5},{22,6},{23,7},{24,8},{25... | collective-permute-start | bytes 1966088 | tf_op jit(solution)/shard_map/ppermute | solution.py:38
  59.1 5.9 %collective-permute-start.9 = (f32[4,80,512]{2,1,0:T(8,128)S(1)}, f32[4,80,512]{2,1,0:T(8,128)}, u32[]{:S(2)}, u32[]{:S(2)}) collective-permute-start(f32[4,80,512]{2,1,0:T(8,128)S(1)} %collective-permute-done.5.refs_2_), channel_id=1, source_target_pairs={{16,0},{17,1},{18,2},{19,3},{20,4},{21,5},{22,6},{23,7},{24,8},{25... | collective-permute-start | bytes 1966088 | tf_op jit(solution)/shard_map/ppermute | solution.py:38
  62.3 4.1 %collective-permute-start.10 = (f32[4,80,512]{2,1,0:T(8,128)S(1)}, f32[4,80,512]{2,1,0:T(8,128)}, u32[]{:S(2)}, u32[]{:S(2)}) collective-permute-start(f32[4,80,512]{2,1,0:T(8,128)S(1)} %collective-permute-done.6.refs_3_), channel_id=1, source_target_pairs={{16,0},{17,1},{18,2},{19,3},{20,4},{21,5},{22,6},{23,7},{24,8},{25... | collective-permute-start | bytes 1966088 | tf_op jit(solution)/shard_map/ppermute | solution.py:38
  76.4 3.1 %collective-permute-start.11 = (f32[1,1408]{1,0:T(1,128)S(1)}, f32[1,1408]{1,0:T(1,128)S(1)}, u32[]{:S(2)}, u32[]{:S(2)}) collective-permute-start(f32[1,1408]{1,0:T(1,128)S(1)} %get-tuple-element.15), channel_id=1, source_target_pairs={{16,0},{17,1},{18,2},{19,3},{20,4},{21,5},{22,6},{23,7},{24,8},{25... | collective-permute-start | bytes 16904 | tf_op jit(solution)/shard_map/ppermute | solution.py:38
  104.0 3.1 %collective-permute-start.12 = (f32[1,1408]{1,0:T(1,128)S(1)}, f32[1,1408]{1,0:T(1,128)S(1)}, u32[]{:S(2)}, u32[]{:S(2)}) collective-permute-start(f32[1,1408]{1,0:T(1,128)S(1)} %reduce_sum.12.sums), channel_id=1, source_target_pairs={{16,0},{17,1},{18,2},{19,3},{20,4},{21,5},{22,6},{23,7},{24,8},{25... | collective-permute-start | bytes 16904 | tf_op jit(solution)/shard_map/ppermute | solution.py:38
  117.9 5.1 %collective-permute-start.14 = (f32[2,4,88,512]{3,2,1,0:T(8,128)S(1)}, f32[2,4,88,512]{3,2,1,0:T(8,128)S(1)}, u32[]{:S(2)}, u32[]{:S(2)}) collective-permute-start(f32[2,4,88,512]{3,2,1,0:T(8,128)S(1)} %get-tuple-element.21), channel_id=1, source_target_pairs={{16,0},{17,1},{18,2},{19,3},{20,4},{21,5},{22,6},{23,7},{24,8},{25... | collective-permute-start | bytes 4325384 | tf_op jit(solution)/shard_map/ppermute | solution.py:38
  120.0 10.0 %collective-permute-start.13 = (f32[2,4,88,512]{3,2,1,0:T(8,128)}, f32[2,4,88,512]{3,2,1,0:T(8,128)S(1)}, u32[]{:S(2)}, u32[]{:S(2)}) collective-permute-start(f32[2,4,88,512]{3,2,1,0:T(8,128)} %get-tuple-element.19), channel_id=1, source_target_pairs={{16,0},{17,1},{18,2},{19,3},{20,4},{21,5},{22,6},{23,7},{24,8},{25... | collective-permute-start | bytes 4325384 | tf_op jit(solution)/shard_map/ppermute | solution.py:38
  123.4 9.7 %collective-permute-start.15 = (f32[2,88,512]{2,1,0:T(8,128)S(1)}, f32[2,88,512]{2,1,0:T(8,128)S(1)}, u32[]{:S(2)}, u32[]{:S(2)}) collective-permute-start(f32[2,88,512]{2,1,0:T(8,128)S(1)} %get-tuple-element.27), channel_id=1, source_target_pairs={{384,0},{385,1},{386,2},{387,3},{388,4},{389,5},{390,6},{391,7},{3... | collective-permute-start | bytes 1081352 | tf_op jit(solution)/shard_map/ppermute | solution.py:38
  125.4 9.8 %collective-permute-start.17 = (f32[2,88,512]{2,1,0:T(8,128)S(1)}, f32[2,88,512]{2,1,0:T(8,128)S(1)}, u32[]{:S(2)}, u32[]{:S(2)}) collective-permute-start(f32[2,88,512]{2,1,0:T(8,128)S(1)} %get-tuple-element.26), channel_id=1, source_target_pairs={{128,0},{129,1},{130,2},{131,3},{132,4},{133,5},{134,6},{135,7},{1... | collective-permute-start | bytes 1081352 | tf_op jit(solution)/shard_map/ppermute | solution.py:38
  133.2 13.5 %collective-permute-start.16 = (f32[4,88,512]{2,1,0:T(8,128)S(1)}, f32[4,88,512]{2,1,0:T(8,128)S(1)}, u32[]{:S(2)}, u32[]{:S(2)}) collective-permute-start(f32[4,88,512]{2,1,0:T(8,128)S(1)} %pad_maximum_fusion), channel_id=1, source_target_pairs={{384,0},{385,1},{386,2},{387,3},{388,4},{389,5},{390,6},{391,7},{3... | collective-permute-start | bytes 2162696 | tf_op jit(solution)/shard_map/ppermute | solution.py:38
  135.3 12.8 %collective-permute-start.18 = (f32[4,88,512]{2,1,0:T(8,128)S(1)}, f32[4,88,512]{2,1,0:T(8,128)S(1)}, u32[]{:S(2)}, u32[]{:S(2)}) collective-permute-start(f32[4,88,512]{2,1,0:T(8,128)S(1)} %pad_maximum_fusion.1), channel_id=1, source_target_pairs={{128,0},{129,1},{130,2},{131,3},{132,4},{133,5},{134,6},{135,7},{1... | collective-permute-start | bytes 2162696 | tf_op jit(solution)/shard_map/ppermute | solution.py:38
  148.3 31.1 %copy-start = (f32[40,512]{1,0:T(8,128)S(1)}, f32[40,512]{1,0:T(8,128)}, u32[]{:S(2)}) copy-start(f32[40,512]{1,0:T(8,128)} %packet.1) | copy-start | bytes 245764
  148.3 31.1 %copy-start.1 = (f32[40,512]{1,0:T(8,128)S(1)}, f32[40,512]{1,0:T(8,128)}, u32[]{:S(2)}) copy-start(f32[40,512]{1,0:T(8,128)} %header.1) | copy-start | bytes 245764
  148.3 16.4 %collective-permute-start.19 = (f32[88,512]{1,0:T(8,128)S(1)}, f32[88,512]{1,0:T(8,128)S(1)}, u32[]{:S(2)}, u32[]{:S(2)}) collective-permute-start(f32[88,512]{1,0:T(8,128)S(1)} %get-tuple-element.28), channel_id=1, source_target_pairs={{1,0},{0,1},{3,2},{2,3},{5,4},{4,5},{7,6},{6,7},{9,8},{8,9},{11,10... | collective-permute-start | bytes 540680 | tf_op jit(solution)/shard_map/ppermute | solution.py:38
  150.4 16.3 %collective-permute-start.21 = (f32[88,512]{1,0:T(8,128)S(1)}, f32[88,512]{1,0:T(8,128)S(1)}, u32[]{:S(2)}, u32[]{:S(2)}) collective-permute-start(f32[88,512]{1,0:T(8,128)S(1)} %get-tuple-element.29), channel_id=1, source_target_pairs={{1,0},{0,1},{3,2},{2,3},{5,4},{4,5},{7,6},{6,7},{9,8},{8,9},{11,10... | collective-permute-start | bytes 540680 | tf_op jit(solution)/shard_map/ppermute | solution.py:38
  164.8 11.3 %collective-permute-start.20 = (f32[88,512]{1,0:T(8,128)S(1)}, f32[88,512]{1,0:T(8,128)S(1)}, u32[]{:S(2)}, u32[]{:S(2)}) collective-permute-start(f32[88,512]{1,0:T(8,128)S(1)} %fusion.4), channel_id=1, source_target_pairs={{2,0},{3,1},{0,2},{1,3},{6,4},{7,5},{4,6},{5,7},{10,8},{11,9},{8,1... | collective-permute-start | bytes 540680 | tf_op jit(solution)/shard_map/ppermute | solution.py:38
  176.2 3.2 %collective-permute-start.22 = (f32[48,512]{1,0:T(8,128)S(1)}, f32[48,512]{1,0:T(8,128)S(1)}, u32[]{:S(2)}, u32[]{:S(2)}) collective-permute-start(f32[48,512]{1,0:T(8,128)S(1)} %slice.84), channel_id=1, source_target_pairs={{16,0},{17,1},{18,2},{19,3},{20,4},{21,5},{22,6},{23,7},{24,8},{25... | collective-permute-start | bytes 294920 | tf_op jit(solution)/shard_map/ppermute | solution.py:38

commit v9 on v8

--- a/solution.py
+++ b/solution.py
@@ -146,9 +146,9 @@
 
     def fill(rows_in, cols_in, other):
         for j, k, block in col_blocks(y, zh, zl):
-            block_at(hunit, block)[...] = unit(cols_in[j][k, other * B : (other + 1) * B, :])
+            block_at(hunit, block)[...] = cols_in[j][k, other * B : (other + 1) * B, :]
         for j, k, core, block in row_blocks(x, zl):
-            block_at(punit, block)[...] = unit(rows_in[j][k, core * B : (core + 1) * B, :])
+            block_at(punit, block)[...] = rows_in[j][k, core * B : (core + 1) * B, :]
 
     @pl.when(c == 0)
     def _():
@@ -158,6 +158,7 @@
     def _():
         fill(others, mine, 0)
 
+    hunit[...] = unit(hunit[...])
     hh[...], hlow[...] = split(hunit[...])
     turned_high, turned_low = split(hunit[...].T)
     whole = [
@@ -178,7 +179,7 @@
     total = positive = jnp.zeros((8, COLS), jnp.float32)
     for i in range(ROWS // STEP):
         here = pl.ds(i * STEP, STEP)
-        high, low = split(punit[here, :])
+        high, low = split(unit(punit[here, :]))
         ph[here, :] = high
         plow[here, :] = low
         cosines = product(high, low, turned_high, turned_low, ((1,), (0,)))

time: 182 us -> 182 us (level)
  no operation moved by 1% of the time
where the time goes in v9:
time: 182 us; the launch traced here: 181 us
  starting transfers between devices  80.3 us (44%)
  waiting for transfers between devices  49.7 us (27%)
  blocking collectives  24.4 us (13%)
  Pallas kernels  21.9 us (12%)
  other arithmetic  2.23 us (1%)
    ppermute x23, starting transfers between devices, permute(): return lax.ppermute(value, ALL, pairs)  80.3 us
    ppermute x23, waiting for transfers between devices, permute(): return lax.ppermute(value, ALL, pairs)  49.7 us
    all_to_all x1, blocking collectives, per_device(): lax.all_to_all(jnp.broadcast_to((keep + swap_core(send))[None], (16, 1, S...  24.4 us
    pallas_call x3, Pallas kernels, call(): pl.pallas_call(kernel, in_specs=[IN_SMEM] + in_specs, out_specs=out_specs...  21.9 us
  transfers between devices with their start and end apart: 23, of which 15 were waited for; matrix products, arithmetic and copies ran while one was open for 1% of the time, Pallas kernels for 0%

profile of v9, /device:TPU:39, one launch (start us, length us, event | category | flops | bytes accessed | tf_op | source)
XLA Modules:
  0.0 180.8 jit_solution(17850053213306680756)
XLA Ops:
  1.6 2.6 %collective-permute-start = (f32[40,512]{1,0:T(8,128)S(1)}, f32[40,512]{1,0:T(8,128)S(1)}, u32[]{:S(2)}, u32[]{:S(2)}) collective-permute-start(f32[40,512]{1,0:T(8,128)S(1)} %get-tuple-element.33), channel_id=1, source_target_pairs={{16,0},{17,1},{18,2},{19,3},{20,4},{21,5},{22,6},{23,7},{24,8},{25... | collective-permute-start | bytes 245768 | tf_op jit(solution)/shard_map/ppermute | solution.py:38
  5.2 8.8 %collective-permute-start.1 = (f32[80,512]{1,0:T(8,128)S(1)}, f32[80,512]{1,0:T(8,128)S(1)}, u32[]{:S(2)}, u32[]{:S(2)}) collective-permute-start(f32[80,512]{1,0:T(8,128)S(1)} %get-tuple-element.31), channel_id=1, source_target_pairs={{2,0},{3,1},{0,2},{1,3},{6,4},{7,5},{4,6},{5,7},{10,8},{11,9},{8,1... | collective-permute-start | bytes 491528 | tf_op jit(solution)/shard_map/ppermute | solution.py:38
  14.0 4.7 %collective-permute-start.2 = (f32[80,512]{1,0:T(8,128)S(1)}, f32[80,512]{1,0:T(8,128)S(1)}, u32[]{:S(2)}, u32[]{:S(2)}) collective-permute-start(f32[80,512]{1,0:T(8,128)S(1)} %get-tuple-element.31), channel_id=1, source_target_pairs={{1,0},{0,1},{3,2},{2,3},{5,4},{4,5},{7,6},{6,7},{9,8},{8,9},{11,10... | collective-permute-start | bytes 491528 | tf_op jit(solution)/shard_map/ppermute | solution.py:38
  19.6 9.6 %collective-permute-start.3 = (f32[80,512]{1,0:T(8,128)S(1)}, f32[80,512]{1,0:T(8,128)S(1)}, u32[]{:S(2)}, u32[]{:S(2)}) collective-permute-start(f32[80,512]{1,0:T(8,128)S(1)} %collective-permute-done.1), channel_id=1, source_target_pairs={{1,0},{0,1},{3,2},{2,3},{5,4},{4,5},{7,6},{6,7},{9,8},{8,9},{11,10... | collective-permute-start | bytes 491528 | tf_op jit(solution)/shard_map/ppermute | solution.py:38
  29.2 8.0 %collective-permute-done.3 = f32[80,512]{1,0:T(8,128)S(1)} collective-permute-done((f32[80,512]{1,0:T(8,128)S(1)}, f32[80,512]{1,0:T(8,128)S(1)}, u32[]{:S(2)}, u32[]{:S(2)}) %collective-permute-start.3) | collective-permute-done | bytes 163872 | tf_op jit(solution)/shard_map/ppermute | solution.py:38
  37.3 4.6 %collective-permute-start.4 = (f32[4,80,512]{2,1,0:T(8,128)S(1)}, f32[4,80,512]{2,1,0:T(8,128)S(1)}, u32[]{:S(2)}, u32[]{:S(2)}) collective-permute-start(f32[4,80,512]{2,1,0:T(8,128)S(1)} %pad_maximum_fusion.2.refs_0_), channel_id=1, source_target_pairs={{128,0},{129,1},{130,2},{131,3},{132,4},{133,5},{134,6},{135,7},{1... | collective-permute-start | bytes 1966088 | tf_op jit(solution)/shard_map/ppermute | solution.py:38
  41.9 1.9 %collective-permute-start.5 = (f32[4,80,512]{2,1,0:T(8,128)S(1)}, f32[4,80,512]{2,1,0:T(8,128)S(1)}, u32[]{:S(2)}, u32[]{:S(2)}) collective-permute-start(f32[4,80,512]{2,1,0:T(8,128)S(1)} %pad_maximum_fusion.2.refs_0_), channel_id=1, source_target_pairs={{384,0},{385,1},{386,2},{387,3},{388,4},{389,5},{390,6},{391,7},{3... | collective-permute-start | bytes 1966088 | tf_op jit(solution)/shard_map/ppermute | solution.py:38
  43.9 5.6 %collective-permute-done.4.refs_1_ = f32[4,80,512]{2,1,0:T(8,128)S(1)} collective-permute-done((f32[4,80,512]{2,1,0:T(8,128)S(1)}, f32[4,80,512]{2,1,0:T(8,128)S(1)}, u32[]{:S(2)}, u32[]{:S(2)}) %collective-permute-start.4) | collective-permute-done | bytes 655392 | tf_op jit(solution)/shard_map/ppermute | solution.py:38
  49.5 5.3 %collective-permute-start.6 = (f32[4,80,512]{2,1,0:T(8,128)S(1)}, f32[4,80,512]{2,1,0:T(8,128)S(1)}, u32[]{:S(2)}, u32[]{:S(2)}) collective-permute-start(f32[4,80,512]{2,1,0:T(8,128)S(1)} %collective-permute-done.4.refs_1_), channel_id=1, source_target_pairs={{128,0},{129,1},{130,2},{131,3},{132,4},{133,5},{134,6},{135,7},{1... | collective-permute-start | bytes 1966088 | tf_op jit(solution)/shard_map/ppermute | solution.py:38
  54.8 1.9 %collective-permute-start.7 = (f32[4,80,512]{2,1,0:T(8,128)S(1)}, f32[4,80,512]{2,1,0:T(8,128)}, u32[]{:S(2)}, u32[]{:S(2)}) collective-permute-start(f32[4,80,512]{2,1,0:T(8,128)S(1)} %pad_maximum_fusion.2.refs_0_), channel_id=1, source_target_pairs={{16,0},{17,1},{18,2},{19,3},{20,4},{21,5},{22,6},{23,7},{24,8},{25... | collective-permute-start | bytes 1966088 | tf_op jit(solution)/shard_map/ppermute | solution.py:38
  56.7 2.4 %collective-permute-start.8 = (f32[4,80,512]{2,1,0:T(8,128)S(1)}, f32[4,80,512]{2,1,0:T(8,128)}, u32[]{:S(2)}, u32[]{:S(2)}) collective-permute-start(f32[4,80,512]{2,1,0:T(8,128)S(1)} %collective-permute-done.4.refs_1_), channel_id=1, source_target_pairs={{16,0},{17,1},{18,2},{19,3},{20,4},{21,5},{22,6},{23,7},{24,8},{25... | collective-permute-start | bytes 1966088 | tf_op jit(solution)/shard_map/ppermute | solution.py:38
  59.1 1.9 %collective-permute-start.9 = (f32[4,80,512]{2,1,0:T(8,128)S(1)}, f32[4,80,512]{2,1,0:T(8,128)}, u32[]{:S(2)}, u32[]{:S(2)}) collective-permute-start(f32[4,80,512]{2,1,0:T(8,128)S(1)} %collective-permute-done.5.refs_2_), channel_id=1, source_target_pairs={{16,0},{17,1},{18,2},{19,3},{20,4},{21,5},{22,6},{23,7},{24,8},{25... | collective-permute-start | bytes 1966088 | tf_op jit(solution)/shard_map/ppermute | solution.py:38
  62.3 1.9 %collective-permute-start.10 = (f32[4,80,512]{2,1,0:T(8,128)S(1)}, f32[4,80,512]{2,1,0:T(8,128)}, u32[]{:S(2)}, u32[]{:S(2)}) collective-permute-start(f32[4,80,512]{2,1,0:T(8,128)S(1)} %collective-permute-done.6.refs_3_), channel_id=1, source_target_pairs={{16,0},{17,1},{18,2},{19,3},{20,4},{21,5},{22,6},{23,7},{24,8},{25... | collective-permute-start | bytes 1966088 | tf_op jit(solution)/shard_map/ppermute | solution.py:38
  66.4 9.7 %shard_map.67 = (f32[7680,640]{1,0:T(8,128)}, bf16[20480,512]{1,0:T(8,128)(2,1)}, f32[1,1408]{1,0:T(1,128)S(1)}, f32[1,1408]{1,0:T(1,128)S(1)}) custom-call(s32[5]{0:T(128)S(1)} %stack.38.place, s32[1,640]{1,0:T(1,128)S(1)} %add.54.ids, s32[1280,1]{1,0:T(8,128)S(1)} %reshape.25.wanted, f32[4,80,512]{2,1,0:T(8,128)S(1)} %pad_maximum_fusion.2.refs_0_, ...), custom_call_target="tpu_custom_call" | custom-call | flops 2516582400 | bytes 8388608 | tf_op jit(solution)/shard_map/pallas_call | solution.py:317
  76.1 2.0 %collective-permute-start.11 = (f32[1,1408]{1,0:T(1,128)S(1)}, f32[1,1408]{1,0:T(1,128)S(1)}, u32[]{:S(2)}, u32[]{:S(2)}) collective-permute-start(f32[1,1408]{1,0:T(1,128)S(1)} %get-tuple-element.15), channel_id=1, source_target_pairs={{16,0},{17,1},{18,2},{19,3},{20,4},{21,5},{22,6},{23,7},{24,8},{25... | collective-permute-start | bytes 16904 | tf_op jit(solution)/shard_map/ppermute | solution.py:38
  79.3 24.4 %all_to_all.5 = f32[16,1,1408]{2,1,0:T(1,128)S(1)} all-to-all(f32[16,1,1408]{2,1,0:T(1,128)S(1)} %broadcast_in_dim.10), channel_id=1, replica_groups={{0,1,2,3,128,129,130,131,256,257,258,259,384,385,386,387},{16,20,24,28,..., dimensions={0} | all-to-all | bytes 180224 | tf_op jit(solution)/shard_map/all_to_all | solution.py:393
  103.8 2.1 %collective-permute-start.12 = (f32[1,1408]{1,0:T(1,128)S(1)}, f32[1,1408]{1,0:T(1,128)S(1)}, u32[]{:S(2)}, u32[]{:S(2)}) collective-permute-start(f32[1,1408]{1,0:T(1,128)S(1)} %reduce_sum.12.sums), channel_id=1, source_target_pairs={{16,0},{17,1},{18,2},{19,3},{20,4},{21,5},{22,6},{23,7},{24,8},{25... | collective-permute-start | bytes 16904 | tf_op jit(solution)/shard_map/ppermute | solution.py:38
  106.8 10.8 %shard_map.68 = (f32[2,4,88,512]{3,2,1,0:T(8,128)S(1)}, f32[2,4,88,512]{3,2,1,0:T(8,128)S(1)}, f32[2,4,88,512]{3,2,1,0:T(8,128)S(1)}, f32[2,4,88,512]{3,2,1,0:T(8,128)}) custom-call(s32[5]{0:T(128)S(1)} %stack.38.place, s32[1,640]{1,0:T(1,128)S(1)} %add.54.ids, s32[1280,1]{1,0:T(8,128)S(1)} %reshape.25.wanted, f32[1,1408]{1,0:T(1,128)S(1)} %reduce_sum.12.sums, ...), custom_call_target="tpu_custom_call" | custom-call | flops 5033164800 | bytes 8388608 | tf_op jit(solution)/shard_map/pallas_call | solution.py:317
  117.7 2.1 %collective-permute-start.14 = (f32[2,4,88,512]{3,2,1,0:T(8,128)S(1)}, f32[2,4,88,512]{3,2,1,0:T(8,128)S(1)}, u32[]{:S(2)}, u32[]{:S(2)}) collective-permute-start(f32[2,4,88,512]{3,2,1,0:T(8,128)S(1)} %get-tuple-element.21), channel_id=1, source_target_pairs={{16,0},{17,1},{18,2},{19,3},{20,4},{21,5},{22,6},{23,7},{24,8},{25... | collective-permute-start | bytes 4325384 | tf_op jit(solution)/shard_map/ppermute | solution.py:38
  119.7 2.3 %collective-permute-start.13 = (f32[2,4,88,512]{3,2,1,0:T(8,128)}, f32[2,4,88,512]{3,2,1,0:T(8,128)S(1)}, u32[]{:S(2)}, u32[]{:S(2)}) collective-permute-start(f32[2,4,88,512]{3,2,1,0:T(8,128)} %get-tuple-element.19), channel_id=1, source_target_pairs={{16,0},{17,1},{18,2},{19,3},{20,4},{21,5},{22,6},{23,7},{24,8},{25... | collective-permute-start | bytes 4325384 | tf_op jit(solution)/shard_map/ppermute | solution.py:38
  123.2 1.9 %collective-permute-start.15 = (f32[2,88,512]{2,1,0:T(8,128)S(1)}, f32[2,88,512]{2,1,0:T(8,128)S(1)}, u32[]{:S(2)}, u32[]{:S(2)}) collective-permute-start(f32[2,88,512]{2,1,0:T(8,128)S(1)} %get-tuple-element.27), channel_id=1, source_target_pairs={{384,0},{385,1},{386,2},{387,3},{388,4},{389,5},{390,6},{391,7},{3... | collective-permute-start | bytes 1081352 | tf_op jit(solution)/shard_map/ppermute | solution.py:38
  125.1 4.6 %collective-permute-start.17 = (f32[2,88,512]{2,1,0:T(8,128)S(1)}, f32[2,88,512]{2,1,0:T(8,128)S(1)}, u32[]{:S(2)}, u32[]{:S(2)}) collective-permute-start(f32[2,88,512]{2,1,0:T(8,128)S(1)} %get-tuple-element.26), channel_id=1, source_target_pairs={{128,0},{129,1},{130,2},{131,3},{132,4},{133,5},{134,6},{135,7},{1... | collective-permute-start | bytes 1081352 | tf_op jit(solution)/shard_map/ppermute | solution.py:38
  130.1 2.8 %collective-permute-done.15 = f32[2,88,512]{2,1,0:T(8,128)S(1)} collective-permute-done((f32[2,88,512]{2,1,0:T(8,128)S(1)}, f32[2,88,512]{2,1,0:T(8,128)S(1)}, u32[]{:S(2)}, u32[]{:S(2)}) %collective-permute-start.15) | collective-permute-done | bytes 360480 | tf_op jit(solution)/shard_map/ppermute | solution.py:38
  133.0 1.9 %collective-permute-start.16 = (f32[4,88,512]{2,1,0:T(8,128)S(1)}, f32[4,88,512]{2,1,0:T(8,128)S(1)}, u32[]{:S(2)}, u32[]{:S(2)}) collective-permute-start(f32[4,88,512]{2,1,0:T(8,128)S(1)} %pad_maximum_fusion), channel_id=1, source_target_pairs={{384,0},{385,1},{386,2},{387,3},{388,4},{389,5},{390,6},{391,7},{3... | collective-permute-start | bytes 2162696 | tf_op jit(solution)/shard_map/ppermute | solution.py:38
  135.1 4.6 %collective-permute-start.18 = (f32[4,88,512]{2,1,0:T(8,128)S(1)}, f32[4,88,512]{2,1,0:T(8,128)S(1)}, u32[]{:S(2)}, u32[]{:S(2)}) collective-permute-start(f32[4,88,512]{2,1,0:T(8,128)S(1)} %pad_maximum_fusion.1), channel_id=1, source_target_pairs={{128,0},{129,1},{130,2},{131,3},{132,4},{133,5},{134,6},{135,7},{1... | collective-permute-start | bytes 2162696 | tf_op jit(solution)/shard_map/ppermute | solution.py:38
  139.6 6.9 %collective-permute-done.16 = f32[4,88,512]{2,1,0:T(8,128)S(1)} collective-permute-done((f32[4,88,512]{2,1,0:T(8,128)S(1)}, f32[4,88,512]{2,1,0:T(8,128)S(1)}, u32[]{:S(2)}, u32[]{:S(2)}) %collective-permute-start.16) | collective-permute-done | bytes 720928 | tf_op jit(solution)/shard_map/ppermute | solution.py:38
  148.1 2.1 %collective-permute-start.19 = (f32[88,512]{1,0:T(8,128)S(1)}, f32[88,512]{1,0:T(8,128)S(1)}, u32[]{:S(2)}, u32[]{:S(2)}) collective-permute-start(f32[88,512]{1,0:T(8,128)S(1)} %get-tuple-element.28), channel_id=1, source_target_pairs={{1,0},{0,1},{3,2},{2,3},{5,4},{4,5},{7,6},{6,7},{9,8},{8,9},{11,10... | collective-permute-start | bytes 540680 | tf_op jit(solution)/shard_map/ppermute | solution.py:38
  150.2 7.3 %collective-permute-start.21 = (f32[88,512]{1,0:T(8,128)S(1)}, f32[88,512]{1,0:T(8,128)S(1)}, u32[]{:S(2)}, u32[]{:S(2)}) collective-permute-start(f32[88,512]{1,0:T(8,128)S(1)} %get-tuple-element.29), channel_id=1, source_target_pairs={{1,0},{0,1},{3,2},{2,3},{5,4},{4,5},{7,6},{6,7},{9,8},{8,9},{11,10... | collective-permute-start | bytes 540680 | tf_op jit(solution)/shard_map/ppermute | solution.py:38
  157.5 7.1 %collective-permute-done.19 = f32[88,512]{1,0:T(8,128)S(1)} collective-permute-done((f32[88,512]{1,0:T(8,128)S(1)}, f32[88,512]{1,0:T(8,128)S(1)}, u32[]{:S(2)}, u32[]{:S(2)}) %collective-permute-start.19) | collective-permute-done | bytes 180256 | tf_op jit(solution)/shard_map/ppermute | solution.py:38
  164.6 1.9 %collective-permute-start.20 = (f32[88,512]{1,0:T(8,128)S(1)}, f32[88,512]{1,0:T(8,128)S(1)}, u32[]{:S(2)}, u32[]{:S(2)}) collective-permute-start(f32[88,512]{1,0:T(8,128)S(1)} %fusion.4), channel_id=1, source_target_pairs={{2,0},{3,1},{0,2},{1,3},{6,4},{7,5},{4,6},{5,7},{10,8},{11,9},{8,1... | collective-permute-start | bytes 540680 | tf_op jit(solution)/shard_map/ppermute | solution.py:38
  166.5 9.5 %collective-permute-done.20 = f32[88,512]{1,0:T(8,128)S(1)} collective-permute-done((f32[88,512]{1,0:T(8,128)S(1)}, f32[88,512]{1,0:T(8,128)S(1)}, u32[]{:S(2)}, u32[]{:S(2)}) %collective-permute-start.20) | collective-permute-done | bytes 180256 | tf_op jit(solution)/shard_map/ppermute | solution.py:38
  176.1 1.9 %collective-permute-start.22 = (f32[48,512]{1,0:T(8,128)S(1)}, f32[48,512]{1,0:T(8,128)S(1)}, u32[]{:S(2)}, u32[]{:S(2)}) collective-permute-start(f32[48,512]{1,0:T(8,128)S(1)} %slice.84), channel_id=1, source_target_pairs={{16,0},{17,1},{18,2},{19,3},{20,4},{21,5},{22,6},{23,7},{24,8},{25... | collective-permute-start | bytes 294920 | tf_op jit(solution)/shard_map/ppermute | solution.py:38
  (52 shorter events, 14.4 us)
Async XLA Ops:
  0.6 63.6 %copy-start.3 = (s32[640]{0:T(1024)S(1)}, s32[640]{0:T(1024)}, u32[]{:S(2)}) copy-start(s32[640]{0:T(1024)} %constant.33.clone) | copy-start | bytes 7684
  0.6 63.6 %copy-start.2 = (s32[20480]{0:T(1024)S(1)}, s32[20480]{0:T(1024)}, u32[]{:S(2)}) copy-start(s32[20480]{0:T(1024)} %param.6) | copy-start | bytes 245764
  1.6 3.5 %collective-permute-start = (f32[40,512]{1,0:T(8,128)S(1)}, f32[40,512]{1,0:T(8,128)S(1)}, u32[]{:S(2)}, u32[]{:S(2)}) collective-permute-start(f32[40,512]{1,0:T(8,128)S(1)} %get-tuple-element.33), channel_id=1, source_target_pairs={{16,0},{17,1},{18,2},{19,3},{20,4},{21,5},{22,6},{23,7},{24,8},{25... | collective-permute-start | bytes 245768 | tf_op jit(solution)/shard_map/ppermute | solution.py:38
  5.2 14.5 %collective-permute-start.1 = (f32[80,512]{1,0:T(8,128)S(1)}, f32[80,512]{1,0:T(8,128)S(1)}, u32[]{:S(2)}, u32[]{:S(2)}) collective-permute-start(f32[80,512]{1,0:T(8,128)S(1)} %get-tuple-element.31), channel_id=1, source_target_pairs={{2,0},{3,1},{0,2},{1,3},{6,4},{7,5},{4,6},{5,7},{10,8},{11,9},{8,1... | collective-permute-start | bytes 491528 | tf_op jit(solution)/shard_map/ppermute | solution.py:38
  14.0 15.3 %collective-permute-start.2 = (f32[80,512]{1,0:T(8,128)S(1)}, f32[80,512]{1,0:T(8,128)S(1)}, u32[]{:S(2)}, u32[]{:S(2)}) collective-permute-start(f32[80,512]{1,0:T(8,128)S(1)} %get-tuple-element.31), channel_id=1, source_target_pairs={{1,0},{0,1},{3,2},{2,3},{5,4},{4,5},{7,6},{6,7},{9,8},{8,9},{11,10... | collective-permute-start | bytes 491528 | tf_op jit(solution)/shard_map/ppermute | solution.py:38
  19.6 17.6 %collective-permute-start.3 = (f32[80,512]{1,0:T(8,128)S(1)}, f32[80,512]{1,0:T(8,128)S(1)}, u32[]{:S(2)}, u32[]{:S(2)}) collective-permute-start(f32[80,512]{1,0:T(8,128)S(1)} %collective-permute-done.1), channel_id=1, source_target_pairs={{1,0},{0,1},{3,2},{2,3},{5,4},{4,5},{7,6},{6,7},{9,8},{8,9},{11,10... | collective-permute-start | bytes 491528 | tf_op jit(solution)/shard_map/ppermute | solution.py:38
  37.3 12.2 %collective-permute-start.4 = (f32[4,80,512]{2,1,0:T(8,128)S(1)}, f32[4,80,512]{2,1,0:T(8,128)S(1)}, u32[]{:S(2)}, u32[]{:S(2)}) collective-permute-start(f32[4,80,512]{2,1,0:T(8,128)S(1)} %pad_maximum_fusion.2.refs_0_), channel_id=1, source_target_pairs={{128,0},{129,1},{130,2},{131,3},{132,4},{133,5},{134,6},{135,7},{1... | collective-permute-start | bytes 1966088 | tf_op jit(solution)/shard_map/ppermute | solution.py:38
  41.9 17.2 %collective-permute-start.5 = (f32[4,80,512]{2,1,0:T(8,128)S(1)}, f32[4,80,512]{2,1,0:T(8,128)S(1)}, u32[]{:S(2)}, u32[]{:S(2)}) collective-permute-start(f32[4,80,512]{2,1,0:T(8,128)S(1)} %pad_maximum_fusion.2.refs_0_), channel_id=1, source_target_pairs={{384,0},{385,1},{386,2},{387,3},{388,4},{389,5},{390,6},{391,7},{3... | collective-permute-start | bytes 1966088 | tf_op jit(solution)/shard_map/ppermute | solution.py:38
  49.5 12.8 %collective-permute-start.6 = (f32[4,80,512]{2,1,0:T(8,128)S(1)}, f32[4,80,512]{2,1,0:T(8,128)S(1)}, u32[]{:S(2)}, u32[]{:S(2)}) collective-permute-start(f32[4,80,512]{2,1,0:T(8,128)S(1)} %collective-permute-done.4.refs_1_), channel_id=1, source_target_pairs={{128,0},{129,1},{130,2},{131,3},{132,4},{133,5},{134,6},{135,7},{1... | collective-permute-start | bytes 1966088 | tf_op jit(solution)/shard_map/ppermute | solution.py:38
  54.8 10.2 %collective-permute-start.7 = (f32[4,80,512]{2,1,0:T(8,128)S(1)}, f32[4,80,512]{2,1,0:T(8,128)}, u32[]{:S(2)}, u32[]{:S(2)}) collective-permute-start(f32[4,80,512]{2,1,0:T(8,128)S(1)} %pad_maximum_fusion.2.refs_0_), channel_id=1, source_target_pairs={{16,0},{17,1},{18,2},{19,3},{20,4},{21,5},{22,6},{23,7},{24,8},{25... | collective-permute-start | bytes 1966088 | tf_op jit(solution)/shard_map/ppermute | solution.py:38
  56.7 8.3 %collective-permute-start.8 = (f32[4,80,512]{2,1,0:T(8,128)S(1)}, f32[4,80,512]{2,1,0:T(8,128)}, u32[]{:S(2)}, u32[]{:S(2)}) collective-permute-start(f32[4,80,512]{2,1,0:T(8,128)S(1)} %collective-permute-done.4.refs_1_), channel_id=1, source_target_pairs={{16,0},{17,1},{18,2},{19,3},{20,4},{21,5},{22,6},{23,7},{24,8},{25... | collective-permute-start | bytes 1966088 | tf_op jit(solution)/shard_map/ppermute | solution.py:38
  59.1 5.9 %collective-permute-start.9 = (f32[4,80,512]{2,1,0:T(8,128)S(1)}, f32[4,80,512]{2,1,0:T(8,128)}, u32[]{:S(2)}, u32[]{:S(2)}) collective-permute-start(f32[4,80,512]{2,1,0:T(8,128)S(1)} %collective-permute-done.5.refs_2_), channel_id=1, source_target_pairs={{16,0},{17,1},{18,2},{19,3},{20,4},{21,5},{22,6},{23,7},{24,8},{25... | collective-permute-start | bytes 1966088 | tf_op jit(solution)/shard_map/ppermute | solution.py:38
  62.3 4.1 %collective-permute-start.10 = (f32[4,80,512]{2,1,0:T(8,128)S(1)}, f32[4,80,512]{2,1,0:T(8,128)}, u32[]{:S(2)}, u32[]{:S(2)}) collective-permute-start(f32[4,80,512]{2,1,0:T(8,128)S(1)} %collective-permute-done.6.refs_3_), channel_id=1, source_target_pairs={{16,0},{17,1},{18,2},{19,3},{20,4},{21,5},{22,6},{23,7},{24,8},{25... | collective-permute-start | bytes 1966088 | tf_op jit(solution)/shard_map/ppermute | solution.py:38
  76.1 3.1 %collective-permute-start.11 = (f32[1,1408]{1,0:T(1,128)S(1)}, f32[1,1408]{1,0:T(1,128)S(1)}, u32[]{:S(2)}, u32[]{:S(2)}) collective-permute-start(f32[1,1408]{1,0:T(1,128)S(1)} %get-tuple-element.15), channel_id=1, source_target_pairs={{16,0},{17,1},{18,2},{19,3},{20,4},{21,5},{22,6},{23,7},{24,8},{25... | collective-permute-start | bytes 16904 | tf_op jit(solution)/shard_map/ppermute | solution.py:38
  103.8 3.1 %collective-permute-start.12 = (f32[1,1408]{1,0:T(1,128)S(1)}, f32[1,1408]{1,0:T(1,128)S(1)}, u32[]{:S(2)}, u32[]{:S(2)}) collective-permute-start(f32[1,1408]{1,0:T(1,128)S(1)} %reduce_sum.12.sums), channel_id=1, source_target_pairs={{16,0},{17,1},{18,2},{19,3},{20,4},{21,5},{22,6},{23,7},{24,8},{25... | collective-permute-start | bytes 16904 | tf_op jit(solution)/shard_map/ppermute | solution.py:38
  117.7 5.1 %collective-permute-start.14 = (f32[2,4,88,512]{3,2,1,0:T(8,128)S(1)}, f32[2,4,88,512]{3,2,1,0:T(8,128)S(1)}, u32[]{:S(2)}, u32[]{:S(2)}) collective-permute-start(f32[2,4,88,512]{3,2,1,0:T(8,128)S(1)} %get-tuple-element.21), channel_id=1, source_target_pairs={{16,0},{17,1},{18,2},{19,3},{20,4},{21,5},{22,6},{23,7},{24,8},{25... | collective-permute-start | bytes 4325384 | tf_op jit(solution)/shard_map/ppermute | solution.py:38
  119.7 10.0 %collective-permute-start.13 = (f32[2,4,88,512]{3,2,1,0:T(8,128)}, f32[2,4,88,512]{3,2,1,0:T(8,128)S(1)}, u32[]{:S(2)}, u32[]{:S(2)}) collective-permute-start(f32[2,4,88,512]{3,2,1,0:T(8,128)} %get-tuple-element.19), channel_id=1, source_target_pairs={{16,0},{17,1},{18,2},{19,3},{20,4},{21,5},{22,6},{23,7},{24,8},{25... | collective-permute-start | bytes 4325384 | tf_op jit(solution)/shard_map/ppermute | solution.py:38
  123.2 9.7 %collective-permute-start.15 = (f32[2,88,512]{2,1,0:T(8,128)S(1)}, f32[2,88,512]{2,1,0:T(8,128)S(1)}, u32[]{:S(2)}, u32[]{:S(2)}) collective-permute-start(f32[2,88,512]{2,1,0:T(8,128)S(1)} %get-tuple-element.27), channel_id=1, source_target_pairs={{384,0},{385,1},{386,2},{387,3},{388,4},{389,5},{390,6},{391,7},{3... | collective-permute-start | bytes 1081352 | tf_op jit(solution)/shard_map/ppermute | solution.py:38
  125.1 9.8 %collective-permute-start.17 = (f32[2,88,512]{2,1,0:T(8,128)S(1)}, f32[2,88,512]{2,1,0:T(8,128)S(1)}, u32[]{:S(2)}, u32[]{:S(2)}) collective-permute-start(f32[2,88,512]{2,1,0:T(8,128)S(1)} %get-tuple-element.26), channel_id=1, source_target_pairs={{128,0},{129,1},{130,2},{131,3},{132,4},{133,5},{134,6},{135,7},{1... | collective-permute-start | bytes 1081352 | tf_op jit(solution)/shard_map/ppermute | solution.py:38
  133.0 13.5 %collective-permute-start.16 = (f32[4,88,512]{2,1,0:T(8,128)S(1)}, f32[4,88,512]{2,1,0:T(8,128)S(1)}, u32[]{:S(2)}, u32[]{:S(2)}) collective-permute-start(f32[4,88,512]{2,1,0:T(8,128)S(1)} %pad_maximum_fusion), channel_id=1, source_target_pairs={{384,0},{385,1},{386,2},{387,3},{388,4},{389,5},{390,6},{391,7},{3... | collective-permute-start | bytes 2162696 | tf_op jit(solution)/shard_map/ppermute | solution.py:38
  135.1 12.8 %collective-permute-start.18 = (f32[4,88,512]{2,1,0:T(8,128)S(1)}, f32[4,88,512]{2,1,0:T(8,128)S(1)}, u32[]{:S(2)}, u32[]{:S(2)}) collective-permute-start(f32[4,88,512]{2,1,0:T(8,128)S(1)} %pad_maximum_fusion.1), channel_id=1, source_target_pairs={{128,0},{129,1},{130,2},{131,3},{132,4},{133,5},{134,6},{135,7},{1... | collective-permute-start | bytes 2162696 | tf_op jit(solution)/shard_map/ppermute | solution.py:38
  148.1 31.2 %copy-start = (f32[40,512]{1,0:T(8,128)S(1)}, f32[40,512]{1,0:T(8,128)}, u32[]{:S(2)}) copy-start(f32[40,512]{1,0:T(8,128)} %packet.1) | copy-start | bytes 245764
  148.1 31.2 %copy-start.1 = (f32[40,512]{1,0:T(8,128)S(1)}, f32[40,512]{1,0:T(8,128)}, u32[]{:S(2)}) copy-start(f32[40,512]{1,0:T(8,128)} %header.1) | copy-start | bytes 245764
  148.1 16.4 %collective-permute-start.19 = (f32[88,512]{1,0:T(8,128)S(1)}, f32[88,512]{1,0:T(8,128)S(1)}, u32[]{:S(2)}, u32[]{:S(2)}) collective-permute-start(f32[88,512]{1,0:T(8,128)S(1)} %get-tuple-element.28), channel_id=1, source_target_pairs={{1,0},{0,1},{3,2},{2,3},{5,4},{4,5},{7,6},{6,7},{9,8},{8,9},{11,10... | collective-permute-start | bytes 540680 | tf_op jit(solution)/shard_map/ppermute | solution.py:38
  150.2 16.3 %collective-permute-start.21 = (f32[88,512]{1,0:T(8,128)S(1)}, f32[88,512]{1,0:T(8,128)S(1)}, u32[]{:S(2)}, u32[]{:S(2)}) collective-permute-start(f32[88,512]{1,0:T(8,128)S(1)} %get-tuple-element.29), channel_id=1, source_target_pairs={{1,0},{0,1},{3,2},{2,3},{5,4},{4,5},{7,6},{6,7},{9,8},{8,9},{11,10... | collective-permute-start | bytes 540680 | tf_op jit(solution)/shard_map/ppermute | solution.py:38
  164.6 11.4 %collective-permute-start.20 = (f32[88,512]{1,0:T(8,128)S(1)}, f32[88,512]{1,0:T(8,128)S(1)}, u32[]{:S(2)}, u32[]{:S(2)}) collective-permute-start(f32[88,512]{1,0:T(8,128)S(1)} %fusion.4), channel_id=1, source_target_pairs={{2,0},{3,1},{0,2},{1,3},{6,4},{7,5},{4,6},{5,7},{10,8},{11,9},{8,1... | collective-permute-start | bytes 540680 | tf_op jit(solution)/shard_map/ppermute | solution.py:38
  176.1 3.2 %collective-permute-start.22 = (f32[48,512]{1,0:T(8,128)S(1)}, f32[48,512]{1,0:T(8,128)S(1)}, u32[]{:S(2)}, u32[]{:S(2)}) collective-permute-start(f32[48,512]{1,0:T(8,128)S(1)} %slice.84), channel_id=1, source_target_pairs={{16,0},{17,1},{18,2},{19,3},{20,4},{21,5},{22,6},{23,7},{24,8},{25... | collective-permute-start | bytes 294920 | tf_op jit(solution)/shard_map/ppermute | solution.py:38
